TPU v7x, 32 devices: a whole 2x2x4 slice. The times are simulated.
32 devices in a mesh: groups: 2 (over x), rows: 16 (over z, y, core).
Axes of the slice: x: 2, y: 2, z: 4, core: 2. Of those that a mesh axis runs over, the one named last changes fastest.
Arguments:
- token_ids: int32 [1, 256], P(None, 'groups'), parts along dimension 1, may hold values from 0 to 32767
- parents: int32 [1, 8, 32], P(None, 'groups'), parts along dimension 1, may hold values from 0 to 31, as said below
- states: bfloat16 [256, 16, 128, 128], P(('groups', 'rows')), parts along dimension 0, may hold values from -1.75 to 1.75
- embed_table: bfloat16 [32768, 2048], P(None, 'rows'), may hold values from -6 to 6
- qkv_weight: bfloat16 [2048, 3, 2048], P(None, None, 'rows'), may hold values from -0.125 to 0.125
- gate_weight: float32 [16, 128], replicated, may hold values from -6 to 6
- gate_bias: float32 [16], replicated, may hold values from -2 to 3
- norm_gain: float32 [2048], replicated, may hold values from 0.1 to 1.9
- out_weight: bfloat16 [2048, 2048], P(None, 'rows'), may hold values from -0.125 to 0.125
Outputs:
- layer_out: bfloat16 [1, 256, 2048], P(None, 'groups', 'rows'), parts along dimension 1
- final_states: bfloat16 [256, 16, 128, 128], P(('groups', 'rows')), parts along dimension 0
There are 2 independent parts, one for each index of `groups`. A program takes and returns all parts, laid end to end along the dimension named above; an argument that names none is the same for every part. Nothing has to cross between parts.
Inputs may be any that keep to these rules, and one draw needn't show every extreme that they name: The 32 beams of a user fall into 4 aligned blocks of 8. In every step and for every user, at most 2 children of one block have parents in any one other block, and in every step some user has exactly 2 children of one block with parents in another block.
All inputs are finite; a program needn't handle non-finite values.
Results may differ from a plain program's by a relative error of at most 0.0074.
Values may be sent and summed in bfloat16 or wider, within the bound.
No kernel may reach another device: no remote copies, remote signals or barrier semaphores. Data moves between devices by JAX's collectives and lax.ppermute only.
A program may use at most 64 MiB of HBM per device.

v0:
```python
import math

import jax
import jax.numpy as jnp
from jax import lax
from jax.sharding import PartitionSpec as P

CAP = 2


def from_partner(block, axis, stride):
    count = lax.axis_size(axis)
    route = []
    for low in range(count):
        high = low | 1 << stride
        if high != low and high < count:
            route += [(low, high), (high, low)]
    return lax.ppermute(block, axis, route)


def outgoing(state_now, parent_list, member, row_local, partner):
    target = jnp.bitwise_xor(member, partner)
    children = lax.dynamic_slice_in_dim(parent_list, target * row_local, row_local, 0)
    needed = children // row_local == member
    rank_index = jnp.cumsum(needed.astype(jnp.int32)) - 1
    slot_ids = jnp.arange(CAP, dtype=jnp.int32)
    chosen = jnp.sum(
        jnp.where(
            needed[None, :] & (rank_index[None, :] == slot_ids[:, None]),
            (children % row_local)[None, :],
            0,
        ),
        axis=1,
    )
    return jnp.take(state_now, chosen, axis=0)


def route(state_now, parent_list, member, row_local):
    first_out = outgoing(state_now, parent_list, member, row_local, 1)
    second_out = outgoing(state_now, parent_list, member, row_local, 2)
    corner_out = outgoing(state_now, parent_list, member, row_local, 3)
    got_one = from_partner(first_out, "rows", 0)
    got_two = from_partner(second_out, "rows", 1)
    relayed = from_partner(corner_out, "rows", 0)
    got_three = from_partner(relayed, "rows", 1)
    own_list = lax.dynamic_slice_in_dim(parent_list, member * row_local, row_local, 0)
    source = own_list // row_local
    partner = jnp.bitwise_xor(source, member)
    slot_index = jnp.arange(row_local, dtype=jnp.int32)
    earlier = (source[:, None] == source[None, :]) & (slot_index[:, None] > slot_index[None, :])
    rank_index = jnp.sum(earlier.astype(jnp.int32), axis=1)
    position = jnp.where(
        partner == 0, own_list % row_local, row_local + (partner - 1) * CAP + rank_index
    )
    pooled = jnp.concatenate([state_now, got_one, got_two, got_three], 0)
    return jnp.take(pooled, position, axis=0)


def per_device(
    token_ids,
    parents,
    states,
    embed_table,
    qkv_weight,
    gate_weight,
    gate_bias,
    norm_gain,
    out_weight,
):
    row_local = states.shape[0]
    heads = states.shape[1]
    head_size = states.shape[2]
    width = heads * head_size
    column_local = embed_table.shape[1]
    row_total = token_ids.shape[1]
    device = lax.axis_index("rows")
    member = device % 4
    user_index = device // 4
    weight_flat = qkv_weight.reshape(qkv_weight.shape[0], 3 * column_local)
    local_columns = jnp.take(embed_table, token_ids, axis=0)
    every_proj = jnp.einsum(
        "...rc,cf->...rf",
        lax.all_gather(local_columns, "rows", axis=2, tiled=True),
        weight_flat,
        preferred_element_type=jnp.float32,
    )
    state_now = states
    step_proj = every_proj[0]
    projected = step_proj.astype(jnp.bfloat16).reshape(row_total, 3, column_local)
    mine = lax.all_to_all(projected, "rows", split_axis=0, concat_axis=2, tiled=True)
    queries = mine[:, 0].reshape(row_local, heads, head_size)
    key_float = mine[:, 1].reshape(row_local, heads, head_size).astype(jnp.float32)
    values = mine[:, 2].reshape(row_local, heads, head_size).astype(jnp.float32)
    gate_logit = jnp.sum(key_float * gate_weight, axis=-1) / math.sqrt(head_size) + gate_bias
    decay_rate = jax.nn.sigmoid(gate_logit)
    key_unit = key_float * lax.rsqrt(jnp.sum(key_float * key_float, axis=-1, keepdims=True) + 1e-06)
    parent_list = lax.dynamic_index_in_dim(parents[0], user_index, 0, keepdims=False)
    prior_state = route(state_now, parent_list, member, row_local)
    new_state = (
        decay_rate[:, :, None, None] * prior_state.astype(jnp.float32)
        + key_unit[:, :, :, None] * values[:, :, None, :]
    )
    state_now = new_state.astype(jnp.bfloat16)
    readout = jnp.einsum("rhd,rhde->rhe", queries, state_now, preferred_element_type=jnp.float32)
    scaled = readout * lax.rsqrt(jnp.mean(readout * readout, axis=-1, keepdims=True) + 1e-05)
    normed = (scaled.reshape(row_local, width) * norm_gain).astype(jnp.bfloat16)
    attention = jnp.dot(
        lax.all_gather(normed, "rows", axis=0, tiled=True),
        out_weight,
        preferred_element_type=jnp.float32,
    )
    outputs = [(local_columns[0].astype(jnp.float32) + attention).astype(jnp.bfloat16)]
    return (jnp.stack(outputs), state_now)


def solution(mesh):
    placed = (
        P(None, "groups"),
        P(None, "groups", None),
        P(("groups", "rows"), None, None, None),
        P(None, "rows"),
        P(None, None, "rows"),
        P(),
        P(),
        P(),
        P(None, "rows"),
    )
    return jax.shard_map(
        per_device,
        mesh=mesh,
        in_specs=placed,
        out_specs=(P(None, "groups", "rows"), P(("groups", "rows"), None, None, None)),
        check_vma=False,
    )
```

profile of v0, /device:TPU:1, one launch (start us, length us, event | category | flops | bytes accessed | tf_op | source)
XLA Modules:
  0.0 127.4 jit_solution(7853263627772895128)
XLA Ops:
  0.6 0.0 copy-start
  0.7 0.9 compare_convert_fusion.2
  1.6 0.2 reduce-window.25
  1.8 0.1 fusion.16
  2.0 2.9 %gather_fusion.3 = bf16[2,16,128,128]{3,2,1,0:T(8,128)(2,1)S(1)} fusion(bf16[8,16,128,128]{3,2,1,0:T(8,128)(2,1)} %param.13, s32[1024]{0:T(1024)S(1)} %pad_clamp_fusion.2), kind=kCustom, calls=%fused_computation.1.clone | custom fusion | bytes 2097160 | tf_op jit(solution)/shard_map/jit(_take)/gather | solution.py:35
  4.9 1.1 broadcast_select_fusion.1
  6.1 2.1 %collective-permute-start.1 = (bf16[2,16,128,128]{3,2,1,0:T(8,128)(2,1)}, bf16[2,16,128,128]{3,2,1,0:T(8,128)(2,1)}, u32[]{:S(2)}, u32[]{:S(2)}) collective-permute-start(bf16[2,16,128,128]{3,2,1,0:T(8,128)(2,1)} %broadcast_select_fusion.1), channel_id=1, source_target_pairs={{0,2},{2,0},{1,3},{3,1},{4,6},{6,4},{5,7},{7,5},{8,10},{10,8},{9,1... | collective-permute-start | bytes 3145736 | tf_op jit(solution)/shard_map/ppermute | solution.py:18
  8.1 0.2 reduce-window.24
  8.3 0.1 fusion.15
  8.5 0.0 copy-start.5
  8.5 2.9 %gather_fusion.2 = bf16[2,16,128,128]{3,2,1,0:T(8,128)(2,1)S(1)} fusion(bf16[8,16,128,128]{3,2,1,0:T(8,128)(2,1)} %param.13, s32[1024]{0:T(1024)S(1)} %pad_clamp_fusion.3), kind=kCustom, calls=%fused_computation.clone | custom fusion | bytes 2097160 | tf_op jit(solution)/shard_map/jit(_take)/gather | solution.py:35
  11.4 1.2 broadcast_select_fusion.2
  12.6 1.0 collective-permute-start
  13.6 0.2 reduce-window.26
  13.8 0.1 fusion.17
  14.0 2.9 %gather_fusion.4 = bf16[2,16,128,128]{3,2,1,0:T(8,128)(2,1)S(1)} fusion(bf16[8,16,128,128]{3,2,1,0:T(8,128)(2,1)} %param.13, s32[1024]{0:T(1024)S(1)} %pad_clamp_fusion.1), kind=kCustom, calls=%fused_computation.2.clone | custom fusion | bytes 2097160 | tf_op jit(solution)/shard_map/jit(_take)/gather | solution.py:35
  16.9 0.0 copy-start.2
  16.9 1.1 broadcast_select_fusion
  18.0 0.0 collective-permute-start.2
  18.0 0.0 copy-done.5
  18.1 5.1 %gather_fusion = bf16[128,128]{1,0:T(8,128)(2,1)S(1)} fusion(bf16[32768,128]{1,0:T(8,128)(2,1)} %param.14, s32[1024]{0:T(1024)S(1)} %pad_clamp_fusion.4), kind=kCustom, calls=%fused_computation.3 | custom fusion | bytes 66048 | tf_op jit(solution)/shard_map/jit(_take)/gather | solution.py:80
  23.2 0.1 bitcast_select_fusion
  23.3 26.4 %all_gather.6 = bf16[1,128,2048]{2,1,0:T(8,128)(2,1)S(1)} all-gather(bf16[1,128,128]{2,1,0:T(8,128)(2,1)S(1)} %bitcast_select_fusion), channel_id=1, replica_groups=mesh['groups'=2,'rows'=16] {'rows'}, dimensions={2}, use_global_device_ids=true | all-gather | bytes 557056 | tf_op jit(solution)/shard_map/all_gather | solution.py:83
  49.7 1.7 %copy.31 = bf16[2048,3,128]{0,2,1:T(8,128)(2,1)S(1)} copy(bf16[2048,3,128]{2,0,1:T(8,128)(2,1)} %param.15) | data formatting | bytes 3145728 | tf_op args[4]
  51.5 0.6 fusion.2
  52.1 0.7 copy.32
  52.8 3.5 %all-to-all-start = ((bf16[128,3,128]{2,1,0:T(4,128)(2,1)}), bf16[128,3,128]{2,1,0:T(4,128)(2,1)S(1)}, u32[]{:S(2)}, u32[]{:S(2)}) async-start(bf16[128,3,128]{2,1,0:T(4,128)(2,1)} %copy.32), calls=%async_computation | async-start | bytes 262144 | tf_op jit(solution)/shard_map/all_to_all | solution.py:90
  56.3 0.8 and_select_fusion.15
  57.0 0.2 convert_reduce_fusion
  57.3 0.0 collective-permute-done.2
  57.3 1.5 %collective-permute-start.3 = (bf16[2,16,128,128]{3,2,1,0:T(8,128)(2,1)}, bf16[2,16,128,128]{3,2,1,0:T(8,128)(2,1)S(1)}, u32[]{:S(2)}, u32[]{:S(2)}) collective-permute-start(bf16[2,16,128,128]{3,2,1,0:T(8,128)(2,1)} %collective-permute-done.2), channel_id=1, source_target_pairs={{0,2},{2,0},{1,3},{3,1},{4,6},{6,4},{5,7},{7,5},{8,10},{10,8},{9,1... | collective-permute-start | bytes 3145736 | tf_op jit(solution)/shard_map/ppermute | solution.py:18
  58.7 4.5 %all-to-all-done = bf16[128,3,128]{2,1,0:T(4,128)(2,1)S(1)} async-done(((bf16[128,3,128]{2,1,0:T(4,128)(2,1)}), bf16[128,3,128]{2,1,0:T(4,128)(2,1)S(1)}, u32[]{:S(2)}, u32[]{:S(2)}) %all-to-all-start) | async-done | bytes 98336 | tf_op jit(solution)/shard_map/all_to_all | solution.py:90
  63.3 0.1 fusion.8
  63.5 0.1 convert_multiply_fusion
  63.6 0.1 copy.34
  63.7 0.0 collective-permute-done.1
  63.7 0.0 collective-permute-done
  63.7 19.5 %collective-permute-done.3 = bf16[2,16,128,128]{3,2,1,0:T(8,128)(2,1)S(1)} collective-permute-done((bf16[2,16,128,128]{3,2,1,0:T(8,128)(2,1)}, bf16[2,16,128,128]{3,2,1,0:T(8,128)(2,1)S(1)}, u32[]{:S(2)}, u32[]{:S(2)}) %collective-permute-start.3) | collective-permute-done | bytes 1048608 | tf_op jit(solution)/shard_map/ppermute | solution.py:18
  83.2 8.1 %pad_maximum_fusion = bf16[14,16,128,128]{3,2,1,0:T(8,128)(2,1)} fusion(bf16[2,16,128,128]{3,2,1,0:T(8,128)(2,1)S(1)} %collective-permute-done.3, bf16[2,16,128,128]{3,2,1,0:T(8,128)(2,1)} %collective-permute-done.1, bf16[2,16,128,128]{3,2,1,0:T(8,128)(2,1)} %collective-permute-done, bf16[8,16,128,128]{3,2,1,0:T(8,128)(2,1)} %param.13), kind=kLoop, calls=%fused_computation.6 | loop fusion | flops 11010048 | bytes 14680064 | tf_op jit(solution)/shard_map/concatenate | solution.py:55
  91.3 6.2 %gather_fusion.1 = bf16[8,16,128,128]{3,2,1,0:T(8,128)(2,1)} fusion(bf16[14,16,128,128]{3,2,1,0:T(8,128)(2,1)} %pad_maximum_fusion, s32[1024]{0:T(1024)S(1)} %pad_clamp_fusion), kind=kCustom, calls=%fused_computation.4 | custom fusion | bytes 8388640 | tf_op jit(solution)/shard_map/jit(_take)/gather | solution.py:56
  97.4 4.6 %add_convert_fusion = bf16[8,16,128,128]{3,2,1,0:T(8,128)(2,1)S(1)} fusion(f32[8,16,128]{2,1,0:T(8,128)S(1)} %copy.36, f32[8,16,128]{2,1,0:T(8,128)S(1)} %copy.35, bf16[8,16,128,128]{3,2,1,0:T(8,128)(2,1)} %gather_fusion.1, f32[8,16]{1,0:T(8,128)S(1)} %add_divide_fusion, pred[8]{0:T(512)(128)(4,1)S(1)} %compare_and_fusion.3), kind=kLoop, calls=%fused_computation.5 | loop fusion | flops 12582912 | bytes 8520200 | tf_op jit(solution)/shard_map/convert_element_type | solution.py:103
  102.1 0.0 copy-start.1
  102.1 0.0 copy-start.3
  102.1 1.2 fusion.11
  103.3 0.1 multiply_reduce_fusion
  103.4 0.1 multiply_bitcast_fusion
  103.6 22.9 %all_gather.7 = bf16[128,2048]{1,0:T(8,128)(2,1)S(1)} all-gather(bf16[8,2048]{1,0:T(8,128)(2,1)S(1)} %fusion.10), channel_id=1, replica_groups=mesh['groups'=2,'rows'=16] {'rows'}, dimensions={0}, use_global_device_ids=true | all-gather | bytes 557056 | tf_op jit(solution)/shard_map/all_gather | solution.py:108
  126.5 0.9 fusion.6
  (37 shorter events, 0.4 us)
Async XLA Ops:
  0.6 125.8 %copy-start = (bf16[2048,128]{1,0:T(8,128)(2,1)S(1)}, bf16[2048,128]{1,0:T(8,128)(2,1)}, u32[]{:S(2)}) copy-start(bf16[2048,128]{1,0:T(8,128)(2,1)} %param.19) | copy-start | bytes 1572868
  6.1 57.6 %collective-permute-start.1 = (bf16[2,16,128,128]{3,2,1,0:T(8,128)(2,1)}, bf16[2,16,128,128]{3,2,1,0:T(8,128)(2,1)}, u32[]{:S(2)}, u32[]{:S(2)}) collective-permute-start(bf16[2,16,128,128]{3,2,1,0:T(8,128)(2,1)} %broadcast_select_fusion.1), channel_id=1, source_target_pairs={{0,2},{2,0},{1,3},{3,1},{4,6},{6,4},{5,7},{7,5},{8,10},{10,8},{9,1... | collective-permute-start | bytes 3145736 | tf_op jit(solution)/shard_map/ppermute | solution.py:18
  8.5 9.6 %copy-start.5 = (s32[1,128]{1,0:T(1,128)S(1)}, s32[1,128]{1,0:T(1,128)}, u32[]{:S(2)}) copy-start(s32[1,128]{1,0:T(1,128)} %param.11) | copy-start | bytes 1540
  12.6 51.1 %collective-permute-start = (bf16[2,16,128,128]{3,2,1,0:T(8,128)(2,1)}, bf16[2,16,128,128]{3,2,1,0:T(8,128)(2,1)}, u32[]{:S(2)}, u32[]{:S(2)}) collective-permute-start(bf16[2,16,128,128]{3,2,1,0:T(8,128)(2,1)} %broadcast_select_fusion.2), channel_id=1, source_target_pairs={{0,1},{1,0},{2,3},{3,2},{4,5},{5,4},{6,7},{7,6},{8,9},{9,8},{10,11... | collective-permute-start | bytes 3145736 | tf_op jit(solution)/shard_map/ppermute | solution.py:18
  16.9 46.4 %copy-start.2 = (f32[16,128]{1,0:T(8,128)S(1)}, f32[16,128]{1,0:T(8,128)}, u32[]{:S(2)}) copy-start(f32[16,128]{1,0:T(8,128)} %param.16) | copy-start | bytes 24580
  18.0 45.6 %copy-start.4 = (f32[16]{0:T(128)S(1)}, f32[16]{0:T(128)}, u32[]{:S(2)}) copy-start(f32[16]{0:T(128)} %param.17) | copy-start | bytes 196
  18.0 39.2 %collective-permute-start.2 = (bf16[2,16,128,128]{3,2,1,0:T(8,128)(2,1)}, bf16[2,16,128,128]{3,2,1,0:T(8,128)(2,1)}, u32[]{:S(2)}, u32[]{:S(2)}) collective-permute-start(bf16[2,16,128,128]{3,2,1,0:T(8,128)(2,1)} %broadcast_select_fusion), channel_id=1, source_target_pairs={{0,1},{1,0},{2,3},{3,2},{4,5},{5,4},{6,7},{7,6},{8,9},{9,8},{10,11... | collective-permute-start | bytes 3145736 | tf_op jit(solution)/shard_map/ppermute | solution.py:18
  52.8 10.4 %all-to-all-start = ((bf16[128,3,128]{2,1,0:T(4,128)(2,1)}), bf16[128,3,128]{2,1,0:T(4,128)(2,1)S(1)}, u32[]{:S(2)}, u32[]{:S(2)}) async-start(bf16[128,3,128]{2,1,0:T(4,128)(2,1)} %copy.32), calls=%async_computation | async-start | bytes 262144 | tf_op jit(solution)/shard_map/all_to_all | solution.py:90
  57.3 25.9 %collective-permute-start.3 = (bf16[2,16,128,128]{3,2,1,0:T(8,128)(2,1)}, bf16[2,16,128,128]{3,2,1,0:T(8,128)(2,1)S(1)}, u32[]{:S(2)}, u32[]{:S(2)}) collective-permute-start(bf16[2,16,128,128]{3,2,1,0:T(8,128)(2,1)} %collective-permute-done.2), channel_id=1, source_target_pairs={{0,2},{2,0},{1,3},{3,1},{4,6},{6,4},{5,7},{7,5},{8,10},{10,8},{9,1... | collective-permute-start | bytes 3145736 | tf_op jit(solution)/shard_map/ppermute | solution.py:18
  102.1 25.3 %copy-start.1 = (bf16[8,16,128,128]{3,2,1,0:T(8,128)(2,1)}, bf16[8,16,128,128]{3,2,1,0:T(8,128)(2,1)S(1)}, u32[]{:S(2)}) copy-start(bf16[8,16,128,128]{3,2,1,0:T(8,128)(2,1)S(1)} %add_convert_fusion) | copy-start | bytes 12582916
  102.1 1.4 %copy-start.3 = (f32[2048]{0:T(1024)S(1)}, f32[2048]{0:T(1024)}, u32[]{:S(2)}) copy-start(f32[2048]{0:T(1024)} %param.18) | copy-start | bytes 24580
where the time goes:
time: 128 us; the launch traced here: 127 us
  blocking collectives  49.4 us (39%)
  waiting for transfers between devices  24 us (19%)
  local copies, waits for them, and re-layouts  22.8 us (18%)
  other arithmetic  19.6 us (15%)
  starting transfers between devices  7.95 us (6%)
  matrix products  2.7 us (2%)
    all_gather x1, blocking collectives, per_device(): lax.all_gather(local_columns, 'rows', axis=2, tiled=True)  26.4 us
    all_gather x1, blocking collectives, per_device(): lax.all_gather(normed, 'rows', axis=0, tiled=True)  22.9 us
    ppermute x4, waiting for transfers between devices, from_partner(): return lax.ppermute(block, axis, route)  19.5 us
    gather x3, local copies, waits for them, and re-layouts, outgoing(): return jnp.take(state_now, chosen, axis=0)  8.82 us
    concatenate x1, other arithmetic, route(): pooled = jnp.concatenate([state_now, got_one, got_two, got_three], 0)  8.06 us
    gather x1, local copies, waits for them, and re-layouts, route(): return jnp.take(pooled, position, axis=0)  6.18 us
    gather x1, local copies, waits for them, and re-layouts, per_device(): local_columns = jnp.take(embed_table, token_ids, axis=0)  5.12 us
    convert_element_type x1, other arithmetic, per_device(): state_now = new_state.astype(jnp.bfloat16)  4.63 us
  transfers between devices with their start and end apart: 5, of which 2 were waited for; matrix products, arithmetic and copies ran while one was open for 15% of the time, Pallas kernels for 0%

commit v1 on v0

v1 whole, which is shorter than its diff:
```python
import functools
import math

import jax
import jax.numpy as jnp
from jax import lax
from jax.experimental import pallas as pl
from jax.experimental.pallas import tpu as pltpu
from jax.sharding import PartitionSpec as P

CAP = 2
TILE = 16
VMEM_BYTES = 48 * 1024 * 1024
WHOLE = pl.BlockSpec(memory_space=pltpu.VMEM)
SCALARS = pl.BlockSpec(memory_space=pltpu.SMEM)
PLACED = pl.BlockSpec(memory_space=pl.ANY)


def params():
    return pltpu.CompilerParams(vmem_limit_bytes=VMEM_BYTES)


def xor_permute(block, distance):
    count = lax.axis_size("rows")
    return lax.ppermute(block, "rows", [(i, i ^ distance) for i in range(count)])


def stage_plan(count):
    if count == 1:
        return []
    if count == 2:
        return [[1]]
    if count == 4:
        return [[2], [1]]
    plan = [[6], [4, 8, 12] if count >= 16 else [4]]
    bit = 16
    while bit < count:
        plan.append([bit])
        bit *= 2
    return plan + [[1]]


def plan_order(plan):
    order = [0]
    for stage in plan:
        order = [near ^ far for near in order for far in [0] + stage]
    return order


def gather_all(block, plan):
    gathered, order = block[None], [0]
    for stage in plan:
        gathered = jnp.concatenate([gathered] + [xor_permute(gathered, d) for d in stage], 0)
        order = [near ^ far for far in [0] + stage for near in order]
    return gathered, order


def exchange_all(pieces, plan):
    tail = pieces.shape[1:]
    lengths = tuple(len(stage) + 1 for stage in plan)
    held = pieces.reshape(lengths + tail)
    for axis, stage in enumerate(plan):
        parts = [lax.index_in_dim(held, 0, axis, keepdims=True)]
        for place, distance in enumerate(stage):
            parts.append(xor_permute(lax.index_in_dim(held, place + 1, axis, keepdims=True), distance))
        held = jnp.concatenate(parts, axis)
    return held.reshape((len(pieces),) + tail)


def fetch_kernel(token_ref, send_ref, low_ref, table_ref, states_ref, x_ref, y_ref, d_ref, c_ref, rows_ref, row_sem, state_sem):
    count = token_ref.shape[0]

    def start_row(r, carry):
        first = pl.multiple_of(token_ref[r] // TILE * TILE, TILE)
        pltpu.make_async_copy(
            table_ref.at[pl.ds(first, TILE)],
            rows_ref.at[pl.ds(pl.multiple_of(r * TILE, TILE), TILE)],
            row_sem,
        ).start()
        return carry

    lax.fori_loop(0, count, start_row, 0, unroll=8)
    copies = []
    for partner, out in ((2, y_ref), (3, d_ref), (1, c_ref)):
        for slot in range(CAP):
            place = (partner - 1) * CAP + slot
            copies.append(
                pltpu.make_async_copy(states_ref.at[send_ref[place]], out.at[slot], state_sem.at[place])
            )
            copies[-1].start()
    pltpu.make_async_copy(table_ref.at[pl.ds(0, count * TILE)], rows_ref, row_sem).wait()
    step = math.gcd(count, 128)
    for first in range(0, count, step):
        wanted = lax.broadcasted_iota(jnp.int32, (step, 1), 0) * TILE + low_ref[first : first + step, :]
        chosen = lax.broadcasted_iota(jnp.int32, (step, step * TILE), 1) == wanted
        x_ref[first : first + step, :] = jnp.dot(
            chosen.astype(jnp.float32).astype(jnp.bfloat16),
            rows_ref[first * TILE : (first + step) * TILE, :],
            preferred_element_type=jnp.float32,
        ).astype(jnp.bfloat16)
    for copy in copies:
        copy.wait()


def project_kernel(order, me_ref, x_ref, weight_ref, index_ref, out_ref):
    me = me_ref[0]
    columns = x_ref.shape[2]
    total = None
    for place, distance in enumerate(order):
        first = pl.multiple_of((me ^ distance) * columns, columns)
        term = jnp.dot(x_ref[place], weight_ref[pl.ds(first, columns), :], preferred_element_type=jnp.float32)
        total = term if total is None else total + term
    rounded = total.astype(jnp.bfloat16)
    shape = (index_ref.shape[0], rounded.shape[0])
    chosen = lax.broadcasted_iota(jnp.int32, shape, 1) == index_ref[...]
    out_ref[...] = jnp.dot(
        chosen.astype(jnp.float32).astype(jnp.bfloat16), rounded, preferred_element_type=jnp.float32
    ).astype(jnp.bfloat16)


def head_terms(piece, gate_row, bias, size):
    keys = piece[:, size : 2 * size].astype(jnp.float32)
    values = piece[:, 2 * size :].astype(jnp.float32)
    logit = jnp.sum(keys * gate_row, axis=-1, keepdims=True) / math.sqrt(size) + bias
    decay = 1.0 / (1.0 + jnp.exp(-logit))
    inverse = lax.rsqrt(jnp.sum(keys * keys, axis=-1, keepdims=True) + 1e-06)
    return keys, values, decay, inverse


def readout_kernel(
    own_rows, lane_ref, bias_ref, recv_ref, states_ref, near_ref, place_ref, gate_ref, gain_ref, out_ref, norm_ref
):
    step, block, size = pl.program_id(0), states_ref.shape[1], states_ref.shape[2]
    place = place_ref[...]
    for part in range(block):
        head = step * block + part
        piece = recv_ref[lane_ref[head]]
        keys, values, decay, inverse = head_terms(piece, gate_ref[pl.ds(head, 1), :], bias_ref[head], size)
        queries = piece[:, :size]
        query_float = queries.astype(jnp.float32)
        zero = jnp.zeros_like(query_float)
        prior_part = None
        for ref, first in ((states_ref, 0), (near_ref, own_rows)):
            count = ref.shape[0]
            spread = jnp.concatenate(
                [jnp.where(place == first + p, query_float, zero).astype(jnp.bfloat16) for p in range(count)], 1
            )
            term = jnp.dot(spread, ref[:, part].reshape(count * size, size), preferred_element_type=jnp.float32)
            prior_part = term if prior_part is None else prior_part + term
        overlap = jnp.sum(query_float * keys, axis=-1, keepdims=True) * inverse
        readout = decay * prior_part + overlap * values
        scale = lax.rsqrt(jnp.mean(readout * readout, axis=-1, keepdims=True) + 1e-05)
        norm_ref[head] = readout * scale * gain_ref[pl.ds(head, 1), :]

    @pl.when(step == pl.num_programs(0) - 1)
    def _():
        heads = norm_ref.shape[0]
        halves = []
        for first in (0, heads // 2):
            halves.append(jnp.concatenate([norm_ref[h] for h in range(first, first + heads // 2)], 1))
        foreign = own_rows + 2 * CAP
        out_ref[...] = jnp.concatenate(
            [half[:own_rows] for half in halves] + [half[own_rows:foreign] for half in halves], 0
        ).astype(jnp.bfloat16)


def output_kernel(x_ref, normed_ref, weight_ref, low_ref, high_ref, out_ref):
    half = normed_ref.shape[1]
    shape = (x_ref.shape[0], normed_ref.shape[0])
    total = x_ref[...].astype(jnp.float32)
    for part, index_ref in enumerate((low_ref, high_ref)):
        product = jnp.dot(
            normed_ref[...], weight_ref[part * half : (part + 1) * half, :], preferred_element_type=jnp.float32
        )
        chosen = (lax.broadcasted_iota(jnp.int32, shape, 1) == index_ref[...]).astype(jnp.float32)
        total = total + jnp.dot(
            chosen, product, preferred_element_type=jnp.float32, precision=lax.Precision.HIGHEST
        )
    out_ref[...] = total.astype(jnp.bfloat16)


def near_update_kernel(lane_ref, bias_ref, source_ref, recv_ref, states_ref, near_ref, gate_ref, out_ref):
    own_rows, block, size = states_ref.shape[0], states_ref.shape[1], states_ref.shape[2]
    step = pl.program_id(0)
    for part in range(block):
        head = step * block + part
        piece = recv_ref[lane_ref[head]]
        keys, values, decay, inverse = head_terms(piece, gate_ref[pl.ds(head, 1), :], bias_ref[head], size)
        turned = jnp.transpose(keys * inverse)
        for row in range(own_rows):

            def store(prior, row=row, part=part, turned=turned, values=values, decay=decay):
                fresh = decay[row : row + 1, :] * prior.astype(jnp.float32)
                fresh = fresh + turned[:, row : row + 1] * values[row : row + 1, :]
                out_ref[row, part] = fresh.astype(jnp.bfloat16)

            source = source_ref[row]

            @pl.when((source >= 0) & (source < own_rows))
            def _():
                store(states_ref[jnp.clip(source, 0, own_rows - 1), part])

            @pl.when(source >= own_rows)
            def _():
                store(near_ref[jnp.clip(source - own_rows, 0, near_ref.shape[0] - 1), part])


def far_update_kernel(
    block, lane_ref, bias_ref, child_ref, recv_ref, got_ref, gate_ref, old_ref, out_ref, in_ref, new_ref, in_sem, out_sem
):
    count, heads, size = got_ref.shape[0], got_ref.shape[1], got_ref.shape[2]
    chunks = heads // block

    def load(slot, chunk):
        span = pl.ds(chunk * block, block)
        return pltpu.make_async_copy(got_ref.at[slot, span], in_ref.at[slot, span], in_sem.at[slot, chunk])

    def save(slot, chunk):
        span = pl.ds(chunk * block, block)
        child = jnp.maximum(child_ref[slot], 0)
        return pltpu.make_async_copy(new_ref.at[slot, span], out_ref.at[child, span], out_sem.at[slot, chunk])

    def if_used(slot, action):
        @pl.when(child_ref[slot] >= 0)
        def _():
            action()

    for chunk in range(chunks):
        for slot in range(count):
            if_used(slot, load(slot, chunk).start)
    for chunk in range(chunks):
        for slot in range(count):

            def work(slot=slot, chunk=chunk):
                load(slot, chunk).wait()
                child = child_ref[slot]
                for head in range(chunk * block, (chunk + 1) * block):
                    piece = recv_ref[lane_ref[head]]
                    keys, values, decay, inverse = head_terms(piece, gate_ref[head : head + 1, :], bias_ref[head], size)
                    mine = lax.broadcasted_iota(jnp.int32, (keys.shape[0], 1), 0) == child
                    key_row = jnp.sum(jnp.where(mine, keys * inverse, 0.0), axis=0, keepdims=True)
                    value_row = jnp.sum(jnp.where(mine, values, 0.0), axis=0, keepdims=True)
                    decay_one = jnp.sum(jnp.where(mine, decay, 0.0), axis=0, keepdims=True)
                    turned = jnp.transpose(jnp.broadcast_to(key_row, (8, size)))[:, 0:1]
                    fresh = decay_one * in_ref[slot, head].astype(jnp.float32) + turned * value_row
                    new_ref[slot, head] = fresh.astype(jnp.bfloat16)
                save(slot, chunk).start()

            if_used(slot, work)
    for chunk in range(chunks):
        for slot in range(count):
            if_used(slot, save(slot, chunk).wait)


def per_device(
    token_ids,
    parents,
    states,
    embed_table,
    qkv_weight,
    gate_weight,
    gate_bias,
    norm_gain,
    out_weight,
):
    own_rows, heads, size = states.shape[0], states.shape[1], states.shape[2]
    width = heads * size
    columns = embed_table.shape[1]
    row_total = token_ids.shape[1]
    users, beam = parents.shape[1], parents.shape[2]
    blocks = beam // own_rows
    count = lax.axis_size("rows")
    me = lax.axis_index("rows").astype(jnp.int32)
    user, member = me // blocks, me % blocks
    plan = stage_plan(count)
    slots = own_rows + 4 * CAP
    state_slab = (CAP, heads, size, size)
    bf16, int32 = jnp.bfloat16, jnp.int32

    parent_block = (parents[0] // own_rows).reshape(users, blocks, own_rows)
    parent_row = (parents[0] % own_rows).reshape(users, blocks, own_rows)
    along = jnp.arange(own_rows, dtype=int32)
    same = parent_block[..., :, None] == parent_block[..., None, :]
    rank = jnp.sum((same & (along[None, :] < along[:, None])).astype(int32), axis=-1)
    block_ids = jnp.arange(blocks, dtype=int32)
    rank_ids = jnp.arange(CAP, dtype=int32)
    hit = (parent_block[:, :, None, None, :] == block_ids[:, None, None]) & (
        rank[:, :, None, None, :] == rank_ids[:, None]
    )
    child_at = jnp.sum(jnp.where(hit, along + 1, 0), axis=-1) - 1
    state_at = jnp.sum(jnp.where(hit, parent_row[:, :, None, None, :], 0), axis=-1)

    my_children = lax.dynamic_index_in_dim(child_at, user, 0, keepdims=False)
    my_states = lax.dynamic_index_in_dim(state_at, user, 0, keepdims=False)
    partners = member ^ jnp.arange(1, 4, dtype=int32)
    send = lax.dynamic_index_in_dim(my_states, member, 1, keepdims=False)[partners]

    tokens = token_ids[0]
    local_columns, y_out, d_out, c_out = pl.pallas_call(
        fetch_kernel,
        in_specs=[SCALARS, SCALARS, WHOLE, PLACED, PLACED],
        out_specs=[WHOLE, PLACED, PLACED, PLACED],
        out_shape=[jax.ShapeDtypeStruct((row_total, columns), bf16)] + [jax.ShapeDtypeStruct(state_slab, bf16)] * 3,
        scratch_shapes=[
            pltpu.VMEM((row_total * TILE, columns), bf16),
            pltpu.SemaphoreType.DMA,
            pltpu.SemaphoreType.DMA((3 * CAP,)),
        ],
        compiler_params=params(),
        name="fetch",
    )(tokens, send.reshape(-1), (tokens % TILE)[:, None], embed_table, states)
    y_got = xor_permute(y_out, 2)
    d_got = xor_permute(d_out, 3)
    near_got = xor_permute(c_out, 1)

    device_ids = me ^ jnp.array(plan_order(plan), int32)
    device_user, device_member = device_ids // blocks, device_ids % blocks
    own_list = device_ids[:, None] * own_rows + along
    foreign_lists = []
    for partner in (2, 3):
        child_block = device_member ^ partner
        child = child_at[device_user, child_block, device_member]
        row = (device_user * blocks + child_block)[:, None] * own_rows + child
        foreign_lists.append(jnp.where(child >= 0, row, -1))
    unused = jnp.full((count, 2 * CAP), -1, int32)
    row_list = jnp.concatenate([own_list] + foreign_lists + [unused], 1).reshape(count * slots, 1)

    every_input, order = gather_all(local_columns, plan)
    pieces = pl.pallas_call(
        functools.partial(project_kernel, order),
        in_specs=[SCALARS, WHOLE, WHOLE, WHOLE],
        out_specs=WHOLE,
        out_shape=jax.ShapeDtypeStruct((count * slots, 3 * columns), bf16),
        compiler_params=params(),
        name="project",
    )(me[None], every_input, qkv_weight.reshape(qkv_weight.shape[0], 3 * columns), row_list)
    received = exchange_all(pieces.reshape(count, slots, 3 * columns), plan)
    recv_order = plan_order(plan)
    places = jnp.array([recv_order.index(d) for d in range(count)], int32)
    lanes = places[jnp.arange(count, dtype=int32) ^ me]
    by_head = received
    if columns != size:
        by_head = jnp.take(received, lanes, axis=0).reshape(count, slots, 3, columns).transpose(1, 2, 0, 3)
        by_head = by_head.reshape(slots, 3, heads, size).transpose(2, 0, 1, 3).reshape(heads, slots, 3 * size)
        lanes = jnp.arange(heads, dtype=int32)

    my_parent_block = lax.dynamic_index_in_dim(parent_block, user, 0, keepdims=False)[member]
    my_parent_row = lax.dynamic_index_in_dim(parent_row, user, 0, keepdims=False)[member]
    my_rank = lax.dynamic_index_in_dim(rank, user, 0, keepdims=False)[member]
    away = my_parent_block ^ member
    source = jnp.where(away == 0, my_parent_row, jnp.where(away == 1, own_rows + my_rank, -1))
    foreign_places = []
    for partner in (2, 3):
        child = my_children[member ^ partner, member]
        foreign_places.append(jnp.where(child >= 0, my_states[member ^ partner, member], -1))
    place = jnp.concatenate([source] + foreign_places + [jnp.full((2 * CAP,), -1, int32)])[:, None]

    head_block = math.gcd(heads, 4)
    by_heads = lambda rows: pl.BlockSpec((rows, head_block, size, size), lambda i: (0, i, 0, 0))
    state_bytes = 2 * own_rows * heads * size * size
    normed = pl.pallas_call(
        functools.partial(readout_kernel, own_rows),
        grid=(heads // head_block,),
        in_specs=[SCALARS, SCALARS, WHOLE, by_heads(own_rows), by_heads(CAP), WHOLE, WHOLE, WHOLE],
        out_specs=WHOLE,
        out_shape=jax.ShapeDtypeStruct((2 * (own_rows + 2 * CAP), width // 2), bf16),
        scratch_shapes=[pltpu.VMEM((heads, slots, size), jnp.float32)],
        compiler_params=params(),
        name="readout",
    )(lanes, gate_bias, by_head, states, near_got, place, gate_weight, norm_gain.reshape(heads, size))

    near_done = pl.pallas_call(
        near_update_kernel,
        grid=(heads // head_block,),
        in_specs=[SCALARS, SCALARS, SCALARS, WHOLE, by_heads(own_rows), by_heads(CAP), WHOLE],
        out_specs=by_heads(own_rows),
        out_shape=jax.ShapeDtypeStruct(states.shape, bf16),
        compiler_params=params(),
        cost_estimate=pl.CostEstimate(flops=4 * state_bytes, bytes_accessed=3 * state_bytes, transcendentals=0),
        name="near_update",
    )(lanes, gate_bias, source, by_head, states, near_got, gate_weight)

    def far_update(before, got, children, name):
        chunk = math.gcd(heads, 4)
        return pl.pallas_call(
            functools.partial(far_update_kernel, chunk),
            in_specs=[SCALARS, SCALARS, SCALARS, WHOLE, PLACED, WHOLE, PLACED],
            out_specs=PLACED,
            out_shape=jax.ShapeDtypeStruct(states.shape, bf16),
            scratch_shapes=[
                pltpu.VMEM(state_slab, bf16),
                pltpu.VMEM(state_slab, bf16),
                pltpu.SemaphoreType.DMA((CAP, heads // chunk)),
                pltpu.SemaphoreType.DMA((CAP, heads // chunk)),
            ],
            input_output_aliases={6: 0},
            compiler_params=params(),
            cost_estimate=pl.CostEstimate(flops=state_bytes, bytes_accessed=state_bytes // 2, transcendentals=0),
            name=name,
        )(lanes, gate_bias, children, by_head, got, gate_weight, before)

    y_done = far_update(near_done, y_got, my_children[member, member ^ 2], "y_update")
    final = far_update(y_done, d_got, my_children[member, member ^ 3], "corner_update")

    every_normed, normed_order = gather_all(normed, plan)
    normed_rows = normed.shape[0]
    all_away = parent_block ^ block_ids[None, :, None]
    over_y = all_away >= 2
    user_ids = jnp.arange(users, dtype=int32)[:, None, None]
    holder = user_ids * blocks + jnp.where(over_y, parent_block, block_ids[None, :, None])
    place_of = jnp.array([normed_order.index(d) for d in range(count)], int32)
    base = (place_of[holder ^ me] * normed_rows).reshape(row_total, 1)
    foreign_slot = jnp.where(over_y, (all_away - 2) * CAP + rank, 0).reshape(row_total, 1)
    over_y = over_y.reshape(row_total, 1)
    own_slot = jnp.broadcast_to(along, (users, blocks, own_rows)).reshape(row_total, 1)
    low = base + jnp.where(over_y, 2 * own_rows + foreign_slot, own_slot)
    high = low + jnp.where(over_y, 2 * CAP, own_rows)
    layer_out = pl.pallas_call(
        output_kernel,
        in_specs=[WHOLE] * 5,
        out_specs=WHOLE,
        out_shape=jax.ShapeDtypeStruct((row_total, columns), bf16),
        compiler_params=params(),
        name="output",
    )(local_columns, every_normed.reshape(count * normed_rows, width // 2), out_weight, low, high)
    return (layer_out[None], final)


def solution(mesh):
    placed = (
        P(None, "groups"),
        P(None, "groups", None),
        P(("groups", "rows"), None, None, None),
        P(None, "rows"),
        P(None, None, "rows"),
        P(),
        P(),
        P(),
        P(None, "rows"),
    )
    return jax.shard_map(
        per_device,
        mesh=mesh,
        in_specs=placed,
        out_specs=(P(None, "groups", "rows"), P(("groups", "rows"), None, None, None)),
        check_vma=False,
    )
```

time: 128 us -> 136 us (1.062)
  the two profiles are of different devices: /device:TPU:1 before, /device:TPU:4 now
where the time goes in v1:
time: 136 us; the launch traced here: 135 us
  Pallas kernels  64.5 us (47%)
  local copies, waits for them, and re-layouts  28.6 us (21%)
  waiting for transfers between devices  18.5 us (14%)
  starting transfers between devices  18.4 us (14%)
  other arithmetic  3.41 us (3%)
    pallas_call x1, Pallas kernels, per_device(): pl.pallas_call(fetch_kernel, in_specs=[SCALARS, SCALARS, WHOLE, PLACED, P...  34.5 us
    ppermute x18, waiting for transfers between devices, xor_permute(): lax.ppermute(block, 'rows', [(i, i ^ distance) for i in range(count)])  18.5 us
    ppermute x18, starting transfers between devices, xor_permute(): lax.ppermute(block, 'rows', [(i, i ^ distance) for i in range(count)])  18.4 us
    unnamed x39, local copies, waits for them, and re-layouts  13.8 us
    pallas_call x2, Pallas kernels, far_update(): pl.pallas_call(functools.partial(far_update_kernel, chunk), in_specs=[SCA...  13.7 us
    pallas_call x1, Pallas kernels, per_device(): pl.pallas_call(near_update_kernel, grid=(heads // head_block,), in_specs=...  10.6 us
  transfers between devices with their start and end apart: 18, of which 8 were waited for; matrix products, arithmetic and copies ran while one was open for 15% of the time, Pallas kernels for 21%

profile of v1, /device:TPU:4, one launch (start us, length us, event | category | flops | bytes accessed | tf_op | source)
XLA Modules:
  0.0 134.5 jit_solution(12147480026613649969)
XLA Ops:
  0.7 0.8 squeeze.38
  1.5 0.8 squeeze.41
  2.9 1.2 fusion.1
  5.1 0.8 copy.50
  5.9 0.6 copy-done.6
  6.5 34.5 %fetch.1 = (bf16[128,128]{1,0:T(8,128)(2,1)S(1)}, bf16[2,16,128,128]{3,2,1,0:T(8,128)(2,1)S(1)}, bf16[2,16,128,128]{3,2,1,0:T(8,128)(2,1)S(1)}, bf16[2,16,128,128]{3,2,1,0:T(8,128)(2,1)}) custom-call(s32[128]{0:T(128)S(1)} %bitcast.48, s32[6]{0:T(128)S(1)} %reshape.573.send_ref, s32[128,1]{1,0:T(8,128)S(1)} %add_select_fusion.1.low_ref, ...), custom_call_target="tpu_custom_call" | custom-call | tf_op jit(solution)/shard_map/fetch/pallas_call | solution.py:299
  41.0 1.0 copy-done.7
  42.0 1.0 copy-done.8
  43.0 1.5 %collective-permute-start = (bf16[1,128,128]{2,1,0:T(8,128)(2,1)S(1)}, bf16[1,128,128]{2,1,0:T(8,128)(2,1)S(1)}, u32[]{:S(2)}, u32[]{:S(2)}) collective-permute-start(bf16[1,128,128]{2,1,0:T(8,128)(2,1)S(1)} %bitcast.44), channel_id=1, source_target_pairs={{0,6},{1,7},{2,4},{3,5},{4,2},{5,3},{6,0},{7,1},{8,14},{9,15},{10,... | collective-permute-start | bytes 98312 | tf_op jit(solution)/shard_map/ppermute | solution.py:25
  47.8 3.7 %collective-permute-start.3 = (bf16[2,128,128]{2,1,0:T(8,128)(2,1)S(1)}, bf16[2,128,128]{2,1,0:T(8,128)(2,1)S(1)}, u32[]{:S(2)}, u32[]{:S(2)}) collective-permute-start(bf16[2,128,128]{2,1,0:T(8,128)(2,1)S(1)} %pad_maximum_fusion.3), channel_id=1, source_target_pairs={{0,12},{1,13},{2,14},{3,15},{4,8},{5,9},{6,10},{7,11},{8,4},{9,5},... | collective-permute-start | bytes 196616 | tf_op jit(solution)/shard_map/ppermute | solution.py:25
  51.5 0.8 collective-permute-start.1
  52.9 3.1 %collective-permute-done.1 = bf16[2,128,128]{2,1,0:T(8,128)(2,1)S(1)} collective-permute-done((bf16[2,128,128]{2,1,0:T(8,128)(2,1)S(1)}, bf16[2,128,128]{2,1,0:T(8,128)(2,1)S(1)}, u32[]{:S(2)}, u32[]{:S(2)}) %collective-permute-start.1) | collective-permute-done | bytes 65568 | tf_op jit(solution)/shard_map/ppermute | solution.py:25
  57.1 0.6 constant_dynamic-update-slice_fusion.1
  57.7 0.6 constant_dynamic-update-slice_fusion
  58.6 1.6 %copy.53 = bf16[2048,3,128]{0,2,1:T(8,128)(2,1)} copy(bf16[2048,3,128]{2,0,1:T(8,128)(2,1)S(1)} %copy-done.11) | data formatting | bytes 3145728 | tf_op args[4]
  60.2 1.9 %copy.55.weight_ref = bf16[2048,384]{1,0:T(8,128)(2,1)S(1)} copy(bf16[2048,384]{0,1:T(8,128)(2,1)} %bitcast.49) | data formatting | bytes 3145728 | tf_op jit(solution)/shard_map/reshape | solution.py:336
  62.2 1.0 constant_dynamic-update-slice_fusion.5.x_ref
  63.1 0.8 project.1
  64.0 1.7 %collective-permute-start.5 = (bf16[1,4,2,16,384]{4,3,2,1,0:T(8,128)(2,1)S(1)}, bf16[1,4,2,16,384]{4,3,2,1,0:T(8,128)(2,1)S(1)}, u32[]{:S(2)}, u32[]{:S(2)}) collective-permute-start(bf16[1,4,2,16,384]{4,3,2,1,0:T(8,128)(2,1)S(1)} %bitcast.51), channel_id=1, source_target_pairs={{0,6},{1,7},{2,4},{3,5},{4,2},{5,3},{6,0},{7,1},{8,14},{9,15},{10,... | collective-permute-start | bytes 294920 | tf_op jit(solution)/shard_map/ppermute | solution.py:25
  66.2 4.1 %collective-permute-done.5 = bf16[1,4,2,16,384]{4,3,2,1,0:T(8,128)(2,1)S(1)} collective-permute-done((bf16[1,4,2,16,384]{4,3,2,1,0:T(8,128)(2,1)S(1)}, bf16[1,4,2,16,384]{4,3,2,1,0:T(8,128)(2,1)S(1)}, u32[]{:S(2)}, u32[]{:S(2)}) %collective-permute-start.5) | collective-permute-done | bytes 98336 | tf_op jit(solution)/shard_map/ppermute | solution.py:25
  70.3 0.8 collective-permute-start.6
  71.2 2.9 %collective-permute-start.8 = (bf16[2,1,2,16,384]{4,3,2,1,0:T(8,128)(2,1)S(1)}, bf16[2,1,2,16,384]{4,3,2,1,0:T(8,128)(2,1)S(1)}, u32[]{:S(2)}, u32[]{:S(2)}) collective-permute-start(bf16[2,1,2,16,384]{4,3,2,1,0:T(8,128)(2,1)S(1)} %get-tuple-element.21), channel_id=1, source_target_pairs={{0,12},{1,13},{2,14},{3,15},{4,8},{5,9},{6,10},{7,11},{8,4},{9,5},... | collective-permute-start | bytes 147464 | tf_op jit(solution)/shard_map/ppermute | solution.py:25
  74.1 0.7 reduce_sum.33
  74.8 0.7 squeeze.45
  75.6 0.7 xor.128
  76.4 0.7 reshape.647
  77.1 1.0 collective-permute-start.17
  78.1 1.0 collective-permute-done.7
  79.3 0.7 gather_fusion.1
  80.0 1.2 gather_fusion.4
  81.3 2.2 %copy-done = bf16[8,16,128,128]{3,2,1,0:T(8,128)(2,1)S(1)} copy-done((bf16[8,16,128,128]{3,2,1,0:T(8,128)(2,1)S(1)}, bf16[8,16,128,128]{3,2,1,0:T(8,128)(2,1)}, u32[]{:S(2)}) %copy-start) | copy-done | bytes 4194328
  83.5 2.6 %readout.1 = bf16[24,1024]{1,0:T(8,128)(2,1)S(1)} custom-call(s32[16]{0:T(128)S(1)} %gather_fusion.1, f32[16]{0:T(128)S(1)} %copy-done.5, bf16[16,16,384]{2,1,0:T(8,128)(2,1)S(1)} %bitcast.37, bf16[8,16,128,128]{3,2,1,0:T(8,128)(2,1)S(1)} %copy-done, bf16[2,16,128,128]{3,2,1,0:T(8,128)(2,1)S(1)} %collective-permute-done.10.near_ref, ...), custom_call_target="tpu_custom_call" | custom-call | tf_op jit(solution)/shard_map/readout/pallas_call | solution.py:361
  86.1 1.0 collective-permute-start.11
  87.7 3.6 %collective-permute-done.11 = bf16[1,24,1024]{2,1,0:T(8,128)(2,1)S(1)} collective-permute-done((bf16[1,24,1024]{2,1,0:T(8,128)(2,1)S(1)}, bf16[1,24,1024]{2,1,0:T(8,128)(2,1)S(1)}, u32[]{:S(2)}, u32[]{:S(2)}) %collective-permute-start.11) | collective-permute-done | bytes 49184 | tf_op jit(solution)/shard_map/ppermute | solution.py:25
  91.3 2.2 %collective-permute-start.14 = (bf16[2,24,1024]{2,1,0:T(8,128)(2,1)S(1)}, bf16[2,24,1024]{2,1,0:T(8,128)(2,1)S(1)}, u32[]{:S(2)}, u32[]{:S(2)}) collective-permute-start(bf16[2,24,1024]{2,1,0:T(8,128)(2,1)S(1)} %pad_maximum_fusion.2), channel_id=1, source_target_pairs={{0,12},{1,13},{2,14},{3,15},{4,8},{5,9},{6,10},{7,11},{8,4},{9,5},... | collective-permute-start | bytes 294920 | tf_op jit(solution)/shard_map/ppermute | solution.py:25
  93.7 2.1 %collective-permute-start.12 = (bf16[2,24,1024]{2,1,0:T(8,128)(2,1)S(1)}, bf16[2,24,1024]{2,1,0:T(8,128)(2,1)S(1)}, u32[]{:S(2)}, u32[]{:S(2)}) collective-permute-start(bf16[2,24,1024]{2,1,0:T(8,128)(2,1)S(1)} %pad_maximum_fusion.2), channel_id=1, source_target_pairs={{0,4},{1,5},{2,6},{3,7},{4,0},{5,1},{6,2},{7,3},{8,12},{9,13},{10,... | collective-permute-start | bytes 294920 | tf_op jit(solution)/shard_map/ppermute | solution.py:25
  96.4 3.7 %collective-permute-done.12 = bf16[2,24,1024]{2,1,0:T(8,128)(2,1)S(1)} collective-permute-done((bf16[2,24,1024]{2,1,0:T(8,128)(2,1)S(1)}, bf16[2,24,1024]{2,1,0:T(8,128)(2,1)S(1)}, u32[]{:S(2)}, u32[]{:S(2)}) %collective-permute-start.12) | collective-permute-done | bytes 98336 | tf_op jit(solution)/shard_map/ppermute | solution.py:25
  100.1 0.7 constant_dynamic-update-slice_fusion.13
  100.8 1.8 %collective-permute-done.13 = bf16[2,24,1024]{2,1,0:T(8,128)(2,1)S(1)} collective-permute-done((bf16[2,24,1024]{2,1,0:T(8,128)(2,1)S(1)}, bf16[2,24,1024]{2,1,0:T(8,128)(2,1)S(1)}, u32[]{:S(2)}, u32[]{:S(2)}) %collective-permute-start.13) | collective-permute-done | bytes 98336 | tf_op jit(solution)/shard_map/ppermute | solution.py:25
  102.6 0.7 constant_dynamic-update-slice_fusion.12
  103.2 0.6 constant_dynamic-update-slice_fusion.11
  103.9 0.7 copy.67
  104.6 1.0 select_add_fusion
  105.7 2.2 %copy-done.1 = bf16[8,16,128,128]{3,2,1,0:T(8,128)(2,1)S(1)} copy-done((bf16[8,16,128,128]{3,2,1,0:T(8,128)(2,1)S(1)}, bf16[8,16,128,128]{3,2,1,0:T(8,128)(2,1)}, u32[]{:S(2)}) %copy-start.1) | copy-done | bytes 4194328
  107.8 10.6 %near_update.1.old_ref = bf16[8,16,128,128]{3,2,1,0:T(8,128)(2,1)} custom-call(s32[16]{0:T(128)S(1)} %gather_fusion.1, f32[16]{0:T(128)S(1)} %copy-done.5, s32[8]{0:T(128)S(1)} %fusion.12.source_ref, bf16[16,16,384]{2,1,0:T(8,128)(2,1)S(1)} %bitcast.38, bf16[8,16,128,128]{3,2,1,0:T(8,128)(2,1)S(1)} %copy-done.1, ...), custom_call_target="tpu_custom_call" | custom-call | flops 16777216 | bytes 12582912 | tf_op jit(solution)/shard_map/near_update/pallas_call | solution.py:372
  118.5 6.6 %y_update.1.old_ref = bf16[8,16,128,128]{3,2,1,0:T(8,128)(2,1)} custom-call(s32[16]{0:T(128)S(1)} %gather_fusion.1, f32[16]{0:T(128)S(1)} %copy-done.5, s32[2]{0:T(128)S(1)} %get-tuple-element.41.child_ref, bf16[16,16,384]{2,1,0:T(8,128)(2,1)S(1)} %bitcast.39, ...), custom_call_target="tpu_custom_call", output_to_operand_aliasing={{}: (6, {})} | custom-call | flops 4194304 | bytes 2097152 | tf_op jit(solution)/shard_map/y_update/pallas_call | solution.py:385
  125.1 7.1 %corner_update.1 = bf16[8,16,128,128]{3,2,1,0:T(8,128)(2,1)} custom-call(s32[16]{0:T(128)S(1)} %gather_fusion.1, f32[16]{0:T(128)S(1)} %copy-done.5, s32[2]{0:T(128)S(1)} %get-tuple-element.42.child_ref, bf16[16,16,384]{2,1,0:T(8,128)(2,1)S(1)} %bitcast.40, ...), custom_call_target="tpu_custom_call", output_to_operand_aliasing={{}: (6, {})} | custom-call | flops 4194304 | bytes 2097152 | tf_op jit(solution)/shard_map/corner_update/pallas_call | solution.py:385
  132.3 2.2 %output.1 = bf16[128,128]{1,0:T(8,128)(2,1)} custom-call(bf16[128,128]{1,0:T(8,128)(2,1)S(1)} %get-tuple-element.6.x_ref, bf16[384,1024]{1,0:T(8,128)(2,1)S(1)} %bitcast.41, bf16[2048,128]{1,0:T(8,128)(2,1)S(1)} %copy-done.2, s32[128,1]{1,0:T(8,128)S(1)} %get-tuple-element.13.low_ref, s32[128,1]{1,0:T(8,128)S(1)} %get-tuple-element.12.high_ref), custom_call_target="tpu_custom_call" | custom-call | tf_op jit(solution)/shard_map/output/pallas_call | solution.py:418
  (96 shorter events, 9.1 us)
Async XLA Ops:
  5.9 0.7 copy-start.6
  6.5 38.7 %copy-start.13 = (s32[16]{0:T(128)S(1)}, s32[16]{0:T(128)}, u32[]{:S(2)}) copy-start(s32[16]{0:T(128)} %constant.336.clone) | copy-start | bytes 196
  6.5 52.1 %copy-start.11 = (bf16[2048,3,128]{2,0,1:T(8,128)(2,1)S(1)}, bf16[2048,3,128]{2,0,1:T(8,128)(2,1)}, u32[]{:S(2)}) copy-start(bf16[2048,3,128]{2,0,1:T(8,128)(2,1)} %param.16) | copy-start | bytes 4718596
  41.0 1.0 copy-start.7
  42.0 1.0 copy-start.8
  43.0 4.8 %collective-permute-start = (bf16[1,128,128]{2,1,0:T(8,128)(2,1)S(1)}, bf16[1,128,128]{2,1,0:T(8,128)(2,1)S(1)}, u32[]{:S(2)}, u32[]{:S(2)}) collective-permute-start(bf16[1,128,128]{2,1,0:T(8,128)(2,1)S(1)} %bitcast.44), channel_id=1, source_target_pairs={{0,6},{1,7},{2,4},{3,5},{4,2},{5,3},{6,0},{7,1},{8,14},{9,15},{10,... | collective-permute-start | bytes 98312 | tf_op jit(solution)/shard_map/ppermute | solution.py:25
  44.5 36.7 %collective-permute-start.10 = (bf16[2,16,128,128]{3,2,1,0:T(8,128)(2,1)}, bf16[2,16,128,128]{3,2,1,0:T(8,128)(2,1)S(1)}, u32[]{:S(2)}, u32[]{:S(2)}) collective-permute-start(bf16[2,16,128,128]{3,2,1,0:T(8,128)(2,1)} %get-tuple-element.7), channel_id=1, source_target_pairs={{0,1},{1,0},{2,3},{3,2},{4,5},{5,4},{6,7},{7,6},{8,9},{9,8},{10,11... | collective-permute-start | bytes 3145736 | tf_op jit(solution)/shard_map/ppermute | solution.py:25
  47.8 9.9 %collective-permute-start.3 = (bf16[2,128,128]{2,1,0:T(8,128)(2,1)S(1)}, bf16[2,128,128]{2,1,0:T(8,128)(2,1)S(1)}, u32[]{:S(2)}, u32[]{:S(2)}) collective-permute-start(bf16[2,128,128]{2,1,0:T(8,128)(2,1)S(1)} %pad_maximum_fusion.3), channel_id=1, source_target_pairs={{0,12},{1,13},{2,14},{3,15},{4,8},{5,9},{6,10},{7,11},{8,4},{9,5},... | collective-permute-start | bytes 196616 | tf_op jit(solution)/shard_map/ppermute | solution.py:25
  51.5 5.6 %collective-permute-start.2 = (bf16[2,128,128]{2,1,0:T(8,128)(2,1)S(1)}, bf16[2,128,128]{2,1,0:T(8,128)(2,1)S(1)}, u32[]{:S(2)}, u32[]{:S(2)}) collective-permute-start(bf16[2,128,128]{2,1,0:T(8,128)(2,1)S(1)} %pad_maximum_fusion.3), channel_id=1, source_target_pairs={{0,8},{1,9},{2,10},{3,11},{4,12},{5,13},{6,14},{7,15},{8,0},{9,1},... | collective-permute-start | bytes 196616 | tf_op jit(solution)/shard_map/ppermute | solution.py:25
  51.5 4.5 %collective-permute-start.1 = (bf16[2,128,128]{2,1,0:T(8,128)(2,1)S(1)}, bf16[2,128,128]{2,1,0:T(8,128)(2,1)S(1)}, u32[]{:S(2)}, u32[]{:S(2)}) collective-permute-start(bf16[2,128,128]{2,1,0:T(8,128)(2,1)S(1)} %pad_maximum_fusion.3), channel_id=1, source_target_pairs={{0,4},{1,5},{2,6},{3,7},{4,0},{5,1},{6,2},{7,3},{8,12},{9,13},{10,... | collective-permute-start | bytes 196616 | tf_op jit(solution)/shard_map/ppermute | solution.py:25
  58.4 3.8 %collective-permute-start.4 = (bf16[8,128,128]{2,1,0:T(8,128)(2,1)}, bf16[8,128,128]{2,1,0:T(8,128)(2,1)}, u32[]{:S(2)}, u32[]{:S(2)}) collective-permute-start(bf16[8,128,128]{2,1,0:T(8,128)(2,1)} %get-tuple-element.31), channel_id=1, source_target_pairs={{0,1},{1,0},{2,3},{3,2},{4,5},{5,4},{6,7},{7,6},{8,9},{9,8},{10,11... | collective-permute-start | bytes 786440 | tf_op jit(solution)/shard_map/ppermute | solution.py:25
  60.2 14.6 %copy-start.12 = (s32[1,4,32]{2,1,0:T(4,128)S(1)}, s32[1,4,32]{2,1,0:T(4,128)}, u32[]{:S(2)}) copy-start(s32[1,4,32]{2,1,0:T(4,128)} %param.13) | copy-start | bytes 1540
  60.2 19.0 %copy-start.10 = (s32[16]{0:T(128)S(1)}, s32[16]{0:T(128)}, u32[]{:S(2)}) copy-start(s32[16]{0:T(128)} %constant.337.clone) | copy-start | bytes 196
  60.2 19.7 %copy-start.9 = (s32[16]{0:T(128)S(1)}, s32[16]{0:T(128)}, u32[]{:S(2)}) copy-start(s32[16]{0:T(128)} %constant.338.clone) | copy-start | bytes 196
  64.0 6.3 %collective-permute-start.5 = (bf16[1,4,2,16,384]{4,3,2,1,0:T(8,128)(2,1)S(1)}, bf16[1,4,2,16,384]{4,3,2,1,0:T(8,128)(2,1)S(1)}, u32[]{:S(2)}, u32[]{:S(2)}) collective-permute-start(bf16[1,4,2,16,384]{4,3,2,1,0:T(8,128)(2,1)S(1)} %bitcast.51), channel_id=1, source_target_pairs={{0,6},{1,7},{2,4},{3,5},{4,2},{5,3},{6,0},{7,1},{8,14},{9,15},{10,... | collective-permute-start | bytes 294920 | tf_op jit(solution)/shard_map/ppermute | solution.py:25
  65.7 59.4 %collective-permute-start.16 = (bf16[2,16,128,128]{3,2,1,0:T(8,128)(2,1)}, bf16[2,16,128,128]{3,2,1,0:T(8,128)(2,1)S(1)}, u32[]{:S(2)}, u32[]{:S(2)}) collective-permute-start(bf16[2,16,128,128]{3,2,1,0:T(8,128)(2,1)} %copy-done.7), channel_id=1, source_target_pairs={{0,3},{1,2},{2,1},{3,0},{4,7},{5,6},{6,5},{7,4},{8,11},{9,10},{10,... | collective-permute-start | bytes 3145736 | tf_op jit(solution)/shard_map/ppermute | solution.py:25
  70.3 6.7 %collective-permute-start.6 = (bf16[2,1,2,16,384]{4,3,2,1,0:T(8,128)(2,1)S(1)}, bf16[2,1,2,16,384]{4,3,2,1,0:T(8,128)(2,1)S(1)}, u32[]{:S(2)}, u32[]{:S(2)}) collective-permute-start(bf16[2,1,2,16,384]{4,3,2,1,0:T(8,128)(2,1)S(1)} %get-tuple-element.20), channel_id=1, source_target_pairs={{0,4},{1,5},{2,6},{3,7},{4,0},{5,1},{6,2},{7,3},{8,12},{9,13},{10,... | collective-permute-start | bytes 147464 | tf_op jit(solution)/shard_map/ppermute | solution.py:25
  71.2 7.0 %collective-permute-start.8 = (bf16[2,1,2,16,384]{4,3,2,1,0:T(8,128)(2,1)S(1)}, bf16[2,1,2,16,384]{4,3,2,1,0:T(8,128)(2,1)S(1)}, u32[]{:S(2)}, u32[]{:S(2)}) collective-permute-start(bf16[2,1,2,16,384]{4,3,2,1,0:T(8,128)(2,1)S(1)} %get-tuple-element.21), channel_id=1, source_target_pairs={{0,12},{1,13},{2,14},{3,15},{4,8},{5,9},{6,10},{7,11},{8,4},{9,5},... | collective-permute-start | bytes 147464 | tf_op jit(solution)/shard_map/ppermute | solution.py:25
  74.1 5.0 %collective-permute-start.7 = (bf16[2,1,2,16,384]{4,3,2,1,0:T(8,128)(2,1)S(1)}, bf16[2,1,2,16,384]{4,3,2,1,0:T(8,128)(2,1)S(1)}, u32[]{:S(2)}, u32[]{:S(2)}) collective-permute-start(bf16[2,1,2,16,384]{4,3,2,1,0:T(8,128)(2,1)S(1)} %get-tuple-element.22), channel_id=1, source_target_pairs={{0,8},{1,9},{2,10},{3,11},{4,12},{5,13},{6,14},{7,15},{8,0},{9,1},... | collective-permute-start | bytes 147464 | tf_op jit(solution)/shard_map/ppermute | solution.py:25
  77.1 41.4 %collective-permute-start.17 = (bf16[2,16,128,128]{3,2,1,0:T(8,128)(2,1)}, bf16[2,16,128,128]{3,2,1,0:T(8,128)(2,1)}, u32[]{:S(2)}, u32[]{:S(2)}) collective-permute-start(bf16[2,16,128,128]{3,2,1,0:T(8,128)(2,1)} %copy-done.8), channel_id=1, source_target_pairs={{0,2},{1,3},{2,0},{3,1},{4,6},{5,7},{6,4},{7,5},{8,10},{9,11},{10,... | collective-permute-start | bytes 3145736 | tf_op jit(solution)/shard_map/ppermute | solution.py:25
  79.2 2.0 %collective-permute-start.9 = (bf16[2,4,1,16,384]{4,3,2,1,0:T(8,128)(2,1)S(1)}, bf16[2,4,1,16,384]{4,3,2,1,0:T(8,128)(2,1)S(1)}, u32[]{:S(2)}, u32[]{:S(2)}) collective-permute-start(bf16[2,4,1,16,384]{4,3,2,1,0:T(8,128)(2,1)S(1)} %get-tuple-element.18), channel_id=1, source_target_pairs={{0,1},{1,0},{2,3},{3,2},{4,5},{5,4},{6,7},{7,6},{8,9},{9,8},{10,11... | collective-permute-start | bytes 294920 | tf_op jit(solution)/shard_map/ppermute | solution.py:25
  79.9 1.3 copy-start.3
  79.9 1.3 copy-start.4
  80.0 1.3 copy-start.5
  81.3 2.2 %copy-start = (bf16[8,16,128,128]{3,2,1,0:T(8,128)(2,1)S(1)}, bf16[8,16,128,128]{3,2,1,0:T(8,128)(2,1)}, u32[]{:S(2)}) copy-start(bf16[8,16,128,128]{3,2,1,0:T(8,128)(2,1)} %states_ref.5) | copy-start | bytes 12582916
  86.1 5.2 %collective-permute-start.11 = (bf16[1,24,1024]{2,1,0:T(8,128)(2,1)S(1)}, bf16[1,24,1024]{2,1,0:T(8,128)(2,1)S(1)}, u32[]{:S(2)}, u32[]{:S(2)}) collective-permute-start(bf16[1,24,1024]{2,1,0:T(8,128)(2,1)S(1)} %bitcast.42), channel_id=1, source_target_pairs={{0,6},{1,7},{2,4},{3,5},{4,2},{5,3},{6,0},{7,1},{8,14},{9,15},{10,... | collective-permute-start | bytes 147464 | tf_op jit(solution)/shard_map/ppermute | solution.py:25
  91.3 11.9 %collective-permute-start.14 = (bf16[2,24,1024]{2,1,0:T(8,128)(2,1)S(1)}, bf16[2,24,1024]{2,1,0:T(8,128)(2,1)S(1)}, u32[]{:S(2)}, u32[]{:S(2)}) collective-permute-start(bf16[2,24,1024]{2,1,0:T(8,128)(2,1)S(1)} %pad_maximum_fusion.2), channel_id=1, source_target_pairs={{0,12},{1,13},{2,14},{3,15},{4,8},{5,9},{6,10},{7,11},{8,4},{9,5},... | collective-permute-start | bytes 294920 | tf_op jit(solution)/shard_map/ppermute | solution.py:25
  93.5 9.1 %collective-permute-start.13 = (bf16[2,24,1024]{2,1,0:T(8,128)(2,1)S(1)}, bf16[2,24,1024]{2,1,0:T(8,128)(2,1)S(1)}, u32[]{:S(2)}, u32[]{:S(2)}) collective-permute-start(bf16[2,24,1024]{2,1,0:T(8,128)(2,1)S(1)} %pad_maximum_fusion.2), channel_id=1, source_target_pairs={{0,8},{1,9},{2,10},{3,11},{4,12},{5,13},{6,14},{7,15},{8,0},{9,1},... | collective-permute-start | bytes 294920 | tf_op jit(solution)/shard_map/ppermute | solution.py:25
  93.7 6.4 %collective-permute-start.12 = (bf16[2,24,1024]{2,1,0:T(8,128)(2,1)S(1)}, bf16[2,24,1024]{2,1,0:T(8,128)(2,1)S(1)}, u32[]{:S(2)}, u32[]{:S(2)}) collective-permute-start(bf16[2,24,1024]{2,1,0:T(8,128)(2,1)S(1)} %pad_maximum_fusion.2), channel_id=1, source_target_pairs={{0,4},{1,5},{2,6},{3,7},{4,0},{5,1},{6,2},{7,3},{8,12},{9,13},{10,... | collective-permute-start | bytes 294920 | tf_op jit(solution)/shard_map/ppermute | solution.py:25
  103.9 28.4 %collective-permute-start.15 = (bf16[8,24,1024]{2,1,0:T(8,128)(2,1)}, bf16[8,24,1024]{2,1,0:T(8,128)(2,1)S(1)}, u32[]{:S(2)}, u32[]{:S(2)}) collective-permute-start(bf16[8,24,1024]{2,1,0:T(8,128)(2,1)} %get-tuple-element.25), channel_id=1, source_target_pairs={{0,1},{1,0},{2,3},{3,2},{4,5},{5,4},{6,7},{7,6},{8,9},{9,8},{10,11... | collective-permute-start | bytes 1179656 | tf_op jit(solution)/shard_map/ppermute | solution.py:25
  105.7 2.2 %copy-start.1 = (bf16[8,16,128,128]{3,2,1,0:T(8,128)(2,1)S(1)}, bf16[8,16,128,128]{3,2,1,0:T(8,128)(2,1)}, u32[]{:S(2)}) copy-start(bf16[8,16,128,128]{3,2,1,0:T(8,128)(2,1)} %states_ref.5) | copy-start | bytes 12582916
  125.1 7.2 %copy-start.2 = (bf16[2048,128]{1,0:T(8,128)(2,1)S(1)}, bf16[2048,128]{1,0:T(8,128)(2,1)}, u32[]{:S(2)}) copy-start(bf16[2048,128]{1,0:T(8,128)(2,1)} %weight_ref.1) | copy-start | bytes 1572868

commit v2 on v1

--- a/solution.py
+++ b/solution.py
@@ -48,11 +48,13 @@
 
 
 def gather_all(block, plan):
-    gathered, order = block[None], [0]
+    held, order = [block], [0]
     for stage in plan:
-        gathered = jnp.concatenate([gathered] + [xor_permute(gathered, d) for d in stage], 0)
+        held = held + [xor_permute(part, distance) for distance in stage for part in held]
         order = [near ^ far for far in [0] + stage for near in order]
-    return gathered, order
+        if len(held) == 2:
+            held = [jnp.concatenate(held, 0)]
+    return held, order
 
 
 def exchange_all(pieces, plan):
@@ -67,11 +69,37 @@
     return held.reshape((len(pieces),) + tail)
 
 
-def fetch_kernel(token_ref, send_ref, low_ref, table_ref, states_ref, x_ref, y_ref, d_ref, c_ref, rows_ref, row_sem, state_sem):
-    count = token_ref.shape[0]
+def column_of(row):
+    spread = jnp.broadcast_to(row.astype(jnp.float32), (8, row.shape[1]))
+    return jnp.transpose(spread)[:, 0:1]
+
+
+def chosen_rows(column, width):
+    shape = (column.shape[0], width)
+    return (lax.broadcasted_iota(jnp.int32, shape, 1).astype(jnp.float32) == column).astype(jnp.float32)
+
+
+def fetch_kernel(
+    blocks, me_ref, parent_ref, token_ref, tokens_ref, table_ref, states_ref, x_ref, y_ref, d_ref, c_ref, rows_ref, row_sem, state_sem
+):
+    count, own_rows = token_ref.shape[0], states_ref.shape[0]
+    user, member = lax.div(me_ref[0], blocks), lax.rem(me_ref[0], blocks)
+    copies = []
+    for partner, out in ((2, y_ref), (3, d_ref), (1, c_ref)):
+        first = (user * blocks + (member ^ partner)) * own_rows
+        chosen, found = [jnp.int32(0)] * CAP, jnp.int32(0)
+        for child in range(own_rows):
+            parent = parent_ref[first + child]
+            hit = lax.div(parent, own_rows) == member
+            chosen = [jnp.where(hit & (found == j), lax.rem(parent, own_rows), old) for j, old in enumerate(chosen)]
+            found = found + hit.astype(jnp.int32)
+        for slot in range(CAP):
+            place = (partner - 1) * CAP + slot
+            copies.append(pltpu.make_async_copy(states_ref.at[chosen[slot]], out.at[slot], state_sem.at[place]))
+            copies[-1].start()
 
     def start_row(r, carry):
-        first = pl.multiple_of(token_ref[r] // TILE * TILE, TILE)
+        first = pl.multiple_of(lax.div(token_ref[r], TILE) * TILE, TILE)
         pltpu.make_async_copy(
             table_ref.at[pl.ds(first, TILE)],
             rows_ref.at[pl.ds(pl.multiple_of(r * TILE, TILE), TILE)],
@@ -80,42 +108,38 @@
         return carry
 
     lax.fori_loop(0, count, start_row, 0, unroll=8)
-    copies = []
-    for partner, out in ((2, y_ref), (3, d_ref), (1, c_ref)):
-        for slot in range(CAP):
-            place = (partner - 1) * CAP + slot
-            copies.append(
-                pltpu.make_async_copy(states_ref.at[send_ref[place]], out.at[slot], state_sem.at[place])
-            )
-            copies[-1].start()
+    step = math.gcd(count, 128)
+    picks = []
+    for first in range(0, count, step):
+        low = column_of(lax.rem(tokens_ref[:, first : first + step], TILE))
+        wanted = low + lax.broadcasted_iota(jnp.int32, (step, 1), 0).astype(jnp.float32) * TILE
+        picks.append(chosen_rows(wanted, step * TILE).astype(jnp.bfloat16))
     pltpu.make_async_copy(table_ref.at[pl.ds(0, count * TILE)], rows_ref, row_sem).wait()
-    step = math.gcd(count, 128)
-    for first in range(0, count, step):
-        wanted = lax.broadcasted_iota(jnp.int32, (step, 1), 0) * TILE + low_ref[first : first + step, :]
-        chosen = lax.broadcasted_iota(jnp.int32, (step, step * TILE), 1) == wanted
+    for first, pick in zip(range(0, count, step), picks):
         x_ref[first : first + step, :] = jnp.dot(
-            chosen.astype(jnp.float32).astype(jnp.bfloat16),
-            rows_ref[first * TILE : (first + step) * TILE, :],
-            preferred_element_type=jnp.float32,
+            pick, rows_ref[first * TILE : (first + step) * TILE, :], preferred_element_type=jnp.float32
         ).astype(jnp.bfloat16)
     for copy in copies:
         copy.wait()
 
 
-def project_kernel(order, me_ref, x_ref, weight_ref, index_ref, out_ref):
-    me = me_ref[0]
-    columns = x_ref.shape[2]
-    total = None
+def project_kernel(order, parts, me_ref, weight_ref, index_ref, *refs):
+    held, out_ref = refs[:parts], refs[parts]
+    me, columns = me_ref[0], held[0].shape[1]
+    rows = held[0].shape[0] * parts // len(order)
+    total = [None] * 3
     for place, distance in enumerate(order):
+        ref, within = held[place * parts // len(order)], place % (len(order) // parts)
+        block = ref[within * rows : (within + 1) * rows, :]
         first = pl.multiple_of((me ^ distance) * columns, columns)
-        term = jnp.dot(x_ref[place], weight_ref[pl.ds(first, columns), :], preferred_element_type=jnp.float32)
-        total = term if total is None else total + term
-    rounded = total.astype(jnp.bfloat16)
-    shape = (index_ref.shape[0], rounded.shape[0])
-    chosen = lax.broadcasted_iota(jnp.int32, shape, 1) == index_ref[...]
-    out_ref[...] = jnp.dot(
-        chosen.astype(jnp.float32).astype(jnp.bfloat16), rounded, preferred_element_type=jnp.float32
-    ).astype(jnp.bfloat16)
+        for slab in range(3):
+            term = jnp.dot(block, weight_ref[slab, pl.ds(first, columns), :], preferred_element_type=jnp.float32)
+            total[slab] = term if total[slab] is None else total[slab] + term
+    pick = chosen_rows(column_of(index_ref[...]), rows).astype(jnp.bfloat16)
+    for slab in range(3):
+        out_ref[:, slab * columns : (slab + 1) * columns] = jnp.dot(
+            pick, total[slab].astype(jnp.bfloat16), preferred_element_type=jnp.float32
+        ).astype(jnp.bfloat16)
 
 
 def head_terms(piece, gate_row, bias, size):
@@ -131,7 +155,7 @@
     own_rows, lane_ref, bias_ref, recv_ref, states_ref, near_ref, place_ref, gate_ref, gain_ref, out_ref, norm_ref
 ):
     step, block, size = pl.program_id(0), states_ref.shape[1], states_ref.shape[2]
-    place = place_ref[...]
+    place = column_of(place_ref[...])[: recv_ref.shape[1]]
     for part in range(block):
         head = step * block + part
         piece = recv_ref[lane_ref[head]]
@@ -143,7 +167,7 @@
         for ref, first in ((states_ref, 0), (near_ref, own_rows)):
             count = ref.shape[0]
             spread = jnp.concatenate(
-                [jnp.where(place == first + p, query_float, zero).astype(jnp.bfloat16) for p in range(count)], 1
+                [jnp.where(place == float(first + p), query_float, zero).astype(jnp.bfloat16) for p in range(count)], 1
             )
             term = jnp.dot(spread, ref[:, part].reshape(count * size, size), preferred_element_type=jnp.float32)
             prior_part = term if prior_part is None else prior_part + term
@@ -164,49 +188,48 @@
         ).astype(jnp.bfloat16)
 
 
-def output_kernel(x_ref, normed_ref, weight_ref, low_ref, high_ref, out_ref):
-    half = normed_ref.shape[1]
-    shape = (x_ref.shape[0], normed_ref.shape[0])
+def output_kernel(x_ref, weight_ref, low_ref, high_ref, *refs):
+    parts, out_ref = refs[:-1], refs[-1]
+    half = parts[0].shape[1]
     total = x_ref[...].astype(jnp.float32)
-    for part, index_ref in enumerate((low_ref, high_ref)):
-        product = jnp.dot(
-            normed_ref[...], weight_ref[part * half : (part + 1) * half, :], preferred_element_type=jnp.float32
-        )
-        chosen = (lax.broadcasted_iota(jnp.int32, shape, 1) == index_ref[...]).astype(jnp.float32)
-        total = total + jnp.dot(
-            chosen, product, preferred_element_type=jnp.float32, precision=lax.Precision.HIGHEST
-        )
+    for side, index_ref in enumerate((low_ref, high_ref)):
+        weight = weight_ref[side * half : (side + 1) * half, :]
+        product = jnp.concatenate([jnp.dot(part[...], weight, preferred_element_type=jnp.float32) for part in parts], 0)
+        pick = chosen_rows(column_of(index_ref[...]), product.shape[0])
+        total = total + jnp.dot(pick, product, preferred_element_type=jnp.float32, precision=lax.Precision.HIGHEST)
     out_ref[...] = total.astype(jnp.bfloat16)
 
 
-def near_update_kernel(lane_ref, bias_ref, source_ref, recv_ref, states_ref, near_ref, gate_ref, out_ref):
+def near_update_kernel(lane_ref, bias_ref, source_ref, recv_ref, states_ref, near_ref, gate_ref, out_ref, turned_ref, terms_ref):
     own_rows, block, size = states_ref.shape[0], states_ref.shape[1], states_ref.shape[2]
-    step = pl.program_id(0)
+    step, slots = pl.program_id(0), recv_ref.shape[1]
     for part in range(block):
         head = step * block + part
         piece = recv_ref[lane_ref[head]]
-        keys, values, decay, inverse = head_terms(piece, gate_ref[pl.ds(head, 1), :], bias_ref[head], size)
-        turned = jnp.transpose(keys * inverse)
+        keys, _, decay, inverse = head_terms(piece, gate_ref[pl.ds(head, 1), :], bias_ref[head], size)
+        turned = jnp.transpose(keys)
+        turned_ref[part] = turned.astype(jnp.bfloat16)
+        terms_ref[0, part] = jnp.broadcast_to(decay, (slots, size))
+        terms_ref[1, part] = jnp.broadcast_to(inverse, (slots, size))
+        lane = lax.broadcasted_iota(jnp.int32, (size, slots), 1)
+        spread = jnp.concatenate(
+            [jnp.where(lane == row, turned, 0.0).astype(jnp.bfloat16) for row in range(own_rows)], 0
+        )
+        outer = jnp.dot(spread, piece[:, 2 * size :], preferred_element_type=jnp.float32)
         for row in range(own_rows):
-
-            def store(prior, row=row, part=part, turned=turned, values=values, decay=decay):
-                fresh = decay[row : row + 1, :] * prior.astype(jnp.float32)
-                fresh = fresh + turned[:, row : row + 1] * values[row : row + 1, :]
-                out_ref[row, part] = fresh.astype(jnp.bfloat16)
-
             source = source_ref[row]
-
-            @pl.when((source >= 0) & (source < own_rows))
-            def _():
-                store(states_ref[jnp.clip(source, 0, own_rows - 1), part])
-
-            @pl.when(source >= own_rows)
-            def _():
-                store(near_ref[jnp.clip(source - own_rows, 0, near_ref.shape[0] - 1), part])
+            prior = jnp.where(
+                source >= own_rows,
+                near_ref[jnp.clip(source - own_rows, 0, near_ref.shape[0] - 1), part],
+                states_ref[jnp.clip(source, 0, own_rows - 1), part],
+            )
+            fresh = decay[row : row + 1, :] * prior.astype(jnp.float32)
+            fresh = fresh + inverse[row : row + 1, :] * outer[row * size : (row + 1) * size, :]
+            out_ref[row, part] = fresh.astype(jnp.bfloat16)
 
 
 def far_update_kernel(
-    block, lane_ref, bias_ref, child_ref, recv_ref, got_ref, gate_ref, old_ref, out_ref, in_ref, new_ref, in_sem, out_sem
+    block, lane_ref, child_ref, recv_ref, turned_ref, terms_ref, got_ref, old_ref, out_ref, in_ref, new_ref, in_sem, out_sem
 ):
     count, heads, size = got_ref.shape[0], got_ref.shape[1], got_ref.shape[2]
     chunks = heads // block
@@ -234,15 +257,14 @@
             def work(slot=slot, chunk=chunk):
                 load(slot, chunk).wait()
                 child = child_ref[slot]
+                lane = lax.broadcasted_iota(jnp.int32, (size, turned_ref.shape[2]), 1)
                 for head in range(chunk * block, (chunk + 1) * block):
-                    piece = recv_ref[lane_ref[head]]
-                    keys, values, decay, inverse = head_terms(piece, gate_ref[head : head + 1, :], bias_ref[head], size)
-                    mine = lax.broadcasted_iota(jnp.int32, (keys.shape[0], 1), 0) == child
-                    key_row = jnp.sum(jnp.where(mine, keys * inverse, 0.0), axis=0, keepdims=True)
-                    value_row = jnp.sum(jnp.where(mine, values, 0.0), axis=0, keepdims=True)
-                    decay_one = jnp.sum(jnp.where(mine, decay, 0.0), axis=0, keepdims=True)
-                    turned = jnp.transpose(jnp.broadcast_to(key_row, (8, size)))[:, 0:1]
-                    fresh = decay_one * in_ref[slot, head].astype(jnp.float32) + turned * value_row
+                    turned = turned_ref[head].astype(jnp.float32)
+                    key = jnp.where(lane == child, turned, 0.0).astype(jnp.bfloat16)
+                    values = recv_ref[lane_ref[head]][:, 2 * size :]
+                    outer = jnp.dot(key, values, preferred_element_type=jnp.float32)
+                    fresh = terms_ref[0, head, pl.ds(child, 1), :] * in_ref[slot, head].astype(jnp.float32)
+                    fresh = fresh + terms_ref[1, head, pl.ds(child, 1), :] * outer
                     new_ref[slot, head] = fresh.astype(jnp.bfloat16)
                 save(slot, chunk).start()
 
@@ -292,14 +314,10 @@
 
     my_children = lax.dynamic_index_in_dim(child_at, user, 0, keepdims=False)
     my_states = lax.dynamic_index_in_dim(state_at, user, 0, keepdims=False)
-    partners = member ^ jnp.arange(1, 4, dtype=int32)
-    send = lax.dynamic_index_in_dim(my_states, member, 1, keepdims=False)[partners]
-
-    tokens = token_ids[0]
     local_columns, y_out, d_out, c_out = pl.pallas_call(
-        fetch_kernel,
-        in_specs=[SCALARS, SCALARS, WHOLE, PLACED, PLACED],
-        out_specs=[WHOLE, PLACED, PLACED, PLACED],
+        functools.partial(fetch_kernel, blocks),
+        in_specs=[SCALARS, SCALARS, SCALARS, WHOLE, PLACED, PLACED],
+        out_specs=[WHOLE] * 4,
         out_shape=[jax.ShapeDtypeStruct((row_total, columns), bf16)] + [jax.ShapeDtypeStruct(state_slab, bf16)] * 3,
         scratch_shapes=[
             pltpu.VMEM((row_total * TILE, columns), bf16),
@@ -308,7 +326,7 @@
         ],
         compiler_params=params(),
         name="fetch",
-    )(tokens, send.reshape(-1), (tokens % TILE)[:, None], embed_table, states)
+    )(me[None], parents.reshape(-1), token_ids.reshape(-1), token_ids, embed_table, states)
     y_got = xor_permute(y_out, 2)
     d_got = xor_permute(d_out, 3)
     near_got = xor_permute(c_out, 1)
@@ -323,17 +341,18 @@
         row = (device_user * blocks + child_block)[:, None] * own_rows + child
         foreign_lists.append(jnp.where(child >= 0, row, -1))
     unused = jnp.full((count, 2 * CAP), -1, int32)
-    row_list = jnp.concatenate([own_list] + foreign_lists + [unused], 1).reshape(count * slots, 1)
+    row_list = jnp.concatenate([own_list] + foreign_lists + [unused], 1).reshape(1, count * slots)
 
     every_input, order = gather_all(local_columns, plan)
+    weight = jnp.transpose(qkv_weight, (1, 0, 2))
     pieces = pl.pallas_call(
-        functools.partial(project_kernel, order),
-        in_specs=[SCALARS, WHOLE, WHOLE, WHOLE],
+        functools.partial(project_kernel, order, len(every_input)),
+        in_specs=[SCALARS] + [WHOLE] * (2 + len(every_input)),
         out_specs=WHOLE,
         out_shape=jax.ShapeDtypeStruct((count * slots, 3 * columns), bf16),
         compiler_params=params(),
         name="project",
-    )(me[None], every_input, qkv_weight.reshape(qkv_weight.shape[0], 3 * columns), row_list)
+    )(me[None], weight, row_list, *every_input)
     received = exchange_all(pieces.reshape(count, slots, 3 * columns), plan)
     recv_order = plan_order(plan)
     places = jnp.array([recv_order.index(d) for d in range(count)], int32)
@@ -353,11 +372,11 @@
     for partner in (2, 3):
         child = my_children[member ^ partner, member]
         foreign_places.append(jnp.where(child >= 0, my_states[member ^ partner, member], -1))
-    place = jnp.concatenate([source] + foreign_places + [jnp.full((2 * CAP,), -1, int32)])[:, None]
+    idle = jnp.full((128 - own_rows - 2 * CAP,), -1, int32)
+    place = jnp.concatenate([source] + foreign_places + [idle])[None]
 
     head_block = math.gcd(heads, 4)
     by_heads = lambda rows: pl.BlockSpec((rows, head_block, size, size), lambda i: (0, i, 0, 0))
-    state_bytes = 2 * own_rows * heads * size * size
     normed = pl.pallas_call(
         functools.partial(readout_kernel, own_rows),
         grid=(heads // head_block,),
@@ -369,14 +388,22 @@
         name="readout",
     )(lanes, gate_bias, by_head, states, near_got, place, gate_weight, norm_gain.reshape(heads, size))
 
-    near_done = pl.pallas_call(
+    turned_shape, terms_shape = (heads, size, slots), (2, heads, slots, size)
+    near_done, turned, terms = pl.pallas_call(
         near_update_kernel,
         grid=(heads // head_block,),
         in_specs=[SCALARS, SCALARS, SCALARS, WHOLE, by_heads(own_rows), by_heads(CAP), WHOLE],
-        out_specs=by_heads(own_rows),
-        out_shape=jax.ShapeDtypeStruct(states.shape, bf16),
+        out_specs=[
+            by_heads(own_rows),
+            pl.BlockSpec((head_block, size, slots), lambda i: (i, 0, 0)),
+            pl.BlockSpec((2, head_block, slots, size), lambda i: (0, i, 0, 0)),
+        ],
+        out_shape=[
+            jax.ShapeDtypeStruct(states.shape, bf16),
+            jax.ShapeDtypeStruct(turned_shape, bf16),
+            jax.ShapeDtypeStruct(terms_shape, jnp.float32),
+        ],
         compiler_params=params(),
-        cost_estimate=pl.CostEstimate(flops=4 * state_bytes, bytes_accessed=3 * state_bytes, transcendentals=0),
         name="near_update",
     )(lanes, gate_bias, source, by_head, states, near_got, gate_weight)
 
@@ -384,7 +411,7 @@
         chunk = math.gcd(heads, 4)
         return pl.pallas_call(
             functools.partial(far_update_kernel, chunk),
-            in_specs=[SCALARS, SCALARS, SCALARS, WHOLE, PLACED, WHOLE, PLACED],
+            in_specs=[SCALARS, SCALARS, WHOLE, WHOLE, WHOLE, PLACED, PLACED],
             out_specs=PLACED,
             out_shape=jax.ShapeDtypeStruct(states.shape, bf16),
             scratch_shapes=[
@@ -395,9 +422,8 @@
             ],
             input_output_aliases={6: 0},
             compiler_params=params(),
-            cost_estimate=pl.CostEstimate(flops=state_bytes, bytes_accessed=state_bytes // 2, transcendentals=0),
             name=name,
-        )(lanes, gate_bias, children, by_head, got, gate_weight, before)
+        )(lanes, children, by_head, turned, terms, got, before)
 
     y_done = far_update(near_done, y_got, my_children[member, member ^ 2], "y_update")
     final = far_update(y_done, d_got, my_children[member, member ^ 3], "corner_update")
@@ -409,20 +435,20 @@
     user_ids = jnp.arange(users, dtype=int32)[:, None, None]
     holder = user_ids * blocks + jnp.where(over_y, parent_block, block_ids[None, :, None])
     place_of = jnp.array([normed_order.index(d) for d in range(count)], int32)
-    base = (place_of[holder ^ me] * normed_rows).reshape(row_total, 1)
-    foreign_slot = jnp.where(over_y, (all_away - 2) * CAP + rank, 0).reshape(row_total, 1)
-    over_y = over_y.reshape(row_total, 1)
-    own_slot = jnp.broadcast_to(along, (users, blocks, own_rows)).reshape(row_total, 1)
+    base = (place_of[holder ^ me] * normed_rows).reshape(1, row_total)
+    foreign_slot = jnp.where(over_y, (all_away - 2) * CAP + rank, 0).reshape(1, row_total)
+    over_y = over_y.reshape(1, row_total)
+    own_slot = jnp.broadcast_to(along, (users, blocks, own_rows)).reshape(1, row_total)
     low = base + jnp.where(over_y, 2 * own_rows + foreign_slot, own_slot)
     high = low + jnp.where(over_y, 2 * CAP, own_rows)
     layer_out = pl.pallas_call(
         output_kernel,
-        in_specs=[WHOLE] * 5,
+        in_specs=[WHOLE] * (4 + len(every_normed)),
         out_specs=WHOLE,
         out_shape=jax.ShapeDtypeStruct((row_total, columns), bf16),
         compiler_params=params(),
         name="output",
-    )(local_columns, every_normed.reshape(count * normed_rows, width // 2), out_weight, low, high)
+    )(local_columns, out_weight, low, high, *every_normed)
     return (layer_out[None], final)
 
 

time: 136 us -> 83.2 us (0.61)
  the two profiles are of different devices: /device:TPU:4 before, /device:TPU:1 now
where the time goes in v2:
time: 83.2 us; the launch traced here: 82.9 us
  starting transfers between devices  28.2 us (34%)
  Pallas kernels  23.9 us (29%)
  waiting for transfers between devices  17.5 us (21%)
  local copies, waits for them, and re-layouts  10 us (12%)
  other arithmetic  2.26 us (3%)
  between operations  0.96 us (1%)
    ppermute x24, starting transfers between devices, xor_permute(): lax.ppermute(block, 'rows', [(i, i ^ distance) for i in range(count)])  28.2 us
    ppermute x24, waiting for transfers between devices, xor_permute(): lax.ppermute(block, 'rows', [(i, i ^ distance) for i in range(count)])  17.5 us
    pallas_call x2, Pallas kernels, far_update(): pl.pallas_call(functools.partial(far_update_kernel, chunk), in_specs=[SCA...  7.73 us
    pallas_call x1, Pallas kernels, per_device(): pl.pallas_call(near_update_kernel, grid=(heads // head_block,), in_specs=...  6.33 us
    unnamed x29, local copies, waits for them, and re-layouts  5.01 us
    pallas_call x1, Pallas kernels, per_device(): pl.pallas_call(functools.partial(fetch_kernel, blocks), in_specs=[SCALARS...  4.18 us
    pallas_call x1, Pallas kernels, per_device(): pl.pallas_call(functools.partial(readout_kernel, own_rows), grid=(heads /...  2.9 us
    pallas_call x1, Pallas kernels, per_device(): pl.pallas_call(output_kernel, in_specs=[WHOLE] * (4 + len(every_normed)),...  1.88 us
  transfers between devices with their start and end apart: 24, of which 10 were waited for; matrix products, arithmetic and copies ran while one was open for 8% of the time, Pallas kernels for 22%

profile of v2, /device:TPU:1, one launch (start us, length us, event | category | flops | bytes accessed | tf_op | source)
XLA Modules:
  0.0 82.9 jit_solution(12182618118286693072)
XLA Ops:
  0.6 0.8 reshape.497.parent_ref
  1.4 0.7 copy-done.6
  2.1 4.2 %fetch.1 = (bf16[128,128]{1,0:T(8,128)(2,1)S(1)}, bf16[2,16,128,128]{3,2,1,0:T(8,128)(2,1)S(1)}, bf16[2,16,128,128]{3,2,1,0:T(8,128)(2,1)S(1)}, bf16[2,16,128,128]{3,2,1,0:T(8,128)(2,1)}) custom-call(s32[1]{0:T(128)} %bitcast.me_ref, s32[128]{0:T(128)S(1)} %reshape.497.parent_ref, s32[128]{0:T(128)S(1)} %bitcast.33, s32[1,128]{1,0:T(1,128)S(1)} %copy-done.6, ...), custom_call_target="tpu_custom_call" | custom-call | tf_op jit(solution)/shard_map/fetch/pallas_call | solution.py:317
  6.3 1.0 %copy-done.7 = bf16[2,16,128,128]{3,2,1,0:T(8,128)(2,1)} copy-done((bf16[2,16,128,128]{3,2,1,0:T(8,128)(2,1)}, bf16[2,16,128,128]{3,2,1,0:T(8,128)(2,1)S(1)}, u32[]{:S(2)}) %copy-start.7) | copy-done | bytes 1048600
  7.2 1.0 %copy-done.8 = bf16[2,16,128,128]{3,2,1,0:T(8,128)(2,1)} copy-done((bf16[2,16,128,128]{3,2,1,0:T(8,128)(2,1)}, bf16[2,16,128,128]{3,2,1,0:T(8,128)(2,1)S(1)}, u32[]{:S(2)}) %copy-start.8) | copy-done | bytes 1048600
  8.2 3.2 %collective-permute-start = (bf16[128,128]{1,0:T(8,128)(2,1)S(1)}, bf16[128,128]{1,0:T(8,128)(2,1)S(1)}, u32[]{:S(2)}, u32[]{:S(2)}) collective-permute-start(bf16[128,128]{1,0:T(8,128)(2,1)S(1)} %get-tuple-element.9.x_ref), channel_id=1, source_target_pairs={{0,6},{1,7},{2,4},{3,5},{4,2},{5,3},{6,0},{7,1},{8,14},{9,15},{10,... | collective-permute-start | bytes 98312 | tf_op jit(solution)/shard_map/ppermute | solution.py:25
  11.4 1.0 %collective-permute-start.13 = (bf16[2,16,128,128]{3,2,1,0:T(8,128)(2,1)}, bf16[2,16,128,128]{3,2,1,0:T(8,128)(2,1)S(1)}, u32[]{:S(2)}, u32[]{:S(2)}) collective-permute-start(bf16[2,16,128,128]{3,2,1,0:T(8,128)(2,1)} %get-tuple-element.10), channel_id=1, source_target_pairs={{0,1},{1,0},{2,3},{3,2},{4,5},{5,4},{6,7},{7,6},{8,9},{9,8},{10,11... | collective-permute-start | bytes 3145736 | tf_op jit(solution)/shard_map/ppermute | solution.py:25
  12.7 0.4 convert_reduce_fusion
  13.1 1.2 %fusion.1 = (s32[4,4,4,2]{2,3,1,0:T(2,128)S(1)}, s32[4,4,4,2]{2,3,1,0:T(2,128)S(1)}) fusion(s32[4,4,8]{2,1,0:T(4,128)S(1)} %get-tuple-element.37, pred[4,4,2,8]{3,2,1,0:T(4,128)(4,1)S(1)} %iota_compare_fusion.1, pred[4,4,4,8]{3,2,1,0:T(4,128)(4,1)S(1)} %iota_compare_fusion, s32[8]{0:T(128)S(1)} %iota_add_fusion.1), kind=kLoop, calls=%fused_computation.16 | loop fusion | flops 4864 | bytes 2336 | tf_op jit(solution)/shard_map/reduce_sum | solution.py:313
  14.6 0.2 copy.16
  14.8 0.6 gather_fusion.3
  15.5 0.6 gather_fusion.2
  16.4 2.2 %collective-permute-start.3 = (bf16[256,128]{1,0:T(8,128)(2,1)S(1)}, bf16[256,128]{1,0:T(8,128)(2,1)S(1)}, u32[]{:S(2)}, u32[]{:S(2)}) collective-permute-start(bf16[256,128]{1,0:T(8,128)(2,1)S(1)} %constant_dynamic-update-slice_fusion.refs_0_), channel_id=1, source_target_pairs={{0,12},{1,13},{2,14},{3,15},{4,8},{5,9},{6,10},{7,11},{8,4},{9,5},... | collective-permute-start | bytes 196616 | tf_op jit(solution)/shard_map/ppermute | solution.py:25
  18.6 0.2 collective-permute-start.2
  18.8 1.2 %collective-permute-start.1 = (bf16[256,128]{1,0:T(8,128)(2,1)S(1)}, bf16[256,128]{1,0:T(8,128)(2,1)S(1)}, u32[]{:S(2)}, u32[]{:S(2)}) collective-permute-start(bf16[256,128]{1,0:T(8,128)(2,1)S(1)} %constant_dynamic-update-slice_fusion.refs_0_), channel_id=1, source_target_pairs={{0,4},{1,5},{2,6},{3,7},{4,0},{5,1},{6,2},{7,3},{8,12},{9,13},{10,... | collective-permute-start | bytes 196616 | tf_op jit(solution)/shard_map/ppermute | solution.py:25
  20.0 0.8 %collective-permute-start.4 = (bf16[256,128]{1,0:T(8,128)(2,1)S(1)}, bf16[256,128]{1,0:T(8,128)(2,1)S(1)}, u32[]{:S(2)}, u32[]{:S(2)}) collective-permute-start(bf16[256,128]{1,0:T(8,128)(2,1)S(1)} %constant_dynamic-update-slice_fusion.refs_0_), channel_id=1, source_target_pairs={{0,1},{1,0},{2,3},{3,2},{4,5},{5,4},{6,7},{7,6},{8,9},{9,8},{10,11... | collective-permute-start | bytes 196616 | tf_op jit(solution)/shard_map/ppermute | solution.py:25
  20.9 1.2 %collective-permute-done.3.refs_3_ = bf16[256,128]{1,0:T(8,128)(2,1)S(1)} collective-permute-done((bf16[256,128]{1,0:T(8,128)(2,1)S(1)}, bf16[256,128]{1,0:T(8,128)(2,1)S(1)}, u32[]{:S(2)}, u32[]{:S(2)}) %collective-permute-start.3) | collective-permute-done | bytes 65568 | tf_op jit(solution)/shard_map/ppermute | solution.py:25
  22.0 0.9 %collective-permute-start.7 = (bf16[256,128]{1,0:T(8,128)(2,1)S(1)}, bf16[256,128]{1,0:T(8,128)(2,1)S(1)}, u32[]{:S(2)}, u32[]{:S(2)}) collective-permute-start(bf16[256,128]{1,0:T(8,128)(2,1)S(1)} %collective-permute-done.3.refs_3_), channel_id=1, source_target_pairs={{0,1},{1,0},{2,3},{3,2},{4,5},{5,4},{6,7},{7,6},{8,9},{9,8},{10,11... | collective-permute-start | bytes 196616 | tf_op jit(solution)/shard_map/ppermute | solution.py:25
  23.0 2.5 %collective-permute-done.2.refs_2_ = bf16[256,128]{1,0:T(8,128)(2,1)S(1)} collective-permute-done((bf16[256,128]{1,0:T(8,128)(2,1)S(1)}, bf16[256,128]{1,0:T(8,128)(2,1)S(1)}, u32[]{:S(2)}, u32[]{:S(2)}) %collective-permute-start.2) | collective-permute-done | bytes 65568 | tf_op jit(solution)/shard_map/ppermute | solution.py:25
  25.4 0.6 collective-permute-start.6
  26.0 0.7 collective-permute-start.23
  26.8 0.2 collective-permute-done.6.refs_6_
  26.9 0.4 collective-permute-done.5.refs_5_
  27.3 0.9 %project.1 = bf16[256,384]{1,0:T(8,128)(2,1)S(1)} custom-call(s32[1]{0:T(128)} %bitcast.me_ref, bf16[3,2048,128]{2,1,0:T(8,128)(2,1)S(1)} %bitcast.31, s32[1,256]{1,0:T(1,128)S(1)} %reshape.500.index_ref, bf16[256,128]{1,0:T(8,128)(2,1)S(1)} %constant_dynamic-update-slice_fusion.refs_0_, bf16[256,128]{1,0:T(8,128)(2,1)S(1)} %collective-permute-done.1.refs_1_, ...), custom_call_target="tpu_custom_call" | custom-call | tf_op jit(solution)/shard_map/project/pallas_call | solution.py:348
  28.3 5.0 %collective-permute-done.8 = bf16[1,4,2,16,384]{4,3,2,1,0:T(8,128)(2,1)S(1)} collective-permute-done((bf16[1,4,2,16,384]{4,3,2,1,0:T(8,128)(2,1)S(1)}, bf16[1,4,2,16,384]{4,3,2,1,0:T(8,128)(2,1)S(1)}, u32[]{:S(2)}, u32[]{:S(2)}) %collective-permute-start.8) | collective-permute-done | bytes 98336 | tf_op jit(solution)/shard_map/ppermute | solution.py:25
  33.4 2.4 %collective-permute-start.11 = (bf16[2,1,2,16,384]{4,3,2,1,0:T(8,128)(2,1)S(1)}, bf16[2,1,2,16,384]{4,3,2,1,0:T(8,128)(2,1)S(1)}, u32[]{:S(2)}, u32[]{:S(2)}) collective-permute-start(bf16[2,1,2,16,384]{4,3,2,1,0:T(8,128)(2,1)S(1)} %get-tuple-element.27), channel_id=1, source_target_pairs={{0,12},{1,13},{2,14},{3,15},{4,8},{5,9},{6,10},{7,11},{8,4},{9,5},... | collective-permute-start | bytes 147464 | tf_op jit(solution)/shard_map/ppermute | solution.py:25
  35.8 0.2 collective-permute-start.10
  36.2 0.7 gather_fusion.1
  36.8 2.9 %collective-permute-start.22 = (bf16[2,16,128,128]{3,2,1,0:T(8,128)(2,1)}, bf16[2,16,128,128]{3,2,1,0:T(8,128)(2,1)S(1)}, u32[]{:S(2)}, u32[]{:S(2)}) collective-permute-start(bf16[2,16,128,128]{3,2,1,0:T(8,128)(2,1)} %copy-done.7), channel_id=1, source_target_pairs={{0,3},{1,2},{2,1},{3,0},{4,7},{5,6},{6,5},{7,4},{8,11},{9,10},{10,... | collective-permute-start | bytes 3145736 | tf_op jit(solution)/shard_map/ppermute | solution.py:25
  39.7 1.3 %collective-permute-done.10 = bf16[2,1,2,16,384]{4,3,2,1,0:T(8,128)(2,1)S(1)} collective-permute-done((bf16[2,1,2,16,384]{4,3,2,1,0:T(8,128)(2,1)S(1)}, bf16[2,1,2,16,384]{4,3,2,1,0:T(8,128)(2,1)S(1)}, u32[]{:S(2)}, u32[]{:S(2)}) %collective-permute-start.10) | collective-permute-done | bytes 49184 | tf_op jit(solution)/shard_map/ppermute | solution.py:25
  41.1 1.3 %collective-permute-start.12 = (bf16[2,4,1,16,384]{4,3,2,1,0:T(8,128)(2,1)S(1)}, bf16[2,4,1,16,384]{4,3,2,1,0:T(8,128)(2,1)S(1)}, u32[]{:S(2)}, u32[]{:S(2)}) collective-permute-start(bf16[2,4,1,16,384]{4,3,2,1,0:T(8,128)(2,1)S(1)} %get-tuple-element.24), channel_id=1, source_target_pairs={{0,1},{1,0},{2,3},{3,2},{4,5},{5,4},{6,7},{7,6},{8,9},{9,8},{10,11... | collective-permute-start | bytes 294920 | tf_op jit(solution)/shard_map/ppermute | solution.py:25
  42.5 0.9 %collective-permute-done.12 = bf16[2,4,1,16,384]{4,3,2,1,0:T(8,128)(2,1)S(1)} collective-permute-done((bf16[2,4,1,16,384]{4,3,2,1,0:T(8,128)(2,1)S(1)}, bf16[2,4,1,16,384]{4,3,2,1,0:T(8,128)(2,1)S(1)}, u32[]{:S(2)}, u32[]{:S(2)}) %collective-permute-start.12) | collective-permute-done | bytes 98336 | tf_op jit(solution)/shard_map/ppermute | solution.py:25
  43.5 2.2 %copy-done = bf16[8,16,128,128]{3,2,1,0:T(8,128)(2,1)S(1)} copy-done((bf16[8,16,128,128]{3,2,1,0:T(8,128)(2,1)S(1)}, bf16[8,16,128,128]{3,2,1,0:T(8,128)(2,1)}, u32[]{:S(2)}) %copy-start) | copy-done | bytes 4194328
  45.6 2.9 %readout.1 = bf16[24,1024]{1,0:T(8,128)(2,1)S(1)} custom-call(s32[16]{0:T(128)S(1)} %gather_fusion.1, f32[16]{0:T(128)S(1)} %copy-done.5, bf16[16,16,384]{2,1,0:T(8,128)(2,1)S(1)} %bitcast.27, bf16[8,16,128,128]{3,2,1,0:T(8,128)(2,1)S(1)} %copy-done, bf16[2,16,128,128]{3,2,1,0:T(8,128)(2,1)S(1)} %collective-permute-done.13.near_ref, ...), custom_call_target="tpu_custom_call" | custom-call | tf_op jit(solution)/shard_map/readout/pallas_call | solution.py:380
  48.5 1.2 %collective-permute-start.14 = (bf16[24,1024]{1,0:T(8,128)(2,1)S(1)}, bf16[24,1024]{1,0:T(8,128)(2,1)S(1)}, u32[]{:S(2)}, u32[]{:S(2)}) collective-permute-start(bf16[24,1024]{1,0:T(8,128)(2,1)S(1)} %readout.1), channel_id=1, source_target_pairs={{0,6},{1,7},{2,4},{3,5},{4,2},{5,3},{6,0},{7,1},{8,14},{9,15},{10,... | collective-permute-start | bytes 147464 | tf_op jit(solution)/shard_map/ppermute | solution.py:25
  50.3 2.2 %collective-permute-done.14 = bf16[24,1024]{1,0:T(8,128)(2,1)S(1)} collective-permute-done((bf16[24,1024]{1,0:T(8,128)(2,1)S(1)}, bf16[24,1024]{1,0:T(8,128)(2,1)S(1)}, u32[]{:S(2)}, u32[]{:S(2)}) %collective-permute-start.14) | collective-permute-done | bytes 49184 | tf_op jit(solution)/shard_map/ppermute | solution.py:25
  52.6 2.2 %collective-permute-start.17 = (bf16[48,1024]{1,0:T(8,128)(2,1)S(1)}, bf16[48,1024]{1,0:T(8,128)(2,1)S(1)}, u32[]{:S(2)}, u32[]{:S(2)}) collective-permute-start(bf16[48,1024]{1,0:T(8,128)(2,1)S(1)} %pad_maximum_fusion.2.refs_0_), channel_id=1, source_target_pairs={{0,12},{1,13},{2,14},{3,15},{4,8},{5,9},{6,10},{7,11},{8,4},{9,5},... | collective-permute-start | bytes 294920 | tf_op jit(solution)/shard_map/ppermute | solution.py:25
  54.8 1.4 %collective-permute-start.15 = (bf16[48,1024]{1,0:T(8,128)(2,1)S(1)}, bf16[48,1024]{1,0:T(8,128)(2,1)S(1)}, u32[]{:S(2)}, u32[]{:S(2)}) collective-permute-start(bf16[48,1024]{1,0:T(8,128)(2,1)S(1)} %pad_maximum_fusion.2.refs_0_), channel_id=1, source_target_pairs={{0,4},{1,5},{2,6},{3,7},{4,0},{5,1},{6,2},{7,3},{8,12},{9,13},{10,... | collective-permute-start | bytes 294920 | tf_op jit(solution)/shard_map/ppermute | solution.py:25
  56.2 1.2 %gather_fusion = s32[128]{0:T(128)S(1)} fusion(s32[16]{0:T(128)S(1)} %copy-done.9, s32[1024]{0:T(1024)S(1)} %pad_clamp_fusion.1), kind=kCustom, calls=%fused_computation | custom fusion | bytes 1536 | tf_op jit(solution)/shard_map/gather | solution.py:438
  57.4 2.4 %collective-permute-start.18 = (bf16[48,1024]{1,0:T(8,128)(2,1)S(1)}, bf16[48,1024]{1,0:T(8,128)(2,1)S(1)}, u32[]{:S(2)}, u32[]{:S(2)}) collective-permute-start(bf16[48,1024]{1,0:T(8,128)(2,1)S(1)} %pad_maximum_fusion.2.refs_0_), channel_id=1, source_target_pairs={{0,1},{1,0},{2,3},{3,2},{4,5},{5,4},{6,7},{7,6},{8,9},{9,8},{10,11... | collective-permute-start | bytes 294920 | tf_op jit(solution)/shard_map/ppermute | solution.py:25
  59.8 1.7 %collective-permute-start.21 = (bf16[48,1024]{1,0:T(8,128)(2,1)S(1)}, bf16[48,1024]{1,0:T(8,128)(2,1)S(1)}, u32[]{:S(2)}, u32[]{:S(2)}) collective-permute-start(bf16[48,1024]{1,0:T(8,128)(2,1)S(1)} %collective-permute-done.17.refs_3_), channel_id=1, source_target_pairs={{0,1},{1,0},{2,3},{3,2},{4,5},{5,4},{6,7},{7,6},{8,9},{9,8},{10,11... | collective-permute-start | bytes 294920 | tf_op jit(solution)/shard_map/ppermute | solution.py:25
  61.5 2.0 %collective-permute-done.16.refs_2_ = bf16[48,1024]{1,0:T(8,128)(2,1)S(1)} collective-permute-done((bf16[48,1024]{1,0:T(8,128)(2,1)S(1)}, bf16[48,1024]{1,0:T(8,128)(2,1)S(1)}, u32[]{:S(2)}, u32[]{:S(2)}) %collective-permute-start.16) | collective-permute-done | bytes 98336 | tf_op jit(solution)/shard_map/ppermute | solution.py:25
  63.5 1.4 %collective-permute-start.20 = (bf16[48,1024]{1,0:T(8,128)(2,1)S(1)}, bf16[48,1024]{1,0:T(8,128)(2,1)S(1)}, u32[]{:S(2)}, u32[]{:S(2)}) collective-permute-start(bf16[48,1024]{1,0:T(8,128)(2,1)S(1)} %collective-permute-done.16.refs_2_), channel_id=1, source_target_pairs={{0,1},{1,0},{2,3},{3,2},{4,5},{5,4},{6,7},{7,6},{8,9},{9,8},{10,11... | collective-permute-start | bytes 294920 | tf_op jit(solution)/shard_map/ppermute | solution.py:25
  64.9 6.3 %near_update.1 = (bf16[8,16,128,128]{3,2,1,0:T(8,128)(2,1)}, bf16[16,128,16]{2,1,0:T(8,128)(2,1)S(1)}, f32[2,16,16,128]{3,2,1,0:T(8,128)S(1)}) custom-call(s32[16]{0:T(128)S(1)} %gather_fusion.1, f32[16]{0:T(128)S(1)} %copy-done.5, s32[8]{0:T(128)S(1)} %fusion.8.source_ref, bf16[16,16,384]{2,1,0:T(8,128)(2,1)S(1)} %bitcast.28, ...), custom_call_target="tpu_custom_call" | custom-call | tf_op jit(solution)/shard_map/near_update/pallas_call | solution.py:392
  71.3 3.6 %y_update.1.old_ref = bf16[8,16,128,128]{3,2,1,0:T(8,128)(2,1)} custom-call(s32[16]{0:T(128)S(1)} %gather_fusion.1, s32[2]{0:T(128)S(1)} %get-tuple-element.31.child_ref, bf16[16,16,384]{2,1,0:T(8,128)(2,1)S(1)} %bitcast.29, bf16[16,128,16]{2,1,0:T(8,128)(2,1)S(1)} %get-tuple-element.11.turned_ref, ...), custom_call_target="tpu_custom_call", output_to_operand_aliasing={{}: (6, {})} | custom-call | tf_op jit(solution)/shard_map/y_update/pallas_call | solution.py:412
  74.9 1.9 %collective-permute-done.22.got_ref = bf16[2,16,128,128]{3,2,1,0:T(8,128)(2,1)S(1)} collective-permute-done((bf16[2,16,128,128]{3,2,1,0:T(8,128)(2,1)}, bf16[2,16,128,128]{3,2,1,0:T(8,128)(2,1)S(1)}, u32[]{:S(2)}, u32[]{:S(2)}) %collective-permute-start.22) | collective-permute-done | bytes 1048608 | tf_op jit(solution)/shard_map/ppermute | solution.py:25
  76.8 4.1 %corner_update.1 = bf16[8,16,128,128]{3,2,1,0:T(8,128)(2,1)} custom-call(s32[16]{0:T(128)S(1)} %gather_fusion.1, s32[2]{0:T(128)S(1)} %get-tuple-element.32.child_ref, bf16[16,16,384]{2,1,0:T(8,128)(2,1)S(1)} %bitcast.30, bf16[16,128,16]{2,1,0:T(8,128)(2,1)S(1)} %get-tuple-element.11.turned_ref, ...), custom_call_target="tpu_custom_call", output_to_operand_aliasing={{}: (6, {})} | custom-call | tf_op jit(solution)/shard_map/corner_update/pallas_call | solution.py:412
  81.0 1.9 %output.1 = bf16[128,128]{1,0:T(8,128)(2,1)} custom-call(bf16[128,128]{1,0:T(8,128)(2,1)S(1)} %get-tuple-element.9.x_ref, bf16[2048,128]{1,0:T(8,128)(2,1)S(1)} %copy-done.2, s32[1,128]{1,0:T(1,128)S(1)} %get-tuple-element.22.low_ref, s32[1,128]{1,0:T(1,128)S(1)} %get-tuple-element.21.high_ref, bf16[48,1024]{1,0:T(8,128)(2,1)S(1)} %pad_maximum_fusion.2.refs_0_, ...), custom_call_target="tpu_custom_call" | custom-call | tf_op jit(solution)/shard_map/output/pallas_call | solution.py:444
  (85 shorter events, 2.0 us)
Async XLA Ops:
  1.4 0.7 copy-start.6
  2.1 10.3 %copy-start.11 = (s32[1,4,32]{2,1,0:T(4,128)S(1)}, s32[1,4,32]{2,1,0:T(4,128)}, u32[]{:S(2)}) copy-start(s32[1,4,32]{2,1,0:T(4,128)} %param.13) | copy-start | bytes 1540
  2.1 10.5 %copy-start.12 = (s32[16]{0:T(128)S(1)}, s32[16]{0:T(128)}, u32[]{:S(2)}) copy-start(s32[16]{0:T(128)} %constant.296.clone) | copy-start | bytes 196
  2.1 25.2 %copy-start.1 = (bf16[2048,3,128]{2,0,1:T(8,128)(2,1)S(1)}, bf16[2048,3,128]{2,0,1:T(8,128)(2,1)}, u32[]{:S(2)}) copy-start(bf16[2048,3,128]{2,0,1:T(8,128)(2,1)} %param.16) | copy-start | bytes 4718596
  6.2 1.0 %copy-start.7 = (bf16[2,16,128,128]{3,2,1,0:T(8,128)(2,1)}, bf16[2,16,128,128]{3,2,1,0:T(8,128)(2,1)S(1)}, u32[]{:S(2)}) copy-start(bf16[2,16,128,128]{3,2,1,0:T(8,128)(2,1)S(1)} %get-tuple-element.13) | copy-start | bytes 3145732
  7.2 1.0 %copy-start.8 = (bf16[2,16,128,128]{3,2,1,0:T(8,128)(2,1)}, bf16[2,16,128,128]{3,2,1,0:T(8,128)(2,1)S(1)}, u32[]{:S(2)}) copy-start(bf16[2,16,128,128]{3,2,1,0:T(8,128)(2,1)S(1)} %get-tuple-element.14) | copy-start | bytes 3145732
  8.2 28.0 %copy-start.10 = (s32[16]{0:T(128)S(1)}, s32[16]{0:T(128)}, u32[]{:S(2)}) copy-start(s32[16]{0:T(128)} %constant.297.clone) | copy-start | bytes 196
  8.2 35.2 %copy-start.3 = (f32[16,128]{1,0:T(8,128)S(1)}, f32[16,128]{1,0:T(8,128)}, u32[]{:S(2)}) copy-start(f32[16,128]{1,0:T(8,128)} %gate_ref.3) | copy-start | bytes 24580
  8.2 35.2 %copy-start.4 = (f32[2048]{0:T(1024)S(1)}, f32[2048]{0:T(1024)}, u32[]{:S(2)}) copy-start(f32[2048]{0:T(1024)} %param.19) | copy-start | bytes 24580
  8.2 35.2 %copy-start.5 = (f32[16]{0:T(128)S(1)}, f32[16]{0:T(128)}, u32[]{:S(2)}) copy-start(f32[16]{0:T(128)} %bias_ref.3) | copy-start | bytes 196
  8.2 8.1 %collective-permute-start = (bf16[128,128]{1,0:T(8,128)(2,1)S(1)}, bf16[128,128]{1,0:T(8,128)(2,1)S(1)}, u32[]{:S(2)}, u32[]{:S(2)}) collective-permute-start(bf16[128,128]{1,0:T(8,128)(2,1)S(1)} %get-tuple-element.9.x_ref), channel_id=1, source_target_pairs={{0,6},{1,7},{2,4},{3,5},{4,2},{5,3},{6,0},{7,1},{8,14},{9,15},{10,... | collective-permute-start | bytes 98312 | tf_op jit(solution)/shard_map/ppermute | solution.py:25
  11.4 32.0 %collective-permute-start.13 = (bf16[2,16,128,128]{3,2,1,0:T(8,128)(2,1)}, bf16[2,16,128,128]{3,2,1,0:T(8,128)(2,1)S(1)}, u32[]{:S(2)}, u32[]{:S(2)}) collective-permute-start(bf16[2,16,128,128]{3,2,1,0:T(8,128)(2,1)} %get-tuple-element.10), channel_id=1, source_target_pairs={{0,1},{1,0},{2,3},{3,2},{4,5},{5,4},{6,7},{7,6},{8,9},{9,8},{10,11... | collective-permute-start | bytes 3145736 | tf_op jit(solution)/shard_map/ppermute | solution.py:25
  16.4 5.6 %collective-permute-start.3 = (bf16[256,128]{1,0:T(8,128)(2,1)S(1)}, bf16[256,128]{1,0:T(8,128)(2,1)S(1)}, u32[]{:S(2)}, u32[]{:S(2)}) collective-permute-start(bf16[256,128]{1,0:T(8,128)(2,1)S(1)} %constant_dynamic-update-slice_fusion.refs_0_), channel_id=1, source_target_pairs={{0,12},{1,13},{2,14},{3,15},{4,8},{5,9},{6,10},{7,11},{8,4},{9,5},... | collective-permute-start | bytes 196616 | tf_op jit(solution)/shard_map/ppermute | solution.py:25
  18.6 6.8 %collective-permute-start.2 = (bf16[256,128]{1,0:T(8,128)(2,1)S(1)}, bf16[256,128]{1,0:T(8,128)(2,1)S(1)}, u32[]{:S(2)}, u32[]{:S(2)}) collective-permute-start(bf16[256,128]{1,0:T(8,128)(2,1)S(1)} %constant_dynamic-update-slice_fusion.refs_0_), channel_id=1, source_target_pairs={{0,8},{1,9},{2,10},{3,11},{4,12},{5,13},{6,14},{7,15},{8,0},{9,1},... | collective-permute-start | bytes 196616 | tf_op jit(solution)/shard_map/ppermute | solution.py:25
  18.8 7.2 %collective-permute-start.1 = (bf16[256,128]{1,0:T(8,128)(2,1)S(1)}, bf16[256,128]{1,0:T(8,128)(2,1)S(1)}, u32[]{:S(2)}, u32[]{:S(2)}) collective-permute-start(bf16[256,128]{1,0:T(8,128)(2,1)S(1)} %constant_dynamic-update-slice_fusion.refs_0_), channel_id=1, source_target_pairs={{0,4},{1,5},{2,6},{3,7},{4,0},{5,1},{6,2},{7,3},{8,12},{9,13},{10,... | collective-permute-start | bytes 196616 | tf_op jit(solution)/shard_map/ppermute | solution.py:25
  20.0 6.0 %collective-permute-start.4 = (bf16[256,128]{1,0:T(8,128)(2,1)S(1)}, bf16[256,128]{1,0:T(8,128)(2,1)S(1)}, u32[]{:S(2)}, u32[]{:S(2)}) collective-permute-start(bf16[256,128]{1,0:T(8,128)(2,1)S(1)} %constant_dynamic-update-slice_fusion.refs_0_), channel_id=1, source_target_pairs={{0,1},{1,0},{2,3},{3,2},{4,5},{5,4},{6,7},{7,6},{8,9},{9,8},{10,11... | collective-permute-start | bytes 196616 | tf_op jit(solution)/shard_map/ppermute | solution.py:25
  22.0 4.7 %collective-permute-start.7 = (bf16[256,128]{1,0:T(8,128)(2,1)S(1)}, bf16[256,128]{1,0:T(8,128)(2,1)S(1)}, u32[]{:S(2)}, u32[]{:S(2)}) collective-permute-start(bf16[256,128]{1,0:T(8,128)(2,1)S(1)} %collective-permute-done.3.refs_3_), channel_id=1, source_target_pairs={{0,1},{1,0},{2,3},{3,2},{4,5},{5,4},{6,7},{7,6},{8,9},{9,8},{10,11... | collective-permute-start | bytes 196616 | tf_op jit(solution)/shard_map/ppermute | solution.py:25
  25.4 1.5 %collective-permute-start.6 = (bf16[256,128]{1,0:T(8,128)(2,1)S(1)}, bf16[256,128]{1,0:T(8,128)(2,1)S(1)}, u32[]{:S(2)}, u32[]{:S(2)}) collective-permute-start(bf16[256,128]{1,0:T(8,128)(2,1)S(1)} %collective-permute-done.2.refs_2_), channel_id=1, source_target_pairs={{0,1},{1,0},{2,3},{3,2},{4,5},{5,4},{6,7},{7,6},{8,9},{9,8},{10,11... | collective-permute-start | bytes 196616 | tf_op jit(solution)/shard_map/ppermute | solution.py:25
  26.0 1.3 %collective-permute-start.5 = (bf16[256,128]{1,0:T(8,128)(2,1)S(1)}, bf16[256,128]{1,0:T(8,128)(2,1)S(1)}, u32[]{:S(2)}, u32[]{:S(2)}) collective-permute-start(bf16[256,128]{1,0:T(8,128)(2,1)S(1)} %collective-permute-done.1.refs_1_), channel_id=1, source_target_pairs={{0,1},{1,0},{2,3},{3,2},{4,5},{5,4},{6,7},{7,6},{8,9},{9,8},{10,11... | collective-permute-start | bytes 196616 | tf_op jit(solution)/shard_map/ppermute | solution.py:25
  26.0 31.4 %collective-permute-start.23 = (bf16[2,16,128,128]{3,2,1,0:T(8,128)(2,1)}, bf16[2,16,128,128]{3,2,1,0:T(8,128)(2,1)}, u32[]{:S(2)}, u32[]{:S(2)}) collective-permute-start(bf16[2,16,128,128]{3,2,1,0:T(8,128)(2,1)} %copy-done.8), channel_id=1, source_target_pairs={{0,2},{1,3},{2,0},{3,1},{4,6},{5,7},{6,4},{7,5},{8,10},{9,11},{10,... | collective-permute-start | bytes 3145736 | tf_op jit(solution)/shard_map/ppermute | solution.py:25
  28.2 28.0 %copy-start.9 = (s32[16]{0:T(128)S(1)}, s32[16]{0:T(128)}, u32[]{:S(2)}) copy-start(s32[16]{0:T(128)} %constant.298.clone) | copy-start | bytes 196
  28.2 5.1 %collective-permute-start.8 = (bf16[1,4,2,16,384]{4,3,2,1,0:T(8,128)(2,1)S(1)}, bf16[1,4,2,16,384]{4,3,2,1,0:T(8,128)(2,1)S(1)}, u32[]{:S(2)}, u32[]{:S(2)}) collective-permute-start(bf16[1,4,2,16,384]{4,3,2,1,0:T(8,128)(2,1)S(1)} %bitcast.35), channel_id=1, source_target_pairs={{0,6},{1,7},{2,4},{3,5},{4,2},{5,3},{6,0},{7,1},{8,14},{9,15},{10,... | collective-permute-start | bytes 294920 | tf_op jit(solution)/shard_map/ppermute | solution.py:25
  33.3 3.5 %collective-permute-start.9 = (bf16[2,1,2,16,384]{4,3,2,1,0:T(8,128)(2,1)S(1)}, bf16[2,1,2,16,384]{4,3,2,1,0:T(8,128)(2,1)S(1)}, u32[]{:S(2)}, u32[]{:S(2)}) collective-permute-start(bf16[2,1,2,16,384]{4,3,2,1,0:T(8,128)(2,1)S(1)} %get-tuple-element.26), channel_id=1, source_target_pairs={{0,4},{1,5},{2,6},{3,7},{4,0},{5,1},{6,2},{7,3},{8,12},{9,13},{10,... | collective-permute-start | bytes 147464 | tf_op jit(solution)/shard_map/ppermute | solution.py:25
  33.4 6.3 %collective-permute-start.11 = (bf16[2,1,2,16,384]{4,3,2,1,0:T(8,128)(2,1)S(1)}, bf16[2,1,2,16,384]{4,3,2,1,0:T(8,128)(2,1)S(1)}, u32[]{:S(2)}, u32[]{:S(2)}) collective-permute-start(bf16[2,1,2,16,384]{4,3,2,1,0:T(8,128)(2,1)S(1)} %get-tuple-element.27), channel_id=1, source_target_pairs={{0,12},{1,13},{2,14},{3,15},{4,8},{5,9},{6,10},{7,11},{8,4},{9,5},... | collective-permute-start | bytes 147464 | tf_op jit(solution)/shard_map/ppermute | solution.py:25
  35.8 5.2 %collective-permute-start.10 = (bf16[2,1,2,16,384]{4,3,2,1,0:T(8,128)(2,1)S(1)}, bf16[2,1,2,16,384]{4,3,2,1,0:T(8,128)(2,1)S(1)}, u32[]{:S(2)}, u32[]{:S(2)}) collective-permute-start(bf16[2,1,2,16,384]{4,3,2,1,0:T(8,128)(2,1)S(1)} %get-tuple-element.28), channel_id=1, source_target_pairs={{0,8},{1,9},{2,10},{3,11},{4,12},{5,13},{6,14},{7,15},{8,0},{9,1},... | collective-permute-start | bytes 147464 | tf_op jit(solution)/shard_map/ppermute | solution.py:25
  36.8 40.0 %collective-permute-start.22 = (bf16[2,16,128,128]{3,2,1,0:T(8,128)(2,1)}, bf16[2,16,128,128]{3,2,1,0:T(8,128)(2,1)S(1)}, u32[]{:S(2)}, u32[]{:S(2)}) collective-permute-start(bf16[2,16,128,128]{3,2,1,0:T(8,128)(2,1)} %copy-done.7), channel_id=1, source_target_pairs={{0,3},{1,2},{2,1},{3,0},{4,7},{5,6},{6,5},{7,4},{8,11},{9,10},{10,... | collective-permute-start | bytes 3145736 | tf_op jit(solution)/shard_map/ppermute | solution.py:25
  41.1 2.3 %collective-permute-start.12 = (bf16[2,4,1,16,384]{4,3,2,1,0:T(8,128)(2,1)S(1)}, bf16[2,4,1,16,384]{4,3,2,1,0:T(8,128)(2,1)S(1)}, u32[]{:S(2)}, u32[]{:S(2)}) collective-permute-start(bf16[2,4,1,16,384]{4,3,2,1,0:T(8,128)(2,1)S(1)} %get-tuple-element.24), channel_id=1, source_target_pairs={{0,1},{1,0},{2,3},{3,2},{4,5},{5,4},{6,7},{7,6},{8,9},{9,8},{10,11... | collective-permute-start | bytes 294920 | tf_op jit(solution)/shard_map/ppermute | solution.py:25
  43.4 2.2 %copy-start = (bf16[8,16,128,128]{3,2,1,0:T(8,128)(2,1)S(1)}, bf16[8,16,128,128]{3,2,1,0:T(8,128)(2,1)}, u32[]{:S(2)}) copy-start(bf16[8,16,128,128]{3,2,1,0:T(8,128)(2,1)} %states_ref.5) | copy-start | bytes 12582916
  48.5 4.0 %collective-permute-start.14 = (bf16[24,1024]{1,0:T(8,128)(2,1)S(1)}, bf16[24,1024]{1,0:T(8,128)(2,1)S(1)}, u32[]{:S(2)}, u32[]{:S(2)}) collective-permute-start(bf16[24,1024]{1,0:T(8,128)(2,1)S(1)} %readout.1), channel_id=1, source_target_pairs={{0,6},{1,7},{2,4},{3,5},{4,2},{5,3},{6,0},{7,1},{8,14},{9,15},{10,... | collective-permute-start | bytes 147464 | tf_op jit(solution)/shard_map/ppermute | solution.py:25
  52.6 7.2 %collective-permute-start.17 = (bf16[48,1024]{1,0:T(8,128)(2,1)S(1)}, bf16[48,1024]{1,0:T(8,128)(2,1)S(1)}, u32[]{:S(2)}, u32[]{:S(2)}) collective-permute-start(bf16[48,1024]{1,0:T(8,128)(2,1)S(1)} %pad_maximum_fusion.2.refs_0_), channel_id=1, source_target_pairs={{0,12},{1,13},{2,14},{3,15},{4,8},{5,9},{6,10},{7,11},{8,4},{9,5},... | collective-permute-start | bytes 294920 | tf_op jit(solution)/shard_map/ppermute | solution.py:25
  54.8 8.7 %collective-permute-start.16 = (bf16[48,1024]{1,0:T(8,128)(2,1)S(1)}, bf16[48,1024]{1,0:T(8,128)(2,1)S(1)}, u32[]{:S(2)}, u32[]{:S(2)}) collective-permute-start(bf16[48,1024]{1,0:T(8,128)(2,1)S(1)} %pad_maximum_fusion.2.refs_0_), channel_id=1, source_target_pairs={{0,8},{1,9},{2,10},{3,11},{4,12},{5,13},{6,14},{7,15},{8,0},{9,1},... | collective-permute-start | bytes 294920 | tf_op jit(solution)/shard_map/ppermute | solution.py:25
  54.8 10.1 %collective-permute-start.15 = (bf16[48,1024]{1,0:T(8,128)(2,1)S(1)}, bf16[48,1024]{1,0:T(8,128)(2,1)S(1)}, u32[]{:S(2)}, u32[]{:S(2)}) collective-permute-start(bf16[48,1024]{1,0:T(8,128)(2,1)S(1)} %pad_maximum_fusion.2.refs_0_), channel_id=1, source_target_pairs={{0,4},{1,5},{2,6},{3,7},{4,0},{5,1},{6,2},{7,3},{8,12},{9,13},{10,... | collective-permute-start | bytes 294920 | tf_op jit(solution)/shard_map/ppermute | solution.py:25
  57.4 23.5 %collective-permute-start.18 = (bf16[48,1024]{1,0:T(8,128)(2,1)S(1)}, bf16[48,1024]{1,0:T(8,128)(2,1)S(1)}, u32[]{:S(2)}, u32[]{:S(2)}) collective-permute-start(bf16[48,1024]{1,0:T(8,128)(2,1)S(1)} %pad_maximum_fusion.2.refs_0_), channel_id=1, source_target_pairs={{0,1},{1,0},{2,3},{3,2},{4,5},{5,4},{6,7},{7,6},{8,9},{9,8},{10,11... | collective-permute-start | bytes 294920 | tf_op jit(solution)/shard_map/ppermute | solution.py:25
  59.8 21.2 %collective-permute-start.21 = (bf16[48,1024]{1,0:T(8,128)(2,1)S(1)}, bf16[48,1024]{1,0:T(8,128)(2,1)S(1)}, u32[]{:S(2)}, u32[]{:S(2)}) collective-permute-start(bf16[48,1024]{1,0:T(8,128)(2,1)S(1)} %collective-permute-done.17.refs_3_), channel_id=1, source_target_pairs={{0,1},{1,0},{2,3},{3,2},{4,5},{5,4},{6,7},{7,6},{8,9},{9,8},{10,11... | collective-permute-start | bytes 294920 | tf_op jit(solution)/shard_map/ppermute | solution.py:25
  63.5 17.5 %collective-permute-start.20 = (bf16[48,1024]{1,0:T(8,128)(2,1)S(1)}, bf16[48,1024]{1,0:T(8,128)(2,1)S(1)}, u32[]{:S(2)}, u32[]{:S(2)}) collective-permute-start(bf16[48,1024]{1,0:T(8,128)(2,1)S(1)} %collective-permute-done.16.refs_2_), channel_id=1, source_target_pairs={{0,1},{1,0},{2,3},{3,2},{4,5},{5,4},{6,7},{7,6},{8,9},{9,8},{10,11... | collective-permute-start | bytes 294920 | tf_op jit(solution)/shard_map/ppermute | solution.py:25
  64.9 16.1 %collective-permute-start.19 = (bf16[48,1024]{1,0:T(8,128)(2,1)S(1)}, bf16[48,1024]{1,0:T(8,128)(2,1)S(1)}, u32[]{:S(2)}, u32[]{:S(2)}) collective-permute-start(bf16[48,1024]{1,0:T(8,128)(2,1)S(1)} %collective-permute-done.15.refs_1_), channel_id=1, source_target_pairs={{0,1},{1,0},{2,3},{3,2},{4,5},{5,4},{6,7},{7,6},{8,9},{9,8},{10,11... | collective-permute-start | bytes 294920 | tf_op jit(solution)/shard_map/ppermute | solution.py:25
  76.8 4.2 %copy-start.2 = (bf16[2048,128]{1,0:T(8,128)(2,1)S(1)}, bf16[2048,128]{1,0:T(8,128)(2,1)}, u32[]{:S(2)}) copy-start(bf16[2048,128]{1,0:T(8,128)(2,1)} %weight_ref.1) | copy-start | bytes 1572868

commit v3 on v2

v3 whole, which is shorter than its diff:
```python
import functools
import math

import jax
import jax.numpy as jnp
from jax import lax
from jax.experimental import pallas as pl
from jax.experimental.pallas import tpu as pltpu
from jax.sharding import PartitionSpec as P

CAP = 2
TILE = 16
VMEM_BYTES = 24 * 1024 * 1024
WHOLE = pl.BlockSpec(memory_space=pltpu.VMEM)
SCALARS = pl.BlockSpec(memory_space=pltpu.SMEM)
PLACED = pl.BlockSpec(memory_space=pl.ANY)


def params():
    return pltpu.CompilerParams(vmem_limit_bytes=VMEM_BYTES)


def in_hbm(array):
    return pltpu.with_memory_space_constraint(array, pltpu.HBM)


def xor_permute(block, distance):
    count = lax.axis_size("rows")
    return lax.ppermute(block, "rows", [(i, i ^ distance) for i in range(count)])


def stage_plan(count):
    if count == 1:
        return []
    if count == 2:
        return [[1]]
    if count == 4:
        return [[2], [1]]
    plan = [[6], [4, 8, 12] if count >= 16 else [4]]
    bit = 16
    while bit < count:
        plan.append([bit])
        bit *= 2
    return plan + [[1]]


def plan_order(plan):
    order = [0]
    for stage in plan:
        order = [near ^ far for near in order for far in [0] + stage]
    return order


def gather_order(plan):
    order = [0]
    for stage in plan:
        order = [near ^ far for far in [0] + stage for near in order]
    return order


def gather_all(block, plan, after=lambda stage, held: held):
    held = [block]
    for number, stage in enumerate(plan):
        held = held + [xor_permute(part, distance) for distance in stage for part in held]
        if len(held) == 2:
            held = [jnp.concatenate(held, 0)]
        held = after(number, held)
    return held


def exchange_all(pieces, plan, after=lambda stage, held: held):
    tail = pieces.shape[1:]
    held = [pieces.reshape(tuple(len(stage) + 1 for stage in plan) + tail)]
    for axis, stage in enumerate(plan):
        slab = lambda part, place: lax.index_in_dim(part, place, axis, keepdims=True)
        fresh = []
        for part in held:
            fresh.append(slab(part, 0))
            fresh += [xor_permute(slab(part, place + 1), distance) for place, distance in enumerate(stage)]
        held = after(axis, [jnp.concatenate(fresh, 0)] if axis == 0 else fresh)
    return [part.reshape((-1,) + tail) for part in held]


def split(number, size):
    if size & (size - 1) == 0:
        return lax.shift_right_logical(number, size.bit_length() - 1), number & (size - 1)
    return lax.div(number, size), lax.rem(number, size)


def place_in(order, distance):
    place, bit = distance & 0, 0
    while 1 << bit < len(order):
        place = place ^ ((lax.shift_right_logical(distance, bit) & 1) * order.index(1 << bit))
        bit += 1
    return place


def row_facts(parent_row, blocks, own_rows):
    lane = lax.broadcasted_iota(jnp.int32, parent_row.shape, 1)
    device, child = split(lane, own_rows)
    parent_block, parent_place = split(parent_row, own_rows)
    rank = jnp.zeros_like(lane)
    for earlier in range(1, own_rows):
        same = (pltpu.roll(parent_block, earlier, 1) == parent_block) & (child >= earlier)
        rank = rank + same.astype(jnp.int32)
    away = parent_block ^ (device & (blocks - 1))
    over = away >= 2
    slot = own_rows + (away - 2) * CAP + rank
    near_place = jnp.where(away == 0, parent_place, own_rows + rank)
    return device, child, over, device ^ away, slot, parent_place, near_place


def column_of(row):
    spread = jnp.broadcast_to(row[0:1].astype(jnp.float32), (8, row.shape[1]))
    return jnp.transpose(spread)[:, 0:1]


def chosen_rows(column, width):
    shape = (column.shape[0], width)
    return (lax.broadcasted_iota(jnp.int32, shape, 1).astype(jnp.float32) == column).astype(jnp.float32)


def matching_children(parent_ref, user, child_block, parent_block, own_rows, none):
    children, parents, found = [jnp.int32(none)] * CAP, [jnp.int32(0)] * CAP, jnp.int32(0)
    for child in range(own_rows):
        block, place = split(parent_ref[0, user, child_block * own_rows + child], own_rows)
        hit = block == parent_block
        for j in range(CAP):
            children[j] = jnp.where(hit & (found == j), child, children[j])
            parents[j] = jnp.where(hit & (found == j), place, parents[j])
        found = found + hit.astype(jnp.int32)
    return children, parents


def fetch_kernel(
    blocks, me_ref, parent_ref, token_ref, tokens_ref, table_ref, states_ref, x_ref, first_ref, rows_ref, row_sem, state_sem
):
    count, own_rows = token_ref.shape[1], states_ref.shape[0]
    user, member = split(me_ref[0], blocks)
    _, chosen = matching_children(parent_ref, user, member ^ 2, member, own_rows, 0)
    state_copy = pltpu.make_async_copy(states_ref.at[chosen[0]], first_ref.at[0], state_sem)
    state_copy.start()

    def start_row(r, carry):
        first = pl.multiple_of(split(token_ref[0, r], TILE)[0] * TILE, TILE)
        pltpu.make_async_copy(
            table_ref.at[pl.ds(first, TILE)],
            rows_ref.at[pl.ds(pl.multiple_of(r * TILE, TILE), TILE)],
            row_sem,
        ).start()
        return carry

    lax.fori_loop(0, count, start_row, 0, unroll=8)
    step = math.gcd(count, 128)
    picks = []
    for first in range(0, count, step):
        low = column_of(split(tokens_ref[:, first : first + step], TILE)[1])
        wanted = low + lax.broadcasted_iota(jnp.int32, (step, 1), 0).astype(jnp.float32) * TILE
        picks.append(chosen_rows(wanted, step * TILE).astype(jnp.bfloat16))
    pltpu.make_async_copy(table_ref.at[pl.ds(0, count * TILE)], rows_ref, row_sem).wait()
    for first, pick in zip(range(0, count, step), picks):
        x_ref[first : first + step, :] = jnp.dot(
            pick, rows_ref[first * TILE : (first + step) * TILE, :], preferred_element_type=jnp.float32
        ).astype(jnp.bfloat16)
    state_copy.wait()


def stage_kernel(
    blocks, slots, send_order, normed_order, me_ref, parent_ref, parents_ref, states_ref,
    second_ref, third_ref, fourth_ref, near_ref, send_pick_ref, place_ref, low_pick_ref, high_pick_ref, hold_ref, in_sem, out_sem,
):
    me, own_rows = me_ref[0], states_ref.shape[0]
    user, member = split(me, blocks)
    wanted = []
    for partner in (2, 3, 1):
        wanted += matching_children(parent_ref, user, member ^ partner, member, own_rows, 0)[1]
    outs = [second_ref.at[0], third_ref.at[0], fourth_ref.at[0], near_ref.at[0], near_ref.at[1]]
    loads, saves = [], []
    for place, (row, out) in enumerate(zip(wanted[1:], outs)):
        loads.append(pltpu.make_async_copy(states_ref.at[row], hold_ref.at[place], in_sem.at[place]))
        saves.append(pltpu.make_async_copy(hold_ref.at[place], out, out_sem.at[place]))
        loads[-1].start()
    device, child, over, holder, slot, parent_place, near_place = row_facts(parents_ref[...], blocks, own_rows)
    rows = parents_ref.shape[1]
    own_target = place_in(send_order, device ^ me) * slots + child
    far_target = jnp.where(over, place_in(send_order, holder ^ me) * slots + slot, -1)
    line = lax.broadcasted_iota(jnp.int32, (len(send_order) * slots, rows), 0)
    send_pick_ref[...] = ((line == own_target[0:1]) | (line == far_target[0:1])).astype(jnp.float32).astype(jnp.bfloat16)
    for load, save in zip(loads, saves):
        load.wait()
        save.start()
    line = lax.broadcasted_iota(jnp.int32, (slots, rows), 0)
    own = (line == jnp.where((device == me) & ~over, child, -1)[0:1]).astype(jnp.float32)
    far = (line == jnp.where((holder == me) & over, slot, -1)[0:1]).astype(jnp.float32)
    place = own * (near_place[0:1] + 1).astype(jnp.float32) + far * (parent_place[0:1] + 1).astype(jnp.float32)
    place_ref[...] = jnp.broadcast_to(jnp.sum(place, axis=1, keepdims=True) - 1.0, place_ref.shape)
    piece = 2 * (own_rows + 2 * CAP)
    low = place_in(normed_order, jnp.where(over, holder, device) ^ me) * piece + jnp.where(over, own_rows + slot, child)
    high = low + jnp.where(over, 2 * CAP, own_rows)
    for index, ref in ((low, low_pick_ref), (high, high_pick_ref)):
        ref[...] = chosen_rows(column_of(index), ref.shape[1]).astype(jnp.bfloat16)
    for save in saves:
        save.wait()


def project_kernel(order, me_ref, weight_ref, pick_ref, *refs):
    held, out_ref = refs[:-1], refs[-1]
    me, columns, parts = me_ref[0], held[0].shape[1], len(held)
    rows = pick_ref.shape[1]
    total = [None] * 3
    for place, distance in enumerate(order):
        ref, within = held[place * parts // len(order)], place % (len(order) // parts)
        block = ref[within * rows : (within + 1) * rows, :]
        first = pl.multiple_of((me ^ distance) * columns, columns)
        for slab in range(3):
            term = jnp.dot(block, weight_ref[slab, pl.ds(first, columns), :], preferred_element_type=jnp.float32)
            total[slab] = term if total[slab] is None else total[slab] + term
    for slab in range(3):
        out_ref[:, slab * columns : (slab + 1) * columns] = jnp.dot(
            pick_ref[...], total[slab].astype(jnp.bfloat16), preferred_element_type=jnp.float32
        ).astype(jnp.bfloat16)


def head_terms(piece, gate_row, bias, size):
    keys = piece[:, size : 2 * size].astype(jnp.float32)
    values = piece[:, 2 * size :].astype(jnp.float32)
    logit = jnp.sum(keys * gate_row, axis=-1, keepdims=True) / math.sqrt(size) + bias
    decay = 1.0 / (1.0 + jnp.exp(-logit))
    inverse = lax.rsqrt(jnp.sum(keys * keys, axis=-1, keepdims=True) + 1e-06)
    return keys, values, decay, inverse


def lane_of(recv_order, me, head):
    return head if recv_order is None else place_in(recv_order, me ^ head)


def readout_kernel(recv_order, me_ref, bias_ref, place_ref, states_ref, near_ref, gate_ref, gain_ref, *refs):
    parts, (out_ref, recv_ref, norm_ref) = refs[:-3], refs[-3:]
    own_rows, block, size = states_ref.shape[0], states_ref.shape[1], states_ref.shape[2]
    step = pl.program_id(0)

    @pl.when(step == 0)
    def _():
        for number, part in enumerate(parts):
            for within in range(part.shape[0]):
                recv_ref[within * len(parts) + number] = part[within]

    place = place_ref[:, 0:1]
    for part in range(block):
        head = step * block + part
        piece = recv_ref[lane_of(recv_order, me_ref[0], head)]
        keys, values, decay, inverse = head_terms(piece, gate_ref[pl.ds(head, 1), :], bias_ref[head], size)
        queries = piece[:, :size].astype(jnp.float32)
        prior_part = None
        for ref, first in ((states_ref, 0), (near_ref, own_rows)):
            count = ref.shape[0]
            spread = jnp.concatenate(
                [jnp.where(place == float(first + p), queries, 0.0).astype(jnp.bfloat16) for p in range(count)], 1
            )
            states = ref[:, part].reshape(count * size, size)
            term = jnp.dot(spread, states, preferred_element_type=jnp.float32)
            prior_part = term if prior_part is None else prior_part + term
        overlap = jnp.sum(queries * keys, axis=-1, keepdims=True) * inverse
        readout = decay * prior_part + overlap * values
        scale = lax.rsqrt(jnp.mean(readout * readout, axis=-1, keepdims=True) + 1e-05)
        norm_ref[head] = readout * scale * gain_ref[pl.ds(head, 1), :]

    @pl.when(step == pl.num_programs(0) - 1)
    def _():
        heads = norm_ref.shape[0]
        halves = []
        for first in (0, heads // 2):
            halves.append(jnp.concatenate([norm_ref[h] for h in range(first, first + heads // 2)], 1))
        foreign = own_rows + 2 * CAP
        out_ref[...] = jnp.concatenate(
            [half[:own_rows] for half in halves] + [half[own_rows:foreign] for half in halves], 0
        ).astype(jnp.bfloat16)


def output_kernel(x_ref, weight_ref, low_pick_ref, high_pick_ref, *refs):
    parts, out_ref = refs[:-1], refs[-1]
    half, columns = parts[0].shape[1], x_ref.shape[1]
    total = x_ref[...].astype(jnp.float32)
    for side, pick_ref in enumerate((low_pick_ref, high_pick_ref)):
        weight = weight_ref[side * half : (side + 1) * half, :]
        rest = jnp.concatenate([jnp.dot(part[...], weight, preferred_element_type=jnp.float32) for part in parts], 0)
        for _ in range(3):
            term = rest.astype(jnp.bfloat16)
            rest = rest - term.astype(jnp.float32)
            total = total + jnp.dot(pick_ref[...], term, preferred_element_type=jnp.float32)
    out_ref[...] = total.astype(jnp.bfloat16)


def main_update_kernel(
    recv_order, blocks, arrived, me_ref, parent_ref, bias_ref, recv_ref, states_ref, near_ref, gate_ref, *refs
):
    far_refs, (out_ref, turned_ref, terms_ref) = refs[: len(arrived)], refs[len(arrived) :]
    own_rows, block, size = states_ref.shape[0], states_ref.shape[1], states_ref.shape[2]
    slots, step = recv_ref.shape[1], pl.program_id(0)
    user, member = split(me_ref[0], blocks)
    sources, found = [], [jnp.int32(0)] * 4
    for row in range(own_rows):
        parent_block, place = split(parent_ref[0, user, member * own_rows + row], own_rows)
        away = parent_block ^ member
        far = [(away == partner) & (found[partner] == rank) for partner, rank in arrived]
        sources.append((place, away == 1, jnp.minimum(found[1], CAP - 1), far))
        found = [count + (away == partner).astype(jnp.int32) for partner, count in enumerate(found)]
    line = lax.broadcasted_iota(jnp.int32, (slots, size), 0)
    for part in range(block):
        head = step * block + part
        piece = recv_ref[lane_of(recv_order, me_ref[0], head)]
        keys, values, decay, inverse = head_terms(piece, gate_ref[pl.ds(head, 1), :], bias_ref[head], size)
        turned = jnp.transpose(keys).astype(jnp.bfloat16)
        turned_ref[part] = turned
        terms_ref[0, part] = jnp.broadcast_to(decay, (slots, size))
        terms_ref[1, part] = jnp.broadcast_to(inverse, (slots, size))
        spread = [jnp.where(line == row, values, 0.0).astype(jnp.bfloat16) for row in range(own_rows)]
        outer = jnp.dot(turned, jnp.concatenate(spread, 1), preferred_element_type=jnp.float32)
        for row in range(own_rows):
            place, is_near, rank, far = sources[row]
            prior = jnp.where(is_near, near_ref[rank, part], states_ref[place, part])
            for ref, is_far in zip(far_refs, far):
                prior = jnp.where(is_far, ref[0, part], prior)
            fresh = decay[row : row + 1, :] * prior.astype(jnp.float32)
            fresh = fresh + inverse[row : row + 1, :] * outer[:, row * size : (row + 1) * size]
            out_ref[row, part] = fresh.astype(jnp.bfloat16)


def last_update_kernel(
    recv_order, block, blocks, own_rows, partner, rank, me_ref, parent_ref, recv_ref, turned_ref, terms_ref, got_ref, old_ref,
    out_ref, new_ref, out_sem,
):
    heads, size = got_ref.shape[1], got_ref.shape[2]
    user, member = split(me_ref[0], blocks)
    child = matching_children(parent_ref, user, member, member ^ partner, own_rows, -1)[0][rank]
    line = lax.broadcasted_iota(jnp.int32, (recv_ref.shape[1], size), 0)

    def save(step):
        span = pl.ds(step * block, block)
        return pltpu.make_async_copy(new_ref.at[span], out_ref.at[jnp.maximum(child, 0), span], out_sem.at[step])

    @pl.when(child >= 0)
    def _():
        def work(step, carry):
            for part in range(block):
                head = step * block + part
                values = recv_ref[lane_of(recv_order, me_ref[0], head)][:, 2 * size :].astype(jnp.float32)
                value = jnp.where(line == child, values, 0.0).astype(jnp.bfloat16)
                outer = jnp.dot(turned_ref[head], value, preferred_element_type=jnp.float32)
                fresh = terms_ref[0, head, pl.ds(child, 1), :] * got_ref[0, head].astype(jnp.float32)
                fresh = fresh + terms_ref[1, head, pl.ds(child, 1), :] * outer
                new_ref[head] = fresh.astype(jnp.bfloat16)
            save(step).start()
            return carry

        lax.fori_loop(0, heads // block, work, 0)
        for step in range(heads // block):
            save(step).wait()


def per_device(
    token_ids,
    parents,
    states,
    embed_table,
    qkv_weight,
    gate_weight,
    gate_bias,
    norm_gain,
    out_weight,
):
    own_rows, heads, size = states.shape[0], states.shape[1], states.shape[2]
    width = heads * size
    columns = embed_table.shape[1]
    row_total = token_ids.shape[1]
    users, beam = parents.shape[1], parents.shape[2]
    blocks = beam // own_rows
    count = lax.axis_size("rows")
    me = lax.axis_index("rows").astype(jnp.int32)
    user, member = me // blocks, me % blocks
    plan = stage_plan(count)
    slots = own_rows + 4 * CAP
    state_slab = (CAP, heads, size, size)
    bf16, int32 = jnp.bfloat16, jnp.int32
    mine = me[None]
    parent_row = jnp.broadcast_to(parents.reshape(1, row_total), (8, row_total))
    head_block = math.gcd(heads, 4)

    one_state = (1, heads, size, size)
    local_columns, first_out = pl.pallas_call(
        functools.partial(fetch_kernel, blocks),
        in_specs=[SCALARS, SCALARS, SCALARS, WHOLE, PLACED, PLACED],
        out_specs=[WHOLE] * 2,
        out_shape=[pltpu.VMEM((row_total, columns), bf16), pltpu.VMEM(one_state, bf16)],
        scratch_shapes=[
            pltpu.VMEM((row_total * TILE, columns), bf16),
            pltpu.SemaphoreType.DMA,
            pltpu.SemaphoreType.DMA,
        ],
        compiler_params=params(),
        name="fetch",
    )(mine, in_hbm(parents), in_hbm(token_ids), in_hbm(token_ids), in_hbm(embed_table), in_hbm(states))

    recv_order, normed_order = plan_order(plan), gather_order(plan)
    piece_rows = 2 * (own_rows + 2 * CAP)
    moved = 2 * CAP + 1
    second_out, third_out, fourth_out, near_out, send_pick, place, low_pick, high_pick = pl.pallas_call(
        functools.partial(stage_kernel, blocks, slots, recv_order, normed_order),
        in_specs=[SCALARS, SCALARS, WHOLE, PLACED],
        out_specs=[PLACED] * 4 + [WHOLE] * 4,
        out_shape=[pltpu.HBM(one_state, bf16)] * 3
        + [
            pltpu.HBM(state_slab, bf16),
            jax.ShapeDtypeStruct((count * slots, row_total), bf16),
            jax.ShapeDtypeStruct((slots, 128), jnp.float32),
            jax.ShapeDtypeStruct((row_total, count * piece_rows), bf16),
            jax.ShapeDtypeStruct((row_total, count * piece_rows), bf16),
        ],
        scratch_shapes=[
            pltpu.VMEM((moved, heads, size, size), bf16),
            pltpu.SemaphoreType.DMA((moved,)),
            pltpu.SemaphoreType.DMA((moved,)),
        ],
        compiler_params=params(),
        name="stage",
    )(mine, in_hbm(parents), parent_row, in_hbm(states))
    sends = [first_out, second_out, third_out, fourth_out]
    arrivals = [(partner, rank) for partner in (2, 3) for rank in range(CAP)]
    gots = [xor_permute(block, partner) for block, (partner, _) in zip(sends, arrivals)]
    near_got = xor_permute(near_out, 1)

    weight = jnp.transpose(qkv_weight, (1, 0, 2))
    tied = {}

    def in_inputs(stage, parts):
        if stage == 0:
            *parts, tied["weight"], tied["pick"] = lax.optimization_barrier((*parts, weight, send_pick))
        if stage == 1:
            *parts, gots[0] = lax.optimization_barrier((*parts, gots[0]))
        return parts

    every_input = gather_all(local_columns, plan, in_inputs)
    pieces = pl.pallas_call(
        functools.partial(project_kernel, normed_order),
        in_specs=[SCALARS] + [WHOLE] * (2 + len(every_input)),
        out_specs=WHOLE,
        out_shape=jax.ShapeDtypeStruct((count * slots, 3 * columns), bf16),
        compiler_params=params(),
        name="project",
    )(mine, tied["weight"], tied["pick"], *every_input)

    def in_exchange(stage, parts):
        if stage == 1:
            *parts, gots[1] = lax.optimization_barrier((*parts, gots[1]))
        return parts

    received = exchange_all(pieces.reshape(count, slots, 3 * columns), plan, in_exchange)
    if columns != size:
        every_piece = jnp.stack(received, 1).reshape(count, slots, 3 * columns)
        places = jnp.array([recv_order.index(d) for d in range(count)], int32)[jnp.arange(count, dtype=int32) ^ me]
        every_piece = jnp.take(every_piece, places, axis=0).reshape(count, slots, 3, columns).transpose(1, 2, 0, 3)
        received = [every_piece.reshape(slots, 3, heads, size).transpose(2, 0, 1, 3).reshape(heads, slots, 3 * size)]
        recv_order = None

    by_heads = lambda rows: pl.BlockSpec((rows, head_block, size, size), lambda i: (0, i, 0, 0))
    normed, by_head = pl.pallas_call(
        functools.partial(readout_kernel, recv_order),
        grid=(heads // head_block,),
        in_specs=[SCALARS] * 2 + [WHOLE, by_heads(own_rows), by_heads(CAP)] + [WHOLE] * (2 + len(received)),
        out_specs=[WHOLE] * 2,
        out_shape=[
            jax.ShapeDtypeStruct((piece_rows, width // 2), bf16),
            jax.ShapeDtypeStruct((heads, slots, 3 * size), bf16),
        ],
        scratch_shapes=[pltpu.VMEM((heads, slots, size), jnp.float32)],
        compiler_params=params(),
        name="readout",
    )(mine, gate_bias, place, in_hbm(states), near_got, gate_weight, norm_gain.reshape(heads, size), *received)

    early = len(arrivals) - 1
    main_done, turned, terms = pl.pallas_call(
        functools.partial(main_update_kernel, recv_order, blocks, arrivals[:early]),
        grid=(heads // head_block,),
        in_specs=[SCALARS] * 3
        + [WHOLE, by_heads(own_rows), by_heads(CAP), WHOLE]
        + [by_heads(1)] * early,
        out_specs=[
            by_heads(own_rows),
            pl.BlockSpec((head_block, size, slots), lambda i: (i, 0, 0)),
            pl.BlockSpec((2, head_block, slots, size), lambda i: (0, i, 0, 0)),
        ],
        out_shape=[
            jax.ShapeDtypeStruct(states.shape, bf16),
            jax.ShapeDtypeStruct((heads, size, slots), bf16),
            jax.ShapeDtypeStruct((2, heads, slots, size), jnp.float32),
        ],
        compiler_params=params(),
        name="main_update",
    )(mine, parents, gate_bias, by_head, in_hbm(states), near_got, gate_weight, *gots[:early])

    def in_normed(stage, parts):
        if stage == 1:
            parts[-1], tied["done"], tied["turned"] = lax.optimization_barrier((parts[-1], main_done, turned))
        return parts

    every_normed = gather_all(normed, plan, in_normed)
    final = pl.pallas_call(
        functools.partial(last_update_kernel, recv_order, head_block, blocks, own_rows, *arrivals[early]),
        in_specs=[SCALARS] * 2 + [WHOLE] * 4 + [PLACED],
        out_specs=PLACED,
        out_shape=jax.ShapeDtypeStruct(states.shape, bf16),
        scratch_shapes=[pltpu.VMEM(one_state[1:], bf16), pltpu.SemaphoreType.DMA((heads // head_block,))],
        input_output_aliases={6: 0},
        compiler_params=params(),
        name="last_update",
    )(mine, parents, by_head, tied["turned"], terms, gots[early], tied["done"])
    layer_out = pl.pallas_call(
        output_kernel,
        in_specs=[WHOLE] * (4 + len(every_normed)),
        out_specs=WHOLE,
        out_shape=jax.ShapeDtypeStruct((row_total, columns), bf16),
        compiler_params=params(),
        name="output",
    )(local_columns, out_weight, low_pick, high_pick, *every_normed)
    return (layer_out[None], final)


def solution(mesh):
    placed = (
        P(None, "groups"),
        P(None, "groups", None),
        P(("groups", "rows"), None, None, None),
        P(None, "rows"),
        P(None, None, "rows"),
        P(),
        P(),
        P(),
        P(None, "rows"),
    )
    return jax.shard_map(
        per_device,
        mesh=mesh,
        in_specs=placed,
        out_specs=(P(None, "groups", "rows"), P(("groups", "rows"), None, None, None)),
        check_vma=False,
    )
```

time: 83.2 us -> 68.9 us (0.83)
  local copies, waits for them, and re-layouts: 10 us -> 0.18 us
  other arithmetic: 2.26 us -> 0.03 us
  Pallas kernels: 23.9 us -> 21.9 us
  starting transfers between devices: 28.2 us -> 27.1 us
    unnamed x29 -> x15, local copies, waits for them, and re-layouts: 5.01 us -> 0.04 us
    gather x4 -> x0, local copies, waits for them, and re-layouts: 3.15 us -> none  [the longest x2 1.26 us: per_device(): child = child_at[device_user, child_block, device_member]]
    reduce_sum x2 -> x0, other arithmetic: 1.64 us -> none  [the longest x1 1.21 us: per_device(): jnp.sum(jnp.where(hit, parent_row[:, :, None, None, :], 0), axis=-1)]
    pallas_call x1, Pallas kernels: 4.18 us -> 2.67 us  [per_device(): pl.pallas_call(functools.partial(fetch_kernel, blocks), in_specs=[SCALARS...]
    ppermute x24 -> x29, starting transfers between devices: 28.2 us -> 27.1 us  [xor_permute(): lax.ppermute(block, 'rows', [(i, i ^ distance) for i in range(count)])]
    reshape x3 -> x0, local copies, waits for them, and re-layouts: 0.93 us -> none  [the longest x1 0.77 us: per_device(): parents.reshape(-1)]
    ppermute x24 -> x29, waiting for transfers between devices: 17.5 us -> 17.8 us  [xor_permute(): lax.ppermute(block, 'rows', [(i, i ^ distance) for i in range(count)])]
  transfers between devices with their start and end apart: 24 -> 29, of which waited for: 10 -> 11; matrix products, arithmetic and copies ran while one was open for 8% -> 0% of each run, Pallas kernels for 22% -> 26%
where the time goes in v3:
time: 68.9 us; the launch traced here: 67.9 us
  starting transfers between devices  27.1 us (39%)
  Pallas kernels  21.9 us (32%)
  waiting for transfers between devices  17.8 us (26%)
  between operations  0.84 us (1%)
    ppermute x29, starting transfers between devices, xor_permute(): lax.ppermute(block, 'rows', [(i, i ^ distance) for i in range(count)])  27.1 us
    ppermute x29, waiting for transfers between devices, xor_permute(): lax.ppermute(block, 'rows', [(i, i ^ distance) for i in range(count)])  17.8 us
    pallas_call x1, Pallas kernels, per_device(): pl.pallas_call(functools.partial(main_update_kernel, recv_order, blocks,...  6.78 us
    pallas_call x1, Pallas kernels, per_device(): pl.pallas_call(functools.partial(readout_kernel, recv_order), grid=(heads...  3.98 us
    pallas_call x1, Pallas kernels, per_device(): pl.pallas_call(functools.partial(stage_kernel, blocks, slots, recv_order,...  3.95 us
    pallas_call x1, Pallas kernels, per_device(): pl.pallas_call(functools.partial(fetch_kernel, blocks), in_specs=[SCALARS...  2.67 us
    pallas_call x1, Pallas kernels, per_device(): pl.pallas_call(functools.partial(last_update_kernel, recv_order, head_blo...  1.98 us
    pallas_call x1, Pallas kernels, per_device(): pl.pallas_call(output_kernel, in_specs=[WHOLE] * (4 + len(every_normed)),...  1.7 us
  transfers between devices with their start and end apart: 29, of which 11 were waited for; matrix products, arithmetic and copies ran while one was open for 0% of the time, Pallas kernels for 26%

profile of v3, /device:TPU:1, one launch (start us, length us, event | category | flops | bytes accessed | tf_op | source)
XLA Modules:
  0.0 67.9 jit_solution(6365688492513025900)
XLA Ops:
  0.6 0.0 copy-start.2
  0.6 2.7 %fetch.1 = (bf16[128,128]{1,0:T(8,128)(2,1)S(1)}, bf16[1,16,128,128]{3,2,1,0:T(8,128)(2,1)S(1)}) custom-call(s32[1]{0:T(128)} %bitcast.me_ref, s32[1,4,32]{2,1,0:T(4,128)} %parent_ref.7, s32[1,128]{1,0:T(1,128)} %tokens_ref.1, s32[1,128]{1,0:T(1,128)} %tokens_ref.1, bf16[32768,128]{1,0:T(8,128)(2,1)} %table_ref.1, bf16[8,16,128,128]{3,2,1,0:T(8,128)(2,1)} %states_ref.7), custom_call_target="tpu_custom_call" | custom-call | tf_op jit(solution)/shard_map/fetch/pallas_call | solution.py:390
  3.4 2.1 %collective-permute-start.5 = (bf16[1,16,128,128]{3,2,1,0:T(8,128)(2,1)S(1)}, bf16[1,16,128,128]{3,2,1,0:T(8,128)(2,1)S(1)}, u32[]{:S(2)}, u32[]{:S(2)}) collective-permute-start(bf16[1,16,128,128]{3,2,1,0:T(8,128)(2,1)S(1)} %get-tuple-element.42), channel_id=1, source_target_pairs={{0,2},{1,3},{2,0},{3,1},{4,6},{5,7},{6,4},{7,5},{8,10},{9,11},{10,... | collective-permute-start | bytes 1572872 | tf_op jit(solution)/shard_map/ppermute | solution.py:29
  5.5 1.2 %collective-permute-start.1 = (bf16[128,128]{1,0:T(8,128)(2,1)S(1)}, bf16[128,128]{1,0:T(8,128)(2,1)S(1)}, u32[]{:S(2)}, u32[]{:S(2)}) collective-permute-start(bf16[128,128]{1,0:T(8,128)(2,1)S(1)} %get-tuple-element.33.x_ref), channel_id=1, source_target_pairs={{0,6},{1,7},{2,4},{3,5},{4,2},{5,3},{6,0},{7,1},{8,14},{9,15},{10,... | collective-permute-start | bytes 98312 | tf_op jit(solution)/shard_map/ppermute | solution.py:29
  6.8 0.1 broadcast_in_dim.14
  6.8 4.0 %stage.1 = (bf16[1,16,128,128]{3,2,1,0:T(8,128)(2,1)}, bf16[1,16,128,128]{3,2,1,0:T(8,128)(2,1)}, bf16[1,16,128,128]{3,2,1,0:T(8,128)(2,1)}, bf16[2,16,128,128]{...) custom-call(s32[1]{0:T(128)} %bitcast.me_ref, ...), custom_call_target="tpu_custom_call" | custom-call | tf_op jit(solution)/shard_map/stage/pallas_call | solution.py:407
  10.8 0.1 collective-permute-start.2
  10.9 2.4 %collective-permute-start.3 = (bf16[256,128]{1,0:T(8,128)(2,1)S(1)}, bf16[256,128]{1,0:T(8,128)(2,1)S(1)}, u32[]{:S(2)}, u32[]{:S(2)}) collective-permute-start(bf16[256,128]{1,0:T(8,128)(2,1)S(1)} %pad_maximum_fusion.refs_0_), channel_id=1, source_target_pairs={{0,8},{1,9},{2,10},{3,11},{4,12},{5,13},{6,14},{7,15},{8,0},{9,1},... | collective-permute-start | bytes 196616 | tf_op jit(solution)/shard_map/ppermute | solution.py:29
  13.3 1.1 %collective-permute-start.4 = (bf16[256,128]{1,0:T(8,128)(2,1)S(1)}, bf16[256,128]{1,0:T(8,128)(2,1)S(1)}, u32[]{:S(2)}, u32[]{:S(2)}) collective-permute-start(bf16[256,128]{1,0:T(8,128)(2,1)S(1)} %pad_maximum_fusion.refs_0_), channel_id=1, source_target_pairs={{0,12},{1,13},{2,14},{3,15},{4,8},{5,9},{6,10},{7,11},{8,4},{9,5},... | collective-permute-start | bytes 196616 | tf_op jit(solution)/shard_map/ppermute | solution.py:29
  14.4 0.6 collective-permute-done.3.refs_2_
  15.1 4.0 %collective-permute-done.4.refs_3_ = bf16[256,128]{1,0:T(8,128)(2,1)S(1)} collective-permute-done((bf16[256,128]{1,0:T(8,128)(2,1)S(1)}, bf16[256,128]{1,0:T(8,128)(2,1)S(1)}, u32[]{:S(2)}, u32[]{:S(2)}) %collective-permute-start.4) | collective-permute-done | bytes 65568 | tf_op jit(solution)/shard_map/ppermute | solution.py:29
  19.1 2.6 %collective-permute-start.6 = (bf16[256,128]{1,0:T(8,128)(2,1)S(1)}, bf16[256,128]{1,0:T(8,128)(2,1)S(1)}, u32[]{:S(2)}, u32[]{:S(2)}) collective-permute-start(bf16[256,128]{1,0:T(8,128)(2,1)S(1)} %pad_maximum_fusion.refs_0_), channel_id=1, source_target_pairs={{0,1},{1,0},{2,3},{3,2},{4,5},{5,4},{6,7},{7,6},{8,9},{9,8},{10,11... | collective-permute-start | bytes 196616 | tf_op jit(solution)/shard_map/ppermute | solution.py:29
  21.7 0.5 collective-permute-start.8
  22.2 0.4 collective-permute-start.14
  22.6 0.3 collective-permute-done.7.refs_5_
  23.0 0.2 collective-permute-done.8.refs_6_
  23.1 0.4 collective-permute-done.9.refs_7_
  23.5 0.8 %project.1 = bf16[256,384]{1,0:T(8,128)(2,1)S(1)} custom-call(s32[1]{0:T(128)} %bitcast.me_ref, bf16[3,2048,128]{2,1,0:T(8,128)(2,1)S(1)} %bitcast.18, bf16[256,128]{1,0:T(8,128)(2,1)S(1)} %get-tuple-element.40.pick_ref, bf16[256,128]{1,0:T(8,128)(2,1)S(1)} %pad_maximum_fusion.refs_0_, bf16[256,128]{1,0:T(8,128)(2,1)S(1)} %collective-permute-done.2.refs_1_, ...), custom_call_target="tpu_custom_call" | custom-call | tf_op jit(solution)/shard_map/project/pallas_call | solution.py:443
  24.3 1.3 %collective-permute-start.10 = (bf16[1,4,2,16,384]{4,3,0,2,1:T(8,128)(2,1)S(1)}, bf16[1,4,2,16,384]{4,3,0,2,1:T(8,128)(2,1)S(1)}, u32[]{:S(2)}, u32[]{:S(2)}) collective-permute-start(bf16[1,4,2,16,384]{4,3,0,2,1:T(8,128)(2,1)S(1)} %bitcast.25), channel_id=1, source_target_pairs={{0,6},{1,7},{2,4},{3,5},{4,2},{5,3},{6,0},{7,1},{8,14},{9,15},{10,... | collective-permute-start | bytes 294920 | tf_op jit(solution)/shard_map/ppermute | solution.py:29
  25.6 0.4 collective-permute-start
  26.0 3.6 %collective-permute-done.10 = bf16[1,4,2,16,384]{4,3,0,2,1:T(8,128)(2,1)S(1)} collective-permute-done((bf16[1,4,2,16,384]{4,3,0,2,1:T(8,128)(2,1)S(1)}, bf16[1,4,2,16,384]{4,3,0,2,1:T(8,128)(2,1)S(1)}, u32[]{:S(2)}, u32[]{:S(2)}) %collective-permute-start.10) | collective-permute-done | bytes 98336 | tf_op jit(solution)/shard_map/ppermute | solution.py:29
  29.6 0.1 collective-permute-start.11
  29.7 1.1 %collective-permute-start.12 = (bf16[2,1,2,16,384]{4,3,0,2,1:T(8,128)(2,1)S(1)}, bf16[2,1,2,16,384]{4,3,0,2,1:T(8,128)(2,1)S(1)}, u32[]{:S(2)}, u32[]{:S(2)}) collective-permute-start(bf16[2,1,2,16,384]{4,3,0,2,1:T(8,128)(2,1)S(1)} %get-tuple-element.67), channel_id=1, source_target_pairs={{0,8},{1,9},{2,10},{3,11},{4,12},{5,13},{6,14},{7,15},{8,0},{9,1},... | collective-permute-start | bytes 147464 | tf_op jit(solution)/shard_map/ppermute | solution.py:29
  30.8 2.4 %collective-permute-start.13 = (bf16[2,1,2,16,384]{4,3,0,2,1:T(8,128)(2,1)S(1)}, bf16[2,1,2,16,384]{4,3,0,2,1:T(8,128)(2,1)S(1)}, u32[]{:S(2)}, u32[]{:S(2)}) collective-permute-start(bf16[2,1,2,16,384]{4,3,0,2,1:T(8,128)(2,1)S(1)} %get-tuple-element.64), channel_id=1, source_target_pairs={{0,12},{1,13},{2,14},{3,15},{4,8},{5,9},{6,10},{7,11},{8,4},{9,5},... | collective-permute-start | bytes 147464 | tf_op jit(solution)/shard_map/ppermute | solution.py:29
  33.2 4.3 %collective-permute-done.14.refs_1_ = bf16[1,16,128,128]{3,2,1,0:T(8,128)(2,1)S(1)} collective-permute-done((bf16[1,16,128,128]{3,2,1,0:T(8,128)(2,1)}, bf16[1,16,128,128]{3,2,1,0:T(8,128)(2,1)S(1)}, u32[]{:S(2)}, u32[]{:S(2)}) %collective-permute-start.14) | collective-permute-done | bytes 524320 | tf_op jit(solution)/shard_map/ppermute | solution.py:29
  37.5 1.7 %collective-permute-start.23 = (bf16[1,16,128,128]{3,2,1,0:T(8,128)(2,1)}, bf16[1,16,128,128]{3,2,1,0:T(8,128)(2,1)S(1)}, u32[]{:S(2)}, u32[]{:S(2)}) collective-permute-start(bf16[1,16,128,128]{3,2,1,0:T(8,128)(2,1)} %get-tuple-element.56), channel_id=1, source_target_pairs={{0,3},{1,2},{2,1},{3,0},{4,7},{5,6},{6,5},{7,4},{8,11},{9,10},{10,... | collective-permute-start | bytes 1572872 | tf_op jit(solution)/shard_map/ppermute | solution.py:29
  39.2 0.1 collective-permute-start.28
  39.3 1.4 %collective-permute-start.15 = (bf16[2,1,1,16,384]{4,3,0,2,1:T(8,128)(2,1)S(1)}, bf16[2,1,1,16,384]{4,3,0,2,1:T(8,128)(2,1)S(1)}, u32[]{:S(2)}, u32[]{:S(2)}) collective-permute-start(bf16[2,1,1,16,384]{4,3,0,2,1:T(8,128)(2,1)S(1)} %get-tuple-element.76), channel_id=1, source_target_pairs={{0,1},{1,0},{2,3},{3,2},{4,5},{5,4},{6,7},{7,6},{8,9},{9,8},{10,11... | collective-permute-start | bytes 73736 | tf_op jit(solution)/shard_map/ppermute | solution.py:29
  40.7 0.1 collective-permute-start.16
  40.8 0.7 %collective-permute-done.15 = bf16[2,1,1,16,384]{4,3,0,2,1:T(8,128)(2,1)S(1)} collective-permute-done((bf16[2,1,1,16,384]{4,3,0,2,1:T(8,128)(2,1)S(1)}, bf16[2,1,1,16,384]{4,3,0,2,1:T(8,128)(2,1)S(1)}, u32[]{:S(2)}, u32[]{:S(2)}) %collective-permute-start.15) | collective-permute-done | bytes 24608 | tf_op jit(solution)/shard_map/ppermute | solution.py:29
  41.6 0.3 collective-permute-start.17
  41.9 0.0 collective-permute-done.16
  41.9 0.2 collective-permute-start.18
  42.1 0.7 collective-permute-done.17
  42.7 0.4 collective-permute-done.18
  43.1 4.0 %readout.1 = (bf16[24,1024]{1,0:T(8,128)(2,1)S(1)}, bf16[16,16,384]{2,1,0:T(8,128)(2,1)S(1)}) custom-call(s32[1]{0:T(128)} %bitcast.me_ref, f32[16]{0:T(128)S(1)} %copy-done.6, f32[16,128]{1,0:T(8,128)S(1)} %get-tuple-element.36.place_ref, bf16[8,16,128,128]{3,2,1,0:T(8,128)(2,1)} %states_ref.7, bf16[2,16,128,128]{3,2,1,0:T(8,128)(2,1)S(1)} %collective-permute-done.near_ref, ...), custom_call_target="tpu_custom_call" | custom-call | tf_op jit(solution)/shard_map/readout/pallas_call | solution.py:466
  47.1 1.3 %collective-permute-start.19 = (bf16[24,1024]{1,0:T(8,128)(2,1)S(1)}, bf16[24,1024]{1,0:T(8,128)(2,1)S(1)}, u32[]{:S(2)}, u32[]{:S(2)}) collective-permute-start(bf16[24,1024]{1,0:T(8,128)(2,1)S(1)} %get-tuple-element.52), channel_id=1, source_target_pairs={{0,6},{1,7},{2,4},{3,5},{4,2},{5,3},{6,0},{7,1},{8,14},{9,15},{10,... | collective-permute-start | bytes 147464 | tf_op jit(solution)/shard_map/ppermute | solution.py:29
  48.4 2.8 %collective-permute-done.19 = bf16[24,1024]{1,0:T(8,128)(2,1)S(1)} collective-permute-done((bf16[24,1024]{1,0:T(8,128)(2,1)S(1)}, bf16[24,1024]{1,0:T(8,128)(2,1)S(1)}, u32[]{:S(2)}, u32[]{:S(2)}) %collective-permute-start.19) | collective-permute-done | bytes 49184 | tf_op jit(solution)/shard_map/ppermute | solution.py:29
  51.1 1.6 %collective-permute-start.22 = (bf16[48,1024]{1,0:T(8,128)(2,1)S(1)}, bf16[48,1024]{1,0:T(8,128)(2,1)S(1)}, u32[]{:S(2)}, u32[]{:S(2)}) collective-permute-start(bf16[48,1024]{1,0:T(8,128)(2,1)S(1)} %constant_dynamic-update-slice_fusion.refs_0_), channel_id=1, source_target_pairs={{0,12},{1,13},{2,14},{3,15},{4,8},{5,9},{6,10},{7,11},{8,4},{9,5},... | collective-permute-start | bytes 294920 | tf_op jit(solution)/shard_map/ppermute | solution.py:29
  52.8 0.0 collective-permute-start.20
  52.8 1.9 %collective-permute-start.21 = (bf16[48,1024]{1,0:T(8,128)(2,1)S(1)}, bf16[48,1024]{1,0:T(8,128)(2,1)S(1)}, u32[]{:S(2)}, u32[]{:S(2)}) collective-permute-start(bf16[48,1024]{1,0:T(8,128)(2,1)S(1)} %constant_dynamic-update-slice_fusion.refs_0_), channel_id=1, source_target_pairs={{0,8},{1,9},{2,10},{3,11},{4,12},{5,13},{6,14},{7,15},{8,0},{9,1},... | collective-permute-start | bytes 294920 | tf_op jit(solution)/shard_map/ppermute | solution.py:29
  54.7 6.8 %main_update.1 = (bf16[8,16,128,128]{3,2,1,0:T(8,128)(2,1)}, bf16[16,128,16]{2,1,0:T(8,128)(2,1)S(1)}, f32[2,16,16,128]{3,2,1,0:T(8,128)S(1)}) custom-call(s32[1]{0:T(128)} %bitcast.me_ref, s32[1,4,32]{2,1,0:T(4,128)S(1)} %copy-done.3, f32[16]{0:T(128)S(1)} %copy-done.6, bf16[16,16,384]{2,1,0:T(8,128)(2,1)S(1)} %get-tuple-element.53.recv_ref, ...), custom_call_target="tpu_custom_call" | custom-call | tf_op jit(solution)/shard_map/main_update/pallas_call | solution.py:481
  61.5 2.1 %collective-permute-start.24 = (bf16[48,1024]{1,0:T(8,128)(2,1)S(1)}, bf16[48,1024]{1,0:T(8,128)(2,1)S(1)}, u32[]{:S(2)}, u32[]{:S(2)}) collective-permute-start(bf16[48,1024]{1,0:T(8,128)(2,1)S(1)} %constant_dynamic-update-slice_fusion.refs_0_), channel_id=1, source_target_pairs={{0,1},{1,0},{2,3},{3,2},{4,5},{5,4},{6,7},{7,6},{8,9},{9,8},{10,11... | collective-permute-start | bytes 294920 | tf_op jit(solution)/shard_map/ppermute | solution.py:29
  63.6 0.1 collective-permute-start.25
  63.7 0.4 collective-permute-start.26
  64.1 0.1 collective-permute-start.27
  64.2 2.0 %last_update.1 = bf16[8,16,128,128]{3,2,1,0:T(8,128)(2,1)} custom-call(s32[1]{0:T(128)} %bitcast.me_ref, s32[1,4,32]{2,1,0:T(4,128)S(1)} %copy-done.3, bf16[16,16,384]{2,1,0:T(8,128)(2,1)S(1)} %get-tuple-element.53.recv_ref, bf16[16,128,16]{2,1,0:T(8,128)(2,1)S(1)} %get-tuple-element.60.turned_ref, ...), custom_call_target="tpu_custom_call", output_to_operand_aliasing={{}: (6, {})} | custom-call | tf_op jit(solution)/shard_map/last_update/pallas_call | solution.py:507
  66.2 1.7 %output.1 = bf16[128,128]{1,0:T(8,128)(2,1)} custom-call(bf16[128,128]{1,0:T(8,128)(2,1)S(1)} %get-tuple-element.33.x_ref, bf16[2048,128]{1,0:T(8,128)(2,1)S(1)} %copy-done.1, bf16[128,384]{1,0:T(8,128)(2,1)S(1)} %get-tuple-element.34.low_pick_ref, bf16[128,384]{1,0:T(8,128)(2,1)S(1)} %get-tuple-element.35.high_pick_ref, ...), custom_call_target="tpu_custom_call" | custom-call | tf_op jit(solution)/shard_map/output/pallas_call | solution.py:517
  (42 shorter events, 0.2 us)
Async XLA Ops:
  0.6 6.1 %copy-start.2 = (s32[1,4,32]{2,1,0:T(4,128)S(1)}, s32[1,4,32]{2,1,0:T(4,128)}, u32[]{:S(2)}) copy-start(s32[1,4,32]{2,1,0:T(4,128)} %parent_ref.7) | copy-start | bytes 1540
  3.3 20.1 %copy-start = (bf16[2048,3,128]{2,0,1:T(8,128)(2,1)S(1)}, bf16[2048,3,128]{2,0,1:T(8,128)(2,1)}, u32[]{:S(2)}) copy-start(bf16[2048,3,128]{2,0,1:T(8,128)(2,1)} %param.13) | copy-start | bytes 4718596
  3.3 39.8 %copy-start.4 = (f32[16,128]{1,0:T(8,128)S(1)}, f32[16,128]{1,0:T(8,128)}, u32[]{:S(2)}) copy-start(f32[16,128]{1,0:T(8,128)} %gate_ref.3) | copy-start | bytes 24580
  3.4 39.8 %copy-start.5 = (f32[2048]{0:T(1024)S(1)}, f32[2048]{0:T(1024)}, u32[]{:S(2)}) copy-start(f32[2048]{0:T(1024)} %param.16) | copy-start | bytes 24580
  3.4 39.8 %copy-start.6 = (f32[16]{0:T(128)S(1)}, f32[16]{0:T(128)}, u32[]{:S(2)}) copy-start(f32[16]{0:T(128)} %bias_ref.3) | copy-start | bytes 196
  3.4 15.7 %collective-permute-start.5 = (bf16[1,16,128,128]{3,2,1,0:T(8,128)(2,1)S(1)}, bf16[1,16,128,128]{3,2,1,0:T(8,128)(2,1)S(1)}, u32[]{:S(2)}, u32[]{:S(2)}) collective-permute-start(bf16[1,16,128,128]{3,2,1,0:T(8,128)(2,1)S(1)} %get-tuple-element.42), channel_id=1, source_target_pairs={{0,2},{1,3},{2,0},{3,1},{4,6},{5,7},{6,4},{7,5},{8,10},{9,11},{10,... | collective-permute-start | bytes 1572872 | tf_op jit(solution)/shard_map/ppermute | solution.py:29
  5.5 5.3 %collective-permute-start.1 = (bf16[128,128]{1,0:T(8,128)(2,1)S(1)}, bf16[128,128]{1,0:T(8,128)(2,1)S(1)}, u32[]{:S(2)}, u32[]{:S(2)}) collective-permute-start(bf16[128,128]{1,0:T(8,128)(2,1)S(1)} %get-tuple-element.33.x_ref), channel_id=1, source_target_pairs={{0,6},{1,7},{2,4},{3,5},{4,2},{5,3},{6,0},{7,1},{8,14},{9,15},{10,... | collective-permute-start | bytes 98312 | tf_op jit(solution)/shard_map/ppermute | solution.py:29
  10.8 3.6 %collective-permute-start.2 = (bf16[256,128]{1,0:T(8,128)(2,1)S(1)}, bf16[256,128]{1,0:T(8,128)(2,1)S(1)}, u32[]{:S(2)}, u32[]{:S(2)}) collective-permute-start(bf16[256,128]{1,0:T(8,128)(2,1)S(1)} %pad_maximum_fusion.refs_0_), channel_id=1, source_target_pairs={{0,4},{1,5},{2,6},{3,7},{4,0},{5,1},{6,2},{7,3},{8,12},{9,13},{10,... | collective-permute-start | bytes 196616 | tf_op jit(solution)/shard_map/ppermute | solution.py:29
  10.9 4.1 %collective-permute-start.3 = (bf16[256,128]{1,0:T(8,128)(2,1)S(1)}, bf16[256,128]{1,0:T(8,128)(2,1)S(1)}, u32[]{:S(2)}, u32[]{:S(2)}) collective-permute-start(bf16[256,128]{1,0:T(8,128)(2,1)S(1)} %pad_maximum_fusion.refs_0_), channel_id=1, source_target_pairs={{0,8},{1,9},{2,10},{3,11},{4,12},{5,13},{6,14},{7,15},{8,0},{9,1},... | collective-permute-start | bytes 196616 | tf_op jit(solution)/shard_map/ppermute | solution.py:29
  13.3 5.7 %collective-permute-start.4 = (bf16[256,128]{1,0:T(8,128)(2,1)S(1)}, bf16[256,128]{1,0:T(8,128)(2,1)S(1)}, u32[]{:S(2)}, u32[]{:S(2)}) collective-permute-start(bf16[256,128]{1,0:T(8,128)(2,1)S(1)} %pad_maximum_fusion.refs_0_), channel_id=1, source_target_pairs={{0,12},{1,13},{2,14},{3,15},{4,8},{5,9},{6,10},{7,11},{8,4},{9,5},... | collective-permute-start | bytes 196616 | tf_op jit(solution)/shard_map/ppermute | solution.py:29
  19.1 3.6 %collective-permute-start.6 = (bf16[256,128]{1,0:T(8,128)(2,1)S(1)}, bf16[256,128]{1,0:T(8,128)(2,1)S(1)}, u32[]{:S(2)}, u32[]{:S(2)}) collective-permute-start(bf16[256,128]{1,0:T(8,128)(2,1)S(1)} %pad_maximum_fusion.refs_0_), channel_id=1, source_target_pairs={{0,1},{1,0},{2,3},{3,2},{4,5},{5,4},{6,7},{7,6},{8,9},{9,8},{10,11... | collective-permute-start | bytes 196616 | tf_op jit(solution)/shard_map/ppermute | solution.py:29
  21.7 1.3 %collective-permute-start.7 = (bf16[256,128]{1,0:T(8,128)(2,1)S(1)}, bf16[256,128]{1,0:T(8,128)(2,1)S(1)}, u32[]{:S(2)}, u32[]{:S(2)}) collective-permute-start(bf16[256,128]{1,0:T(8,128)(2,1)S(1)} %collective-permute-done.2.refs_1_), channel_id=1, source_target_pairs={{0,1},{1,0},{2,3},{3,2},{4,5},{5,4},{6,7},{7,6},{8,9},{9,8},{10,11... | collective-permute-start | bytes 196616 | tf_op jit(solution)/shard_map/ppermute | solution.py:29
  21.7 1.4 %collective-permute-start.8 = (bf16[256,128]{1,0:T(8,128)(2,1)S(1)}, bf16[256,128]{1,0:T(8,128)(2,1)S(1)}, u32[]{:S(2)}, u32[]{:S(2)}) collective-permute-start(bf16[256,128]{1,0:T(8,128)(2,1)S(1)} %collective-permute-done.3.refs_2_), channel_id=1, source_target_pairs={{0,1},{1,0},{2,3},{3,2},{4,5},{5,4},{6,7},{7,6},{8,9},{9,8},{10,11... | collective-permute-start | bytes 196616 | tf_op jit(solution)/shard_map/ppermute | solution.py:29
  22.2 1.3 %collective-permute-start.9 = (bf16[256,128]{1,0:T(8,128)(2,1)S(1)}, bf16[256,128]{1,0:T(8,128)(2,1)S(1)}, u32[]{:S(2)}, u32[]{:S(2)}) collective-permute-start(bf16[256,128]{1,0:T(8,128)(2,1)S(1)} %collective-permute-done.4.refs_3_), channel_id=1, source_target_pairs={{0,1},{1,0},{2,3},{3,2},{4,5},{5,4},{6,7},{7,6},{8,9},{9,8},{10,11... | collective-permute-start | bytes 196616 | tf_op jit(solution)/shard_map/ppermute | solution.py:29
  22.2 32.5 %copy-start.3 = (s32[1,4,32]{2,1,0:T(4,128)S(1)}, s32[1,4,32]{2,1,0:T(4,128)}, u32[]{:S(2)}) copy-start(s32[1,4,32]{2,1,0:T(4,128)} %parent_ref.7) | copy-start | bytes 1540
  22.2 15.3 %collective-permute-start.14 = (bf16[1,16,128,128]{3,2,1,0:T(8,128)(2,1)}, bf16[1,16,128,128]{3,2,1,0:T(8,128)(2,1)S(1)}, u32[]{:S(2)}, u32[]{:S(2)}) collective-permute-start(bf16[1,16,128,128]{3,2,1,0:T(8,128)(2,1)} %get-tuple-element.47), channel_id=1, source_target_pairs={{0,2},{1,3},{2,0},{3,1},{4,6},{5,7},{6,4},{7,5},{8,10},{9,11},{10,... | collective-permute-start | bytes 1572872 | tf_op jit(solution)/shard_map/ppermute | solution.py:29
  24.3 5.3 %collective-permute-start.10 = (bf16[1,4,2,16,384]{4,3,0,2,1:T(8,128)(2,1)S(1)}, bf16[1,4,2,16,384]{4,3,0,2,1:T(8,128)(2,1)S(1)}, u32[]{:S(2)}, u32[]{:S(2)}) collective-permute-start(bf16[1,4,2,16,384]{4,3,0,2,1:T(8,128)(2,1)S(1)} %bitcast.25), channel_id=1, source_target_pairs={{0,6},{1,7},{2,4},{3,5},{4,2},{5,3},{6,0},{7,1},{8,14},{9,15},{10,... | collective-permute-start | bytes 294920 | tf_op jit(solution)/shard_map/ppermute | solution.py:29
  25.6 17.5 %collective-permute-start = (bf16[2,16,128,128]{3,2,1,0:T(8,128)(2,1)}, bf16[2,16,128,128]{3,2,1,0:T(8,128)(2,1)S(1)}, u32[]{:S(2)}, u32[]{:S(2)}) collective-permute-start(bf16[2,16,128,128]{3,2,1,0:T(8,128)(2,1)} %get-tuple-element.37), channel_id=1, source_target_pairs={{0,1},{1,0},{2,3},{3,2},{4,5},{5,4},{6,7},{7,6},{8,9},{9,8},{10,11... | collective-permute-start | bytes 3145736 | tf_op jit(solution)/shard_map/ppermute | solution.py:29
  29.6 9.6 %collective-permute-start.11 = (bf16[2,1,2,16,384]{4,3,0,2,1:T(8,128)(2,1)S(1)}, bf16[2,1,2,16,384]{4,3,0,2,1:T(8,128)(2,1)S(1)}, u32[]{:S(2)}, u32[]{:S(2)}) collective-permute-start(bf16[2,1,2,16,384]{4,3,0,2,1:T(8,128)(2,1)S(1)} %get-tuple-element.66), channel_id=1, source_target_pairs={{0,4},{1,5},{2,6},{3,7},{4,0},{5,1},{6,2},{7,3},{8,12},{9,13},{10,... | collective-permute-start | bytes 147464 | tf_op jit(solution)/shard_map/ppermute | solution.py:29
  29.7 9.6 %collective-permute-start.12 = (bf16[2,1,2,16,384]{4,3,0,2,1:T(8,128)(2,1)S(1)}, bf16[2,1,2,16,384]{4,3,0,2,1:T(8,128)(2,1)S(1)}, u32[]{:S(2)}, u32[]{:S(2)}) collective-permute-start(bf16[2,1,2,16,384]{4,3,0,2,1:T(8,128)(2,1)S(1)} %get-tuple-element.67), channel_id=1, source_target_pairs={{0,8},{1,9},{2,10},{3,11},{4,12},{5,13},{6,14},{7,15},{8,0},{9,1},... | collective-permute-start | bytes 147464 | tf_op jit(solution)/shard_map/ppermute | solution.py:29
  30.8 8.4 %collective-permute-start.13 = (bf16[2,1,2,16,384]{4,3,0,2,1:T(8,128)(2,1)S(1)}, bf16[2,1,2,16,384]{4,3,0,2,1:T(8,128)(2,1)S(1)}, u32[]{:S(2)}, u32[]{:S(2)}) collective-permute-start(bf16[2,1,2,16,384]{4,3,0,2,1:T(8,128)(2,1)S(1)} %get-tuple-element.64), channel_id=1, source_target_pairs={{0,12},{1,13},{2,14},{3,15},{4,8},{5,9},{6,10},{7,11},{8,4},{9,5},... | collective-permute-start | bytes 147464 | tf_op jit(solution)/shard_map/ppermute | solution.py:29
  37.5 17.2 %collective-permute-start.23 = (bf16[1,16,128,128]{3,2,1,0:T(8,128)(2,1)}, bf16[1,16,128,128]{3,2,1,0:T(8,128)(2,1)S(1)}, u32[]{:S(2)}, u32[]{:S(2)}) collective-permute-start(bf16[1,16,128,128]{3,2,1,0:T(8,128)(2,1)} %get-tuple-element.56), channel_id=1, source_target_pairs={{0,3},{1,2},{2,1},{3,0},{4,7},{5,6},{6,5},{7,4},{8,11},{9,10},{10,... | collective-permute-start | bytes 1572872 | tf_op jit(solution)/shard_map/ppermute | solution.py:29
  39.2 25.0 %collective-permute-start.28 = (bf16[1,16,128,128]{3,2,1,0:T(8,128)(2,1)}, bf16[1,16,128,128]{3,2,1,0:T(8,128)(2,1)S(1)}, u32[]{:S(2)}, u32[]{:S(2)}) collective-permute-start(bf16[1,16,128,128]{3,2,1,0:T(8,128)(2,1)} %get-tuple-element.62), channel_id=1, source_target_pairs={{0,3},{1,2},{2,1},{3,0},{4,7},{5,6},{6,5},{7,4},{8,11},{9,10},{10,... | collective-permute-start | bytes 1572872 | tf_op jit(solution)/shard_map/ppermute | solution.py:29
  39.3 2.3 %collective-permute-start.15 = (bf16[2,1,1,16,384]{4,3,0,2,1:T(8,128)(2,1)S(1)}, bf16[2,1,1,16,384]{4,3,0,2,1:T(8,128)(2,1)S(1)}, u32[]{:S(2)}, u32[]{:S(2)}) collective-permute-start(bf16[2,1,1,16,384]{4,3,0,2,1:T(8,128)(2,1)S(1)} %get-tuple-element.76), channel_id=1, source_target_pairs={{0,1},{1,0},{2,3},{3,2},{4,5},{5,4},{6,7},{7,6},{8,9},{9,8},{10,11... | collective-permute-start | bytes 73736 | tf_op jit(solution)/shard_map/ppermute | solution.py:29
  40.7 1.2 %collective-permute-start.16 = (bf16[2,1,1,16,384]{4,3,0,2,1:T(8,128)(2,1)S(1)}, bf16[2,1,1,16,384]{4,3,0,2,1:T(8,128)(2,1)S(1)}, u32[]{:S(2)}, u32[]{:S(2)}) collective-permute-start(bf16[2,1,1,16,384]{4,3,0,2,1:T(8,128)(2,1)S(1)} %get-tuple-element.74), channel_id=1, source_target_pairs={{0,1},{1,0},{2,3},{3,2},{4,5},{5,4},{6,7},{7,6},{8,9},{9,8},{10,11... | collective-permute-start | bytes 73736 | tf_op jit(solution)/shard_map/ppermute | solution.py:29
  41.6 1.2 %collective-permute-start.17 = (bf16[2,1,1,16,384]{4,3,0,2,1:T(8,128)(2,1)S(1)}, bf16[2,1,1,16,384]{4,3,0,2,1:T(8,128)(2,1)S(1)}, u32[]{:S(2)}, u32[]{:S(2)}) collective-permute-start(bf16[2,1,1,16,384]{4,3,0,2,1:T(8,128)(2,1)S(1)} %get-tuple-element.72), channel_id=1, source_target_pairs={{0,1},{1,0},{2,3},{3,2},{4,5},{5,4},{6,7},{7,6},{8,9},{9,8},{10,11... | collective-permute-start | bytes 73736 | tf_op jit(solution)/shard_map/ppermute | solution.py:29
  41.9 1.2 %collective-permute-start.18 = (bf16[2,1,1,16,384]{4,3,0,2,1:T(8,128)(2,1)S(1)}, bf16[2,1,1,16,384]{4,3,0,2,1:T(8,128)(2,1)S(1)}, u32[]{:S(2)}, u32[]{:S(2)}) collective-permute-start(bf16[2,1,1,16,384]{4,3,0,2,1:T(8,128)(2,1)S(1)} %get-tuple-element.70), channel_id=1, source_target_pairs={{0,1},{1,0},{2,3},{3,2},{4,5},{5,4},{6,7},{7,6},{8,9},{9,8},{10,11... | collective-permute-start | bytes 73736 | tf_op jit(solution)/shard_map/ppermute | solution.py:29
  47.1 4.0 %collective-permute-start.19 = (bf16[24,1024]{1,0:T(8,128)(2,1)S(1)}, bf16[24,1024]{1,0:T(8,128)(2,1)S(1)}, u32[]{:S(2)}, u32[]{:S(2)}) collective-permute-start(bf16[24,1024]{1,0:T(8,128)(2,1)S(1)} %get-tuple-element.52), channel_id=1, source_target_pairs={{0,6},{1,7},{2,4},{3,5},{4,2},{5,3},{6,0},{7,1},{8,14},{9,15},{10,... | collective-permute-start | bytes 147464 | tf_op jit(solution)/shard_map/ppermute | solution.py:29
  51.1 12.4 %collective-permute-start.22 = (bf16[48,1024]{1,0:T(8,128)(2,1)S(1)}, bf16[48,1024]{1,0:T(8,128)(2,1)S(1)}, u32[]{:S(2)}, u32[]{:S(2)}) collective-permute-start(bf16[48,1024]{1,0:T(8,128)(2,1)S(1)} %constant_dynamic-update-slice_fusion.refs_0_), channel_id=1, source_target_pairs={{0,12},{1,13},{2,14},{3,15},{4,8},{5,9},{6,10},{7,11},{8,4},{9,5},... | collective-permute-start | bytes 294920 | tf_op jit(solution)/shard_map/ppermute | solution.py:29
  52.8 10.8 %collective-permute-start.20 = (bf16[48,1024]{1,0:T(8,128)(2,1)S(1)}, bf16[48,1024]{1,0:T(8,128)(2,1)S(1)}, u32[]{:S(2)}, u32[]{:S(2)}) collective-permute-start(bf16[48,1024]{1,0:T(8,128)(2,1)S(1)} %constant_dynamic-update-slice_fusion.refs_0_), channel_id=1, source_target_pairs={{0,4},{1,5},{2,6},{3,7},{4,0},{5,1},{6,2},{7,3},{8,12},{9,13},{10,... | collective-permute-start | bytes 294920 | tf_op jit(solution)/shard_map/ppermute | solution.py:29
  52.8 10.9 %collective-permute-start.21 = (bf16[48,1024]{1,0:T(8,128)(2,1)S(1)}, bf16[48,1024]{1,0:T(8,128)(2,1)S(1)}, u32[]{:S(2)}, u32[]{:S(2)}) collective-permute-start(bf16[48,1024]{1,0:T(8,128)(2,1)S(1)} %constant_dynamic-update-slice_fusion.refs_0_), channel_id=1, source_target_pairs={{0,8},{1,9},{2,10},{3,11},{4,12},{5,13},{6,14},{7,15},{8,0},{9,1},... | collective-permute-start | bytes 294920 | tf_op jit(solution)/shard_map/ppermute | solution.py:29
  61.5 4.7 %collective-permute-start.24 = (bf16[48,1024]{1,0:T(8,128)(2,1)S(1)}, bf16[48,1024]{1,0:T(8,128)(2,1)S(1)}, u32[]{:S(2)}, u32[]{:S(2)}) collective-permute-start(bf16[48,1024]{1,0:T(8,128)(2,1)S(1)} %constant_dynamic-update-slice_fusion.refs_0_), channel_id=1, source_target_pairs={{0,1},{1,0},{2,3},{3,2},{4,5},{5,4},{6,7},{7,6},{8,9},{9,8},{10,11... | collective-permute-start | bytes 294920 | tf_op jit(solution)/shard_map/ppermute | solution.py:29
  63.6 2.6 %collective-permute-start.25 = (bf16[48,1024]{1,0:T(8,128)(2,1)S(1)}, bf16[48,1024]{1,0:T(8,128)(2,1)S(1)}, u32[]{:S(2)}, u32[]{:S(2)}) collective-permute-start(bf16[48,1024]{1,0:T(8,128)(2,1)S(1)} %collective-permute-done.20.refs_1_), channel_id=1, source_target_pairs={{0,1},{1,0},{2,3},{3,2},{4,5},{5,4},{6,7},{7,6},{8,9},{9,8},{10,11... | collective-permute-start | bytes 294920 | tf_op jit(solution)/shard_map/ppermute | solution.py:29
  63.7 2.5 %collective-permute-start.26 = (bf16[48,1024]{1,0:T(8,128)(2,1)S(1)}, bf16[48,1024]{1,0:T(8,128)(2,1)S(1)}, u32[]{:S(2)}, u32[]{:S(2)}) collective-permute-start(bf16[48,1024]{1,0:T(8,128)(2,1)S(1)} %collective-permute-done.21.refs_2_), channel_id=1, source_target_pairs={{0,1},{1,0},{2,3},{3,2},{4,5},{5,4},{6,7},{7,6},{8,9},{9,8},{10,11... | collective-permute-start | bytes 294920 | tf_op jit(solution)/shard_map/ppermute | solution.py:29
  64.1 2.1 %collective-permute-start.27 = (bf16[48,1024]{1,0:T(8,128)(2,1)S(1)}, bf16[48,1024]{1,0:T(8,128)(2,1)S(1)}, u32[]{:S(2)}, u32[]{:S(2)}) collective-permute-start(bf16[48,1024]{1,0:T(8,128)(2,1)S(1)} %collective-permute-done.22.refs_3_), channel_id=1, source_target_pairs={{0,1},{1,0},{2,3},{3,2},{4,5},{5,4},{6,7},{7,6},{8,9},{9,8},{10,11... | collective-permute-start | bytes 294920 | tf_op jit(solution)/shard_map/ppermute | solution.py:29
  64.2 2.0 %copy-start.1 = (bf16[2048,128]{1,0:T(8,128)(2,1)S(1)}, bf16[2048,128]{1,0:T(8,128)(2,1)}, u32[]{:S(2)}) copy-start(bf16[2048,128]{1,0:T(8,128)(2,1)} %weight_ref.1) | copy-start | bytes 1572868

commit v4 on v3

v4 whole, which is shorter than its diff:
```python
import functools
import math

import jax
import jax.numpy as jnp
from jax import lax
from jax.experimental import pallas as pl
from jax.experimental.pallas import tpu as pltpu
from jax.sharding import PartitionSpec as P

CAP = 2
TILE = 16
VMEM_BYTES = 24 * 1024 * 1024
WHOLE = pl.BlockSpec(memory_space=pltpu.VMEM)
SCALARS = pl.BlockSpec(memory_space=pltpu.SMEM)
PLACED = pl.BlockSpec(memory_space=pl.ANY)


def params():
    return pltpu.CompilerParams(vmem_limit_bytes=VMEM_BYTES)


def in_hbm(array):
    return pltpu.with_memory_space_constraint(array, pltpu.HBM)


def in_vmem(array):
    return pltpu.with_memory_space_constraint(array, pltpu.VMEM)


def xor_permute(block, distance):
    count = lax.axis_size("rows")
    return lax.ppermute(block, "rows", [(i, i ^ distance) for i in range(count)])


def stage_plan(count):
    if count == 1:
        return []
    if count == 2:
        return [[1]]
    if count == 4:
        return [[2], [1]]
    plan = [[6], [4, 8, 12] if count >= 16 else [4]]
    bit = 16
    while bit < count:
        plan.append([bit])
        bit *= 2
    return plan + [[1]]


def plan_order(plan):
    order = [0]
    for stage in plan:
        order = [near ^ far for near in order for far in [0] + stage]
    return order


def gather_order(plan):
    order = [0]
    for stage in plan:
        order = [near ^ far for far in [0] + stage for near in order]
    return order


def gather_all(block, plan, after=lambda stage, held: held):
    held = [block]
    for number, stage in enumerate(plan):
        held = held + [xor_permute(part, distance) for distance in stage for part in held]
        if len(held) == 2:
            held = [jnp.concatenate(held, 0)]
        held = after(number, held)
    return held


def exchange_plan(plan):
    return plan[-1:] + plan[:-1]


def exchange_all(pieces, plan, before=lambda stage, place, slab: slab, after=lambda stage, held: held):
    tail = pieces.shape[1:]
    held = [pieces.reshape(tuple(len(stage) + 1 for stage in plan) + tail)]
    for axis, stage in enumerate(plan):
        fresh = []
        for part in held:
            slabs = [lax.index_in_dim(part, place, axis, keepdims=True) for place in range(len(stage) + 1)]
            fresh.append(slabs[0])
            fresh += [xor_permute(before(axis, place, slabs[place + 1]), far) for place, far in enumerate(stage)]
        held = after(axis, fresh if axis == len(plan) - 1 else [jnp.concatenate(fresh, axis)])
    return [part.reshape((-1,) + tail) for part in held]


def split(number, size):
    if size & (size - 1) == 0:
        return lax.shift_right_logical(number, size.bit_length() - 1), number & (size - 1)
    return lax.div(number, size), lax.rem(number, size)


def place_in(order, distance):
    place, bit = distance & 0, 0
    while 1 << bit < len(order):
        place = place ^ ((lax.shift_right_logical(distance, bit) & 1) * order.index(1 << bit))
        bit += 1
    return place


def row_facts(parent_row, blocks, own_rows):
    lane = lax.broadcasted_iota(jnp.int32, parent_row.shape, 1)
    device, child = split(lane, own_rows)
    parent_block, parent_place = split(parent_row, own_rows)
    rank = jnp.zeros_like(lane)
    for earlier in range(1, own_rows):
        same = (pltpu.roll(parent_block, earlier, 1) == parent_block) & (child >= earlier)
        rank = rank + same.astype(jnp.int32)
    return device, child, parent_block ^ (device & (blocks - 1)), rank, parent_place


def column_of(row):
    spread = jnp.broadcast_to(row[0:1].astype(jnp.float32), (8, row.shape[1]))
    return jnp.transpose(spread)[:, 0:1]


def chosen_rows(column, width):
    shape = (column.shape[0], width)
    return (lax.broadcasted_iota(jnp.int32, shape, 1).astype(jnp.float32) == column).astype(jnp.float32)


def matching_children(parent_ref, user, child_block, parent_block, own_rows, none):
    children, parents, found = [jnp.int32(none)] * CAP, [jnp.int32(0)] * CAP, jnp.int32(0)
    for child in range(own_rows):
        block, place = split(parent_ref[0, user, child_block * own_rows + child], own_rows)
        hit = block == parent_block
        for j in range(CAP):
            children[j] = jnp.where(hit & (found == j), child, children[j])
            parents[j] = jnp.where(hit & (found == j), place, parents[j])
        found = found + hit.astype(jnp.int32)
    return children, parents


def fetch_kernel(
    blocks, me_ref, parent_ref, token_ref, tokens_ref, table_ref, states_ref, x_ref, first_ref, rows_ref, row_sem, state_sem
):
    count, own_rows = token_ref.shape[1], states_ref.shape[0]
    user, member = split(me_ref[0], blocks)
    _, chosen = matching_children(parent_ref, user, member ^ 2, member, own_rows, 0)
    state_copy = pltpu.make_async_copy(states_ref.at[chosen[0]], first_ref.at[0], state_sem)
    state_copy.start()

    def start_row(r, carry):
        first = pl.multiple_of(split(token_ref[0, r], TILE)[0] * TILE, TILE)
        pltpu.make_async_copy(
            table_ref.at[pl.ds(first, TILE)],
            rows_ref.at[pl.ds(pl.multiple_of(r * TILE, TILE), TILE)],
            row_sem,
        ).start()
        return carry

    lax.fori_loop(0, count, start_row, 0, unroll=8)
    step = math.gcd(count, 128)
    picks = []
    for first in range(0, count, step):
        low = column_of(split(tokens_ref[:, first : first + step], TILE)[1])
        wanted = low + lax.broadcasted_iota(jnp.int32, (step, 1), 0).astype(jnp.float32) * TILE
        picks.append(chosen_rows(wanted, step * TILE).astype(jnp.bfloat16))
    pltpu.make_async_copy(table_ref.at[pl.ds(0, count * TILE)], rows_ref, row_sem).wait()
    for first, pick in zip(range(0, count, step), picks):
        x_ref[first : first + step, :] = jnp.dot(
            pick, rows_ref[first * TILE : (first + step) * TILE, :], preferred_element_type=jnp.float32
        ).astype(jnp.bfloat16)
    state_copy.wait()


def pick_kernel(
    blocks, piece, send_order, me_ref, parent_ref, parents_ref, states_ref, pick_ref, second_ref, sem
):
    me, rows, own_rows = me_ref[0], parents_ref.shape[1], states_ref.shape[0]
    user, member = split(me, blocks)
    chosen = matching_children(parent_ref, user, member ^ 2, member, own_rows, 0)[1][1]
    copy = pltpu.make_async_copy(states_ref.at[chosen], second_ref.at[0], sem)
    copy.start()
    device, child, away, rank, _ = row_facts(parents_ref[...], blocks, own_rows)
    own = place_in(send_order, device ^ me) * piece + child
    far = place_in(send_order, device ^ away ^ me) * piece + 3 * own_rows + rank
    line = lax.broadcasted_iota(jnp.int32, (len(send_order) * piece, rows), 0)
    for slab in range(3):
        far_line = jnp.where(away == 3, far + slab * CAP, -1)
        chosen = (line == own[0:1] + slab * own_rows) | (line == far_line[0:1])
        pick_ref[:, slab * rows : (slab + 1) * rows] = chosen.astype(jnp.float32).astype(jnp.bfloat16)
    copy.wait()


def stage_kernel(
    blocks, normed_order, me_ref, parent_ref, parents_ref, states_ref, *refs
):
    outs, (place_ref, pick_ref, hold_ref, in_sem, out_sem) = refs[:-5], refs[-5:]
    me, own_rows = me_ref[0], states_ref.shape[0]
    user, member = split(me, blocks)
    wanted = []
    for partner in (3, 1):
        wanted += matching_children(parent_ref, user, member ^ partner, member, own_rows, 0)[1]
    targets = [ref.at[slot] for ref in outs for slot in range(ref.shape[0])]
    loads, saves = [], []
    for place, (row, target) in enumerate(zip(wanted, targets)):
        loads.append(pltpu.make_async_copy(states_ref.at[row], hold_ref.at[place], in_sem.at[place]))
        saves.append(pltpu.make_async_copy(hold_ref.at[place], target, out_sem.at[place]))
        loads[-1].start()
    device, child, away, rank, parent_place = row_facts(parents_ref[...], blocks, own_rows)
    line = lax.broadcasted_iota(jnp.int32, (place_ref.shape[0], parents_ref.shape[1]), 0)
    own = (line == jnp.where((device == me) & (away < 3), child, -1)[0:1]).astype(jnp.float32)
    far = (line == jnp.where((device ^ away == me) & (away == 3), own_rows + rank, -1)[0:1]).astype(jnp.float32)
    near_place = jnp.where(away == 0, parent_place, own_rows + (away - 1) * CAP + rank)
    place = own * (near_place[0:1] + 1).astype(jnp.float32) + far * (parent_place[0:1] + 1).astype(jnp.float32)
    place_ref[...] = jnp.broadcast_to(jnp.sum(place, axis=1, keepdims=True) - 1.0, place_ref.shape)
    for load, save in zip(loads, saves):
        load.wait()
        save.start()
    total = len(normed_order) * own_rows
    first = place_in(normed_order, jnp.where(away == 3, device ^ away, device) ^ me) * own_rows
    quarters = own_rows // CAP
    for part in range(1 + quarters):
        if part == 0:
            index = jnp.where(away == 3, -1, first + child)
        else:
            index = jnp.where(away == 3, first + rank * quarters + part - 1, -1)
        pick_ref[:, part * total : (part + 1) * total] = chosen_rows(column_of(index), total).astype(jnp.bfloat16)
    for save in saves:
        save.wait()


def hold_kernel(states_ref, held_ref, sem):
    copies = [pltpu.make_async_copy(states_ref.at[row], held_ref.at[row], sem.at[row]) for row in range(states_ref.shape[0])]
    for copy in copies:
        copy.start()
    for copy in copies:
        copy.wait()


def project_kernel(order, me_ref, weight_ref, pick_ref, *refs):
    held, out_ref = refs[:-1], refs[-1]
    me, columns, parts = me_ref[0], held[0].shape[1], len(held)
    rows = pick_ref.shape[1] // 3
    total = [None] * 3
    for place, distance in enumerate(order):
        ref, within = held[place * parts // len(order)], place % (len(order) // parts)
        block = ref[within * rows : (within + 1) * rows, :]
        first = pl.multiple_of((me ^ distance) * columns, columns)
        for slab in range(3):
            term = jnp.dot(block, weight_ref[slab, pl.ds(first, columns), :], preferred_element_type=jnp.float32)
            total[slab] = term if total[slab] is None else total[slab] + term
    every = jnp.concatenate([part.astype(jnp.bfloat16) for part in total], 0)
    out_ref[...] = jnp.dot(pick_ref[...], every, preferred_element_type=jnp.float32).astype(jnp.bfloat16)


def head_rows(piece, own_rows):
    piece = piece.astype(jnp.float32)
    far = piece[3 * own_rows : 4 * own_rows]
    slabs = []
    for slab in range(3):
        shifted = far if slab == 0 else pltpu.roll(far, own_rows - slab * CAP, 0)
        slabs.append(jnp.concatenate([piece[slab * own_rows : (slab + 1) * own_rows], shifted], 0))
    return slabs


def head_factors(keys, gate_row, bias, size):
    logit = jnp.sum(keys * gate_row, axis=-1, keepdims=True) / math.sqrt(size) + bias
    decay = 1.0 / (1.0 + jnp.exp(-logit))
    return decay, lax.rsqrt(jnp.sum(keys * keys, axis=-1, keepdims=True) + 1e-06)


def lane_of(recv_order, me, head):
    return head if recv_order is None else place_in(recv_order, me ^ head)


def readout_kernel(recv_order, block, near_count, me_ref, bias_ref, place_ref, gate_ref, gain_ref, *refs):
    sources, parts, (out_ref, recv_ref, norm_ref) = refs[:near_count], refs[near_count:-3], refs[-3:]
    own_rows, heads, size = sources[0].shape[0], sources[0].shape[1], sources[0].shape[2]
    slots = place_ref.shape[0]
    for number, part in enumerate(parts):
        for within in range(part.shape[0]):
            recv_ref[within * len(parts) + number] = part[within]
    place = place_ref[:, 0:1]
    joint = math.gcd(block, 2)
    states = sum(ref.shape[0] for ref in sources)

    def work(step, carry):
        for group in range(0, block, joint):
            first_head = step * block + group
            rows = [
                head_rows(recv_ref[lane_of(recv_order, me_ref[0], first_head + n)], own_rows) for n in range(joint)
            ]
            spread = [
                jnp.concatenate([jnp.where(place == float(p), row[0], 0.0).astype(jnp.bfloat16) for p in range(states)], 1)
                for row in rows
            ]
            priors = []
            for n in range(joint):
                one = [ref[:, pl.ds(first_head + n, 1)].reshape(ref.shape[0] * size, size) for ref in sources]
                priors.append(jnp.concatenate(one, 0))
            product = jnp.dot(
                jnp.concatenate(spread, 0), jnp.concatenate(priors, 1), preferred_element_type=jnp.float32
            )
            for n in range(joint):
                head = first_head + n
                queries, keys, values = rows[n]
                decay, inverse = head_factors(keys, gate_ref[pl.ds(head, 1), :], bias_ref[head], size)
                overlap = jnp.sum(queries * keys, axis=-1, keepdims=True) * inverse
                readout = decay * product[n * slots : (n + 1) * slots, n * size : (n + 1) * size] + overlap * values
                scale = lax.rsqrt(jnp.mean(readout * readout, axis=-1, keepdims=True) + 1e-05)
                norm_ref[head] = readout * scale * gain_ref[pl.ds(head, 1), :]
        return carry

    lax.fori_loop(0, heads // block, work, 0)
    quarters = own_rows // CAP
    share = heads // quarters
    own = [norm_ref[h][:own_rows] for h in range(heads)]
    far = []
    for rank in range(CAP):
        for quarter in range(quarters):
            line = slice(own_rows + rank, own_rows + rank + 1)
            far.append(jnp.concatenate([norm_ref[h][line] for h in range(quarter * share, (quarter + 1) * share)], 1))
    out_ref[...] = jnp.concatenate(own + [jnp.concatenate(far, 0)], 1).astype(jnp.bfloat16)


def output_kernel(own_rows, x_ref, weight_ref, pick_ref, *refs):
    parts, out_ref = refs[:-1], refs[-1]
    width, columns = weight_ref.shape[0], x_ref.shape[1]
    quarters = own_rows // CAP
    share = width // quarters
    gathered = jnp.concatenate([part[...] for part in parts], 0)
    own = jnp.dot(gathered[:, :width], weight_ref[...], preferred_element_type=jnp.float32)
    weight = jnp.concatenate([weight_ref[q * share : (q + 1) * share, :] for q in range(quarters)], 1)
    far = jnp.dot(gathered[:, width:], weight, preferred_element_type=jnp.float32)
    rest = jnp.concatenate([own] + [far[:, q * columns : (q + 1) * columns] for q in range(quarters)], 0)
    total = x_ref[...].astype(jnp.float32)
    for _ in range(3):
        term = rest.astype(jnp.bfloat16)
        rest = rest - term.astype(jnp.float32)
        total = total + jnp.dot(pick_ref[...], term, preferred_element_type=jnp.float32)
    out_ref[...] = total.astype(jnp.bfloat16)


def near_update_kernel(
    recv_order, block, blocks, me_ref, parent_ref, bias_ref, recv_ref, gate_ref, states_ref, *refs
):
    near_refs, (out_ref, turned_ref, values_ref, terms_ref, new_ref, out_sem) = refs[:CAP], refs[CAP:]
    own_rows, heads, size = states_ref.shape[0], states_ref.shape[1], states_ref.shape[2]
    slots = values_ref.shape[1]
    user, member = split(me_ref[0], blocks)

    def prepare(step, carry):
        for part in range(block):
            head = step * block + part
            _, keys, values = head_rows(recv_ref[lane_of(recv_order, me_ref[0], head)], own_rows)
            decay, inverse = head_factors(keys, gate_ref[pl.ds(head, 1), :], bias_ref[head], size)
            turned_ref[head] = jnp.transpose(keys).astype(jnp.bfloat16)
            values_ref[head] = values
            terms_ref[0, head] = jnp.broadcast_to(decay, (slots, size))
            terms_ref[1, head] = jnp.broadcast_to(inverse, (slots, size))
        return carry

    lax.fori_loop(0, heads // block, prepare, 0)
    line = lax.broadcasted_iota(jnp.int32, (slots, size), 0)

    def save(row):
        return pltpu.make_async_copy(new_ref.at[row], out_ref.at[row], out_sem.at[row])

    def facts(row):
        parent_block, place = split(parent_ref[0, user, member * own_rows + row], own_rows)
        return parent_block ^ member, place

    def update(row, prior_of):
        for head in range(heads):
            value = jnp.where(line == row, values_ref[head], 0.0).astype(jnp.bfloat16)
            outer = jnp.dot(turned_ref[head], value, preferred_element_type=jnp.float32)
            fresh = terms_ref[0, head, pl.ds(row, 1), :] * prior_of(head).astype(jnp.float32)
            fresh = fresh + terms_ref[1, head, pl.ds(row, 1), :] * outer
            new_ref[row, head] = fresh.astype(jnp.bfloat16)
        save(row).start()

    def work(row, found):
        away, place = facts(row)

        @pl.when(away == 0)
        def _():
            update(row, lambda head: states_ref[place, head])

        for rank, ref in enumerate(near_refs):

            @pl.when((away == 1) & (found == rank))
            def _():
                update(row, lambda head: ref[0, head])

        return found + (away == 1).astype(jnp.int32)

    lax.fori_loop(0, own_rows, work, jnp.int32(0))

    def finish(row, carry):
        @pl.when(facts(row)[0] < 2)
        def _():
            save(row).wait()

        return carry

    lax.fori_loop(0, own_rows, finish, 0)


def far_update_kernel(block, blocks, own_rows, entries, me_ref, parent_ref, turned_ref, values_ref, terms_ref, *refs):
    gots, (_, out_ref, new_ref, out_sem) = refs[:-4], refs[-4:]
    heads, size = gots[0].shape[1], gots[0].shape[2]
    user, member = split(me_ref[0], blocks)
    children = [
        matching_children(parent_ref, user, member, member ^ partner, own_rows, -1)[0][rank] for _, _, partner, rank in entries
    ]
    line = lax.broadcasted_iota(jnp.int32, (values_ref.shape[1], size), 0)

    def save(entry, step):
        span = pl.ds(step * block, block)
        target = out_ref.at[jnp.maximum(children[entry], 0), span]
        return pltpu.make_async_copy(new_ref.at[entry, span], target, out_sem.at[entry, step])

    for entry, (array, within, _, _) in enumerate(entries):
        got_ref, child = gots[array], children[entry]

        @pl.when(child >= 0)
        def _():
            for step in range(heads // block):
                for head in range(step * block, (step + 1) * block):
                    value = jnp.where(line == child, values_ref[head], 0.0).astype(jnp.bfloat16)
                    outer = jnp.dot(turned_ref[head], value, preferred_element_type=jnp.float32)
                    fresh = terms_ref[0, head, pl.ds(child, 1), :] * got_ref[within, head].astype(jnp.float32)
                    fresh = fresh + terms_ref[1, head, pl.ds(child, 1), :] * outer
                    new_ref[entry, head] = fresh.astype(jnp.bfloat16)
                save(entry, step).start()

    for entry in range(len(entries)):

        @pl.when(children[entry] >= 0)
        def _():
            for step in range(heads // block):
                save(entry, step).wait()


def per_device(
    token_ids,
    parents,
    states,
    embed_table,
    qkv_weight,
    gate_weight,
    gate_bias,
    norm_gain,
    out_weight,
):
    own_rows, heads, size = states.shape[0], states.shape[1], states.shape[2]
    width = heads * size
    columns = embed_table.shape[1]
    row_total = token_ids.shape[1]
    users, beam = parents.shape[1], parents.shape[2]
    blocks = beam // own_rows
    count = lax.axis_size("rows")
    me = lax.axis_index("rows").astype(jnp.int32)
    user, member = me // blocks, me % blocks
    plan = stage_plan(count)
    steps = exchange_plan(plan)
    recv_order, normed_order = plan_order(steps), gather_order(plan)
    slots, piece = 2 * own_rows, 4 * own_rows
    one_state, two_states = (1, heads, size, size), (CAP, heads, size, size)
    normed_columns = width + CAP * width // own_rows
    bf16, int32 = jnp.bfloat16, jnp.int32
    mine = me[None]
    parent_row = jnp.broadcast_to(parents.reshape(1, row_total), (8, row_total))
    head_block = math.gcd(heads, 4)

    local_columns, first_out = pl.pallas_call(
        functools.partial(fetch_kernel, blocks),
        in_specs=[SCALARS, SCALARS, SCALARS, WHOLE, PLACED, PLACED],
        out_specs=[WHOLE] * 2,
        out_shape=[pltpu.VMEM((row_total, columns), bf16), pltpu.VMEM(one_state, bf16)],
        scratch_shapes=[
            pltpu.VMEM((row_total * TILE, columns), bf16),
            pltpu.SemaphoreType.DMA,
            pltpu.SemaphoreType.DMA,
        ],
        compiler_params=params(),
        name="fetch",
    )(mine, in_hbm(parents), in_hbm(token_ids), in_hbm(token_ids), in_hbm(embed_table), in_hbm(states))
    first_got = xor_permute(first_out, 2)

    send_pick, second_out = pl.pallas_call(
        functools.partial(pick_kernel, blocks, piece, recv_order),
        in_specs=[SCALARS, SCALARS, WHOLE, PLACED],
        out_specs=[WHOLE] * 2,
        out_shape=[jax.ShapeDtypeStruct((count * piece, 3 * row_total), bf16), pltpu.VMEM(one_state, bf16)],
        scratch_shapes=[pltpu.SemaphoreType.DMA],
        compiler_params=params(),
        name="pick",
    )(mine, in_hbm(parents), parent_row, in_hbm(states))
    second_got = xor_permute(second_out, 2)

    corner_out, *near_outs, place, out_pick = pl.pallas_call(
        functools.partial(stage_kernel, blocks, normed_order),
        in_specs=[SCALARS, SCALARS, WHOLE, PLACED],
        out_specs=[PLACED] * (1 + CAP) + [WHOLE] * 2,
        out_shape=[pltpu.HBM(two_states, bf16)]
        + [pltpu.HBM(one_state, bf16)] * CAP
        + [
            jax.ShapeDtypeStruct((slots, 128), jnp.float32),
            jax.ShapeDtypeStruct((row_total, (1 + own_rows // CAP) * row_total), bf16),
        ],
        scratch_shapes=[
            pltpu.VMEM((2 * CAP, heads, size, size), bf16),
            pltpu.SemaphoreType.DMA((2 * CAP,)),
            pltpu.SemaphoreType.DMA((2 * CAP,)),
        ],
        compiler_params=params(),
        name="stage",
    )(mine, in_hbm(parents), parent_row, in_hbm(states))
    corner_got = xor_permute(corner_out, 3)
    near_gots = [xor_permute(block, 1) for block in near_outs]

    held = pl.pallas_call(
        hold_kernel,
        in_specs=[PLACED],
        out_specs=WHOLE,
        out_shape=pltpu.VMEM(states.shape, bf16),
        scratch_shapes=[pltpu.SemaphoreType.DMA((own_rows,))],
        compiler_params=params(),
        name="hold",
    )(in_hbm(states))

    weight = jnp.transpose(qkv_weight, (1, 0, 2))
    tied = {}

    def in_inputs(stage, parts):
        if stage == 0:
            *parts, tied["weight"], tied["pick"] = lax.optimization_barrier((*parts, weight, send_pick))
        if stage == 1:
            *parts, tied["first"], tied["place"] = lax.optimization_barrier((*parts, first_got, place))
        return parts

    every_input = gather_all(local_columns, plan, in_inputs)
    pieces = pl.pallas_call(
        functools.partial(project_kernel, normed_order),
        in_specs=[SCALARS] + [WHOLE] * (2 + len(every_input)),
        out_specs=WHOLE,
        out_shape=jax.ShapeDtypeStruct((count * piece, columns), bf16),
        compiler_params=params(),
        name="project",
    )(mine, tied["weight"], tied["pick"], *every_input)

    def before_exchange(stage, place, slab):
        if stage == 2 and place == 0:
            slab, tied["second"] = lax.optimization_barrier((slab, second_got))
        return slab

    def in_exchange(stage, parts):
        if stage == 1:
            *parts, tied["near"], tied["nearer"] = lax.optimization_barrier((*parts, *near_gots))
        return parts

    received = exchange_all(pieces.reshape(count, piece, columns), steps, before_exchange, in_exchange)
    if columns != size:
        every_piece = jnp.stack(received, 1).reshape(count, piece, columns)
        places = jnp.array([recv_order.index(d) for d in range(count)], int32)[jnp.arange(count, dtype=int32) ^ me]
        every_piece = jnp.take(every_piece, places, axis=0).transpose(1, 0, 2).reshape(piece, heads, size)
        received = [every_piece.transpose(1, 0, 2)]
        recv_order = None

    held, near_gots = in_vmem(held), [tied["near"], tied["nearer"]]
    sources = [held, *near_gots, tied["first"], tied["second"]]
    normed, by_head = pl.pallas_call(
        functools.partial(readout_kernel, recv_order, head_block, len(sources)),
        in_specs=[SCALARS] * 2 + [WHOLE] * (3 + len(sources) + len(received)),
        out_specs=[WHOLE] * 2,
        out_shape=[
            jax.ShapeDtypeStruct((own_rows, normed_columns), bf16),
            jax.ShapeDtypeStruct((heads, piece, size), bf16),
        ],
        scratch_shapes=[pltpu.VMEM((heads, slots, size), jnp.float32)],
        compiler_params=params(),
        name="readout",
    )(mine, gate_bias, tied["place"], gate_weight, norm_gain.reshape(heads, size), *sources, *received)

    near_done, turned, values, terms = pl.pallas_call(
        functools.partial(near_update_kernel, recv_order, head_block, blocks),
        in_specs=[SCALARS] * 3 + [WHOLE] * (3 + CAP),
        out_specs=[PLACED] + [WHOLE] * 3,
        out_shape=[
            pltpu.HBM(states.shape, bf16),
            jax.ShapeDtypeStruct((heads, size, slots), bf16),
            jax.ShapeDtypeStruct((heads, slots, size), jnp.float32),
            jax.ShapeDtypeStruct((2, heads, slots, size), jnp.float32),
        ],
        scratch_shapes=[pltpu.VMEM(states.shape, bf16), pltpu.SemaphoreType.DMA((own_rows,))],
        compiler_params=params(),
        name="near_update",
    )(mine, parents, gate_bias, by_head, gate_weight, held, *near_gots)

    def far_update(before, gots, entries, name):
        return pl.pallas_call(
            functools.partial(far_update_kernel, head_block, blocks, own_rows, entries),
            in_specs=[SCALARS] * 2 + [WHOLE] * (3 + len(gots)) + [PLACED],
            out_specs=PLACED,
            out_shape=jax.ShapeDtypeStruct(states.shape, bf16),
            scratch_shapes=[
                pltpu.VMEM((len(entries),) + one_state[1:], bf16),
                pltpu.SemaphoreType.DMA((len(entries), heads // head_block)),
            ],
            input_output_aliases={5 + len(gots): 0},
            compiler_params=params(),
            name=name,
        )(mine, parents, tied["turned"], values, terms, *gots, before)

    def in_normed(stage, parts):
        if stage == 0:
            *parts, tied["rows"], tied["turned"] = lax.optimization_barrier((*parts, near_done, turned))
        if stage == 1:
            entries = [(rank, 0, 2, rank) for rank in range(CAP)]
            far_done = far_update(tied["rows"], [tied["first"], tied["second"]], entries, "far_update")
            ends = (parts[-1], far_done, corner_got)
            parts[-1], tied["done"], tied["corner"] = lax.optimization_barrier(ends)
        return parts

    every_normed = gather_all(normed, plan, in_normed)
    final = far_update(tied["done"], [tied["corner"]], [(0, rank, 3, rank) for rank in range(CAP)], "last_update")
    layer_out = pl.pallas_call(
        functools.partial(output_kernel, own_rows),
        in_specs=[WHOLE] * (3 + len(every_normed)),
        out_specs=WHOLE,
        out_shape=jax.ShapeDtypeStruct((row_total, columns), bf16),
        compiler_params=params(),
        name="output",
    )(local_columns, out_weight, out_pick, *every_normed)
    return (layer_out[None], final)


def solution(mesh):
    placed = (
        P(None, "groups"),
        P(None, "groups", None),
        P(("groups", "rows"), None, None, None),
        P(None, "rows"),
        P(None, None, "rows"),
        P(),
        P(),
        P(),
        P(None, "rows"),
    )
    return jax.shard_map(
        per_device,
        mesh=mesh,
        in_specs=placed,
        out_specs=(P(None, "groups", "rows"), P(("groups", "rows"), None, None, None)),
        check_vma=False,
    )
```

time: 68.9 us -> 65.9 us (0.956)
  waiting for transfers between devices: 17.8 us -> 12.4 us
  starting transfers between devices: 27.1 us -> 29.3 us
  Pallas kernels: 21.9 us -> 22.6 us
    ppermute x29 -> x26, waiting for transfers between devices: 17.8 us -> 12.4 us  [xor_permute(): lax.ppermute(block, 'rows', [(i, i ^ distance) for i in range(count)])]
    ppermute x29 -> x26, starting transfers between devices: 27.1 us -> 29.3 us  [xor_permute(): lax.ppermute(block, 'rows', [(i, i ^ distance) for i in range(count)])]
    pallas_call x5 -> x8, Pallas kernels: 18.4 us -> 19 us  [the longest x2 3.82 us: far_update(): pl.pallas_call(functools.partial(far_update_kernel, head_block, blocks, o...]
  transfers between devices with their start and end apart: 29 -> 26, of which waited for: 11 -> 7; matrix products, arithmetic and copies ran while one was open for 0% -> 0% of each run, Pallas kernels for 26% -> 29%
where the time goes in v4:
time: 65.9 us; the launch traced here: 65.5 us
  starting transfers between devices  29.3 us (44%)
  Pallas kernels  22.6 us (34%)
  waiting for transfers between devices  12.4 us (19%)
  between operations  0.91 us (1%)
    ppermute x26, starting transfers between devices, xor_permute(): lax.ppermute(block, 'rows', [(i, i ^ distance) for i in range(count)])  29.3 us
    ppermute x26, waiting for transfers between devices, xor_permute(): lax.ppermute(block, 'rows', [(i, i ^ distance) for i in range(count)])  12.4 us
    pallas_call x2, Pallas kernels, far_update(): pl.pallas_call(functools.partial(far_update_kernel, head_block, blocks, o...  3.82 us
    pallas_call x1, Pallas kernels, per_device(): pl.pallas_call(functools.partial(stage_kernel, blocks, normed_order), in_...  3.78 us
    pallas_call x1, Pallas kernels, per_device(): pl.pallas_call(functools.partial(near_update_kernel, recv_order, head_blo...  3.37 us
    pallas_call x1, Pallas kernels, per_device(): pl.pallas_call(functools.partial(fetch_kernel, blocks), in_specs=[SCALARS...  2.67 us
    pallas_call x1, Pallas kernels, per_device(): pl.pallas_call(functools.partial(readout_kernel, recv_order, head_block,...  2.6 us
    pallas_call x1, Pallas kernels, per_device(): pl.pallas_call(hold_kernel, in_specs=[PLACED], out_specs=WHOLE, out_shape...  2.21 us
  transfers between devices with their start and end apart: 26, of which 7 were waited for; matrix products, arithmetic and copies ran while one was open for 0% of the time, Pallas kernels for 29%

profile of v4, /device:TPU:1, one launch (start us, length us, event | category | flops | bytes accessed | tf_op | source)
XLA Modules:
  0.0 65.5 jit_solution(10852620992902114347)
XLA Ops:
  0.6 0.0 copy-start.2
  0.6 2.7 %fetch.1 = (bf16[128,128]{1,0:T(8,128)(2,1)S(1)}, bf16[1,16,128,128]{3,2,1,0:T(8,128)(2,1)S(1)}) custom-call(s32[1]{0:T(128)} %bitcast.me_ref, s32[1,4,32]{2,1,0:T(4,128)} %parent_ref.11, s32[1,128]{1,0:T(1,128)} %tokens_ref.1, s32[1,128]{1,0:T(1,128)} %tokens_ref.1, bf16[32768,128]{1,0:T(8,128)(2,1)} %table_ref.1, bf16[8,16,128,128]{3,2,1,0:T(8,128)(2,1)} %states_ref.7), custom_call_target="tpu_custom_call" | custom-call | tf_op jit(solution)/shard_map/fetch/pallas_call | solution.py:473
  3.3 2.1 %collective-permute-start.4 = (bf16[1,16,128,128]{3,2,1,0:T(8,128)(2,1)S(1)}, bf16[1,16,128,128]{3,2,1,0:T(8,128)(2,1)S(1)}, u32[]{:S(2)}, u32[]{:S(2)}) collective-permute-start(bf16[1,16,128,128]{3,2,1,0:T(8,128)(2,1)S(1)} %get-tuple-element.41), channel_id=1, source_target_pairs={{0,2},{1,3},{2,0},{3,1},{4,6},{5,7},{6,4},{7,5},{8,10},{9,11},{10,... | collective-permute-start | bytes 1572872 | tf_op jit(solution)/shard_map/ppermute | solution.py:33
  5.5 1.2 %collective-permute-start = (bf16[128,128]{1,0:T(8,128)(2,1)S(1)}, bf16[128,128]{1,0:T(8,128)(2,1)S(1)}, u32[]{:S(2)}, u32[]{:S(2)}) collective-permute-start(bf16[128,128]{1,0:T(8,128)(2,1)S(1)} %get-tuple-element.37.x_ref), channel_id=1, source_target_pairs={{0,6},{1,7},{2,4},{3,5},{4,2},{5,3},{6,0},{7,1},{8,14},{9,15},{10,... | collective-permute-start | bytes 98312 | tf_op jit(solution)/shard_map/ppermute | solution.py:33
  6.7 0.1 broadcast_in_dim.14
  6.8 1.9 %pick.1 = (bf16[512,384]{1,0:T(8,128)(2,1)S(1)}, bf16[1,16,128,128]{3,2,1,0:T(8,128)(2,1)S(1)}) custom-call(s32[1]{0:T(128)} %bitcast.me_ref, s32[1,4,32]{2,1,0:T(4,128)} %parent_ref.11, s32[8,128]{1,0:T(8,128)S(1)} %broadcast_in_dim.15.parents_ref, bf16[8,16,128,128]{3,2,1,0:T(8,128)(2,1)} %states_ref.7), custom_call_target="tpu_custom_call" | custom-call | tf_op jit(solution)/shard_map/pick/pallas_call | solution.py:488
  8.7 0.5 collective-permute-done
  9.2 3.3 %collective-permute-start.3 = (bf16[256,128]{1,0:T(8,128)(2,1)S(1)}, bf16[256,128]{1,0:T(8,128)(2,1)S(1)}, u32[]{:S(2)}, u32[]{:S(2)}) collective-permute-start(bf16[256,128]{1,0:T(8,128)(2,1)S(1)} %pad_maximum_fusion.2.refs_0_), channel_id=1, source_target_pairs={{0,12},{1,13},{2,14},{3,15},{4,8},{5,9},{6,10},{7,11},{8,4},{9,5},... | collective-permute-start | bytes 196616 | tf_op jit(solution)/shard_map/ppermute | solution.py:33
  12.6 0.0 collective-permute-start.2
  12.6 0.4 collective-permute-start.1
  12.9 3.8 %stage.1 = (bf16[2,16,128,128]{3,2,1,0:T(8,128)(2,1)}, bf16[1,16,128,128]{3,2,1,0:T(8,128)(2,1)}, bf16[1,16,128,128]{3,2,1,0:T(8,128)(2,1)}, f32[16,128]{1,0:T(8,128)S(1)}, bf16[128,640]{1,0:T(8,128)(2,1)S(1)}) custom-call(s32[1]{0:T(128)} %bitcast.me_ref, s32[1,4,32]{2,1,0:T(4,128)} %parent_ref.11, s32[8,128]{1,0:T(8,128)S(1)} %broadcast_in_dim.15.parents_ref, ...), custom_call_target="tpu_custom_call" | custom-call | tf_op jit(solution)/shard_map/stage/pallas_call | solution.py:499
  16.7 0.9 %collective-permute-done.2.refs_2_ = bf16[256,128]{1,0:T(8,128)(2,1)S(1)} collective-permute-done((bf16[256,128]{1,0:T(8,128)(2,1)S(1)}, bf16[256,128]{1,0:T(8,128)(2,1)S(1)}, u32[]{:S(2)}, u32[]{:S(2)}) %collective-permute-start.2) | collective-permute-done | bytes 65568 | tf_op jit(solution)/shard_map/ppermute | solution.py:33
  17.7 0.1 collective-permute-done.4.refs_3_.refs_0_
  17.8 2.3 %collective-permute-start.5 = (bf16[256,128]{1,0:T(8,128)(2,1)S(1)}, bf16[256,128]{1,0:T(8,128)(2,1)S(1)}, u32[]{:S(2)}, u32[]{:S(2)}) collective-permute-start(bf16[256,128]{1,0:T(8,128)(2,1)S(1)} %pad_maximum_fusion.2.refs_0_), channel_id=1, source_target_pairs={{0,1},{1,0},{2,3},{3,2},{4,5},{5,4},{6,7},{7,6},{8,9},{9,8},{10,11... | collective-permute-start | bytes 196616 | tf_op jit(solution)/shard_map/ppermute | solution.py:33
  20.1 0.1 collective-permute-start.6
  20.2 0.4 collective-permute-start.7
  20.6 0.1 collective-permute-start.8
  20.7 0.3 collective-permute-start.13
  21.0 0.0 collective-permute-done.5.refs_4_
  21.0 0.8 %collective-permute-start.11 = (bf16[1,16,128,128]{3,2,1,0:T(8,128)(2,1)}, bf16[1,16,128,128]{3,2,1,0:T(8,128)(2,1)S(1)}, u32[]{:S(2)}, u32[]{:S(2)}) collective-permute-start(bf16[1,16,128,128]{3,2,1,0:T(8,128)(2,1)} %get-tuple-element.50), channel_id=1, source_target_pairs={{0,1},{1,0},{2,3},{3,2},{4,5},{5,4},{6,7},{7,6},{8,9},{9,8},{10,11... | collective-permute-start | bytes 1572872 | tf_op jit(solution)/shard_map/ppermute | solution.py:33
  21.8 0.1 collective-permute-start.12
  21.9 1.4 %collective-permute-start.21 = (bf16[2,16,128,128]{3,2,1,0:T(8,128)(2,1)}, bf16[2,16,128,128]{3,2,1,0:T(8,128)(2,1)S(1)}, u32[]{:S(2)}, u32[]{:S(2)}) collective-permute-start(bf16[2,16,128,128]{3,2,1,0:T(8,128)(2,1)} %get-tuple-element.68), channel_id=1, source_target_pairs={{0,3},{1,2},{2,1},{3,0},{4,7},{5,6},{6,5},{7,4},{8,11},{9,10},{10,... | collective-permute-start | bytes 3145736 | tf_op jit(solution)/shard_map/ppermute | solution.py:33
  23.3 1.0 %project.1 = bf16[512,128]{1,0:T(8,128)(2,1)S(1)} custom-call(s32[1]{0:T(128)} %bitcast.me_ref, bf16[3,2048,128]{2,1,0:T(8,128)(2,1)S(1)} %bitcast.10, bf16[512,384]{1,0:T(8,128)(2,1)S(1)} %get-tuple-element.45.pick_ref, bf16[256,128]{1,0:T(8,128)(2,1)S(1)} %pad_maximum_fusion.2.refs_0_, bf16[256,128]{1,0:T(8,128)(2,1)S(1)} %collective-permute-done.1.refs_1_, ...), custom_call_target="tpu_custom_call" | custom-call | tf_op jit(solution)/shard_map/project/pallas_call | solution.py:541
  24.4 0.1 collective-permute-start.9
  24.5 1.2 %collective-permute-done.9 = bf16[1,2,4,32,128]{4,3,1,0,2:T(8,128)(2,1)S(1)} collective-permute-done((bf16[1,2,4,32,128]{4,3,1,0,2:T(8,128)(2,1)S(1)}, bf16[1,2,4,32,128]{4,3,1,0,2:T(8,128)(2,1)S(1)}, u32[]{:S(2)}, u32[]{:S(2)}) %collective-permute-start.9) | collective-permute-done | bytes 65568 | tf_op jit(solution)/shard_map/ppermute | solution.py:33
  25.7 1.5 %collective-permute-start.10 = (bf16[2,1,4,32,128]{4,3,1,0,2:T(8,128)(2,1)S(1)}, bf16[2,1,4,32,128]{4,3,1,0,2:T(8,128)(2,1)S(1)}, u32[]{:S(2)}, u32[]{:S(2)}) collective-permute-start(bf16[2,1,4,32,128]{4,3,1,0,2:T(8,128)(2,1)S(1)} %get-tuple-element.77), channel_id=1, source_target_pairs={{0,6},{1,7},{2,4},{3,5},{4,2},{5,3},{6,0},{7,1},{8,14},{9,15},{10,... | collective-permute-start | bytes 196616 | tf_op jit(solution)/shard_map/ppermute | solution.py:33
  27.2 3.1 %collective-permute-done.10 = bf16[2,1,4,32,128]{4,3,1,0,2:T(8,128)(2,1)S(1)} collective-permute-done((bf16[2,1,4,32,128]{4,3,1,0,2:T(8,128)(2,1)S(1)}, bf16[2,1,4,32,128]{4,3,1,0,2:T(8,128)(2,1)S(1)}, u32[]{:S(2)}, u32[]{:S(2)}) %collective-permute-start.10) | collective-permute-done | bytes 65568 | tf_op jit(solution)/shard_map/ppermute | solution.py:33
  30.3 4.9 %collective-permute-done.13.refs_4_.refs_1_ = bf16[1,16,128,128]{3,2,1,0:T(8,128)(2,1)S(1)} collective-permute-done((bf16[1,16,128,128]{3,2,1,0:T(8,128)(2,1)S(1)}, bf16[1,16,128,128]{3,2,1,0:T(8,128)(2,1)S(1)}, u32[]{:S(2)}, u32[]{:S(2)}) %collective-permute-start.13) | collective-permute-done | bytes 524320 | tf_op jit(solution)/shard_map/ppermute | solution.py:33
  35.2 0.5 collective-permute-start.14
  35.7 2.3 %collective-permute-start.16 = (bf16[2,2,1,32,128]{4,3,1,0,2:T(8,128)(2,1)S(1)}, bf16[2,2,1,32,128]{4,3,1,0,2:T(8,128)(2,1)S(1)}, u32[]{:S(2)}, u32[]{:S(2)}) collective-permute-start(bf16[2,2,1,32,128]{4,3,1,0,2:T(8,128)(2,1)S(1)} %get-tuple-element.72), channel_id=1, source_target_pairs={{0,12},{1,13},{2,14},{3,15},{4,8},{5,9},{6,10},{7,11},{8,4},{9,5},... | collective-permute-start | bytes 98312 | tf_op jit(solution)/shard_map/ppermute | solution.py:33
  38.0 0.2 collective-permute-start.15
  38.2 2.2 %hold.1.refs_0_.states_ref = bf16[8,16,128,128]{3,2,1,0:T(8,128)(2,1)S(1)} custom-call(bf16[8,16,128,128]{3,2,1,0:T(8,128)(2,1)} %states_ref.7), custom_call_target="tpu_custom_call" | custom-call | tf_op jit(solution)/shard_map/hold/pallas_call | solution.py:520
  40.4 0.0 copy-start.3
  40.4 1.6 %collective-permute-done.15 = bf16[2,2,1,32,128]{4,3,1,0,2:T(8,128)(2,1)S(1)} collective-permute-done((bf16[2,2,1,32,128]{4,3,1,0,2:T(8,128)(2,1)S(1)}, bf16[2,2,1,32,128]{4,3,1,0,2:T(8,128)(2,1)S(1)}, u32[]{:S(2)}, u32[]{:S(2)}) %collective-permute-start.15) | collective-permute-done | bytes 32800 | tf_op jit(solution)/shard_map/ppermute | solution.py:33
  42.1 2.6 %readout.1 = (bf16[8,2560]{1,0:T(8,128)(2,1)S(1)}, bf16[16,32,128]{2,1,0:T(8,128)(2,1)S(1)}) custom-call(s32[1]{0:T(128)} %bitcast.me_ref, f32[16]{0:T(128)S(1)} %copy-done.6, f32[16,128]{1,0:T(8,128)S(1)} %get-tuple-element.43.place_ref, f32[16,128]{1,0:T(8,128)S(1)} %copy-done.4, f32[16,128]{1,0:T(8,128)S(1)} %bitcast.15, ...), custom_call_target="tpu_custom_call" | custom-call | tf_op jit(solution)/shard_map/readout/pallas_call | solution.py:570
  44.7 0.8 %collective-permute-start.17 = (bf16[8,2560]{1,0:T(8,128)(2,1)S(1)}, bf16[8,2560]{1,0:T(8,128)(2,1)S(1)}, u32[]{:S(2)}, u32[]{:S(2)}) collective-permute-start(bf16[8,2560]{1,0:T(8,128)(2,1)S(1)} %get-tuple-element.59), channel_id=1, source_target_pairs={{0,6},{1,7},{2,4},{3,5},{4,2},{5,3},{6,0},{7,1},{8,14},{9,15},{10,... | collective-permute-start | bytes 122888 | tf_op jit(solution)/shard_map/ppermute | solution.py:33
  45.5 3.4 %near_update.1 = (bf16[8,16,128,128]{3,2,1,0:T(8,128)(2,1)}, bf16[16,128,16]{2,1,0:T(8,128)(2,1)S(1)}, f32[16,16,128]{2,1,0:T(8,128)S(1)}, f32[2,16,16,128]{3,2,1,0:T(8,128)S(1)}) custom-call(s32[1]{0:T(128)} %bitcast.me_ref, s32[1,4,32]{2,1,0:T(4,128)S(1)} %copy-done.3, f32[16]{0:T(128)S(1)} %copy-done.6, ...), custom_call_target="tpu_custom_call" | custom-call | tf_op jit(solution)/shard_map/near_update/pallas_call | solution.py:583
  48.9 1.6 %collective-permute-start.19 = (bf16[16,2560]{1,0:T(8,128)(2,1)S(1)}, bf16[16,2560]{1,0:T(8,128)(2,1)S(1)}, u32[]{:S(2)}, u32[]{:S(2)}) collective-permute-start(bf16[16,2560]{1,0:T(8,128)(2,1)S(1)} %pad_maximum_fusion.1.refs_0_), channel_id=1, source_target_pairs={{0,8},{1,9},{2,10},{3,11},{4,12},{5,13},{6,14},{7,15},{8,0},{9,1},... | collective-permute-start | bytes 245768 | tf_op jit(solution)/shard_map/ppermute | solution.py:33
  50.5 1.0 %collective-permute-start.18 = (bf16[16,2560]{1,0:T(8,128)(2,1)S(1)}, bf16[16,2560]{1,0:T(8,128)(2,1)S(1)}, u32[]{:S(2)}, u32[]{:S(2)}) collective-permute-start(bf16[16,2560]{1,0:T(8,128)(2,1)S(1)} %pad_maximum_fusion.1.refs_0_), channel_id=1, source_target_pairs={{0,4},{1,5},{2,6},{3,7},{4,0},{5,1},{6,2},{7,3},{8,12},{9,13},{10,... | collective-permute-start | bytes 245768 | tf_op jit(solution)/shard_map/ppermute | solution.py:33
  51.5 1.6 %collective-permute-start.20 = (bf16[16,2560]{1,0:T(8,128)(2,1)S(1)}, bf16[16,2560]{1,0:T(8,128)(2,1)S(1)}, u32[]{:S(2)}, u32[]{:S(2)}) collective-permute-start(bf16[16,2560]{1,0:T(8,128)(2,1)S(1)} %pad_maximum_fusion.1.refs_0_), channel_id=1, source_target_pairs={{0,12},{1,13},{2,14},{3,15},{4,8},{5,9},{6,10},{7,11},{8,4},{9,5},... | collective-permute-start | bytes 245768 | tf_op jit(solution)/shard_map/ppermute | solution.py:33
  53.1 5.4 %collective-permute-start.22 = (bf16[16,2560]{1,0:T(8,128)(2,1)S(1)}, bf16[16,2560]{1,0:T(8,128)(2,1)S(1)}, u32[]{:S(2)}, u32[]{:S(2)}) collective-permute-start(bf16[16,2560]{1,0:T(8,128)(2,1)S(1)} %pad_maximum_fusion.1.refs_0_), channel_id=1, source_target_pairs={{0,1},{1,0},{2,3},{3,2},{4,5},{5,4},{6,7},{7,6},{8,9},{9,8},{10,11... | collective-permute-start | bytes 245768 | tf_op jit(solution)/shard_map/ppermute | solution.py:33
  58.5 1.9 %far_update.1.refs_1_ = bf16[8,16,128,128]{3,2,1,0:T(8,128)(2,1)} custom-call(s32[1]{0:T(128)} %bitcast.me_ref, s32[1,4,32]{2,1,0:T(4,128)S(1)} %copy-done.3, bf16[16,128,16]{2,1,0:T(8,128)(2,1)S(1)} %get-tuple-element.64.turned_ref, f32[16,16,128]{2,1,0:T(8,128)S(1)} %get-tuple-element.65.values_ref, ...), custom_call_target="tpu_custom_call", output_to_operand_aliasing={{}: (7, {})} | custom-call | tf_op jit(solution)/shard_map/far_update/pallas_call | solution.py:599
  60.4 0.0 copy-start.1
  60.5 0.1 collective-permute-start.24
  60.5 0.5 collective-permute-start.23
  61.0 1.2 %collective-permute-start.25 = (bf16[16,2560]{1,0:T(8,128)(2,1)S(1)}, bf16[16,2560]{1,0:T(8,128)(2,1)S(1)}, u32[]{:S(2)}, u32[]{:S(2)}) collective-permute-start(bf16[16,2560]{1,0:T(8,128)(2,1)S(1)} %collective-permute-done.20.refs_3_), channel_id=1, source_target_pairs={{0,1},{1,0},{2,3},{3,2},{4,5},{5,4},{6,7},{7,6},{8,9},{9,8},{10,11... | collective-permute-start | bytes 245768 | tf_op jit(solution)/shard_map/ppermute | solution.py:33
  62.3 1.9 %last_update.1 = bf16[8,16,128,128]{3,2,1,0:T(8,128)(2,1)} custom-call(s32[1]{0:T(128)} %bitcast.me_ref, s32[1,4,32]{2,1,0:T(4,128)S(1)} %copy-done.3, bf16[16,128,16]{2,1,0:T(8,128)(2,1)S(1)} %get-tuple-element.64.turned_ref, f32[16,16,128]{2,1,0:T(8,128)S(1)} %get-tuple-element.65.values_ref, ...), custom_call_target="tpu_custom_call", output_to_operand_aliasing={{}: (6, {})} | custom-call | tf_op jit(solution)/shard_map/last_update/pallas_call | solution.py:599
  64.2 1.3 %output.1 = bf16[128,128]{1,0:T(8,128)(2,1)} custom-call(bf16[128,128]{1,0:T(8,128)(2,1)S(1)} %get-tuple-element.37.x_ref, bf16[2048,128]{1,0:T(8,128)(2,1)S(1)} %copy-done.1, bf16[128,640]{1,0:T(8,128)(2,1)S(1)} %get-tuple-element.38.pick_ref, bf16[16,2560]{1,0:T(8,128)(2,1)S(1)} %pad_maximum_fusion.1.refs_0_, ...), custom_call_target="tpu_custom_call" | custom-call | tf_op jit(solution)/shard_map/output/pallas_call | solution.py:625
  (39 shorter events, 0.2 us)
Async XLA Ops:
  0.6 6.1 %copy-start.2 = (s32[1,4,32]{2,1,0:T(4,128)S(1)}, s32[1,4,32]{2,1,0:T(4,128)}, u32[]{:S(2)}) copy-start(s32[1,4,32]{2,1,0:T(4,128)} %parent_ref.11) | copy-start | bytes 1540
  3.3 14.5 %collective-permute-start.4 = (bf16[1,16,128,128]{3,2,1,0:T(8,128)(2,1)S(1)}, bf16[1,16,128,128]{3,2,1,0:T(8,128)(2,1)S(1)}, u32[]{:S(2)}, u32[]{:S(2)}) collective-permute-start(bf16[1,16,128,128]{3,2,1,0:T(8,128)(2,1)S(1)} %get-tuple-element.41), channel_id=1, source_target_pairs={{0,2},{1,3},{2,0},{3,1},{4,6},{5,7},{6,4},{7,5},{8,10},{9,11},{10,... | collective-permute-start | bytes 1572872 | tf_op jit(solution)/shard_map/ppermute | solution.py:33
  5.5 3.8 %collective-permute-start = (bf16[128,128]{1,0:T(8,128)(2,1)S(1)}, bf16[128,128]{1,0:T(8,128)(2,1)S(1)}, u32[]{:S(2)}, u32[]{:S(2)}) collective-permute-start(bf16[128,128]{1,0:T(8,128)(2,1)S(1)} %get-tuple-element.37.x_ref), channel_id=1, source_target_pairs={{0,6},{1,7},{2,4},{3,5},{4,2},{5,3},{6,0},{7,1},{8,14},{9,15},{10,... | collective-permute-start | bytes 98312 | tf_op jit(solution)/shard_map/ppermute | solution.py:33
  6.8 16.5 %copy-start = (bf16[2048,3,128]{2,0,1:T(8,128)(2,1)S(1)}, bf16[2048,3,128]{2,0,1:T(8,128)(2,1)}, u32[]{:S(2)}) copy-start(bf16[2048,3,128]{2,0,1:T(8,128)(2,1)} %param.13) | copy-start | bytes 4718596
  9.2 7.5 %collective-permute-start.3 = (bf16[256,128]{1,0:T(8,128)(2,1)S(1)}, bf16[256,128]{1,0:T(8,128)(2,1)S(1)}, u32[]{:S(2)}, u32[]{:S(2)}) collective-permute-start(bf16[256,128]{1,0:T(8,128)(2,1)S(1)} %pad_maximum_fusion.2.refs_0_), channel_id=1, source_target_pairs={{0,12},{1,13},{2,14},{3,15},{4,8},{5,9},{6,10},{7,11},{8,4},{9,5},... | collective-permute-start | bytes 196616 | tf_op jit(solution)/shard_map/ppermute | solution.py:33
  12.6 5.1 %collective-permute-start.2 = (bf16[256,128]{1,0:T(8,128)(2,1)S(1)}, bf16[256,128]{1,0:T(8,128)(2,1)S(1)}, u32[]{:S(2)}, u32[]{:S(2)}) collective-permute-start(bf16[256,128]{1,0:T(8,128)(2,1)S(1)} %pad_maximum_fusion.2.refs_0_), channel_id=1, source_target_pairs={{0,8},{1,9},{2,10},{3,11},{4,12},{5,13},{6,14},{7,15},{8,0},{9,1},... | collective-permute-start | bytes 196616 | tf_op jit(solution)/shard_map/ppermute | solution.py:33
  12.6 5.1 %collective-permute-start.1 = (bf16[256,128]{1,0:T(8,128)(2,1)S(1)}, bf16[256,128]{1,0:T(8,128)(2,1)S(1)}, u32[]{:S(2)}, u32[]{:S(2)}) collective-permute-start(bf16[256,128]{1,0:T(8,128)(2,1)S(1)} %pad_maximum_fusion.2.refs_0_), channel_id=1, source_target_pairs={{0,4},{1,5},{2,6},{3,7},{4,0},{5,1},{6,2},{7,3},{8,12},{9,13},{10,... | collective-permute-start | bytes 196616 | tf_op jit(solution)/shard_map/ppermute | solution.py:33
  17.8 3.2 %collective-permute-start.5 = (bf16[256,128]{1,0:T(8,128)(2,1)S(1)}, bf16[256,128]{1,0:T(8,128)(2,1)S(1)}, u32[]{:S(2)}, u32[]{:S(2)}) collective-permute-start(bf16[256,128]{1,0:T(8,128)(2,1)S(1)} %pad_maximum_fusion.2.refs_0_), channel_id=1, source_target_pairs={{0,1},{1,0},{2,3},{3,2},{4,5},{5,4},{6,7},{7,6},{8,9},{9,8},{10,11... | collective-permute-start | bytes 196616 | tf_op jit(solution)/shard_map/ppermute | solution.py:33
  20.1 1.7 %collective-permute-start.6 = (bf16[256,128]{1,0:T(8,128)(2,1)S(1)}, bf16[256,128]{1,0:T(8,128)(2,1)S(1)}, u32[]{:S(2)}, u32[]{:S(2)}) collective-permute-start(bf16[256,128]{1,0:T(8,128)(2,1)S(1)} %collective-permute-done.1.refs_1_), channel_id=1, source_target_pairs={{0,1},{1,0},{2,3},{3,2},{4,5},{5,4},{6,7},{7,6},{8,9},{9,8},{10,11... | collective-permute-start | bytes 196616 | tf_op jit(solution)/shard_map/ppermute | solution.py:33
  20.2 1.7 %collective-permute-start.7 = (bf16[256,128]{1,0:T(8,128)(2,1)S(1)}, bf16[256,128]{1,0:T(8,128)(2,1)S(1)}, u32[]{:S(2)}, u32[]{:S(2)}) collective-permute-start(bf16[256,128]{1,0:T(8,128)(2,1)S(1)} %collective-permute-done.2.refs_2_), channel_id=1, source_target_pairs={{0,1},{1,0},{2,3},{3,2},{4,5},{5,4},{6,7},{7,6},{8,9},{9,8},{10,11... | collective-permute-start | bytes 196616 | tf_op jit(solution)/shard_map/ppermute | solution.py:33
  20.6 2.7 %collective-permute-start.8 = (bf16[256,128]{1,0:T(8,128)(2,1)S(1)}, bf16[256,128]{1,0:T(8,128)(2,1)S(1)}, u32[]{:S(2)}, u32[]{:S(2)}) collective-permute-start(bf16[256,128]{1,0:T(8,128)(2,1)S(1)} %collective-permute-done.3.refs_3_), channel_id=1, source_target_pairs={{0,1},{1,0},{2,3},{3,2},{4,5},{5,4},{6,7},{7,6},{8,9},{9,8},{10,11... | collective-permute-start | bytes 196616 | tf_op jit(solution)/shard_map/ppermute | solution.py:33
  20.7 14.5 %collective-permute-start.13 = (bf16[1,16,128,128]{3,2,1,0:T(8,128)(2,1)S(1)}, bf16[1,16,128,128]{3,2,1,0:T(8,128)(2,1)S(1)}, u32[]{:S(2)}, u32[]{:S(2)}) collective-permute-start(bf16[1,16,128,128]{3,2,1,0:T(8,128)(2,1)S(1)} %get-tuple-element.56), channel_id=1, source_target_pairs={{0,2},{1,3},{2,0},{3,1},{4,6},{5,7},{6,4},{7,5},{8,10},{9,11},{10,... | collective-permute-start | bytes 1572872 | tf_op jit(solution)/shard_map/ppermute | solution.py:33
  21.0 9.2 %collective-permute-start.11 = (bf16[1,16,128,128]{3,2,1,0:T(8,128)(2,1)}, bf16[1,16,128,128]{3,2,1,0:T(8,128)(2,1)S(1)}, u32[]{:S(2)}, u32[]{:S(2)}) collective-permute-start(bf16[1,16,128,128]{3,2,1,0:T(8,128)(2,1)} %get-tuple-element.50), channel_id=1, source_target_pairs={{0,1},{1,0},{2,3},{3,2},{4,5},{5,4},{6,7},{7,6},{8,9},{9,8},{10,11... | collective-permute-start | bytes 1572872 | tf_op jit(solution)/shard_map/ppermute | solution.py:33
  21.8 8.4 %collective-permute-start.12 = (bf16[1,16,128,128]{3,2,1,0:T(8,128)(2,1)}, bf16[1,16,128,128]{3,2,1,0:T(8,128)(2,1)S(1)}, u32[]{:S(2)}, u32[]{:S(2)}) collective-permute-start(bf16[1,16,128,128]{3,2,1,0:T(8,128)(2,1)} %get-tuple-element.51), channel_id=1, source_target_pairs={{0,1},{1,0},{2,3},{3,2},{4,5},{5,4},{6,7},{7,6},{8,9},{9,8},{10,11... | collective-permute-start | bytes 1572872 | tf_op jit(solution)/shard_map/ppermute | solution.py:33
  21.9 39.2 %collective-permute-start.21 = (bf16[2,16,128,128]{3,2,1,0:T(8,128)(2,1)}, bf16[2,16,128,128]{3,2,1,0:T(8,128)(2,1)S(1)}, u32[]{:S(2)}, u32[]{:S(2)}) collective-permute-start(bf16[2,16,128,128]{3,2,1,0:T(8,128)(2,1)} %get-tuple-element.68), channel_id=1, source_target_pairs={{0,3},{1,2},{2,1},{3,0},{4,7},{5,6},{6,5},{7,4},{8,11},{9,10},{10,... | collective-permute-start | bytes 3145736 | tf_op jit(solution)/shard_map/ppermute | solution.py:33
  24.4 1.3 %collective-permute-start.9 = (bf16[1,2,4,32,128]{4,3,1,0,2:T(8,128)(2,1)S(1)}, bf16[1,2,4,32,128]{4,3,1,0,2:T(8,128)(2,1)S(1)}, u32[]{:S(2)}, u32[]{:S(2)}) collective-permute-start(bf16[1,2,4,32,128]{4,3,1,0,2:T(8,128)(2,1)S(1)} %copy.13), channel_id=1, source_target_pairs={{0,1},{1,0},{2,3},{3,2},{4,5},{5,4},{6,7},{7,6},{8,9},{9,8},{10,11... | collective-permute-start | bytes 196616 | tf_op jit(solution)/shard_map/ppermute | solution.py:33
  25.7 4.5 %collective-permute-start.10 = (bf16[2,1,4,32,128]{4,3,1,0,2:T(8,128)(2,1)S(1)}, bf16[2,1,4,32,128]{4,3,1,0,2:T(8,128)(2,1)S(1)}, u32[]{:S(2)}, u32[]{:S(2)}) collective-permute-start(bf16[2,1,4,32,128]{4,3,1,0,2:T(8,128)(2,1)S(1)} %get-tuple-element.77), channel_id=1, source_target_pairs={{0,6},{1,7},{2,4},{3,5},{4,2},{5,3},{6,0},{7,1},{8,14},{9,15},{10,... | collective-permute-start | bytes 196616 | tf_op jit(solution)/shard_map/ppermute | solution.py:33
  35.2 5.2 %collective-permute-start.14 = (bf16[2,2,1,32,128]{4,3,1,0,2:T(8,128)(2,1)S(1)}, bf16[2,2,1,32,128]{4,3,1,0,2:T(8,128)(2,1)S(1)}, u32[]{:S(2)}, u32[]{:S(2)}) collective-permute-start(bf16[2,2,1,32,128]{4,3,1,0,2:T(8,128)(2,1)S(1)} %get-tuple-element.58), channel_id=1, source_target_pairs={{0,4},{1,5},{2,6},{3,7},{4,0},{5,1},{6,2},{7,3},{8,12},{9,13},{10,... | collective-permute-start | bytes 98312 | tf_op jit(solution)/shard_map/ppermute | solution.py:33
  35.7 4.8 %collective-permute-start.16 = (bf16[2,2,1,32,128]{4,3,1,0,2:T(8,128)(2,1)S(1)}, bf16[2,2,1,32,128]{4,3,1,0,2:T(8,128)(2,1)S(1)}, u32[]{:S(2)}, u32[]{:S(2)}) collective-permute-start(bf16[2,2,1,32,128]{4,3,1,0,2:T(8,128)(2,1)S(1)} %get-tuple-element.72), channel_id=1, source_target_pairs={{0,12},{1,13},{2,14},{3,15},{4,8},{5,9},{6,10},{7,11},{8,4},{9,5},... | collective-permute-start | bytes 98312 | tf_op jit(solution)/shard_map/ppermute | solution.py:33
  37.9 4.1 %copy-start.4 = (f32[16,128]{1,0:T(8,128)S(1)}, f32[16,128]{1,0:T(8,128)}, u32[]{:S(2)}) copy-start(f32[16,128]{1,0:T(8,128)} %gate_ref.3) | copy-start | bytes 24580
  37.9 4.1 %copy-start.5 = (f32[2048]{0:T(1024)S(1)}, f32[2048]{0:T(1024)}, u32[]{:S(2)}) copy-start(f32[2048]{0:T(1024)} %param.16) | copy-start | bytes 24580
  38.0 4.1 %copy-start.6 = (f32[16]{0:T(128)S(1)}, f32[16]{0:T(128)}, u32[]{:S(2)}) copy-start(f32[16]{0:T(128)} %bias_ref.3) | copy-start | bytes 196
  38.0 4.1 %collective-permute-start.15 = (bf16[2,2,1,32,128]{4,3,1,0,2:T(8,128)(2,1)S(1)}, bf16[2,2,1,32,128]{4,3,1,0,2:T(8,128)(2,1)S(1)}, u32[]{:S(2)}, u32[]{:S(2)}) collective-permute-start(bf16[2,2,1,32,128]{4,3,1,0,2:T(8,128)(2,1)S(1)} %get-tuple-element.73), channel_id=1, source_target_pairs={{0,8},{1,9},{2,10},{3,11},{4,12},{5,13},{6,14},{7,15},{8,0},{9,1},... | collective-permute-start | bytes 98312 | tf_op jit(solution)/shard_map/ppermute | solution.py:33
  40.4 5.1 %copy-start.3 = (s32[1,4,32]{2,1,0:T(4,128)S(1)}, s32[1,4,32]{2,1,0:T(4,128)}, u32[]{:S(2)}) copy-start(s32[1,4,32]{2,1,0:T(4,128)} %parent_ref.11) | copy-start | bytes 1540
  44.7 4.2 %collective-permute-start.17 = (bf16[8,2560]{1,0:T(8,128)(2,1)S(1)}, bf16[8,2560]{1,0:T(8,128)(2,1)S(1)}, u32[]{:S(2)}, u32[]{:S(2)}) collective-permute-start(bf16[8,2560]{1,0:T(8,128)(2,1)S(1)} %get-tuple-element.59), channel_id=1, source_target_pairs={{0,6},{1,7},{2,4},{3,5},{4,2},{5,3},{6,0},{7,1},{8,14},{9,15},{10,... | collective-permute-start | bytes 122888 | tf_op jit(solution)/shard_map/ppermute | solution.py:33
  48.9 11.6 %collective-permute-start.19 = (bf16[16,2560]{1,0:T(8,128)(2,1)S(1)}, bf16[16,2560]{1,0:T(8,128)(2,1)S(1)}, u32[]{:S(2)}, u32[]{:S(2)}) collective-permute-start(bf16[16,2560]{1,0:T(8,128)(2,1)S(1)} %pad_maximum_fusion.1.refs_0_), channel_id=1, source_target_pairs={{0,8},{1,9},{2,10},{3,11},{4,12},{5,13},{6,14},{7,15},{8,0},{9,1},... | collective-permute-start | bytes 245768 | tf_op jit(solution)/shard_map/ppermute | solution.py:33
  50.5 10.1 %collective-permute-start.18 = (bf16[16,2560]{1,0:T(8,128)(2,1)S(1)}, bf16[16,2560]{1,0:T(8,128)(2,1)S(1)}, u32[]{:S(2)}, u32[]{:S(2)}) collective-permute-start(bf16[16,2560]{1,0:T(8,128)(2,1)S(1)} %pad_maximum_fusion.1.refs_0_), channel_id=1, source_target_pairs={{0,4},{1,5},{2,6},{3,7},{4,0},{5,1},{6,2},{7,3},{8,12},{9,13},{10,... | collective-permute-start | bytes 245768 | tf_op jit(solution)/shard_map/ppermute | solution.py:33
  51.5 9.5 %collective-permute-start.20 = (bf16[16,2560]{1,0:T(8,128)(2,1)S(1)}, bf16[16,2560]{1,0:T(8,128)(2,1)S(1)}, u32[]{:S(2)}, u32[]{:S(2)}) collective-permute-start(bf16[16,2560]{1,0:T(8,128)(2,1)S(1)} %pad_maximum_fusion.1.refs_0_), channel_id=1, source_target_pairs={{0,12},{1,13},{2,14},{3,15},{4,8},{5,9},{6,10},{7,11},{8,4},{9,5},... | collective-permute-start | bytes 245768 | tf_op jit(solution)/shard_map/ppermute | solution.py:33
  53.1 11.1 %collective-permute-start.22 = (bf16[16,2560]{1,0:T(8,128)(2,1)S(1)}, bf16[16,2560]{1,0:T(8,128)(2,1)S(1)}, u32[]{:S(2)}, u32[]{:S(2)}) collective-permute-start(bf16[16,2560]{1,0:T(8,128)(2,1)S(1)} %pad_maximum_fusion.1.refs_0_), channel_id=1, source_target_pairs={{0,1},{1,0},{2,3},{3,2},{4,5},{5,4},{6,7},{7,6},{8,9},{9,8},{10,11... | collective-permute-start | bytes 245768 | tf_op jit(solution)/shard_map/ppermute | solution.py:33
  60.4 3.8 %copy-start.1 = (bf16[2048,128]{1,0:T(8,128)(2,1)S(1)}, bf16[2048,128]{1,0:T(8,128)(2,1)}, u32[]{:S(2)}) copy-start(bf16[2048,128]{1,0:T(8,128)(2,1)} %weight_ref.1) | copy-start | bytes 1572868
  60.5 3.7 %collective-permute-start.24 = (bf16[16,2560]{1,0:T(8,128)(2,1)S(1)}, bf16[16,2560]{1,0:T(8,128)(2,1)S(1)}, u32[]{:S(2)}, u32[]{:S(2)}) collective-permute-start(bf16[16,2560]{1,0:T(8,128)(2,1)S(1)} %collective-permute-done.19.refs_2_), channel_id=1, source_target_pairs={{0,1},{1,0},{2,3},{3,2},{4,5},{5,4},{6,7},{7,6},{8,9},{9,8},{10,11... | collective-permute-start | bytes 245768 | tf_op jit(solution)/shard_map/ppermute | solution.py:33
  60.5 3.7 %collective-permute-start.23 = (bf16[16,2560]{1,0:T(8,128)(2,1)S(1)}, bf16[16,2560]{1,0:T(8,128)(2,1)S(1)}, u32[]{:S(2)}, u32[]{:S(2)}) collective-permute-start(bf16[16,2560]{1,0:T(8,128)(2,1)S(1)} %collective-permute-done.18.refs_1_), channel_id=1, source_target_pairs={{0,1},{1,0},{2,3},{3,2},{4,5},{5,4},{6,7},{7,6},{8,9},{9,8},{10,11... | collective-permute-start | bytes 245768 | tf_op jit(solution)/shard_map/ppermute | solution.py:33
  61.0 3.2 %collective-permute-start.25 = (bf16[16,2560]{1,0:T(8,128)(2,1)S(1)}, bf16[16,2560]{1,0:T(8,128)(2,1)S(1)}, u32[]{:S(2)}, u32[]{:S(2)}) collective-permute-start(bf16[16,2560]{1,0:T(8,128)(2,1)S(1)} %collective-permute-done.20.refs_3_), channel_id=1, source_target_pairs={{0,1},{1,0},{2,3},{3,2},{4,5},{5,4},{6,7},{7,6},{8,9},{9,8},{10,11... | collective-permute-start | bytes 245768 | tf_op jit(solution)/shard_map/ppermute | solution.py:33

commit v5 on v4

--- a/solution.py
+++ b/solution.py
@@ -9,6 +9,7 @@
 from jax.sharding import PartitionSpec as P
 
 CAP = 2
+FARS = 2 * CAP - 1
 TILE = 16
 VMEM_BYTES = 24 * 1024 * 1024
 WHOLE = pl.BlockSpec(memory_space=pltpu.VMEM)
@@ -76,7 +77,7 @@
     return plan[-1:] + plan[:-1]
 
 
-def exchange_all(pieces, plan, before=lambda stage, place, slab: slab, after=lambda stage, held: held):
+def exchange_all(pieces, plan, after=lambda stage, held: held):
     tail = pieces.shape[1:]
     held = [pieces.reshape(tuple(len(stage) + 1 for stage in plan) + tail)]
     for axis, stage in enumerate(plan):
@@ -84,7 +85,7 @@
         for part in held:
             slabs = [lax.index_in_dim(part, place, axis, keepdims=True) for place in range(len(stage) + 1)]
             fresh.append(slabs[0])
-            fresh += [xor_permute(before(axis, place, slabs[place + 1]), far) for place, far in enumerate(stage)]
+            fresh += [xor_permute(slab, distance) for slab, distance in zip(slabs[1:], stage)]
         held = after(axis, fresh if axis == len(plan) - 1 else [jnp.concatenate(fresh, axis)])
     return [part.reshape((-1,) + tail) for part in held]
 
@@ -112,6 +113,10 @@
         same = (pltpu.roll(parent_block, earlier, 1) == parent_block) & (child >= earlier)
         rank = rank + same.astype(jnp.int32)
     return device, child, parent_block ^ (device & (blocks - 1)), rank, parent_place
+
+
+def far_number(away, rank):
+    return (away == 3) | ((away == 2) & (rank > 0)), jnp.where(away == 3, rank, CAP + rank - 1)
 
 
 def column_of(row):
@@ -169,59 +174,53 @@
     state_copy.wait()
 
 
-def pick_kernel(
-    blocks, piece, send_order, me_ref, parent_ref, parents_ref, states_ref, pick_ref, second_ref, sem
-):
+def pick_kernel(blocks, piece, send_order, me_ref, parent_ref, parents_ref, states_ref, pick_ref, corner_ref, sem):
     me, rows, own_rows = me_ref[0], parents_ref.shape[1], states_ref.shape[0]
     user, member = split(me, blocks)
-    chosen = matching_children(parent_ref, user, member ^ 2, member, own_rows, 0)[1][1]
-    copy = pltpu.make_async_copy(states_ref.at[chosen], second_ref.at[0], sem)
-    copy.start()
+    copies = []
+    for slot, row in enumerate(matching_children(parent_ref, user, member ^ 3, member, own_rows, 0)[1]):
+        copies.append(pltpu.make_async_copy(states_ref.at[row], corner_ref.at[slot], sem.at[slot]))
+        copies[-1].start()
     device, child, away, rank, _ = row_facts(parents_ref[...], blocks, own_rows)
+    is_far, number = far_number(away, rank)
     own = place_in(send_order, device ^ me) * piece + child
-    far = place_in(send_order, device ^ away ^ me) * piece + 3 * own_rows + rank
+    far = place_in(send_order, device ^ away ^ me) * piece + 3 * own_rows + number
     line = lax.broadcasted_iota(jnp.int32, (len(send_order) * piece, rows), 0)
     for slab in range(3):
-        far_line = jnp.where(away == 3, far + slab * CAP, -1)
+        far_line = jnp.where(is_far, far + slab * FARS, -1)
         chosen = (line == own[0:1] + slab * own_rows) | (line == far_line[0:1])
         pick_ref[:, slab * rows : (slab + 1) * rows] = chosen.astype(jnp.float32).astype(jnp.bfloat16)
-    copy.wait()
-
-
-def stage_kernel(
-    blocks, normed_order, me_ref, parent_ref, parents_ref, states_ref, *refs
-):
+    for copy in copies:
+        copy.wait()
+
+
+def stage_kernel(blocks, normed_order, me_ref, parent_ref, parents_ref, states_ref, *refs):
     outs, (place_ref, pick_ref, hold_ref, in_sem, out_sem) = refs[:-5], refs[-5:]
     me, own_rows = me_ref[0], states_ref.shape[0]
     user, member = split(me, blocks)
-    wanted = []
-    for partner in (3, 1):
-        wanted += matching_children(parent_ref, user, member ^ partner, member, own_rows, 0)[1]
-    targets = [ref.at[slot] for ref in outs for slot in range(ref.shape[0])]
+    wanted = matching_children(parent_ref, user, member ^ 1, member, own_rows, 0)[1]
+    wanted += matching_children(parent_ref, user, member ^ 2, member, own_rows, 0)[1][1:]
     loads, saves = [], []
-    for place, (row, target) in enumerate(zip(wanted, targets)):
+    for place, (row, out) in enumerate(zip(wanted, outs)):
         loads.append(pltpu.make_async_copy(states_ref.at[row], hold_ref.at[place], in_sem.at[place]))
-        saves.append(pltpu.make_async_copy(hold_ref.at[place], target, out_sem.at[place]))
+        saves.append(pltpu.make_async_copy(hold_ref.at[place], out.at[0], out_sem.at[place]))
         loads[-1].start()
     device, child, away, rank, parent_place = row_facts(parents_ref[...], blocks, own_rows)
+    is_far, number = far_number(away, rank)
     line = lax.broadcasted_iota(jnp.int32, (place_ref.shape[0], parents_ref.shape[1]), 0)
-    own = (line == jnp.where((device == me) & (away < 3), child, -1)[0:1]).astype(jnp.float32)
-    far = (line == jnp.where((device ^ away == me) & (away == 3), own_rows + rank, -1)[0:1]).astype(jnp.float32)
-    near_place = jnp.where(away == 0, parent_place, own_rows + (away - 1) * CAP + rank)
-    place = own * (near_place[0:1] + 1).astype(jnp.float32) + far * (parent_place[0:1] + 1).astype(jnp.float32)
+    own = (line == jnp.where((device == me) & ~is_far, child, -1)[0:1]).astype(jnp.float32)
+    far = (line == jnp.where((device ^ away == me) & is_far, own_rows + number, -1)[0:1]).astype(jnp.float32)
+    came = own_rows + jnp.where(away == 1, rank, CAP + rank)
+    own_place = jnp.where(away == 0, parent_place, came)
+    place = own * (own_place[0:1] + 1).astype(jnp.float32) + far * (parent_place[0:1] + 1).astype(jnp.float32)
     place_ref[...] = jnp.broadcast_to(jnp.sum(place, axis=1, keepdims=True) - 1.0, place_ref.shape)
     for load, save in zip(loads, saves):
         load.wait()
         save.start()
-    total = len(normed_order) * own_rows
-    first = place_in(normed_order, jnp.where(away == 3, device ^ away, device) ^ me) * own_rows
-    quarters = own_rows // CAP
-    for part in range(1 + quarters):
-        if part == 0:
-            index = jnp.where(away == 3, -1, first + child)
-        else:
-            index = jnp.where(away == 3, first + rank * quarters + part - 1, -1)
-        pick_ref[:, part * total : (part + 1) * total] = chosen_rows(column_of(index), total).astype(jnp.bfloat16)
+    count = len(normed_order)
+    holder = place_in(normed_order, jnp.where(is_far, device ^ away, device) ^ me)
+    index = jnp.where(is_far, count * own_rows + number * count + holder, holder * own_rows + child)
+    pick_ref[...] = chosen_rows(column_of(index), pick_ref.shape[1]).astype(jnp.bfloat16)
     for save in saves:
         save.wait()
 
@@ -252,11 +251,11 @@
 
 def head_rows(piece, own_rows):
     piece = piece.astype(jnp.float32)
-    far = piece[3 * own_rows : 4 * own_rows]
+    far = piece[3 * own_rows :]
     slabs = []
     for slab in range(3):
-        shifted = far if slab == 0 else pltpu.roll(far, own_rows - slab * CAP, 0)
-        slabs.append(jnp.concatenate([piece[slab * own_rows : (slab + 1) * own_rows], shifted], 0))
+        shifted = far if slab == 0 else pltpu.roll(far, far.shape[0] - slab * FARS, 0)
+        slabs.append(jnp.concatenate([piece[slab * own_rows : (slab + 1) * own_rows], shifted[:own_rows]], 0))
     return slabs
 
 
@@ -309,27 +308,33 @@
         return carry
 
     lax.fori_loop(0, heads // block, work, 0)
-    quarters = own_rows // CAP
-    share = heads // quarters
-    own = [norm_ref[h][:own_rows] for h in range(heads)]
-    far = []
-    for rank in range(CAP):
-        for quarter in range(quarters):
-            line = slice(own_rows + rank, own_rows + rank + 1)
-            far.append(jnp.concatenate([norm_ref[h][line] for h in range(quarter * share, (quarter + 1) * share)], 1))
-    out_ref[...] = jnp.concatenate(own + [jnp.concatenate(far, 0)], 1).astype(jnp.bfloat16)
+    share = heads // own_rows
+    columns = [norm_ref[h][:own_rows] for h in range(heads)]
+    for number in range(own_rows, own_rows + FARS):
+        lines = []
+        for line in range(own_rows):
+            span = range(line * share, (line + 1) * share)
+            lines.append(jnp.concatenate([norm_ref[h][number : number + 1] for h in span], 1))
+        columns.append(jnp.concatenate(lines, 0))
+    out_ref[...] = jnp.concatenate(columns, 1).astype(jnp.bfloat16)
 
 
 def output_kernel(own_rows, x_ref, weight_ref, pick_ref, *refs):
-    parts, out_ref = refs[:-1], refs[-1]
-    width, columns = weight_ref.shape[0], x_ref.shape[1]
-    quarters = own_rows // CAP
-    share = width // quarters
+    parts, (out_ref, far_ref) = refs[:-2], refs[-2:]
+    width = weight_ref.shape[0]
+    share = width // own_rows
     gathered = jnp.concatenate([part[...] for part in parts], 0)
-    own = jnp.dot(gathered[:, :width], weight_ref[...], preferred_element_type=jnp.float32)
-    weight = jnp.concatenate([weight_ref[q * share : (q + 1) * share, :] for q in range(quarters)], 1)
-    far = jnp.dot(gathered[:, width:], weight, preferred_element_type=jnp.float32)
-    rest = jnp.concatenate([own] + [far[:, q * columns : (q + 1) * columns] for q in range(quarters)], 0)
+    count = gathered.shape[0] // own_rows
+    lanes = far_ref.shape[2]
+    for block in range(far_ref.shape[0]):
+        far_ref[block] = gathered[:, width + block * lanes : width + (block + 1) * lanes].astype(jnp.float32)
+    rows = [gathered[:, :width]]
+    blocks = share // lanes
+    for number in range(FARS):
+        spans = range(number * blocks, (number + 1) * blocks)
+        lines = [far_ref[block, pl.ds(line, count, stride=own_rows), :] for line in range(own_rows) for block in spans]
+        rows.append(jnp.concatenate(lines, 1).astype(jnp.bfloat16))
+    rest = jnp.dot(jnp.concatenate(rows, 0), weight_ref[...], preferred_element_type=jnp.float32)
     total = x_ref[...].astype(jnp.float32)
     for _ in range(3):
         term = rest.astype(jnp.bfloat16)
@@ -462,9 +467,9 @@
     plan = stage_plan(count)
     steps = exchange_plan(plan)
     recv_order, normed_order = plan_order(steps), gather_order(plan)
-    slots, piece = 2 * own_rows, 4 * own_rows
+    slots, piece = 2 * own_rows, 5 * own_rows
     one_state, two_states = (1, heads, size, size), (CAP, heads, size, size)
-    normed_columns = width + CAP * width // own_rows
+    normed_columns = width + FARS * width // own_rows
     bf16, int32 = jnp.bfloat16, jnp.int32
     mine = me[None]
     parent_row = jnp.broadcast_to(parents.reshape(1, row_total), (8, row_total))
@@ -485,37 +490,36 @@
     )(mine, in_hbm(parents), in_hbm(token_ids), in_hbm(token_ids), in_hbm(embed_table), in_hbm(states))
     first_got = xor_permute(first_out, 2)
 
-    send_pick, second_out = pl.pallas_call(
+    send_pick, corner_out = pl.pallas_call(
         functools.partial(pick_kernel, blocks, piece, recv_order),
         in_specs=[SCALARS, SCALARS, WHOLE, PLACED],
         out_specs=[WHOLE] * 2,
-        out_shape=[jax.ShapeDtypeStruct((count * piece, 3 * row_total), bf16), pltpu.VMEM(one_state, bf16)],
-        scratch_shapes=[pltpu.SemaphoreType.DMA],
+        out_shape=[jax.ShapeDtypeStruct((count * piece, 3 * row_total), bf16), pltpu.VMEM(two_states, bf16)],
+        scratch_shapes=[pltpu.SemaphoreType.DMA((CAP,))],
         compiler_params=params(),
         name="pick",
     )(mine, in_hbm(parents), parent_row, in_hbm(states))
-    second_got = xor_permute(second_out, 2)
-
-    corner_out, *near_outs, place, out_pick = pl.pallas_call(
+    corner_got = xor_permute(corner_out, 3)
+
+    *near_outs, last_out, place, out_pick = pl.pallas_call(
         functools.partial(stage_kernel, blocks, normed_order),
         in_specs=[SCALARS, SCALARS, WHOLE, PLACED],
-        out_specs=[PLACED] * (1 + CAP) + [WHOLE] * 2,
-        out_shape=[pltpu.HBM(two_states, bf16)]
-        + [pltpu.HBM(one_state, bf16)] * CAP
+        out_specs=[PLACED] * (CAP + 1) + [WHOLE] * 2,
+        out_shape=[pltpu.HBM(one_state, bf16)] * (CAP + 1)
         + [
             jax.ShapeDtypeStruct((slots, 128), jnp.float32),
-            jax.ShapeDtypeStruct((row_total, (1 + own_rows // CAP) * row_total), bf16),
+            jax.ShapeDtypeStruct((row_total, row_total + FARS * count), bf16),
         ],
         scratch_shapes=[
-            pltpu.VMEM((2 * CAP, heads, size, size), bf16),
-            pltpu.SemaphoreType.DMA((2 * CAP,)),
-            pltpu.SemaphoreType.DMA((2 * CAP,)),
+            pltpu.VMEM((CAP + 1, heads, size, size), bf16),
+            pltpu.SemaphoreType.DMA((CAP + 1,)),
+            pltpu.SemaphoreType.DMA((CAP + 1,)),
         ],
         compiler_params=params(),
         name="stage",
     )(mine, in_hbm(parents), parent_row, in_hbm(states))
-    corner_got = xor_permute(corner_out, 3)
     near_gots = [xor_permute(block, 1) for block in near_outs]
+    last_got = xor_permute(last_out, 2)
 
     held = pl.pallas_call(
         hold_kernel,
@@ -547,17 +551,12 @@
         name="project",
     )(mine, tied["weight"], tied["pick"], *every_input)
 
-    def before_exchange(stage, place, slab):
-        if stage == 2 and place == 0:
-            slab, tied["second"] = lax.optimization_barrier((slab, second_got))
-        return slab
-
     def in_exchange(stage, parts):
         if stage == 1:
             *parts, tied["near"], tied["nearer"] = lax.optimization_barrier((*parts, *near_gots))
         return parts
 
-    received = exchange_all(pieces.reshape(count, piece, columns), steps, before_exchange, in_exchange)
+    received = exchange_all(pieces.reshape(count, piece, columns), steps, in_exchange)
     if columns != size:
         every_piece = jnp.stack(received, 1).reshape(count, piece, columns)
         places = jnp.array([recv_order.index(d) for d in range(count)], int32)[jnp.arange(count, dtype=int32) ^ me]
@@ -566,7 +565,7 @@
         recv_order = None
 
     held, near_gots = in_vmem(held), [tied["near"], tied["nearer"]]
-    sources = [held, *near_gots, tied["first"], tied["second"]]
+    sources = [held, *near_gots, tied["first"]]
     normed, by_head = pl.pallas_call(
         functools.partial(readout_kernel, recv_order, head_block, len(sources)),
         in_specs=[SCALARS] * 2 + [WHOLE] * (3 + len(sources) + len(received)),
@@ -614,22 +613,23 @@
         if stage == 0:
             *parts, tied["rows"], tied["turned"] = lax.optimization_barrier((*parts, near_done, turned))
         if stage == 1:
-            entries = [(rank, 0, 2, rank) for rank in range(CAP)]
-            far_done = far_update(tied["rows"], [tied["first"], tied["second"]], entries, "far_update")
-            ends = (parts[-1], far_done, corner_got)
-            parts[-1], tied["done"], tied["corner"] = lax.optimization_barrier(ends)
+            entries = [(0, 0, 2, 0)] + [(1, rank, 3, rank) for rank in range(CAP)]
+            far_done = far_update(tied["rows"], [tied["first"], corner_got], entries, "far_update")
+            parts[-1], tied["done"] = lax.optimization_barrier((parts[-1], far_done))
         return parts
 
     every_normed = gather_all(normed, plan, in_normed)
-    final = far_update(tied["done"], [tied["corner"]], [(0, rank, 3, rank) for rank in range(CAP)], "last_update")
     layer_out = pl.pallas_call(
         functools.partial(output_kernel, own_rows),
         in_specs=[WHOLE] * (3 + len(every_normed)),
         out_specs=WHOLE,
         out_shape=jax.ShapeDtypeStruct((row_total, columns), bf16),
+        scratch_shapes=[pltpu.VMEM(((normed_columns - width) // size, row_total, size), jnp.float32)],
         compiler_params=params(),
         name="output",
     )(local_columns, out_weight, out_pick, *every_normed)
+    layer_out, last_got = lax.optimization_barrier((layer_out, last_got))
+    final = far_update(tied["done"], [last_got], [(0, 0, 2, 1)], "last_update")
     return (layer_out[None], final)
 
 

time: 65.9 us -> 61.9 us (0.939); the launches traced: 65.5 us -> 62.2 us
  waiting for transfers between devices: 12.4 us -> 10.9 us
  starting transfers between devices: 29.3 us -> 28.1 us
    ppermute x26, waiting for transfers between devices: 12.4 us -> 10.9 us  [xor_permute(): lax.ppermute(block, 'rows', [(i, i ^ distance) for i in range(count)])]
    ppermute x26, starting transfers between devices: 29.3 us -> 28.1 us  [xor_permute(): lax.ppermute(block, 'rows', [(i, i ^ distance) for i in range(count)])]
    pallas_call x1, Pallas kernels: 3.78 us -> 2.99 us  [per_device(): pl.pallas_call(functools.partial(stage_kernel, blocks, normed_order), in_...]
where the time goes in v5:
time: 61.9 us; the launch traced here: 62.2 us
  starting transfers between devices  28.1 us (45%)
  Pallas kernels  22 us (36%)
  waiting for transfers between devices  10.9 us (18%)
  between operations  0.89 us (1%)
    ppermute x26, starting transfers between devices, xor_permute(): lax.ppermute(block, 'rows', [(i, i ^ distance) for i in range(count)])  28.1 us
    ppermute x26, waiting for transfers between devices, xor_permute(): lax.ppermute(block, 'rows', [(i, i ^ distance) for i in range(count)])  10.9 us
    pallas_call x2, Pallas kernels, far_update(): pl.pallas_call(functools.partial(far_update_kernel, head_block, blocks, o...  3.82 us
    pallas_call x1, Pallas kernels, per_device(): pl.pallas_call(functools.partial(near_update_kernel, recv_order, head_blo...  3.43 us
    pallas_call x1, Pallas kernels, per_device(): pl.pallas_call(functools.partial(stage_kernel, blocks, normed_order), in_...  2.99 us
    pallas_call x1, Pallas kernels, per_device(): pl.pallas_call(functools.partial(fetch_kernel, blocks), in_specs=[SCALARS...  2.67 us
    pallas_call x1, Pallas kernels, per_device(): pl.pallas_call(functools.partial(readout_kernel, recv_order, head_block,...  2.54 us
    pallas_call x1, Pallas kernels, per_device(): pl.pallas_call(hold_kernel, in_specs=[PLACED], out_specs=WHOLE, out_shape...  2.21 us
  transfers between devices with their start and end apart: 26, of which 7 were waited for; matrix products, arithmetic and copies ran while one was open for 0% of the time, Pallas kernels for 29%

profile of v5, /device:TPU:1, one launch (start us, length us, event | category | flops | bytes accessed | tf_op | source)
XLA Modules:
  0.0 62.2 jit_solution(7085590114192596368)
XLA Ops:
  0.6 0.0 copy-start.2
  0.6 2.7 %fetch.1 = (bf16[128,128]{1,0:T(8,128)(2,1)S(1)}, bf16[1,16,128,128]{3,2,1,0:T(8,128)(2,1)S(1)}) custom-call(s32[1]{0:T(128)} %bitcast.me_ref, s32[1,4,32]{2,1,0:T(4,128)} %parent_ref.11, s32[1,128]{1,0:T(1,128)} %tokens_ref.1, s32[1,128]{1,0:T(1,128)} %tokens_ref.1, bf16[32768,128]{1,0:T(8,128)(2,1)} %table_ref.1, bf16[8,16,128,128]{3,2,1,0:T(8,128)(2,1)} %states_ref.7), custom_call_target="tpu_custom_call" | custom-call | tf_op jit(solution)/shard_map/fetch/pallas_call | solution.py:478
  3.3 2.1 %collective-permute-start.4 = (bf16[1,16,128,128]{3,2,1,0:T(8,128)(2,1)S(1)}, bf16[1,16,128,128]{3,2,1,0:T(8,128)(2,1)S(1)}, u32[]{:S(2)}, u32[]{:S(2)}) collective-permute-start(bf16[1,16,128,128]{3,2,1,0:T(8,128)(2,1)S(1)} %get-tuple-element.40), channel_id=1, source_target_pairs={{0,2},{1,3},{2,0},{3,1},{4,6},{5,7},{6,4},{7,5},{8,10},{9,11},{10,... | collective-permute-start | bytes 1572872 | tf_op jit(solution)/shard_map/ppermute | solution.py:34
  5.5 1.2 %collective-permute-start = (bf16[128,128]{1,0:T(8,128)(2,1)S(1)}, bf16[128,128]{1,0:T(8,128)(2,1)S(1)}, u32[]{:S(2)}, u32[]{:S(2)}) collective-permute-start(bf16[128,128]{1,0:T(8,128)(2,1)S(1)} %get-tuple-element.36.x_ref), channel_id=1, source_target_pairs={{0,6},{1,7},{2,4},{3,5},{4,2},{5,3},{6,0},{7,1},{8,14},{9,15},{10,... | collective-permute-start | bytes 98312 | tf_op jit(solution)/shard_map/ppermute | solution.py:34
  6.7 0.1 broadcast_in_dim.14
  6.8 2.1 %pick.1 = (bf16[640,384]{1,0:T(8,128)(2,1)S(1)}, bf16[2,16,128,128]{3,2,1,0:T(8,128)(2,1)S(1)}) custom-call(s32[1]{0:T(128)} %bitcast.me_ref, s32[1,4,32]{2,1,0:T(4,128)} %parent_ref.11, s32[8,128]{1,0:T(8,128)S(1)} %broadcast_in_dim.15.parents_ref, bf16[8,16,128,128]{3,2,1,0:T(8,128)(2,1)} %states_ref.7), custom_call_target="tpu_custom_call" | custom-call | tf_op jit(solution)/shard_map/pick/pallas_call | solution.py:493
  8.9 0.4 collective-permute-done
  9.2 3.3 %collective-permute-start.3 = (bf16[256,128]{1,0:T(8,128)(2,1)S(1)}, bf16[256,128]{1,0:T(8,128)(2,1)S(1)}, u32[]{:S(2)}, u32[]{:S(2)}) collective-permute-start(bf16[256,128]{1,0:T(8,128)(2,1)S(1)} %pad_maximum_fusion.2.refs_0_), channel_id=1, source_target_pairs={{0,12},{1,13},{2,14},{3,15},{4,8},{5,9},{6,10},{7,11},{8,4},{9,5},... | collective-permute-start | bytes 196616 | tf_op jit(solution)/shard_map/ppermute | solution.py:34
  12.6 0.4 collective-permute-start.1
  12.9 3.0 %stage.1 = (bf16[1,16,128,128]{3,2,1,0:T(8,128)(2,1)}, bf16[1,16,128,128]{3,2,1,0:T(8,128)(2,1)}, bf16[1,16,128,128]{3,2,1,0:T(8,128)(2,1)}, f32[16,128]{1,0:T(8,128)S(1)}, bf16[128,176]{1,0:T(8,128)(2,1)S(1)}) custom-call(s32[1]{0:T(128)} %bitcast.me_ref, s32[1,4,32]{2,1,0:T(4,128)} %parent_ref.11, s32[8,128]{1,0:T(8,128)S(1)} %broadcast_in_dim.15.parents_ref, ...), custom_call_target="tpu_custom_call" | custom-call | tf_op jit(solution)/shard_map/stage/pallas_call | solution.py:504
  15.9 1.8 %collective-permute-done.2.refs_2_ = bf16[256,128]{1,0:T(8,128)(2,1)S(1)} collective-permute-done((bf16[256,128]{1,0:T(8,128)(2,1)S(1)}, bf16[256,128]{1,0:T(8,128)(2,1)S(1)}, u32[]{:S(2)}, u32[]{:S(2)}) %collective-permute-start.2) | collective-permute-done | bytes 65568 | tf_op jit(solution)/shard_map/ppermute | solution.py:34
  17.8 0.0 collective-permute-done.4.refs_3_.refs_0_
  17.8 2.4 %collective-permute-start.5 = (bf16[256,128]{1,0:T(8,128)(2,1)S(1)}, bf16[256,128]{1,0:T(8,128)(2,1)S(1)}, u32[]{:S(2)}, u32[]{:S(2)}) collective-permute-start(bf16[256,128]{1,0:T(8,128)(2,1)S(1)} %pad_maximum_fusion.2.refs_0_), channel_id=1, source_target_pairs={{0,1},{1,0},{2,3},{3,2},{4,5},{5,4},{6,7},{7,6},{8,9},{9,8},{10,11... | collective-permute-start | bytes 196616 | tf_op jit(solution)/shard_map/ppermute | solution.py:34
  20.2 0.1 collective-permute-start.6
  20.3 0.4 collective-permute-start.7
  20.7 0.1 collective-permute-start.8
  20.8 0.6 %collective-permute-start.20 = (bf16[2,16,128,128]{3,2,1,0:T(8,128)(2,1)S(1)}, bf16[2,16,128,128]{3,2,1,0:T(8,128)(2,1)S(1)}, u32[]{:S(2)}, u32[]{:S(2)}) collective-permute-start(bf16[2,16,128,128]{3,2,1,0:T(8,128)(2,1)S(1)} %get-tuple-element.63), channel_id=1, source_target_pairs={{0,3},{1,2},{2,1},{3,0},{4,7},{5,6},{6,5},{7,4},{8,11},{9,10},{10,... | collective-permute-start | bytes 3145736 | tf_op jit(solution)/shard_map/ppermute | solution.py:34
  21.4 0.0 collective-permute-done.5.refs_4_
  21.4 0.0 collective-permute-start.11
  21.5 0.0 collective-permute-done.6.refs_5_
  21.5 0.5 collective-permute-start.12
  21.9 0.0 collective-permute-done.8.refs_7_
  22.0 1.1 %project.1 = bf16[640,128]{1,0:T(8,128)(2,1)S(1)} custom-call(s32[1]{0:T(128)} %bitcast.me_ref, bf16[3,2048,128]{2,1,0:T(8,128)(2,1)S(1)} %bitcast.10, bf16[640,384]{1,0:T(8,128)(2,1)S(1)} %get-tuple-element.44.pick_ref, bf16[256,128]{1,0:T(8,128)(2,1)S(1)} %pad_maximum_fusion.2.refs_0_, bf16[256,128]{1,0:T(8,128)(2,1)S(1)} %collective-permute-done.1.refs_1_, ...), custom_call_target="tpu_custom_call" | custom-call | tf_op jit(solution)/shard_map/project/pallas_call | solution.py:545
  23.1 0.2 collective-permute-start.9
  23.3 1.1 %collective-permute-done.9 = bf16[1,2,4,40,128]{4,3,1,0,2:T(8,128)(2,1)S(1)} collective-permute-done((bf16[1,2,4,40,128]{4,3,1,0,2:T(8,128)(2,1)S(1)}, bf16[1,2,4,40,128]{4,3,1,0,2:T(8,128)(2,1)S(1)}, u32[]{:S(2)}, u32[]{:S(2)}) %collective-permute-start.9) | collective-permute-done | bytes 81952 | tf_op jit(solution)/shard_map/ppermute | solution.py:34
  24.5 1.5 %collective-permute-start.10 = (bf16[2,1,4,40,128]{4,3,1,0,2:T(8,128)(2,1)S(1)}, bf16[2,1,4,40,128]{4,3,1,0,2:T(8,128)(2,1)S(1)}, u32[]{:S(2)}, u32[]{:S(2)}) collective-permute-start(bf16[2,1,4,40,128]{4,3,1,0,2:T(8,128)(2,1)S(1)} %get-tuple-element.75), channel_id=1, source_target_pairs={{0,6},{1,7},{2,4},{3,5},{4,2},{5,3},{6,0},{7,1},{8,14},{9,15},{10,... | collective-permute-start | bytes 245768 | tf_op jit(solution)/shard_map/ppermute | solution.py:34
  25.9 3.4 %collective-permute-done.10 = bf16[2,1,4,40,128]{4,3,1,0,2:T(8,128)(2,1)S(1)} collective-permute-done((bf16[2,1,4,40,128]{4,3,1,0,2:T(8,128)(2,1)S(1)}, bf16[2,1,4,40,128]{4,3,1,0,2:T(8,128)(2,1)S(1)}, u32[]{:S(2)}, u32[]{:S(2)}) %collective-permute-start.10) | collective-permute-done | bytes 81952 | tf_op jit(solution)/shard_map/ppermute | solution.py:34
  29.4 3.4 %collective-permute-start.15 = (bf16[2,2,1,40,128]{4,3,1,0,2:T(8,128)(2,1)S(1)}, bf16[2,2,1,40,128]{4,3,1,0,2:T(8,128)(2,1)S(1)}, u32[]{:S(2)}, u32[]{:S(2)}) collective-permute-start(bf16[2,2,1,40,128]{4,3,1,0,2:T(8,128)(2,1)S(1)} %get-tuple-element.70), channel_id=1, source_target_pairs={{0,12},{1,13},{2,14},{3,15},{4,8},{5,9},{6,10},{7,11},{8,4},{9,5},... | collective-permute-start | bytes 122888 | tf_op jit(solution)/shard_map/ppermute | solution.py:34
  32.8 0.4 collective-permute-start.13
  33.2 2.2 %hold.1.refs_0_.states_ref = bf16[8,16,128,128]{3,2,1,0:T(8,128)(2,1)S(1)} custom-call(bf16[8,16,128,128]{3,2,1,0:T(8,128)(2,1)} %states_ref.7), custom_call_target="tpu_custom_call" | custom-call | tf_op jit(solution)/shard_map/hold/pallas_call | solution.py:524
  35.4 0.0 copy-start.3
  35.4 1.1 %collective-permute-done.14 = bf16[2,2,1,40,128]{4,3,1,0,2:T(8,128)(2,1)S(1)} collective-permute-done((bf16[2,2,1,40,128]{4,3,1,0,2:T(8,128)(2,1)S(1)}, bf16[2,2,1,40,128]{4,3,1,0,2:T(8,128)(2,1)S(1)}, u32[]{:S(2)}, u32[]{:S(2)}) %collective-permute-start.14) | collective-permute-done | bytes 40992 | tf_op jit(solution)/shard_map/ppermute | solution.py:34
  36.6 2.5 %readout.1 = (bf16[8,2816]{1,0:T(8,128)(2,1)S(1)}, bf16[16,40,128]{2,1,0:T(8,128)(2,1)S(1)}) custom-call(s32[1]{0:T(128)} %bitcast.me_ref, f32[16]{0:T(128)S(1)} %copy-done.6, f32[16,128]{1,0:T(8,128)S(1)} %get-tuple-element.42.place_ref, f32[16,128]{1,0:T(8,128)S(1)} %copy-done.4, f32[16,128]{1,0:T(8,128)S(1)} %bitcast.15, ...), custom_call_target="tpu_custom_call" | custom-call | tf_op jit(solution)/shard_map/readout/pallas_call | solution.py:569
  39.2 0.7 %collective-permute-start.16 = (bf16[8,2816]{1,0:T(8,128)(2,1)S(1)}, bf16[8,2816]{1,0:T(8,128)(2,1)S(1)}, u32[]{:S(2)}, u32[]{:S(2)}) collective-permute-start(bf16[8,2816]{1,0:T(8,128)(2,1)S(1)} %get-tuple-element.55), channel_id=1, source_target_pairs={{0,6},{1,7},{2,4},{3,5},{4,2},{5,3},{6,0},{7,1},{8,14},{9,15},{10,... | collective-permute-start | bytes 135176 | tf_op jit(solution)/shard_map/ppermute | solution.py:34
  39.8 0.8 %collective-permute-start.25 = (bf16[1,16,128,128]{3,2,1,0:T(8,128)(2,1)S(1)}, bf16[1,16,128,128]{3,2,1,0:T(8,128)(2,1)S(1)}, u32[]{:S(2)}, u32[]{:S(2)}) collective-permute-start(bf16[1,16,128,128]{3,2,1,0:T(8,128)(2,1)S(1)} %copy-done.7), channel_id=1, source_target_pairs={{0,2},{1,3},{2,0},{3,1},{4,6},{5,7},{6,4},{7,5},{8,10},{9,11},{10,... | collective-permute-start | bytes 1572872 | tf_op jit(solution)/shard_map/ppermute | solution.py:34
  40.7 3.4 %near_update.1 = (bf16[8,16,128,128]{3,2,1,0:T(8,128)(2,1)}, bf16[16,128,16]{2,1,0:T(8,128)(2,1)S(1)}, f32[16,16,128]{2,1,0:T(8,128)S(1)}, f32[2,16,16,128]{3,2,1,0:T(8,128)S(1)}) custom-call(s32[1]{0:T(128)} %bitcast.me_ref, s32[1,4,32]{2,1,0:T(4,128)S(1)} %copy-done.3, f32[16]{0:T(128)S(1)} %copy-done.6, ...), custom_call_target="tpu_custom_call" | custom-call | tf_op jit(solution)/shard_map/near_update/pallas_call | solution.py:582
  44.1 3.0 %collective-permute-start.18 = (bf16[16,2816]{1,0:T(8,128)(2,1)S(1)}, bf16[16,2816]{1,0:T(8,128)(2,1)S(1)}, u32[]{:S(2)}, u32[]{:S(2)}) collective-permute-start(bf16[16,2816]{1,0:T(8,128)(2,1)S(1)} %pad_maximum_fusion.1.refs_0_), channel_id=1, source_target_pairs={{0,8},{1,9},{2,10},{3,11},{4,12},{5,13},{6,14},{7,15},{8,0},{9,1},... | collective-permute-start | bytes 270344 | tf_op jit(solution)/shard_map/ppermute | solution.py:34
  47.1 0.7 %collective-permute-start.17 = (bf16[16,2816]{1,0:T(8,128)(2,1)S(1)}, bf16[16,2816]{1,0:T(8,128)(2,1)S(1)}, u32[]{:S(2)}, u32[]{:S(2)}) collective-permute-start(bf16[16,2816]{1,0:T(8,128)(2,1)S(1)} %pad_maximum_fusion.1.refs_0_), channel_id=1, source_target_pairs={{0,4},{1,5},{2,6},{3,7},{4,0},{5,1},{6,2},{7,3},{8,12},{9,13},{10,... | collective-permute-start | bytes 270344 | tf_op jit(solution)/shard_map/ppermute | solution.py:34
  47.8 0.6 collective-permute-start.19
  48.3 1.7 %collective-permute-done.18.refs_2_ = bf16[16,2816]{1,0:T(8,128)(2,1)S(1)} collective-permute-done((bf16[16,2816]{1,0:T(8,128)(2,1)S(1)}, bf16[16,2816]{1,0:T(8,128)(2,1)S(1)}, u32[]{:S(2)}, u32[]{:S(2)}) %collective-permute-start.18) | collective-permute-done | bytes 90144 | tf_op jit(solution)/shard_map/ppermute | solution.py:34
  50.0 5.2 %collective-permute-start.21 = (bf16[16,2816]{1,0:T(8,128)(2,1)S(1)}, bf16[16,2816]{1,0:T(8,128)(2,1)S(1)}, u32[]{:S(2)}, u32[]{:S(2)}) collective-permute-start(bf16[16,2816]{1,0:T(8,128)(2,1)S(1)} %pad_maximum_fusion.1.refs_0_), channel_id=1, source_target_pairs={{0,1},{1,0},{2,3},{3,2},{4,5},{5,4},{6,7},{7,6},{8,9},{9,8},{10,11... | collective-permute-start | bytes 270344 | tf_op jit(solution)/shard_map/ppermute | solution.py:34
  55.2 0.0 collective-permute-start.23
  55.2 0.5 collective-permute-start.22
  55.8 2.2 %far_update.1.refs_1_ = bf16[8,16,128,128]{3,2,1,0:T(8,128)(2,1)} custom-call(s32[1]{0:T(128)} %bitcast.me_ref, s32[1,4,32]{2,1,0:T(4,128)S(1)} %copy-done.3, bf16[16,128,16]{2,1,0:T(8,128)(2,1)S(1)} %get-tuple-element.60.turned_ref, f32[16,16,128]{2,1,0:T(8,128)S(1)} %get-tuple-element.61.values_ref, ...), custom_call_target="tpu_custom_call", output_to_operand_aliasing={{}: (7, {})} | custom-call | tf_op jit(solution)/shard_map/far_update/pallas_call | solution.py:598
  58.0 0.1 collective-permute-start.24
  58.1 1.2 %collective-permute-done.24.refs_7_ = bf16[16,2816]{1,0:T(8,128)(2,1)S(1)} collective-permute-done((bf16[16,2816]{1,0:T(8,128)(2,1)S(1)}, bf16[16,2816]{1,0:T(8,128)(2,1)S(1)}, u32[]{:S(2)}, u32[]{:S(2)}) %collective-permute-start.24) | collective-permute-done | bytes 90144 | tf_op jit(solution)/shard_map/ppermute | solution.py:34
  59.4 1.2 %output.1 = bf16[128,128]{1,0:T(8,128)(2,1)} custom-call(bf16[128,128]{1,0:T(8,128)(2,1)S(1)} %get-tuple-element.36.x_ref, bf16[2048,128]{1,0:T(8,128)(2,1)S(1)} %copy-done.1, bf16[128,176]{1,0:T(8,128)(2,1)S(1)} %get-tuple-element.37.pick_ref, bf16[16,2816]{1,0:T(8,128)(2,1)S(1)} %pad_maximum_fusion.1.refs_0_, ...), custom_call_target="tpu_custom_call" | custom-call | tf_op jit(solution)/shard_map/output/pallas_call | solution.py:622
  60.6 1.6 %last_update.1 = bf16[8,16,128,128]{3,2,1,0:T(8,128)(2,1)} custom-call(s32[1]{0:T(128)} %bitcast.me_ref, s32[1,4,32]{2,1,0:T(4,128)S(1)} %copy-done.3, bf16[16,128,16]{2,1,0:T(8,128)(2,1)S(1)} %get-tuple-element.60.turned_ref, f32[16,16,128]{2,1,0:T(8,128)S(1)} %get-tuple-element.61.values_ref, ...), custom_call_target="tpu_custom_call", output_to_operand_aliasing={{}: (6, {})} | custom-call | tf_op jit(solution)/shard_map/last_update/pallas_call | solution.py:598
  (41 shorter events, 0.2 us)
Async XLA Ops:
  0.6 6.1 %copy-start.2 = (s32[1,4,32]{2,1,0:T(4,128)S(1)}, s32[1,4,32]{2,1,0:T(4,128)}, u32[]{:S(2)}) copy-start(s32[1,4,32]{2,1,0:T(4,128)} %parent_ref.11) | copy-start | bytes 1540
  3.3 14.5 %collective-permute-start.4 = (bf16[1,16,128,128]{3,2,1,0:T(8,128)(2,1)S(1)}, bf16[1,16,128,128]{3,2,1,0:T(8,128)(2,1)S(1)}, u32[]{:S(2)}, u32[]{:S(2)}) collective-permute-start(bf16[1,16,128,128]{3,2,1,0:T(8,128)(2,1)S(1)} %get-tuple-element.40), channel_id=1, source_target_pairs={{0,2},{1,3},{2,0},{3,1},{4,6},{5,7},{6,4},{7,5},{8,10},{9,11},{10,... | collective-permute-start | bytes 1572872 | tf_op jit(solution)/shard_map/ppermute | solution.py:34
  5.5 3.8 %collective-permute-start = (bf16[128,128]{1,0:T(8,128)(2,1)S(1)}, bf16[128,128]{1,0:T(8,128)(2,1)S(1)}, u32[]{:S(2)}, u32[]{:S(2)}) collective-permute-start(bf16[128,128]{1,0:T(8,128)(2,1)S(1)} %get-tuple-element.36.x_ref), channel_id=1, source_target_pairs={{0,6},{1,7},{2,4},{3,5},{4,2},{5,3},{6,0},{7,1},{8,14},{9,15},{10,... | collective-permute-start | bytes 98312 | tf_op jit(solution)/shard_map/ppermute | solution.py:34
  6.8 15.2 %copy-start = (bf16[2048,3,128]{2,0,1:T(8,128)(2,1)S(1)}, bf16[2048,3,128]{2,0,1:T(8,128)(2,1)}, u32[]{:S(2)}) copy-start(bf16[2048,3,128]{2,0,1:T(8,128)(2,1)} %param.13) | copy-start | bytes 4718596
  9.2 6.7 %collective-permute-start.3 = (bf16[256,128]{1,0:T(8,128)(2,1)S(1)}, bf16[256,128]{1,0:T(8,128)(2,1)S(1)}, u32[]{:S(2)}, u32[]{:S(2)}) collective-permute-start(bf16[256,128]{1,0:T(8,128)(2,1)S(1)} %pad_maximum_fusion.2.refs_0_), channel_id=1, source_target_pairs={{0,12},{1,13},{2,14},{3,15},{4,8},{5,9},{6,10},{7,11},{8,4},{9,5},... | collective-permute-start | bytes 196616 | tf_op jit(solution)/shard_map/ppermute | solution.py:34
  12.6 5.2 %collective-permute-start.2 = (bf16[256,128]{1,0:T(8,128)(2,1)S(1)}, bf16[256,128]{1,0:T(8,128)(2,1)S(1)}, u32[]{:S(2)}, u32[]{:S(2)}) collective-permute-start(bf16[256,128]{1,0:T(8,128)(2,1)S(1)} %pad_maximum_fusion.2.refs_0_), channel_id=1, source_target_pairs={{0,8},{1,9},{2,10},{3,11},{4,12},{5,13},{6,14},{7,15},{8,0},{9,1},... | collective-permute-start | bytes 196616 | tf_op jit(solution)/shard_map/ppermute | solution.py:34
  12.6 5.2 %collective-permute-start.1 = (bf16[256,128]{1,0:T(8,128)(2,1)S(1)}, bf16[256,128]{1,0:T(8,128)(2,1)S(1)}, u32[]{:S(2)}, u32[]{:S(2)}) collective-permute-start(bf16[256,128]{1,0:T(8,128)(2,1)S(1)} %pad_maximum_fusion.2.refs_0_), channel_id=1, source_target_pairs={{0,4},{1,5},{2,6},{3,7},{4,0},{5,1},{6,2},{7,3},{8,12},{9,13},{10,... | collective-permute-start | bytes 196616 | tf_op jit(solution)/shard_map/ppermute | solution.py:34
  17.8 3.6 %collective-permute-start.5 = (bf16[256,128]{1,0:T(8,128)(2,1)S(1)}, bf16[256,128]{1,0:T(8,128)(2,1)S(1)}, u32[]{:S(2)}, u32[]{:S(2)}) collective-permute-start(bf16[256,128]{1,0:T(8,128)(2,1)S(1)} %pad_maximum_fusion.2.refs_0_), channel_id=1, source_target_pairs={{0,1},{1,0},{2,3},{3,2},{4,5},{5,4},{6,7},{7,6},{8,9},{9,8},{10,11... | collective-permute-start | bytes 196616 | tf_op jit(solution)/shard_map/ppermute | solution.py:34
  20.2 1.3 %collective-permute-start.6 = (bf16[256,128]{1,0:T(8,128)(2,1)S(1)}, bf16[256,128]{1,0:T(8,128)(2,1)S(1)}, u32[]{:S(2)}, u32[]{:S(2)}) collective-permute-start(bf16[256,128]{1,0:T(8,128)(2,1)S(1)} %collective-permute-done.1.refs_1_), channel_id=1, source_target_pairs={{0,1},{1,0},{2,3},{3,2},{4,5},{5,4},{6,7},{7,6},{8,9},{9,8},{10,11... | collective-permute-start | bytes 196616 | tf_op jit(solution)/shard_map/ppermute | solution.py:34
  20.3 1.7 %collective-permute-start.7 = (bf16[256,128]{1,0:T(8,128)(2,1)S(1)}, bf16[256,128]{1,0:T(8,128)(2,1)S(1)}, u32[]{:S(2)}, u32[]{:S(2)}) collective-permute-start(bf16[256,128]{1,0:T(8,128)(2,1)S(1)} %collective-permute-done.2.refs_2_), channel_id=1, source_target_pairs={{0,1},{1,0},{2,3},{3,2},{4,5},{5,4},{6,7},{7,6},{8,9},{9,8},{10,11... | collective-permute-start | bytes 196616 | tf_op jit(solution)/shard_map/ppermute | solution.py:34
  20.7 1.3 %collective-permute-start.8 = (bf16[256,128]{1,0:T(8,128)(2,1)S(1)}, bf16[256,128]{1,0:T(8,128)(2,1)S(1)}, u32[]{:S(2)}, u32[]{:S(2)}) collective-permute-start(bf16[256,128]{1,0:T(8,128)(2,1)S(1)} %collective-permute-done.3.refs_3_), channel_id=1, source_target_pairs={{0,1},{1,0},{2,3},{3,2},{4,5},{5,4},{6,7},{7,6},{8,9},{9,8},{10,11... | collective-permute-start | bytes 196616 | tf_op jit(solution)/shard_map/ppermute | solution.py:34
  20.8 34.5 %collective-permute-start.20 = (bf16[2,16,128,128]{3,2,1,0:T(8,128)(2,1)S(1)}, bf16[2,16,128,128]{3,2,1,0:T(8,128)(2,1)S(1)}, u32[]{:S(2)}, u32[]{:S(2)}) collective-permute-start(bf16[2,16,128,128]{3,2,1,0:T(8,128)(2,1)S(1)} %get-tuple-element.63), channel_id=1, source_target_pairs={{0,3},{1,2},{2,1},{3,0},{4,7},{5,6},{6,5},{7,4},{8,11},{9,10},{10,... | collective-permute-start | bytes 3145736 | tf_op jit(solution)/shard_map/ppermute | solution.py:34
  21.4 8.0 %collective-permute-start.11 = (bf16[1,16,128,128]{3,2,1,0:T(8,128)(2,1)}, bf16[1,16,128,128]{3,2,1,0:T(8,128)(2,1)S(1)}, u32[]{:S(2)}, u32[]{:S(2)}) collective-permute-start(bf16[1,16,128,128]{3,2,1,0:T(8,128)(2,1)} %get-tuple-element.49), channel_id=1, source_target_pairs={{0,1},{1,0},{2,3},{3,2},{4,5},{5,4},{6,7},{7,6},{8,9},{9,8},{10,11... | collective-permute-start | bytes 1572872 | tf_op jit(solution)/shard_map/ppermute | solution.py:34
  21.5 8.0 %collective-permute-start.12 = (bf16[1,16,128,128]{3,2,1,0:T(8,128)(2,1)}, bf16[1,16,128,128]{3,2,1,0:T(8,128)(2,1)S(1)}, u32[]{:S(2)}, u32[]{:S(2)}) collective-permute-start(bf16[1,16,128,128]{3,2,1,0:T(8,128)(2,1)} %get-tuple-element.50), channel_id=1, source_target_pairs={{0,1},{1,0},{2,3},{3,2},{4,5},{5,4},{6,7},{7,6},{8,9},{9,8},{10,11... | collective-permute-start | bytes 1572872 | tf_op jit(solution)/shard_map/ppermute | solution.py:34
  23.1 1.3 %collective-permute-start.9 = (bf16[1,2,4,40,128]{4,3,1,0,2:T(8,128)(2,1)S(1)}, bf16[1,2,4,40,128]{4,3,1,0,2:T(8,128)(2,1)S(1)}, u32[]{:S(2)}, u32[]{:S(2)}) collective-permute-start(bf16[1,2,4,40,128]{4,3,1,0,2:T(8,128)(2,1)S(1)} %copy.13), channel_id=1, source_target_pairs={{0,1},{1,0},{2,3},{3,2},{4,5},{5,4},{6,7},{7,6},{8,9},{9,8},{10,11... | collective-permute-start | bytes 245768 | tf_op jit(solution)/shard_map/ppermute | solution.py:34
  24.5 4.9 %collective-permute-start.10 = (bf16[2,1,4,40,128]{4,3,1,0,2:T(8,128)(2,1)S(1)}, bf16[2,1,4,40,128]{4,3,1,0,2:T(8,128)(2,1)S(1)}, u32[]{:S(2)}, u32[]{:S(2)}) collective-permute-start(bf16[2,1,4,40,128]{4,3,1,0,2:T(8,128)(2,1)S(1)} %get-tuple-element.75), channel_id=1, source_target_pairs={{0,6},{1,7},{2,4},{3,5},{4,2},{5,3},{6,0},{7,1},{8,14},{9,15},{10,... | collective-permute-start | bytes 245768 | tf_op jit(solution)/shard_map/ppermute | solution.py:34
  29.4 6.0 %collective-permute-start.15 = (bf16[2,2,1,40,128]{4,3,1,0,2:T(8,128)(2,1)S(1)}, bf16[2,2,1,40,128]{4,3,1,0,2:T(8,128)(2,1)S(1)}, u32[]{:S(2)}, u32[]{:S(2)}) collective-permute-start(bf16[2,2,1,40,128]{4,3,1,0,2:T(8,128)(2,1)S(1)} %get-tuple-element.70), channel_id=1, source_target_pairs={{0,12},{1,13},{2,14},{3,15},{4,8},{5,9},{6,10},{7,11},{8,4},{9,5},... | collective-permute-start | bytes 122888 | tf_op jit(solution)/shard_map/ppermute | solution.py:34
  32.8 3.8 %collective-permute-start.14 = (bf16[2,2,1,40,128]{4,3,1,0,2:T(8,128)(2,1)S(1)}, bf16[2,2,1,40,128]{4,3,1,0,2:T(8,128)(2,1)S(1)}, u32[]{:S(2)}, u32[]{:S(2)}) collective-permute-start(bf16[2,2,1,40,128]{4,3,1,0,2:T(8,128)(2,1)S(1)} %get-tuple-element.71), channel_id=1, source_target_pairs={{0,8},{1,9},{2,10},{3,11},{4,12},{5,13},{6,14},{7,15},{8,0},{9,1},... | collective-permute-start | bytes 122888 | tf_op jit(solution)/shard_map/ppermute | solution.py:34
  32.8 3.8 %copy-start.4 = (f32[16,128]{1,0:T(8,128)S(1)}, f32[16,128]{1,0:T(8,128)}, u32[]{:S(2)}) copy-start(f32[16,128]{1,0:T(8,128)} %gate_ref.3) | copy-start | bytes 24580
  32.8 3.8 %copy-start.5 = (f32[2048]{0:T(1024)S(1)}, f32[2048]{0:T(1024)}, u32[]{:S(2)}) copy-start(f32[2048]{0:T(1024)} %param.16) | copy-start | bytes 24580
  32.8 3.8 %copy-start.6 = (f32[16]{0:T(128)S(1)}, f32[16]{0:T(128)}, u32[]{:S(2)}) copy-start(f32[16]{0:T(128)} %bias_ref.3) | copy-start | bytes 196
  32.8 3.7 %collective-permute-start.13 = (bf16[2,2,1,40,128]{4,3,1,0,2:T(8,128)(2,1)S(1)}, bf16[2,2,1,40,128]{4,3,1,0,2:T(8,128)(2,1)S(1)}, u32[]{:S(2)}, u32[]{:S(2)}) collective-permute-start(bf16[2,2,1,40,128]{4,3,1,0,2:T(8,128)(2,1)S(1)} %get-tuple-element.72), channel_id=1, source_target_pairs={{0,4},{1,5},{2,6},{3,7},{4,0},{5,1},{6,2},{7,3},{8,12},{9,13},{10,... | collective-permute-start | bytes 122888 | tf_op jit(solution)/shard_map/ppermute | solution.py:34
  35.4 4.4 %copy-start.7 = (bf16[1,16,128,128]{3,2,1,0:T(8,128)(2,1)S(1)}, bf16[1,16,128,128]{3,2,1,0:T(8,128)(2,1)}, u32[]{:S(2)}) copy-start(bf16[1,16,128,128]{3,2,1,0:T(8,128)(2,1)} %get-tuple-element.66) | copy-start | bytes 1572868
  35.4 5.2 %copy-start.3 = (s32[1,4,32]{2,1,0:T(4,128)S(1)}, s32[1,4,32]{2,1,0:T(4,128)}, u32[]{:S(2)}) copy-start(s32[1,4,32]{2,1,0:T(4,128)} %parent_ref.11) | copy-start | bytes 1540
  39.2 4.9 %collective-permute-start.16 = (bf16[8,2816]{1,0:T(8,128)(2,1)S(1)}, bf16[8,2816]{1,0:T(8,128)(2,1)S(1)}, u32[]{:S(2)}, u32[]{:S(2)}) collective-permute-start(bf16[8,2816]{1,0:T(8,128)(2,1)S(1)} %get-tuple-element.55), channel_id=1, source_target_pairs={{0,6},{1,7},{2,4},{3,5},{4,2},{5,3},{6,0},{7,1},{8,14},{9,15},{10,... | collective-permute-start | bytes 135176 | tf_op jit(solution)/shard_map/ppermute | solution.py:34
  39.8 20.8 %collective-permute-start.25 = (bf16[1,16,128,128]{3,2,1,0:T(8,128)(2,1)S(1)}, bf16[1,16,128,128]{3,2,1,0:T(8,128)(2,1)S(1)}, u32[]{:S(2)}, u32[]{:S(2)}) collective-permute-start(bf16[1,16,128,128]{3,2,1,0:T(8,128)(2,1)S(1)} %copy-done.7), channel_id=1, source_target_pairs={{0,2},{1,3},{2,0},{3,1},{4,6},{5,7},{6,4},{7,5},{8,10},{9,11},{10,... | collective-permute-start | bytes 1572872 | tf_op jit(solution)/shard_map/ppermute | solution.py:34
  44.1 5.9 %collective-permute-start.18 = (bf16[16,2816]{1,0:T(8,128)(2,1)S(1)}, bf16[16,2816]{1,0:T(8,128)(2,1)S(1)}, u32[]{:S(2)}, u32[]{:S(2)}) collective-permute-start(bf16[16,2816]{1,0:T(8,128)(2,1)S(1)} %pad_maximum_fusion.1.refs_0_), channel_id=1, source_target_pairs={{0,8},{1,9},{2,10},{3,11},{4,12},{5,13},{6,14},{7,15},{8,0},{9,1},... | collective-permute-start | bytes 270344 | tf_op jit(solution)/shard_map/ppermute | solution.py:34
  47.1 8.2 %collective-permute-start.17 = (bf16[16,2816]{1,0:T(8,128)(2,1)S(1)}, bf16[16,2816]{1,0:T(8,128)(2,1)S(1)}, u32[]{:S(2)}, u32[]{:S(2)}) collective-permute-start(bf16[16,2816]{1,0:T(8,128)(2,1)S(1)} %pad_maximum_fusion.1.refs_0_), channel_id=1, source_target_pairs={{0,4},{1,5},{2,6},{3,7},{4,0},{5,1},{6,2},{7,3},{8,12},{9,13},{10,... | collective-permute-start | bytes 270344 | tf_op jit(solution)/shard_map/ppermute | solution.py:34
  47.8 10.2 %collective-permute-start.19 = (bf16[16,2816]{1,0:T(8,128)(2,1)S(1)}, bf16[16,2816]{1,0:T(8,128)(2,1)S(1)}, u32[]{:S(2)}, u32[]{:S(2)}) collective-permute-start(bf16[16,2816]{1,0:T(8,128)(2,1)S(1)} %pad_maximum_fusion.1.refs_0_), channel_id=1, source_target_pairs={{0,12},{1,13},{2,14},{3,15},{4,8},{5,9},{6,10},{7,11},{8,4},{9,5},... | collective-permute-start | bytes 270344 | tf_op jit(solution)/shard_map/ppermute | solution.py:34
  50.0 8.1 %collective-permute-start.21 = (bf16[16,2816]{1,0:T(8,128)(2,1)S(1)}, bf16[16,2816]{1,0:T(8,128)(2,1)S(1)}, u32[]{:S(2)}, u32[]{:S(2)}) collective-permute-start(bf16[16,2816]{1,0:T(8,128)(2,1)S(1)} %pad_maximum_fusion.1.refs_0_), channel_id=1, source_target_pairs={{0,1},{1,0},{2,3},{3,2},{4,5},{5,4},{6,7},{7,6},{8,9},{9,8},{10,11... | collective-permute-start | bytes 270344 | tf_op jit(solution)/shard_map/ppermute | solution.py:34
  55.2 2.9 %collective-permute-start.23 = (bf16[16,2816]{1,0:T(8,128)(2,1)S(1)}, bf16[16,2816]{1,0:T(8,128)(2,1)S(1)}, u32[]{:S(2)}, u32[]{:S(2)}) collective-permute-start(bf16[16,2816]{1,0:T(8,128)(2,1)S(1)} %collective-permute-done.18.refs_2_), channel_id=1, source_target_pairs={{0,1},{1,0},{2,3},{3,2},{4,5},{5,4},{6,7},{7,6},{8,9},{9,8},{10,11... | collective-permute-start | bytes 270344 | tf_op jit(solution)/shard_map/ppermute | solution.py:34
  55.2 2.9 %collective-permute-start.22 = (bf16[16,2816]{1,0:T(8,128)(2,1)S(1)}, bf16[16,2816]{1,0:T(8,128)(2,1)S(1)}, u32[]{:S(2)}, u32[]{:S(2)}) collective-permute-start(bf16[16,2816]{1,0:T(8,128)(2,1)S(1)} %collective-permute-done.17.refs_1_), channel_id=1, source_target_pairs={{0,1},{1,0},{2,3},{3,2},{4,5},{5,4},{6,7},{7,6},{8,9},{9,8},{10,11... | collective-permute-start | bytes 270344 | tf_op jit(solution)/shard_map/ppermute | solution.py:34
  55.8 3.6 %copy-start.1 = (bf16[2048,128]{1,0:T(8,128)(2,1)S(1)}, bf16[2048,128]{1,0:T(8,128)(2,1)}, u32[]{:S(2)}) copy-start(bf16[2048,128]{1,0:T(8,128)(2,1)} %weight_ref.1) | copy-start | bytes 1572868
  58.0 1.4 %collective-permute-start.24 = (bf16[16,2816]{1,0:T(8,128)(2,1)S(1)}, bf16[16,2816]{1,0:T(8,128)(2,1)S(1)}, u32[]{:S(2)}, u32[]{:S(2)}) collective-permute-start(bf16[16,2816]{1,0:T(8,128)(2,1)S(1)} %collective-permute-done.19.refs_3_), channel_id=1, source_target_pairs={{0,1},{1,0},{2,3},{3,2},{4,5},{5,4},{6,7},{7,6},{8,9},{9,8},{10,11... | collective-permute-start | bytes 270344 | tf_op jit(solution)/shard_map/ppermute | solution.py:34

commit v6 on v5

--- a/solution.py
+++ b/solution.py
@@ -142,13 +142,10 @@
 
 
 def fetch_kernel(
-    blocks, me_ref, parent_ref, token_ref, tokens_ref, table_ref, states_ref, x_ref, first_ref, rows_ref, row_sem, state_sem
+    blocks, me_ref, parent_ref, token_ref, tokens_ref, table_ref, states_ref, x_ref, y_ref, rows_ref, row_sem, state_sem
 ):
-    count, own_rows = token_ref.shape[1], states_ref.shape[0]
+    count, own_rows, heads = token_ref.shape[1], states_ref.shape[0], states_ref.shape[1]
     user, member = split(me_ref[0], blocks)
-    _, chosen = matching_children(parent_ref, user, member ^ 2, member, own_rows, 0)
-    state_copy = pltpu.make_async_copy(states_ref.at[chosen[0]], first_ref.at[0], state_sem)
-    state_copy.start()
 
     def start_row(r, carry):
         first = pl.multiple_of(split(token_ref[0, r], TILE)[0] * TILE, TILE)
@@ -160,6 +157,13 @@
         return carry
 
     lax.fori_loop(0, count, start_row, 0, unroll=8)
+    copies = []
+    wanted = matching_children(parent_ref, user, member ^ 2, member, own_rows, 0)[1]
+    extra = y_ref.shape[0] - heads
+    for part, (row, first, size) in enumerate(((wanted[0], 0, heads // 2), (wanted[0], heads // 2, heads // 2), (wanted[1], 0, extra))):
+        span, target = pl.ds(first, size), y_ref.at[pl.ds(part * (heads // 2), size)]
+        copies.append(pltpu.make_async_copy(states_ref.at[row, span], target, state_sem.at[part]))
+        copies[-1].start()
     step = math.gcd(count, 128)
     picks = []
     for first in range(0, count, step):
@@ -171,7 +175,8 @@
         x_ref[first : first + step, :] = jnp.dot(
             pick, rows_ref[first * TILE : (first + step) * TILE, :], preferred_element_type=jnp.float32
         ).astype(jnp.bfloat16)
-    state_copy.wait()
+    for copy in copies:
+        copy.wait()
 
 
 def pick_kernel(blocks, piece, send_order, me_ref, parent_ref, parents_ref, states_ref, pick_ref, corner_ref, sem):
@@ -200,10 +205,12 @@
     user, member = split(me, blocks)
     wanted = matching_children(parent_ref, user, member ^ 1, member, own_rows, 0)[1]
     wanted += matching_children(parent_ref, user, member ^ 2, member, own_rows, 0)[1][1:]
+    heads = states_ref.shape[1]
     loads, saves = [], []
     for place, (row, out) in enumerate(zip(wanted, outs)):
-        loads.append(pltpu.make_async_copy(states_ref.at[row], hold_ref.at[place], in_sem.at[place]))
-        saves.append(pltpu.make_async_copy(hold_ref.at[place], out.at[0], out_sem.at[place]))
+        span, kept = pl.ds(heads - out.shape[0], out.shape[0]), pl.ds(0, out.shape[0])
+        loads.append(pltpu.make_async_copy(states_ref.at[row, span], hold_ref.at[place, kept], in_sem.at[place]))
+        saves.append(pltpu.make_async_copy(hold_ref.at[place, kept], out, out_sem.at[place]))
         loads[-1].start()
     device, child, away, rank, parent_place = row_facts(parents_ref[...], blocks, own_rows)
     is_far, number = far_number(away, rank)
@@ -278,7 +285,7 @@
             recv_ref[within * len(parts) + number] = part[within]
     place = place_ref[:, 0:1]
     joint = math.gcd(block, 2)
-    states = sum(ref.shape[0] for ref in sources)
+    states = sum(ref.shape[0] if len(ref.shape) == 4 else 1 for ref in sources)
 
     def work(step, carry):
         for group in range(0, block, joint):
@@ -292,7 +299,11 @@
             ]
             priors = []
             for n in range(joint):
-                one = [ref[:, pl.ds(first_head + n, 1)].reshape(ref.shape[0] * size, size) for ref in sources]
+                head = first_head + n
+                one = [
+                    ref[:, pl.ds(head, 1)].reshape(ref.shape[0] * size, size) if len(ref.shape) == 4 else ref[head]
+                    for ref in sources
+                ]
                 priors.append(jnp.concatenate(one, 0))
             product = jnp.dot(
                 jnp.concatenate(spread, 0), jnp.concatenate(priors, 1), preferred_element_type=jnp.float32
@@ -392,7 +403,7 @@
 
             @pl.when((away == 1) & (found == rank))
             def _():
-                update(row, lambda head: ref[0, head])
+                update(row, lambda head: ref[head])
 
         return found + (away == 1).astype(jnp.int32)
 
@@ -410,38 +421,37 @@
 
 def far_update_kernel(block, blocks, own_rows, entries, me_ref, parent_ref, turned_ref, values_ref, terms_ref, *refs):
     gots, (_, out_ref, new_ref, out_sem) = refs[:-4], refs[-4:]
-    heads, size = gots[0].shape[1], gots[0].shape[2]
     user, member = split(me_ref[0], blocks)
     children = [
-        matching_children(parent_ref, user, member, member ^ partner, own_rows, -1)[0][rank] for _, _, partner, rank in entries
+        matching_children(parent_ref, user, member, member ^ partner, own_rows, -1)[0][rank] for partner, rank, *_ in entries
     ]
-    line = lax.broadcasted_iota(jnp.int32, (values_ref.shape[1], size), 0)
-
-    def save(entry, step):
-        span = pl.ds(step * block, block)
-        target = out_ref.at[jnp.maximum(children[entry], 0), span]
-        return pltpu.make_async_copy(new_ref.at[entry, span], target, out_sem.at[entry, step])
-
-    for entry, (array, within, _, _) in enumerate(entries):
+    line = lax.broadcasted_iota(jnp.int32, values_ref.shape[1:], 0)
+
+    def save(entry, head):
+        target = out_ref.at[jnp.maximum(children[entry], 0), pl.ds(head, block)]
+        return pltpu.make_async_copy(new_ref.at[entry, pl.ds(head, block)], target, out_sem.at[entry, head // block])
+
+    for entry, (_, _, array, start, heads) in enumerate(entries):
         got_ref, child = gots[array], children[entry]
 
         @pl.when(child >= 0)
         def _():
-            for step in range(heads // block):
-                for head in range(step * block, (step + 1) * block):
-                    value = jnp.where(line == child, values_ref[head], 0.0).astype(jnp.bfloat16)
-                    outer = jnp.dot(turned_ref[head], value, preferred_element_type=jnp.float32)
-                    fresh = terms_ref[0, head, pl.ds(child, 1), :] * got_ref[within, head].astype(jnp.float32)
-                    fresh = fresh + terms_ref[1, head, pl.ds(child, 1), :] * outer
-                    new_ref[entry, head] = fresh.astype(jnp.bfloat16)
-                save(entry, step).start()
-
-    for entry in range(len(entries)):
+            for head in heads:
+                value = jnp.where(line == child, values_ref[head], 0.0).astype(jnp.bfloat16)
+                outer = jnp.dot(turned_ref[head], value, preferred_element_type=jnp.float32)
+                prior = got_ref[start + head - heads[0]].astype(jnp.float32)
+                fresh = terms_ref[0, head, pl.ds(child, 1), :] * prior
+                fresh = fresh + terms_ref[1, head, pl.ds(child, 1), :] * outer
+                new_ref[entry, head] = fresh.astype(jnp.bfloat16)
+                if (head + 1) % block == 0:
+                    save(entry, head + 1 - block).start()
+
+    for entry, (_, _, _, _, heads) in enumerate(entries):
 
         @pl.when(children[entry] >= 0)
         def _():
-            for step in range(heads // block):
-                save(entry, step).wait()
+            for head in heads[::block]:
+                save(entry, head).wait()
 
 
 def per_device(
@@ -468,22 +478,23 @@
     steps = exchange_plan(plan)
     recv_order, normed_order = plan_order(steps), gather_order(plan)
     slots, piece = 2 * own_rows, 5 * own_rows
-    one_state, two_states = (1, heads, size, size), (CAP, heads, size, size)
+    one_state, two_states = (heads, size, size), (CAP, heads, size, size)
     normed_columns = width + FARS * width // own_rows
     bf16, int32 = jnp.bfloat16, jnp.int32
     mine = me[None]
     parent_row = jnp.broadcast_to(parents.reshape(1, row_total), (8, row_total))
     head_block = math.gcd(heads, 4)
+    extra = heads // 4
 
     local_columns, first_out = pl.pallas_call(
         functools.partial(fetch_kernel, blocks),
         in_specs=[SCALARS, SCALARS, SCALARS, WHOLE, PLACED, PLACED],
         out_specs=[WHOLE] * 2,
-        out_shape=[pltpu.VMEM((row_total, columns), bf16), pltpu.VMEM(one_state, bf16)],
+        out_shape=[pltpu.VMEM((row_total, columns), bf16), pltpu.VMEM((heads + extra, size, size), bf16)],
         scratch_shapes=[
             pltpu.VMEM((row_total * TILE, columns), bf16),
             pltpu.SemaphoreType.DMA,
-            pltpu.SemaphoreType.DMA,
+            pltpu.SemaphoreType.DMA((3,)),
         ],
         compiler_params=params(),
         name="fetch",
@@ -505,7 +516,8 @@
         functools.partial(stage_kernel, blocks, normed_order),
         in_specs=[SCALARS, SCALARS, WHOLE, PLACED],
         out_specs=[PLACED] * (CAP + 1) + [WHOLE] * 2,
-        out_shape=[pltpu.HBM(one_state, bf16)] * (CAP + 1)
+        out_shape=[pltpu.HBM(one_state, bf16)] * CAP
+        + [pltpu.HBM((heads - extra, size, size), bf16)]
         + [
             jax.ShapeDtypeStruct((slots, 128), jnp.float32),
             jax.ShapeDtypeStruct((row_total, row_total + FARS * count), bf16),
@@ -538,7 +550,9 @@
         if stage == 0:
             *parts, tied["weight"], tied["pick"] = lax.optimization_barrier((*parts, weight, send_pick))
         if stage == 1:
-            *parts, tied["first"], tied["place"] = lax.optimization_barrier((*parts, first_got, place))
+            *parts, tied["place"] = lax.optimization_barrier((*parts, place))
+        if stage == len(plan) - 1:
+            *parts, tied["first"] = lax.optimization_barrier((*parts, first_got))
         return parts
 
     every_input = gather_all(local_columns, plan, in_inputs)
@@ -594,15 +608,17 @@
         name="near_update",
     )(mine, parents, gate_bias, by_head, gate_weight, held, *near_gots)
 
+    far_block = math.gcd(extra, 4)
+
     def far_update(before, gots, entries, name):
         return pl.pallas_call(
-            functools.partial(far_update_kernel, head_block, blocks, own_rows, entries),
+            functools.partial(far_update_kernel, far_block, blocks, own_rows, entries),
             in_specs=[SCALARS] * 2 + [WHOLE] * (3 + len(gots)) + [PLACED],
             out_specs=PLACED,
             out_shape=jax.ShapeDtypeStruct(states.shape, bf16),
             scratch_shapes=[
-                pltpu.VMEM((len(entries),) + one_state[1:], bf16),
-                pltpu.SemaphoreType.DMA((len(entries), heads // head_block)),
+                pltpu.VMEM((len(entries),) + one_state, bf16),
+                pltpu.SemaphoreType.DMA((len(entries), heads // far_block)),
             ],
             input_output_aliases={5 + len(gots): 0},
             compiler_params=params(),
@@ -613,9 +629,12 @@
         if stage == 0:
             *parts, tied["rows"], tied["turned"] = lax.optimization_barrier((*parts, near_done, turned))
         if stage == 1:
-            entries = [(0, 0, 2, 0)] + [(1, rank, 3, rank) for rank in range(CAP)]
-            far_done = far_update(tied["rows"], [tied["first"], corner_got], entries, "far_update")
-            parts[-1], tied["done"] = lax.optimization_barrier((parts[-1], far_done))
+            every = range(heads)
+            entries = [(2, 0, 0, 0, every), (2, 1, 0, heads, every[:extra])]
+            entries += [(3, rank, 1, rank * heads, every) for rank in range(CAP)]
+            gots = [tied["first"], corner_got.reshape(CAP * heads, size, size)]
+            far_done = far_update(tied["rows"], gots, entries, "far_update")
+            *parts, tied["done"] = lax.optimization_barrier((*parts, far_done))
         return parts
 
     every_normed = gather_all(normed, plan, in_normed)
@@ -629,7 +648,7 @@
         name="output",
     )(local_columns, out_weight, out_pick, *every_normed)
     layer_out, last_got = lax.optimization_barrier((layer_out, last_got))
-    final = far_update(tied["done"], [last_got], [(0, 0, 2, 1)], "last_update")
+    final = far_update(tied["done"], [last_got], [(2, 1, 0, 0, range(extra, heads))], "last_update")
     return (layer_out[None], final)
 
 

time: 61.9 us -> 60.7 us (0.981); the launches traced: 62.2 us -> 60.1 us
  starting transfers between devices: 28.1 us -> 25.9 us
  waiting for transfers between devices: 10.9 us -> 11.7 us
    ppermute x26, starting transfers between devices: 28.1 us -> 25.9 us  [xor_permute(): lax.ppermute(block, 'rows', [(i, i ^ distance) for i in range(count)])]
    pallas_call x2, Pallas kernels: 3.82 us -> 2.38 us  [far_update(): pl.pallas_call(functools.partial(far_update_kernel, far_block, blocks, ow...]
    pallas_call x1, Pallas kernels: 3.43 us -> 4.23 us  [per_device(): pl.pallas_call(functools.partial(near_update_kernel, recv_order, head_blo...]
    ppermute x26, waiting for transfers between devices: 10.9 us -> 11.7 us  [xor_permute(): lax.ppermute(block, 'rows', [(i, i ^ distance) for i in range(count)])]
  transfers between devices with their start and end apart: 26 -> 26, of which waited for: 7 -> 12; matrix products, arithmetic and copies ran while one was open for 0% -> 0% of each run, Pallas kernels for 29% -> 30%
where the time goes in v6:
time: 60.7 us; the launch traced here: 60.1 us
  starting transfers between devices  25.9 us (43%)
  Pallas kernels  21.4 us (35%)
  waiting for transfers between devices  11.7 us (19%)
  between operations  0.87 us (1%)
    ppermute x26, starting transfers between devices, xor_permute(): lax.ppermute(block, 'rows', [(i, i ^ distance) for i in range(count)])  25.9 us
    ppermute x26, waiting for transfers between devices, xor_permute(): lax.ppermute(block, 'rows', [(i, i ^ distance) for i in range(count)])  11.7 us
    pallas_call x1, Pallas kernels, per_device(): pl.pallas_call(functools.partial(near_update_kernel, recv_order, head_blo...  4.23 us
    pallas_call x1, Pallas kernels, per_device(): pl.pallas_call(functools.partial(stage_kernel, blocks, normed_order), in_...  2.93 us
    pallas_call x1, Pallas kernels, per_device(): pl.pallas_call(functools.partial(fetch_kernel, blocks), in_specs=[SCALARS...  2.71 us
    pallas_call x1, Pallas kernels, per_device(): pl.pallas_call(functools.partial(readout_kernel, recv_order, head_block,...  2.55 us
    pallas_call x2, Pallas kernels, far_update(): pl.pallas_call(functools.partial(far_update_kernel, far_block, blocks, ow...  2.38 us
    pallas_call x1, Pallas kernels, per_device(): pl.pallas_call(hold_kernel, in_specs=[PLACED], out_specs=WHOLE, out_shape...  2.21 us
  transfers between devices with their start and end apart: 26, of which 12 were waited for; matrix products, arithmetic and copies ran while one was open for 0% of the time, Pallas kernels for 30%

profile of v6, /device:TPU:1, one launch (start us, length us, event | category | flops | bytes accessed | tf_op | source)
XLA Modules:
  0.0 60.1 jit_solution(14095418129481402863)
XLA Ops:
  0.6 0.0 copy-start.2
  0.6 2.7 %fetch.1 = (bf16[128,128]{1,0:T(8,128)(2,1)S(1)}, bf16[20,128,128]{2,1,0:T(8,128)(2,1)S(1)}) custom-call(s32[1]{0:T(128)} %bitcast.me_ref, s32[1,4,32]{2,1,0:T(4,128)} %parent_ref.11, s32[1,128]{1,0:T(1,128)} %tokens_ref.1, s32[1,128]{1,0:T(1,128)} %tokens_ref.1, bf16[32768,128]{1,0:T(8,128)(2,1)} %table_ref.1, bf16[8,16,128,128]{3,2,1,0:T(8,128)(2,1)} %states_ref.7), custom_call_target="tpu_custom_call" | custom-call | tf_op jit(solution)/shard_map/fetch/pallas_call | solution.py:489
  3.4 2.1 %collective-permute-start.8 = (bf16[20,128,128]{2,1,0:T(8,128)(2,1)S(1)}, bf16[20,128,128]{2,1,0:T(8,128)(2,1)S(1)}, u32[]{:S(2)}, u32[]{:S(2)}) collective-permute-start(bf16[20,128,128]{2,1,0:T(8,128)(2,1)S(1)} %get-tuple-element.59), channel_id=1, source_target_pairs={{0,2},{1,3},{2,0},{3,1},{4,6},{5,7},{6,4},{7,5},{8,10},{9,11},{10,... | collective-permute-start | bytes 1966088 | tf_op jit(solution)/shard_map/ppermute | solution.py:34
  5.5 1.2 %collective-permute-start = (bf16[128,128]{1,0:T(8,128)(2,1)S(1)}, bf16[128,128]{1,0:T(8,128)(2,1)S(1)}, u32[]{:S(2)}, u32[]{:S(2)}) collective-permute-start(bf16[128,128]{1,0:T(8,128)(2,1)S(1)} %get-tuple-element.47.x_ref), channel_id=1, source_target_pairs={{0,6},{1,7},{2,4},{3,5},{4,2},{5,3},{6,0},{7,1},{8,14},{9,15},{10,... | collective-permute-start | bytes 98312 | tf_op jit(solution)/shard_map/ppermute | solution.py:34
  6.7 0.1 broadcast_in_dim.14
  6.8 2.1 %pick.1 = (bf16[640,384]{1,0:T(8,128)(2,1)S(1)}, bf16[2,16,128,128]{3,2,1,0:T(8,128)(2,1)S(1)}) custom-call(s32[1]{0:T(128)} %bitcast.me_ref, s32[1,4,32]{2,1,0:T(4,128)} %parent_ref.11, s32[8,128]{1,0:T(8,128)S(1)} %broadcast_in_dim.15.parents_ref, bf16[8,16,128,128]{3,2,1,0:T(8,128)(2,1)} %states_ref.7), custom_call_target="tpu_custom_call" | custom-call | tf_op jit(solution)/shard_map/pick/pallas_call | solution.py:504
  8.9 0.4 collective-permute-done
  9.3 3.3 %collective-permute-start.3 = (bf16[256,128]{1,0:T(8,128)(2,1)S(1)}, bf16[256,128]{1,0:T(8,128)(2,1)S(1)}, u32[]{:S(2)}, u32[]{:S(2)}) collective-permute-start(bf16[256,128]{1,0:T(8,128)(2,1)S(1)} %pad_maximum_fusion.2.refs_0_), channel_id=1, source_target_pairs={{0,12},{1,13},{2,14},{3,15},{4,8},{5,9},{6,10},{7,11},{8,4},{9,5},... | collective-permute-start | bytes 196616 | tf_op jit(solution)/shard_map/ppermute | solution.py:34
  12.6 0.4 collective-permute-start.1
  12.9 2.9 %stage.1 = (bf16[16,128,128]{2,1,0:T(8,128)(2,1)}, bf16[16,128,128]{2,1,0:T(8,128)(2,1)}, bf16[12,128,128]{2,1,0:T(8,128)(2,1)}, f32[16,128]{1,0:T(8,128)S(1)}, bf16[128,176]{1,0:T(8,128)(2,1)S(1)}) custom-call(s32[1]{0:T(128)} %bitcast.me_ref, s32[1,4,32]{2,1,0:T(4,128)} %parent_ref.11, s32[8,128]{1,0:T(8,128)S(1)} %broadcast_in_dim.15.parents_ref, ...), custom_call_target="tpu_custom_call" | custom-call | tf_op jit(solution)/shard_map/stage/pallas_call | solution.py:515
  15.9 1.8 %collective-permute-done.2.refs_2_ = bf16[256,128]{1,0:T(8,128)(2,1)S(1)} collective-permute-done((bf16[256,128]{1,0:T(8,128)(2,1)S(1)}, bf16[256,128]{1,0:T(8,128)(2,1)S(1)}, u32[]{:S(2)}, u32[]{:S(2)}) %collective-permute-start.2) | collective-permute-done | bytes 65568 | tf_op jit(solution)/shard_map/ppermute | solution.py:34
  17.7 2.4 %collective-permute-start.4 = (bf16[256,128]{1,0:T(8,128)(2,1)S(1)}, bf16[256,128]{1,0:T(8,128)(2,1)S(1)}, u32[]{:S(2)}, u32[]{:S(2)}) collective-permute-start(bf16[256,128]{1,0:T(8,128)(2,1)S(1)} %pad_maximum_fusion.2.refs_0_), channel_id=1, source_target_pairs={{0,1},{1,0},{2,3},{3,2},{4,5},{5,4},{6,7},{7,6},{8,9},{9,8},{10,11... | collective-permute-start | bytes 196616 | tf_op jit(solution)/shard_map/ppermute | solution.py:34
  20.1 0.0 collective-permute-start.5
  20.2 0.5 collective-permute-start.6
  20.7 0.0 collective-permute-start.7
  20.7 0.4 collective-permute-done.4.refs_4_
  21.1 0.4 collective-permute-start.11
  21.4 0.2 collective-permute-start.12
  21.6 0.5 collective-permute-start.20
  22.1 1.1 %project.1 = bf16[640,128]{1,0:T(8,128)(2,1)S(1)} custom-call(s32[1]{0:T(128)} %bitcast.me_ref, bf16[3,2048,128]{2,1,0:T(8,128)(2,1)S(1)} %bitcast.11, bf16[640,384]{1,0:T(8,128)(2,1)S(1)} %get-tuple-element.54.pick_ref, bf16[256,128]{1,0:T(8,128)(2,1)S(1)} %pad_maximum_fusion.2.refs_0_, bf16[256,128]{1,0:T(8,128)(2,1)S(1)} %collective-permute-done.1.refs_1_, ...), custom_call_target="tpu_custom_call" | custom-call | tf_op jit(solution)/shard_map/project/pallas_call | solution.py:559
  23.2 0.2 collective-permute-start.9
  23.5 1.1 %collective-permute-done.9 = bf16[1,2,4,40,128]{4,3,1,0,2:T(8,128)(2,1)S(1)} collective-permute-done((bf16[1,2,4,40,128]{4,3,1,0,2:T(8,128)(2,1)S(1)}, bf16[1,2,4,40,128]{4,3,1,0,2:T(8,128)(2,1)S(1)}, u32[]{:S(2)}, u32[]{:S(2)}) %collective-permute-start.9) | collective-permute-done | bytes 81952 | tf_op jit(solution)/shard_map/ppermute | solution.py:34
  24.6 1.9 %collective-permute-start.10 = (bf16[2,1,4,40,128]{4,3,1,0,2:T(8,128)(2,1)S(1)}, bf16[2,1,4,40,128]{4,3,1,0,2:T(8,128)(2,1)S(1)}, u32[]{:S(2)}, u32[]{:S(2)}) collective-permute-start(bf16[2,1,4,40,128]{4,3,1,0,2:T(8,128)(2,1)S(1)} %get-tuple-element.97), channel_id=1, source_target_pairs={{0,6},{1,7},{2,4},{3,5},{4,2},{5,3},{6,0},{7,1},{8,14},{9,15},{10,... | collective-permute-start | bytes 245768 | tf_op jit(solution)/shard_map/ppermute | solution.py:34
  26.6 3.0 %collective-permute-done.10 = bf16[2,1,4,40,128]{4,3,1,0,2:T(8,128)(2,1)S(1)} collective-permute-done((bf16[2,1,4,40,128]{4,3,1,0,2:T(8,128)(2,1)S(1)}, bf16[2,1,4,40,128]{4,3,1,0,2:T(8,128)(2,1)S(1)}, u32[]{:S(2)}, u32[]{:S(2)}) %collective-permute-start.10) | collective-permute-done | bytes 81952 | tf_op jit(solution)/shard_map/ppermute | solution.py:34
  29.6 2.7 %collective-permute-start.15 = (bf16[2,2,1,40,128]{4,3,1,0,2:T(8,128)(2,1)S(1)}, bf16[2,2,1,40,128]{4,3,1,0,2:T(8,128)(2,1)S(1)}, u32[]{:S(2)}, u32[]{:S(2)}) collective-permute-start(bf16[2,2,1,40,128]{4,3,1,0,2:T(8,128)(2,1)S(1)} %get-tuple-element.92), channel_id=1, source_target_pairs={{0,12},{1,13},{2,14},{3,15},{4,8},{5,9},{6,10},{7,11},{8,4},{9,5},... | collective-permute-start | bytes 122888 | tf_op jit(solution)/shard_map/ppermute | solution.py:34
  32.3 0.9 %collective-permute-start.13 = (bf16[2,2,1,40,128]{4,3,1,0,2:T(8,128)(2,1)S(1)}, bf16[2,2,1,40,128]{4,3,1,0,2:T(8,128)(2,1)S(1)}, u32[]{:S(2)}, u32[]{:S(2)}) collective-permute-start(bf16[2,2,1,40,128]{4,3,1,0,2:T(8,128)(2,1)S(1)} %get-tuple-element.94), channel_id=1, source_target_pairs={{0,4},{1,5},{2,6},{3,7},{4,0},{5,1},{6,2},{7,3},{8,12},{9,13},{10,... | collective-permute-start | bytes 122888 | tf_op jit(solution)/shard_map/ppermute | solution.py:34
  33.2 2.2 %hold.1.refs_0_.states_ref = bf16[8,16,128,128]{3,2,1,0:T(8,128)(2,1)S(1)} custom-call(bf16[8,16,128,128]{3,2,1,0:T(8,128)(2,1)} %states_ref.7), custom_call_target="tpu_custom_call" | custom-call | tf_op jit(solution)/shard_map/hold/pallas_call | solution.py:536
  35.5 0.0 copy-start.3
  35.5 0.8 %collective-permute-done.14 = bf16[2,2,1,40,128]{4,3,1,0,2:T(8,128)(2,1)S(1)} collective-permute-done((bf16[2,2,1,40,128]{4,3,1,0,2:T(8,128)(2,1)S(1)}, bf16[2,2,1,40,128]{4,3,1,0,2:T(8,128)(2,1)S(1)}, u32[]{:S(2)}, u32[]{:S(2)}) %collective-permute-start.14) | collective-permute-done | bytes 40992 | tf_op jit(solution)/shard_map/ppermute | solution.py:34
  36.3 2.5 %readout.1 = (bf16[8,2816]{1,0:T(8,128)(2,1)S(1)}, bf16[16,40,128]{2,1,0:T(8,128)(2,1)S(1)}) custom-call(s32[1]{0:T(128)} %bitcast.me_ref, f32[16]{0:T(128)S(1)} %copy-done.6, f32[16,128]{1,0:T(8,128)S(1)} %get-tuple-element.52.place_ref, f32[16,128]{1,0:T(8,128)S(1)} %copy-done.4, f32[16,128]{1,0:T(8,128)S(1)} %bitcast.17, ...), custom_call_target="tpu_custom_call" | custom-call | tf_op jit(solution)/shard_map/readout/pallas_call | solution.py:583
  38.8 1.1 %collective-permute-start.16 = (bf16[8,2816]{1,0:T(8,128)(2,1)S(1)}, bf16[8,2816]{1,0:T(8,128)(2,1)S(1)}, u32[]{:S(2)}, u32[]{:S(2)}) collective-permute-start(bf16[8,2816]{1,0:T(8,128)(2,1)S(1)} %get-tuple-element.74), channel_id=1, source_target_pairs={{0,6},{1,7},{2,4},{3,5},{4,2},{5,3},{6,0},{7,1},{8,14},{9,15},{10,... | collective-permute-start | bytes 135176 | tf_op jit(solution)/shard_map/ppermute | solution.py:34
  40.0 0.2 collective-permute-start.25
  40.2 4.2 %near_update.1 = (bf16[8,16,128,128]{3,2,1,0:T(8,128)(2,1)}, bf16[16,128,16]{2,1,0:T(8,128)(2,1)S(1)}, f32[16,16,128]{2,1,0:T(8,128)S(1)}, f32[2,16,16,128]{3,2,1,0:T(8,128)S(1)}) custom-call(s32[1]{0:T(128)} %bitcast.me_ref, s32[1,4,32]{2,1,0:T(4,128)S(1)} %copy-done.3, f32[16]{0:T(128)S(1)} %copy-done.6, ...), custom_call_target="tpu_custom_call" | custom-call | tf_op jit(solution)/shard_map/near_update/pallas_call | solution.py:596
  44.5 2.5 %collective-permute-start.19 = (bf16[16,2816]{1,0:T(8,128)(2,1)S(1)}, bf16[16,2816]{1,0:T(8,128)(2,1)S(1)}, u32[]{:S(2)}, u32[]{:S(2)}) collective-permute-start(bf16[16,2816]{1,0:T(8,128)(2,1)S(1)} %pad_maximum_fusion.1.refs_0_), channel_id=1, source_target_pairs={{0,12},{1,13},{2,14},{3,15},{4,8},{5,9},{6,10},{7,11},{8,4},{9,5},... | collective-permute-start | bytes 270344 | tf_op jit(solution)/shard_map/ppermute | solution.py:34
  46.9 1.2 %collective-permute-start.17 = (bf16[16,2816]{1,0:T(8,128)(2,1)S(1)}, bf16[16,2816]{1,0:T(8,128)(2,1)S(1)}, u32[]{:S(2)}, u32[]{:S(2)}) collective-permute-start(bf16[16,2816]{1,0:T(8,128)(2,1)S(1)} %pad_maximum_fusion.1.refs_0_), channel_id=1, source_target_pairs={{0,4},{1,5},{2,6},{3,7},{4,0},{5,1},{6,2},{7,3},{8,12},{9,13},{10,... | collective-permute-start | bytes 270344 | tf_op jit(solution)/shard_map/ppermute | solution.py:34
  48.1 1.7 %collective-permute-done.20 = bf16[2,16,128,128]{3,2,1,0:T(8,128)(2,1)S(1)} collective-permute-done((bf16[2,16,128,128]{3,2,1,0:T(8,128)(2,1)S(1)}, bf16[2,16,128,128]{3,2,1,0:T(8,128)(2,1)S(1)}, u32[]{:S(2)}, u32[]{:S(2)}) %collective-permute-start.20) | collective-permute-done | bytes 1048608 | tf_op jit(solution)/shard_map/ppermute | solution.py:34
  49.8 1.7 %far_update.1.refs_1_ = bf16[8,16,128,128]{3,2,1,0:T(8,128)(2,1)} custom-call(s32[1]{0:T(128)} %bitcast.me_ref, s32[1,4,32]{2,1,0:T(4,128)S(1)} %copy-done.3, bf16[16,128,16]{2,1,0:T(8,128)(2,1)S(1)} %get-tuple-element.79.turned_ref, f32[16,16,128]{2,1,0:T(8,128)S(1)} %get-tuple-element.80.values_ref, ...), custom_call_target="tpu_custom_call", output_to_operand_aliasing={{}: (7, {})} | custom-call | tf_op jit(solution)/shard_map/far_update/pallas_call | solution.py:614
  51.5 1.3 %collective-permute-done.18.refs_2_ = bf16[16,2816]{1,0:T(8,128)(2,1)S(1)} collective-permute-done((bf16[16,2816]{1,0:T(8,128)(2,1)S(1)}, bf16[16,2816]{1,0:T(8,128)(2,1)S(1)}, u32[]{:S(2)}, u32[]{:S(2)}) %collective-permute-start.18) | collective-permute-done | bytes 90144 | tf_op jit(solution)/shard_map/ppermute | solution.py:34
  52.8 3.6 %collective-permute-start.21 = (bf16[16,2816]{1,0:T(8,128)(2,1)S(1)}, bf16[16,2816]{1,0:T(8,128)(2,1)S(1)}, u32[]{:S(2)}, u32[]{:S(2)}) collective-permute-start(bf16[16,2816]{1,0:T(8,128)(2,1)S(1)} %pad_maximum_fusion.1.refs_0_), channel_id=1, source_target_pairs={{0,1},{1,0},{2,3},{3,2},{4,5},{5,4},{6,7},{7,6},{8,9},{9,8},{10,11... | collective-permute-start | bytes 270344 | tf_op jit(solution)/shard_map/ppermute | solution.py:34
  56.4 0.0 collective-permute-start.22
  56.4 0.5 collective-permute-start.23
  56.9 0.0 collective-permute-start.24
  56.9 0.4 collective-permute-done.21.refs_4_
  57.3 0.4 collective-permute-done.22.refs_5_
  57.7 0.2 collective-permute-done.23.refs_6_
  57.8 0.4 collective-permute-done.24.refs_7_
  58.2 1.2 %output.1 = bf16[128,128]{1,0:T(8,128)(2,1)} custom-call(bf16[128,128]{1,0:T(8,128)(2,1)S(1)} %get-tuple-element.47.x_ref, bf16[2048,128]{1,0:T(8,128)(2,1)S(1)} %copy-done.1, bf16[128,176]{1,0:T(8,128)(2,1)S(1)} %get-tuple-element.48.pick_ref, bf16[16,2816]{1,0:T(8,128)(2,1)S(1)} %pad_maximum_fusion.1.refs_0_, ...), custom_call_target="tpu_custom_call" | custom-call | tf_op jit(solution)/shard_map/output/pallas_call | solution.py:641
  59.4 0.6 %last_update.1 = bf16[8,16,128,128]{3,2,1,0:T(8,128)(2,1)} custom-call(s32[1]{0:T(128)} %bitcast.me_ref, s32[1,4,32]{2,1,0:T(4,128)S(1)} %copy-done.3, bf16[16,128,16]{2,1,0:T(8,128)(2,1)S(1)} %get-tuple-element.79.turned_ref, f32[16,16,128]{2,1,0:T(8,128)S(1)} %get-tuple-element.80.values_ref, ...), custom_call_target="tpu_custom_call", output_to_operand_aliasing={{}: (6, {})} | custom-call | tf_op jit(solution)/shard_map/last_update/pallas_call | solution.py:614
  (41 shorter events, 0.2 us)
Async XLA Ops:
  0.6 6.1 %copy-start.2 = (s32[1,4,32]{2,1,0:T(4,128)S(1)}, s32[1,4,32]{2,1,0:T(4,128)}, u32[]{:S(2)}) copy-start(s32[1,4,32]{2,1,0:T(4,128)} %parent_ref.11) | copy-start | bytes 1540
  3.4 18.7 %collective-permute-start.8 = (bf16[20,128,128]{2,1,0:T(8,128)(2,1)S(1)}, bf16[20,128,128]{2,1,0:T(8,128)(2,1)S(1)}, u32[]{:S(2)}, u32[]{:S(2)}) collective-permute-start(bf16[20,128,128]{2,1,0:T(8,128)(2,1)S(1)} %get-tuple-element.59), channel_id=1, source_target_pairs={{0,2},{1,3},{2,0},{3,1},{4,6},{5,7},{6,4},{7,5},{8,10},{9,11},{10,... | collective-permute-start | bytes 1966088 | tf_op jit(solution)/shard_map/ppermute | solution.py:34
  5.5 3.8 %collective-permute-start = (bf16[128,128]{1,0:T(8,128)(2,1)S(1)}, bf16[128,128]{1,0:T(8,128)(2,1)S(1)}, u32[]{:S(2)}, u32[]{:S(2)}) collective-permute-start(bf16[128,128]{1,0:T(8,128)(2,1)S(1)} %get-tuple-element.47.x_ref), channel_id=1, source_target_pairs={{0,6},{1,7},{2,4},{3,5},{4,2},{5,3},{6,0},{7,1},{8,14},{9,15},{10,... | collective-permute-start | bytes 98312 | tf_op jit(solution)/shard_map/ppermute | solution.py:34
  6.8 15.3 %copy-start = (bf16[2048,3,128]{2,0,1:T(8,128)(2,1)S(1)}, bf16[2048,3,128]{2,0,1:T(8,128)(2,1)}, u32[]{:S(2)}) copy-start(bf16[2048,3,128]{2,0,1:T(8,128)(2,1)} %param.13) | copy-start | bytes 4718596
  9.3 6.6 %collective-permute-start.3 = (bf16[256,128]{1,0:T(8,128)(2,1)S(1)}, bf16[256,128]{1,0:T(8,128)(2,1)S(1)}, u32[]{:S(2)}, u32[]{:S(2)}) collective-permute-start(bf16[256,128]{1,0:T(8,128)(2,1)S(1)} %pad_maximum_fusion.2.refs_0_), channel_id=1, source_target_pairs={{0,12},{1,13},{2,14},{3,15},{4,8},{5,9},{6,10},{7,11},{8,4},{9,5},... | collective-permute-start | bytes 196616 | tf_op jit(solution)/shard_map/ppermute | solution.py:34
  12.6 5.1 %collective-permute-start.2 = (bf16[256,128]{1,0:T(8,128)(2,1)S(1)}, bf16[256,128]{1,0:T(8,128)(2,1)S(1)}, u32[]{:S(2)}, u32[]{:S(2)}) collective-permute-start(bf16[256,128]{1,0:T(8,128)(2,1)S(1)} %pad_maximum_fusion.2.refs_0_), channel_id=1, source_target_pairs={{0,8},{1,9},{2,10},{3,11},{4,12},{5,13},{6,14},{7,15},{8,0},{9,1},... | collective-permute-start | bytes 196616 | tf_op jit(solution)/shard_map/ppermute | solution.py:34
  12.6 5.1 %collective-permute-start.1 = (bf16[256,128]{1,0:T(8,128)(2,1)S(1)}, bf16[256,128]{1,0:T(8,128)(2,1)S(1)}, u32[]{:S(2)}, u32[]{:S(2)}) collective-permute-start(bf16[256,128]{1,0:T(8,128)(2,1)S(1)} %pad_maximum_fusion.2.refs_0_), channel_id=1, source_target_pairs={{0,4},{1,5},{2,6},{3,7},{4,0},{5,1},{6,2},{7,3},{8,12},{9,13},{10,... | collective-permute-start | bytes 196616 | tf_op jit(solution)/shard_map/ppermute | solution.py:34
  17.7 3.3 %collective-permute-start.4 = (bf16[256,128]{1,0:T(8,128)(2,1)S(1)}, bf16[256,128]{1,0:T(8,128)(2,1)S(1)}, u32[]{:S(2)}, u32[]{:S(2)}) collective-permute-start(bf16[256,128]{1,0:T(8,128)(2,1)S(1)} %pad_maximum_fusion.2.refs_0_), channel_id=1, source_target_pairs={{0,1},{1,0},{2,3},{3,2},{4,5},{5,4},{6,7},{7,6},{8,9},{9,8},{10,11... | collective-permute-start | bytes 196616 | tf_op jit(solution)/shard_map/ppermute | solution.py:34
  20.1 1.3 %collective-permute-start.5 = (bf16[256,128]{1,0:T(8,128)(2,1)S(1)}, bf16[256,128]{1,0:T(8,128)(2,1)S(1)}, u32[]{:S(2)}, u32[]{:S(2)}) collective-permute-start(bf16[256,128]{1,0:T(8,128)(2,1)S(1)} %collective-permute-done.1.refs_1_), channel_id=1, source_target_pairs={{0,1},{1,0},{2,3},{3,2},{4,5},{5,4},{6,7},{7,6},{8,9},{9,8},{10,11... | collective-permute-start | bytes 196616 | tf_op jit(solution)/shard_map/ppermute | solution.py:34
  20.2 1.4 %collective-permute-start.6 = (bf16[256,128]{1,0:T(8,128)(2,1)S(1)}, bf16[256,128]{1,0:T(8,128)(2,1)S(1)}, u32[]{:S(2)}, u32[]{:S(2)}) collective-permute-start(bf16[256,128]{1,0:T(8,128)(2,1)S(1)} %collective-permute-done.2.refs_2_), channel_id=1, source_target_pairs={{0,1},{1,0},{2,3},{3,2},{4,5},{5,4},{6,7},{7,6},{8,9},{9,8},{10,11... | collective-permute-start | bytes 196616 | tf_op jit(solution)/shard_map/ppermute | solution.py:34
  20.7 1.4 %collective-permute-start.7 = (bf16[256,128]{1,0:T(8,128)(2,1)S(1)}, bf16[256,128]{1,0:T(8,128)(2,1)S(1)}, u32[]{:S(2)}, u32[]{:S(2)}) collective-permute-start(bf16[256,128]{1,0:T(8,128)(2,1)S(1)} %collective-permute-done.3.refs_3_), channel_id=1, source_target_pairs={{0,1},{1,0},{2,3},{3,2},{4,5},{5,4},{6,7},{7,6},{8,9},{9,8},{10,11... | collective-permute-start | bytes 196616 | tf_op jit(solution)/shard_map/ppermute | solution.py:34
  21.1 8.5 %collective-permute-start.11 = (bf16[16,128,128]{2,1,0:T(8,128)(2,1)}, bf16[16,128,128]{2,1,0:T(8,128)(2,1)S(1)}, u32[]{:S(2)}, u32[]{:S(2)}) collective-permute-start(bf16[16,128,128]{2,1,0:T(8,128)(2,1)} %get-tuple-element.68), channel_id=1, source_target_pairs={{0,1},{1,0},{2,3},{3,2},{4,5},{5,4},{6,7},{7,6},{8,9},{9,8},{10,11... | collective-permute-start | bytes 1572872 | tf_op jit(solution)/shard_map/ppermute | solution.py:34
  21.4 8.2 %collective-permute-start.12 = (bf16[16,128,128]{2,1,0:T(8,128)(2,1)}, bf16[16,128,128]{2,1,0:T(8,128)(2,1)S(1)}, u32[]{:S(2)}, u32[]{:S(2)}) collective-permute-start(bf16[16,128,128]{2,1,0:T(8,128)(2,1)} %get-tuple-element.69), channel_id=1, source_target_pairs={{0,1},{1,0},{2,3},{3,2},{4,5},{5,4},{6,7},{7,6},{8,9},{9,8},{10,11... | collective-permute-start | bytes 1572872 | tf_op jit(solution)/shard_map/ppermute | solution.py:34
  21.6 28.2 %collective-permute-start.20 = (bf16[2,16,128,128]{3,2,1,0:T(8,128)(2,1)S(1)}, bf16[2,16,128,128]{3,2,1,0:T(8,128)(2,1)S(1)}, u32[]{:S(2)}, u32[]{:S(2)}) collective-permute-start(bf16[2,16,128,128]{3,2,1,0:T(8,128)(2,1)S(1)} %get-tuple-element.82), channel_id=1, source_target_pairs={{0,3},{1,2},{2,1},{3,0},{4,7},{5,6},{6,5},{7,4},{8,11},{9,10},{10,... | collective-permute-start | bytes 3145736 | tf_op jit(solution)/shard_map/ppermute | solution.py:34
  23.2 1.3 %collective-permute-start.9 = (bf16[1,2,4,40,128]{4,3,1,0,2:T(8,128)(2,1)S(1)}, bf16[1,2,4,40,128]{4,3,1,0,2:T(8,128)(2,1)S(1)}, u32[]{:S(2)}, u32[]{:S(2)}) collective-permute-start(bf16[1,2,4,40,128]{4,3,1,0,2:T(8,128)(2,1)S(1)} %copy.13), channel_id=1, source_target_pairs={{0,1},{1,0},{2,3},{3,2},{4,5},{5,4},{6,7},{7,6},{8,9},{9,8},{10,11... | collective-permute-start | bytes 245768 | tf_op jit(solution)/shard_map/ppermute | solution.py:34
  24.6 4.9 %collective-permute-start.10 = (bf16[2,1,4,40,128]{4,3,1,0,2:T(8,128)(2,1)S(1)}, bf16[2,1,4,40,128]{4,3,1,0,2:T(8,128)(2,1)S(1)}, u32[]{:S(2)}, u32[]{:S(2)}) collective-permute-start(bf16[2,1,4,40,128]{4,3,1,0,2:T(8,128)(2,1)S(1)} %get-tuple-element.97), channel_id=1, source_target_pairs={{0,6},{1,7},{2,4},{3,5},{4,2},{5,3},{6,0},{7,1},{8,14},{9,15},{10,... | collective-permute-start | bytes 245768 | tf_op jit(solution)/shard_map/ppermute | solution.py:34
  29.6 5.9 %collective-permute-start.15 = (bf16[2,2,1,40,128]{4,3,1,0,2:T(8,128)(2,1)S(1)}, bf16[2,2,1,40,128]{4,3,1,0,2:T(8,128)(2,1)S(1)}, u32[]{:S(2)}, u32[]{:S(2)}) collective-permute-start(bf16[2,2,1,40,128]{4,3,1,0,2:T(8,128)(2,1)S(1)} %get-tuple-element.92), channel_id=1, source_target_pairs={{0,12},{1,13},{2,14},{3,15},{4,8},{5,9},{6,10},{7,11},{8,4},{9,5},... | collective-permute-start | bytes 122888 | tf_op jit(solution)/shard_map/ppermute | solution.py:34
  32.3 3.9 %collective-permute-start.14 = (bf16[2,2,1,40,128]{4,3,1,0,2:T(8,128)(2,1)S(1)}, bf16[2,2,1,40,128]{4,3,1,0,2:T(8,128)(2,1)S(1)}, u32[]{:S(2)}, u32[]{:S(2)}) collective-permute-start(bf16[2,2,1,40,128]{4,3,1,0,2:T(8,128)(2,1)S(1)} %get-tuple-element.93), channel_id=1, source_target_pairs={{0,8},{1,9},{2,10},{3,11},{4,12},{5,13},{6,14},{7,15},{8,0},{9,1},... | collective-permute-start | bytes 122888 | tf_op jit(solution)/shard_map/ppermute | solution.py:34
  32.3 3.9 %copy-start.4 = (f32[16,128]{1,0:T(8,128)S(1)}, f32[16,128]{1,0:T(8,128)}, u32[]{:S(2)}) copy-start(f32[16,128]{1,0:T(8,128)} %gate_ref.3) | copy-start | bytes 24580
  32.3 3.9 %copy-start.5 = (f32[2048]{0:T(1024)S(1)}, f32[2048]{0:T(1024)}, u32[]{:S(2)}) copy-start(f32[2048]{0:T(1024)} %param.16) | copy-start | bytes 24580
  32.3 3.9 %copy-start.6 = (f32[16]{0:T(128)S(1)}, f32[16]{0:T(128)}, u32[]{:S(2)}) copy-start(f32[16]{0:T(128)} %bias_ref.3) | copy-start | bytes 196
  32.3 3.9 %collective-permute-start.13 = (bf16[2,2,1,40,128]{4,3,1,0,2:T(8,128)(2,1)S(1)}, bf16[2,2,1,40,128]{4,3,1,0,2:T(8,128)(2,1)S(1)}, u32[]{:S(2)}, u32[]{:S(2)}) collective-permute-start(bf16[2,2,1,40,128]{4,3,1,0,2:T(8,128)(2,1)S(1)} %get-tuple-element.94), channel_id=1, source_target_pairs={{0,4},{1,5},{2,6},{3,7},{4,0},{5,1},{6,2},{7,3},{8,12},{9,13},{10,... | collective-permute-start | bytes 122888 | tf_op jit(solution)/shard_map/ppermute | solution.py:34
  35.4 4.5 %copy-start.7 = (bf16[12,128,128]{2,1,0:T(8,128)(2,1)S(1)}, bf16[12,128,128]{2,1,0:T(8,128)(2,1)}, u32[]{:S(2)}) copy-start(bf16[12,128,128]{2,1,0:T(8,128)(2,1)} %get-tuple-element.88) | copy-start | bytes 1179652
  35.5 4.7 %copy-start.3 = (s32[1,4,32]{2,1,0:T(4,128)S(1)}, s32[1,4,32]{2,1,0:T(4,128)}, u32[]{:S(2)}) copy-start(s32[1,4,32]{2,1,0:T(4,128)} %parent_ref.11) | copy-start | bytes 1540
  38.8 5.6 %collective-permute-start.16 = (bf16[8,2816]{1,0:T(8,128)(2,1)S(1)}, bf16[8,2816]{1,0:T(8,128)(2,1)S(1)}, u32[]{:S(2)}, u32[]{:S(2)}) collective-permute-start(bf16[8,2816]{1,0:T(8,128)(2,1)S(1)} %get-tuple-element.74), channel_id=1, source_target_pairs={{0,6},{1,7},{2,4},{3,5},{4,2},{5,3},{6,0},{7,1},{8,14},{9,15},{10,... | collective-permute-start | bytes 135176 | tf_op jit(solution)/shard_map/ppermute | solution.py:34
  40.0 19.5 %collective-permute-start.25 = (bf16[12,128,128]{2,1,0:T(8,128)(2,1)S(1)}, bf16[12,128,128]{2,1,0:T(8,128)(2,1)S(1)}, u32[]{:S(2)}, u32[]{:S(2)}) collective-permute-start(bf16[12,128,128]{2,1,0:T(8,128)(2,1)S(1)} %copy-done.7), channel_id=1, source_target_pairs={{0,2},{1,3},{2,0},{3,1},{4,6},{5,7},{6,4},{7,5},{8,10},{9,11},{10,... | collective-permute-start | bytes 1179656 | tf_op jit(solution)/shard_map/ppermute | solution.py:34
  44.5 7.1 %collective-permute-start.19 = (bf16[16,2816]{1,0:T(8,128)(2,1)S(1)}, bf16[16,2816]{1,0:T(8,128)(2,1)S(1)}, u32[]{:S(2)}, u32[]{:S(2)}) collective-permute-start(bf16[16,2816]{1,0:T(8,128)(2,1)S(1)} %pad_maximum_fusion.1.refs_0_), channel_id=1, source_target_pairs={{0,12},{1,13},{2,14},{3,15},{4,8},{5,9},{6,10},{7,11},{8,4},{9,5},... | collective-permute-start | bytes 270344 | tf_op jit(solution)/shard_map/ppermute | solution.py:34
  46.9 5.9 %collective-permute-start.18 = (bf16[16,2816]{1,0:T(8,128)(2,1)S(1)}, bf16[16,2816]{1,0:T(8,128)(2,1)S(1)}, u32[]{:S(2)}, u32[]{:S(2)}) collective-permute-start(bf16[16,2816]{1,0:T(8,128)(2,1)S(1)} %pad_maximum_fusion.1.refs_0_), channel_id=1, source_target_pairs={{0,8},{1,9},{2,10},{3,11},{4,12},{5,13},{6,14},{7,15},{8,0},{9,1},... | collective-permute-start | bytes 270344 | tf_op jit(solution)/shard_map/ppermute | solution.py:34
  46.9 5.9 %collective-permute-start.17 = (bf16[16,2816]{1,0:T(8,128)(2,1)S(1)}, bf16[16,2816]{1,0:T(8,128)(2,1)S(1)}, u32[]{:S(2)}, u32[]{:S(2)}) collective-permute-start(bf16[16,2816]{1,0:T(8,128)(2,1)S(1)} %pad_maximum_fusion.1.refs_0_), channel_id=1, source_target_pairs={{0,4},{1,5},{2,6},{3,7},{4,0},{5,1},{6,2},{7,3},{8,12},{9,13},{10,... | collective-permute-start | bytes 270344 | tf_op jit(solution)/shard_map/ppermute | solution.py:34
  49.7 8.5 %copy-start.1 = (bf16[2048,128]{1,0:T(8,128)(2,1)S(1)}, bf16[2048,128]{1,0:T(8,128)(2,1)}, u32[]{:S(2)}) copy-start(bf16[2048,128]{1,0:T(8,128)(2,1)} %weight_ref.1) | copy-start | bytes 1572868
  52.8 4.5 %collective-permute-start.21 = (bf16[16,2816]{1,0:T(8,128)(2,1)S(1)}, bf16[16,2816]{1,0:T(8,128)(2,1)S(1)}, u32[]{:S(2)}, u32[]{:S(2)}) collective-permute-start(bf16[16,2816]{1,0:T(8,128)(2,1)S(1)} %pad_maximum_fusion.1.refs_0_), channel_id=1, source_target_pairs={{0,1},{1,0},{2,3},{3,2},{4,5},{5,4},{6,7},{7,6},{8,9},{9,8},{10,11... | collective-permute-start | bytes 270344 | tf_op jit(solution)/shard_map/ppermute | solution.py:34
  56.4 1.3 %collective-permute-start.22 = (bf16[16,2816]{1,0:T(8,128)(2,1)S(1)}, bf16[16,2816]{1,0:T(8,128)(2,1)S(1)}, u32[]{:S(2)}, u32[]{:S(2)}) collective-permute-start(bf16[16,2816]{1,0:T(8,128)(2,1)S(1)} %collective-permute-done.17.refs_1_), channel_id=1, source_target_pairs={{0,1},{1,0},{2,3},{3,2},{4,5},{5,4},{6,7},{7,6},{8,9},{9,8},{10,11... | collective-permute-start | bytes 270344 | tf_op jit(solution)/shard_map/ppermute | solution.py:34
  56.4 1.4 %collective-permute-start.23 = (bf16[16,2816]{1,0:T(8,128)(2,1)S(1)}, bf16[16,2816]{1,0:T(8,128)(2,1)S(1)}, u32[]{:S(2)}, u32[]{:S(2)}) collective-permute-start(bf16[16,2816]{1,0:T(8,128)(2,1)S(1)} %collective-permute-done.18.refs_2_), channel_id=1, source_target_pairs={{0,1},{1,0},{2,3},{3,2},{4,5},{5,4},{6,7},{7,6},{8,9},{9,8},{10,11... | collective-permute-start | bytes 270344 | tf_op jit(solution)/shard_map/ppermute | solution.py:34
  56.9 1.3 %collective-permute-start.24 = (bf16[16,2816]{1,0:T(8,128)(2,1)S(1)}, bf16[16,2816]{1,0:T(8,128)(2,1)S(1)}, u32[]{:S(2)}, u32[]{:S(2)}) collective-permute-start(bf16[16,2816]{1,0:T(8,128)(2,1)S(1)} %collective-permute-done.19.refs_3_), channel_id=1, source_target_pairs={{0,1},{1,0},{2,3},{3,2},{4,5},{5,4},{6,7},{7,6},{8,9},{9,8},{10,11... | collective-permute-start | bytes 270344 | tf_op jit(solution)/shard_map/ppermute | solution.py:34

commit v7 on v6

--- a/solution.py
+++ b/solution.py
@@ -41,7 +41,7 @@
         return [[1]]
     if count == 4:
         return [[2], [1]]
-    plan = [[6], [4, 8, 12] if count >= 16 else [4]]
+    plan = [[6], [12, 8, 4] if count >= 16 else [4]]
     bit = 16
     while bit < count:
         plan.append([bit])
@@ -245,12 +245,19 @@
     me, columns, parts = me_ref[0], held[0].shape[1], len(held)
     rows = pick_ref.shape[1] // 3
     total = [None] * 3
-    for place, distance in enumerate(order):
+
+    def block_at(place):
         ref, within = held[place * parts // len(order)], place % (len(order) // parts)
-        block = ref[within * rows : (within + 1) * rows, :]
-        first = pl.multiple_of((me ^ distance) * columns, columns)
+        return ref[within * rows : (within + 1) * rows, :]
+
+    odd = (me & 1) == 1
+    for place in range(len(order) // 2):
+        here, other = block_at(place), block_at(order.index(order[place] ^ 1))
+        flip = odd if order[place] & 1 == 0 else ~odd
+        pair = jnp.concatenate([jnp.where(flip, other, here), jnp.where(flip, here, other)], 1)
+        first = pl.multiple_of(((me ^ order[place]) >> 1) * (2 * columns), 2 * columns)
         for slab in range(3):
-            term = jnp.dot(block, weight_ref[slab, pl.ds(first, columns), :], preferred_element_type=jnp.float32)
+            term = jnp.dot(pair, weight_ref[slab, pl.ds(first, 2 * columns), :], preferred_element_type=jnp.float32)
             total[slab] = term if total[slab] is None else total[slab] + term
     every = jnp.concatenate([part.astype(jnp.bfloat16) for part in total], 0)
     out_ref[...] = jnp.dot(pick_ref[...], every, preferred_element_type=jnp.float32).astype(jnp.bfloat16)
@@ -355,9 +362,9 @@
 
 
 def near_update_kernel(
-    recv_order, block, blocks, me_ref, parent_ref, bias_ref, recv_ref, gate_ref, states_ref, *refs
+    recv_order, block, blocks, me_ref, parent_ref, bias_ref, recv_ref, gate_ref, states_ref,
+    out_ref, turned_ref, values_ref, terms_ref, new_ref, out_sem,
 ):
-    near_refs, (out_ref, turned_ref, values_ref, terms_ref, new_ref, out_sem) = refs[:CAP], refs[CAP:]
     own_rows, heads, size = states_ref.shape[0], states_ref.shape[1], states_ref.shape[2]
     slots = values_ref.shape[1]
     user, member = split(me_ref[0], blocks)
@@ -392,25 +399,19 @@
             new_ref[row, head] = fresh.astype(jnp.bfloat16)
         save(row).start()
 
-    def work(row, found):
+    def work(row, carry):
         away, place = facts(row)
 
         @pl.when(away == 0)
         def _():
             update(row, lambda head: states_ref[place, head])
 
-        for rank, ref in enumerate(near_refs):
-
-            @pl.when((away == 1) & (found == rank))
-            def _():
-                update(row, lambda head: ref[head])
-
-        return found + (away == 1).astype(jnp.int32)
-
-    lax.fori_loop(0, own_rows, work, jnp.int32(0))
+        return carry
+
+    lax.fori_loop(0, own_rows, work, 0)
 
     def finish(row, carry):
-        @pl.when(facts(row)[0] < 2)
+        @pl.when(facts(row)[0] == 0)
         def _():
             save(row).wait()
 
@@ -581,7 +582,7 @@
     held, near_gots = in_vmem(held), [tied["near"], tied["nearer"]]
     sources = [held, *near_gots, tied["first"]]
     normed, by_head = pl.pallas_call(
-        functools.partial(readout_kernel, recv_order, head_block, len(sources)),
+        functools.partial(readout_kernel, recv_order, math.gcd(heads, 8), len(sources)),
         in_specs=[SCALARS] * 2 + [WHOLE] * (3 + len(sources) + len(received)),
         out_specs=[WHOLE] * 2,
         out_shape=[
@@ -595,7 +596,7 @@
 
     near_done, turned, values, terms = pl.pallas_call(
         functools.partial(near_update_kernel, recv_order, head_block, blocks),
-        in_specs=[SCALARS] * 3 + [WHOLE] * (3 + CAP),
+        in_specs=[SCALARS] * 3 + [WHOLE] * 3,
         out_specs=[PLACED] + [WHOLE] * 3,
         out_shape=[
             pltpu.HBM(states.shape, bf16),
@@ -606,7 +607,7 @@
         scratch_shapes=[pltpu.VMEM(states.shape, bf16), pltpu.SemaphoreType.DMA((own_rows,))],
         compiler_params=params(),
         name="near_update",
-    )(mine, parents, gate_bias, by_head, gate_weight, held, *near_gots)
+    )(mine, parents, gate_bias, by_head, gate_weight, held)
 
     far_block = math.gcd(extra, 4)
 
@@ -633,7 +634,8 @@
             entries = [(2, 0, 0, 0, every), (2, 1, 0, heads, every[:extra])]
             entries += [(3, rank, 1, rank * heads, every) for rank in range(CAP)]
             gots = [tied["first"], corner_got.reshape(CAP * heads, size, size)]
-            far_done = far_update(tied["rows"], gots, entries, "far_update")
+            entries += [(1, rank, 2 + rank, 0, every) for rank in range(CAP)]
+            far_done = far_update(tied["rows"], gots + near_gots, entries, "far_update")
             *parts, tied["done"] = lax.optimization_barrier((*parts, far_done))
         return parts
 

time: 60.7 us -> 59.8 us (0.985)
  Pallas kernels: 21.4 us -> 20.6 us
  transfers between devices with their start and end apart: 26 -> 26, of which waited for: 12 -> 11; matrix products, arithmetic and copies ran while one was open for 0% -> 0% of each run, Pallas kernels for 30% -> 30%
where the time goes in v7:
time: 59.8 us; the launch traced here: 58.7 us
  starting transfers between devices  25.7 us (43%)
  Pallas kernels  20.6 us (34%)
  waiting for transfers between devices  11.4 us (19%)
  between operations  0.88 us (1%)
    ppermute x26, starting transfers between devices, xor_permute(): lax.ppermute(block, 'rows', [(i, i ^ distance) for i in range(count)])  25.7 us
    ppermute x26, waiting for transfers between devices, xor_permute(): lax.ppermute(block, 'rows', [(i, i ^ distance) for i in range(count)])  11.4 us
    pallas_call x1, Pallas kernels, per_device(): pl.pallas_call(functools.partial(near_update_kernel, recv_order, head_blo...  3.89 us
    pallas_call x1, Pallas kernels, per_device(): pl.pallas_call(functools.partial(stage_kernel, blocks, normed_order), in_...  2.93 us
    pallas_call x2, Pallas kernels, far_update(): pl.pallas_call(functools.partial(far_update_kernel, far_block, blocks, ow...  2.74 us
    pallas_call x1, Pallas kernels, per_device(): pl.pallas_call(functools.partial(fetch_kernel, blocks), in_specs=[SCALARS...  2.59 us
    pallas_call x1, Pallas kernels, per_device(): pl.pallas_call(hold_kernel, in_specs=[PLACED], out_specs=WHOLE, out_shape...  2.21 us
    pallas_call x1, Pallas kernels, per_device(): pl.pallas_call(functools.partial(pick_kernel, blocks, piece, recv_order),...  2.08 us
  transfers between devices with their start and end apart: 26, of which 11 were waited for; matrix products, arithmetic and copies ran while one was open for 0% of the time, Pallas kernels for 30%

profile of v7, /device:TPU:1, one launch (start us, length us, event | category | flops | bytes accessed | tf_op | source)
XLA Modules:
  0.0 58.7 jit_solution(4681233065899464434)
XLA Ops:
  0.6 0.0 copy-start.2
  0.6 2.6 %fetch.1 = (bf16[128,128]{1,0:T(8,128)(2,1)S(1)}, bf16[20,128,128]{2,1,0:T(8,128)(2,1)S(1)}) custom-call(s32[1]{0:T(128)} %bitcast.me_ref, s32[1,4,32]{2,1,0:T(4,128)} %parent_ref.11, s32[1,128]{1,0:T(1,128)} %tokens_ref.1, s32[1,128]{1,0:T(1,128)} %tokens_ref.1, bf16[32768,128]{1,0:T(8,128)(2,1)} %table_ref.1, bf16[8,16,128,128]{3,2,1,0:T(8,128)(2,1)} %states_ref.7), custom_call_target="tpu_custom_call" | custom-call | tf_op jit(solution)/shard_map/fetch/pallas_call | solution.py:490
  3.2 2.1 %collective-permute-start.8 = (bf16[20,128,128]{2,1,0:T(8,128)(2,1)S(1)}, bf16[20,128,128]{2,1,0:T(8,128)(2,1)S(1)}, u32[]{:S(2)}, u32[]{:S(2)}) collective-permute-start(bf16[20,128,128]{2,1,0:T(8,128)(2,1)S(1)} %get-tuple-element.59), channel_id=1, source_target_pairs={{0,2},{1,3},{2,0},{3,1},{4,6},{5,7},{6,4},{7,5},{8,10},{9,11},{10,... | collective-permute-start | bytes 1966088 | tf_op jit(solution)/shard_map/ppermute | solution.py:34
  5.4 1.2 %collective-permute-start = (bf16[128,128]{1,0:T(8,128)(2,1)S(1)}, bf16[128,128]{1,0:T(8,128)(2,1)S(1)}, u32[]{:S(2)}, u32[]{:S(2)}) collective-permute-start(bf16[128,128]{1,0:T(8,128)(2,1)S(1)} %get-tuple-element.47.x_ref), channel_id=1, source_target_pairs={{0,6},{1,7},{2,4},{3,5},{4,2},{5,3},{6,0},{7,1},{8,14},{9,15},{10,... | collective-permute-start | bytes 98312 | tf_op jit(solution)/shard_map/ppermute | solution.py:34
  6.6 0.1 broadcast_in_dim.14
  6.7 2.1 %pick.1 = (bf16[640,384]{1,0:T(8,128)(2,1)S(1)}, bf16[2,16,128,128]{3,2,1,0:T(8,128)(2,1)S(1)}) custom-call(s32[1]{0:T(128)} %bitcast.me_ref, s32[1,4,32]{2,1,0:T(4,128)} %parent_ref.11, s32[8,128]{1,0:T(8,128)S(1)} %broadcast_in_dim.15.parents_ref, bf16[8,16,128,128]{3,2,1,0:T(8,128)(2,1)} %states_ref.7), custom_call_target="tpu_custom_call" | custom-call | tf_op jit(solution)/shard_map/pick/pallas_call | solution.py:505
  8.8 0.4 collective-permute-done
  9.2 3.3 %collective-permute-start.1 = (bf16[256,128]{1,0:T(8,128)(2,1)S(1)}, bf16[256,128]{1,0:T(8,128)(2,1)S(1)}, u32[]{:S(2)}, u32[]{:S(2)}) collective-permute-start(bf16[256,128]{1,0:T(8,128)(2,1)S(1)} %pad_maximum_fusion.2.refs_0_), channel_id=1, source_target_pairs={{0,12},{1,13},{2,14},{3,15},{4,8},{5,9},{6,10},{7,11},{8,4},{9,5},... | collective-permute-start | bytes 196616 | tf_op jit(solution)/shard_map/ppermute | solution.py:34
  12.5 0.0 collective-permute-start.2
  12.5 0.4 collective-permute-start.3
  12.8 2.9 %stage.1 = (bf16[16,128,128]{2,1,0:T(8,128)(2,1)}, bf16[16,128,128]{2,1,0:T(8,128)(2,1)}, bf16[12,128,128]{2,1,0:T(8,128)(2,1)}, f32[16,128]{1,0:T(8,128)S(1)}, bf16[128,176]{1,0:T(8,128)(2,1)S(1)}) custom-call(s32[1]{0:T(128)} %bitcast.me_ref, s32[1,4,32]{2,1,0:T(4,128)} %parent_ref.11, s32[8,128]{1,0:T(8,128)S(1)} %broadcast_in_dim.15.parents_ref, ...), custom_call_target="tpu_custom_call" | custom-call | tf_op jit(solution)/shard_map/stage/pallas_call | solution.py:516
  15.8 1.8 %collective-permute-done.2.refs_2_ = bf16[256,128]{1,0:T(8,128)(2,1)S(1)} collective-permute-done((bf16[256,128]{1,0:T(8,128)(2,1)S(1)}, bf16[256,128]{1,0:T(8,128)(2,1)S(1)}, u32[]{:S(2)}, u32[]{:S(2)}) %collective-permute-start.2) | collective-permute-done | bytes 65568 | tf_op jit(solution)/shard_map/ppermute | solution.py:34
  17.6 2.4 %collective-permute-start.4 = (bf16[256,128]{1,0:T(8,128)(2,1)S(1)}, bf16[256,128]{1,0:T(8,128)(2,1)S(1)}, u32[]{:S(2)}, u32[]{:S(2)}) collective-permute-start(bf16[256,128]{1,0:T(8,128)(2,1)S(1)} %pad_maximum_fusion.2.refs_0_), channel_id=1, source_target_pairs={{0,1},{1,0},{2,3},{3,2},{4,5},{5,4},{6,7},{7,6},{8,9},{9,8},{10,11... | collective-permute-start | bytes 196616 | tf_op jit(solution)/shard_map/ppermute | solution.py:34
  20.0 0.0 collective-permute-start.5
  20.0 0.5 collective-permute-start.6
  20.5 0.0 collective-permute-start.7
  20.5 0.4 collective-permute-done.4.refs_4_
  20.9 0.4 collective-permute-start.11
  21.3 0.2 collective-permute-start.12
  21.5 0.5 collective-permute-start.20
  22.0 0.8 %project.1 = bf16[640,128]{1,0:T(8,128)(2,1)S(1)} custom-call(s32[1]{0:T(128)} %bitcast.me_ref, bf16[3,2048,128]{2,1,0:T(8,128)(2,1)S(1)} %bitcast.11, bf16[640,384]{1,0:T(8,128)(2,1)S(1)} %get-tuple-element.54.pick_ref, bf16[256,128]{1,0:T(8,128)(2,1)S(1)} %pad_maximum_fusion.2.refs_0_, bf16[256,128]{1,0:T(8,128)(2,1)S(1)} %collective-permute-done.1.refs_1_, ...), custom_call_target="tpu_custom_call" | custom-call | tf_op jit(solution)/shard_map/project/pallas_call | solution.py:560
  22.8 0.2 collective-permute-start.9
  23.1 1.1 %collective-permute-done.9 = bf16[1,2,4,40,128]{4,3,1,0,2:T(8,128)(2,1)S(1)} collective-permute-done((bf16[1,2,4,40,128]{4,3,1,0,2:T(8,128)(2,1)S(1)}, bf16[1,2,4,40,128]{4,3,1,0,2:T(8,128)(2,1)S(1)}, u32[]{:S(2)}, u32[]{:S(2)}) %collective-permute-start.9) | collective-permute-done | bytes 81952 | tf_op jit(solution)/shard_map/ppermute | solution.py:34
  24.2 2.0 %collective-permute-start.10 = (bf16[2,1,4,40,128]{4,3,1,0,2:T(8,128)(2,1)S(1)}, bf16[2,1,4,40,128]{4,3,1,0,2:T(8,128)(2,1)S(1)}, u32[]{:S(2)}, u32[]{:S(2)}) collective-permute-start(bf16[2,1,4,40,128]{4,3,1,0,2:T(8,128)(2,1)S(1)} %get-tuple-element.97), channel_id=1, source_target_pairs={{0,6},{1,7},{2,4},{3,5},{4,2},{5,3},{6,0},{7,1},{8,14},{9,15},{10,... | collective-permute-start | bytes 245768 | tf_op jit(solution)/shard_map/ppermute | solution.py:34
  26.2 2.9 %collective-permute-done.10 = bf16[2,1,4,40,128]{4,3,1,0,2:T(8,128)(2,1)S(1)} collective-permute-done((bf16[2,1,4,40,128]{4,3,1,0,2:T(8,128)(2,1)S(1)}, bf16[2,1,4,40,128]{4,3,1,0,2:T(8,128)(2,1)S(1)}, u32[]{:S(2)}, u32[]{:S(2)}) %collective-permute-start.10) | collective-permute-done | bytes 81952 | tf_op jit(solution)/shard_map/ppermute | solution.py:34
  29.2 2.8 %collective-permute-start.13 = (bf16[2,2,1,40,128]{4,3,1,0,2:T(8,128)(2,1)S(1)}, bf16[2,2,1,40,128]{4,3,1,0,2:T(8,128)(2,1)S(1)}, u32[]{:S(2)}, u32[]{:S(2)}) collective-permute-start(bf16[2,2,1,40,128]{4,3,1,0,2:T(8,128)(2,1)S(1)} %get-tuple-element.94), channel_id=1, source_target_pairs={{0,12},{1,13},{2,14},{3,15},{4,8},{5,9},{6,10},{7,11},{8,4},{9,5},... | collective-permute-start | bytes 122888 | tf_op jit(solution)/shard_map/ppermute | solution.py:34
  32.0 0.8 %collective-permute-start.15 = (bf16[2,2,1,40,128]{4,3,1,0,2:T(8,128)(2,1)S(1)}, bf16[2,2,1,40,128]{4,3,1,0,2:T(8,128)(2,1)S(1)}, u32[]{:S(2)}, u32[]{:S(2)}) collective-permute-start(bf16[2,2,1,40,128]{4,3,1,0,2:T(8,128)(2,1)S(1)} %get-tuple-element.92), channel_id=1, source_target_pairs={{0,4},{1,5},{2,6},{3,7},{4,0},{5,1},{6,2},{7,3},{8,12},{9,13},{10,... | collective-permute-start | bytes 122888 | tf_op jit(solution)/shard_map/ppermute | solution.py:34
  32.8 2.2 %hold.1.refs_0_.states_ref = bf16[8,16,128,128]{3,2,1,0:T(8,128)(2,1)S(1)} custom-call(bf16[8,16,128,128]{3,2,1,0:T(8,128)(2,1)} %states_ref.7), custom_call_target="tpu_custom_call" | custom-call | tf_op jit(solution)/shard_map/hold/pallas_call | solution.py:537
  35.0 0.0 copy-start.3
  35.1 0.8 %collective-permute-done.14 = bf16[2,2,1,40,128]{4,3,1,0,2:T(8,128)(2,1)S(1)} collective-permute-done((bf16[2,2,1,40,128]{4,3,1,0,2:T(8,128)(2,1)S(1)}, bf16[2,2,1,40,128]{4,3,1,0,2:T(8,128)(2,1)S(1)}, u32[]{:S(2)}, u32[]{:S(2)}) %collective-permute-start.14) | collective-permute-done | bytes 40992 | tf_op jit(solution)/shard_map/ppermute | solution.py:34
  35.9 2.1 %readout.1 = (bf16[8,2816]{1,0:T(8,128)(2,1)S(1)}, bf16[16,40,128]{2,1,0:T(8,128)(2,1)S(1)}) custom-call(s32[1]{0:T(128)} %bitcast.me_ref, f32[16]{0:T(128)S(1)} %copy-done.6, f32[16,128]{1,0:T(8,128)S(1)} %get-tuple-element.52.place_ref, f32[16,128]{1,0:T(8,128)S(1)} %copy-done.4, f32[16,128]{1,0:T(8,128)S(1)} %bitcast.17, ...), custom_call_target="tpu_custom_call" | custom-call | tf_op jit(solution)/shard_map/readout/pallas_call | solution.py:584
  37.9 1.2 %collective-permute-start.16 = (bf16[8,2816]{1,0:T(8,128)(2,1)S(1)}, bf16[8,2816]{1,0:T(8,128)(2,1)S(1)}, u32[]{:S(2)}, u32[]{:S(2)}) collective-permute-start(bf16[8,2816]{1,0:T(8,128)(2,1)S(1)} %get-tuple-element.74), channel_id=1, source_target_pairs={{0,6},{1,7},{2,4},{3,5},{4,2},{5,3},{6,0},{7,1},{8,14},{9,15},{10,... | collective-permute-start | bytes 135176 | tf_op jit(solution)/shard_map/ppermute | solution.py:34
  39.1 0.2 collective-permute-start.25
  39.4 3.9 %near_update.1 = (bf16[8,16,128,128]{3,2,1,0:T(8,128)(2,1)}, bf16[16,128,16]{2,1,0:T(8,128)(2,1)S(1)}, f32[16,16,128]{2,1,0:T(8,128)S(1)}, f32[2,16,16,128]{3,2,1,0:T(8,128)S(1)}) custom-call(s32[1]{0:T(128)} %bitcast.me_ref, s32[1,4,32]{2,1,0:T(4,128)S(1)} %copy-done.3, f32[16]{0:T(128)S(1)} %copy-done.6, ...), custom_call_target="tpu_custom_call" | custom-call | tf_op jit(solution)/shard_map/near_update/pallas_call | solution.py:597
  43.3 1.9 %collective-permute-start.17 = (bf16[16,2816]{1,0:T(8,128)(2,1)S(1)}, bf16[16,2816]{1,0:T(8,128)(2,1)S(1)}, u32[]{:S(2)}, u32[]{:S(2)}) collective-permute-start(bf16[16,2816]{1,0:T(8,128)(2,1)S(1)} %pad_maximum_fusion.1.refs_0_), channel_id=1, source_target_pairs={{0,12},{1,13},{2,14},{3,15},{4,8},{5,9},{6,10},{7,11},{8,4},{9,5},... | collective-permute-start | bytes 270344 | tf_op jit(solution)/shard_map/ppermute | solution.py:34
  45.2 1.7 %collective-permute-start.19 = (bf16[16,2816]{1,0:T(8,128)(2,1)S(1)}, bf16[16,2816]{1,0:T(8,128)(2,1)S(1)}, u32[]{:S(2)}, u32[]{:S(2)}) collective-permute-start(bf16[16,2816]{1,0:T(8,128)(2,1)S(1)} %pad_maximum_fusion.1.refs_0_), channel_id=1, source_target_pairs={{0,4},{1,5},{2,6},{3,7},{4,0},{5,1},{6,2},{7,3},{8,12},{9,13},{10,... | collective-permute-start | bytes 270344 | tf_op jit(solution)/shard_map/ppermute | solution.py:34
  46.9 2.7 %collective-permute-done.20 = bf16[2,16,128,128]{3,2,1,0:T(8,128)(2,1)S(1)} collective-permute-done((bf16[2,16,128,128]{3,2,1,0:T(8,128)(2,1)S(1)}, bf16[2,16,128,128]{3,2,1,0:T(8,128)(2,1)S(1)}, u32[]{:S(2)}, u32[]{:S(2)}) %collective-permute-start.20) | collective-permute-done | bytes 1048608 | tf_op jit(solution)/shard_map/ppermute | solution.py:34
  49.6 2.1 %far_update.1.refs_1_ = bf16[8,16,128,128]{3,2,1,0:T(8,128)(2,1)} custom-call(s32[1]{0:T(128)} %bitcast.me_ref, s32[1,4,32]{2,1,0:T(4,128)S(1)} %copy-done.3, bf16[16,128,16]{2,1,0:T(8,128)(2,1)S(1)} %get-tuple-element.79.turned_ref, f32[16,16,128]{2,1,0:T(8,128)S(1)} %get-tuple-element.80.values_ref, ...), custom_call_target="tpu_custom_call", output_to_operand_aliasing={{}: (9, {})} | custom-call | tf_op jit(solution)/shard_map/far_update/pallas_call | solution.py:615
  51.8 3.3 %collective-permute-start.21 = (bf16[16,2816]{1,0:T(8,128)(2,1)S(1)}, bf16[16,2816]{1,0:T(8,128)(2,1)S(1)}, u32[]{:S(2)}, u32[]{:S(2)}) collective-permute-start(bf16[16,2816]{1,0:T(8,128)(2,1)S(1)} %pad_maximum_fusion.1.refs_0_), channel_id=1, source_target_pairs={{0,1},{1,0},{2,3},{3,2},{4,5},{5,4},{6,7},{7,6},{8,9},{9,8},{10,11... | collective-permute-start | bytes 270344 | tf_op jit(solution)/shard_map/ppermute | solution.py:34
  55.1 0.0 collective-permute-start.22
  55.1 0.5 collective-permute-start.23
  55.6 0.0 collective-permute-start.24
  55.6 0.4 collective-permute-done.21.refs_4_
  56.0 0.4 collective-permute-done.22.refs_5_
  56.4 0.2 collective-permute-done.23.refs_6_
  56.5 0.4 collective-permute-done.24.refs_7_
  56.9 1.2 %output.1 = bf16[128,128]{1,0:T(8,128)(2,1)} custom-call(bf16[128,128]{1,0:T(8,128)(2,1)S(1)} %get-tuple-element.47.x_ref, bf16[2048,128]{1,0:T(8,128)(2,1)S(1)} %copy-done.1, bf16[128,176]{1,0:T(8,128)(2,1)S(1)} %get-tuple-element.48.pick_ref, bf16[16,2816]{1,0:T(8,128)(2,1)S(1)} %pad_maximum_fusion.1.refs_0_, ...), custom_call_target="tpu_custom_call" | custom-call | tf_op jit(solution)/shard_map/output/pallas_call | solution.py:643
  58.1 0.6 %last_update.1 = bf16[8,16,128,128]{3,2,1,0:T(8,128)(2,1)} custom-call(s32[1]{0:T(128)} %bitcast.me_ref, s32[1,4,32]{2,1,0:T(4,128)S(1)} %copy-done.3, bf16[16,128,16]{2,1,0:T(8,128)(2,1)S(1)} %get-tuple-element.79.turned_ref, f32[16,16,128]{2,1,0:T(8,128)S(1)} %get-tuple-element.80.values_ref, ...), custom_call_target="tpu_custom_call", output_to_operand_aliasing={{}: (6, {})} | custom-call | tf_op jit(solution)/shard_map/last_update/pallas_call | solution.py:615
  (41 shorter events, 0.2 us)
Async XLA Ops:
  0.6 6.0 %copy-start.2 = (s32[1,4,32]{2,1,0:T(4,128)S(1)}, s32[1,4,32]{2,1,0:T(4,128)}, u32[]{:S(2)}) copy-start(s32[1,4,32]{2,1,0:T(4,128)} %parent_ref.11) | copy-start | bytes 1540
  3.2 18.7 %collective-permute-start.8 = (bf16[20,128,128]{2,1,0:T(8,128)(2,1)S(1)}, bf16[20,128,128]{2,1,0:T(8,128)(2,1)S(1)}, u32[]{:S(2)}, u32[]{:S(2)}) collective-permute-start(bf16[20,128,128]{2,1,0:T(8,128)(2,1)S(1)} %get-tuple-element.59), channel_id=1, source_target_pairs={{0,2},{1,3},{2,0},{3,1},{4,6},{5,7},{6,4},{7,5},{8,10},{9,11},{10,... | collective-permute-start | bytes 1966088 | tf_op jit(solution)/shard_map/ppermute | solution.py:34
  5.4 3.8 %collective-permute-start = (bf16[128,128]{1,0:T(8,128)(2,1)S(1)}, bf16[128,128]{1,0:T(8,128)(2,1)S(1)}, u32[]{:S(2)}, u32[]{:S(2)}) collective-permute-start(bf16[128,128]{1,0:T(8,128)(2,1)S(1)} %get-tuple-element.47.x_ref), channel_id=1, source_target_pairs={{0,6},{1,7},{2,4},{3,5},{4,2},{5,3},{6,0},{7,1},{8,14},{9,15},{10,... | collective-permute-start | bytes 98312 | tf_op jit(solution)/shard_map/ppermute | solution.py:34
  6.7 15.3 %copy-start = (bf16[2048,3,128]{2,0,1:T(8,128)(2,1)S(1)}, bf16[2048,3,128]{2,0,1:T(8,128)(2,1)}, u32[]{:S(2)}) copy-start(bf16[2048,3,128]{2,0,1:T(8,128)(2,1)} %param.13) | copy-start | bytes 4718596
  9.2 6.6 %collective-permute-start.1 = (bf16[256,128]{1,0:T(8,128)(2,1)S(1)}, bf16[256,128]{1,0:T(8,128)(2,1)S(1)}, u32[]{:S(2)}, u32[]{:S(2)}) collective-permute-start(bf16[256,128]{1,0:T(8,128)(2,1)S(1)} %pad_maximum_fusion.2.refs_0_), channel_id=1, source_target_pairs={{0,12},{1,13},{2,14},{3,15},{4,8},{5,9},{6,10},{7,11},{8,4},{9,5},... | collective-permute-start | bytes 196616 | tf_op jit(solution)/shard_map/ppermute | solution.py:34
  12.5 5.1 %collective-permute-start.2 = (bf16[256,128]{1,0:T(8,128)(2,1)S(1)}, bf16[256,128]{1,0:T(8,128)(2,1)S(1)}, u32[]{:S(2)}, u32[]{:S(2)}) collective-permute-start(bf16[256,128]{1,0:T(8,128)(2,1)S(1)} %pad_maximum_fusion.2.refs_0_), channel_id=1, source_target_pairs={{0,8},{1,9},{2,10},{3,11},{4,12},{5,13},{6,14},{7,15},{8,0},{9,1},... | collective-permute-start | bytes 196616 | tf_op jit(solution)/shard_map/ppermute | solution.py:34
  12.5 5.1 %collective-permute-start.3 = (bf16[256,128]{1,0:T(8,128)(2,1)S(1)}, bf16[256,128]{1,0:T(8,128)(2,1)S(1)}, u32[]{:S(2)}, u32[]{:S(2)}) collective-permute-start(bf16[256,128]{1,0:T(8,128)(2,1)S(1)} %pad_maximum_fusion.2.refs_0_), channel_id=1, source_target_pairs={{0,4},{1,5},{2,6},{3,7},{4,0},{5,1},{6,2},{7,3},{8,12},{9,13},{10,... | collective-permute-start | bytes 196616 | tf_op jit(solution)/shard_map/ppermute | solution.py:34
  17.6 3.3 %collective-permute-start.4 = (bf16[256,128]{1,0:T(8,128)(2,1)S(1)}, bf16[256,128]{1,0:T(8,128)(2,1)S(1)}, u32[]{:S(2)}, u32[]{:S(2)}) collective-permute-start(bf16[256,128]{1,0:T(8,128)(2,1)S(1)} %pad_maximum_fusion.2.refs_0_), channel_id=1, source_target_pairs={{0,1},{1,0},{2,3},{3,2},{4,5},{5,4},{6,7},{7,6},{8,9},{9,8},{10,11... | collective-permute-start | bytes 196616 | tf_op jit(solution)/shard_map/ppermute | solution.py:34
  20.0 1.3 %collective-permute-start.5 = (bf16[256,128]{1,0:T(8,128)(2,1)S(1)}, bf16[256,128]{1,0:T(8,128)(2,1)S(1)}, u32[]{:S(2)}, u32[]{:S(2)}) collective-permute-start(bf16[256,128]{1,0:T(8,128)(2,1)S(1)} %collective-permute-done.1.refs_1_), channel_id=1, source_target_pairs={{0,1},{1,0},{2,3},{3,2},{4,5},{5,4},{6,7},{7,6},{8,9},{9,8},{10,11... | collective-permute-start | bytes 196616 | tf_op jit(solution)/shard_map/ppermute | solution.py:34
  20.0 1.4 %collective-permute-start.6 = (bf16[256,128]{1,0:T(8,128)(2,1)S(1)}, bf16[256,128]{1,0:T(8,128)(2,1)S(1)}, u32[]{:S(2)}, u32[]{:S(2)}) collective-permute-start(bf16[256,128]{1,0:T(8,128)(2,1)S(1)} %collective-permute-done.2.refs_2_), channel_id=1, source_target_pairs={{0,1},{1,0},{2,3},{3,2},{4,5},{5,4},{6,7},{7,6},{8,9},{9,8},{10,11... | collective-permute-start | bytes 196616 | tf_op jit(solution)/shard_map/ppermute | solution.py:34
  20.5 1.4 %collective-permute-start.7 = (bf16[256,128]{1,0:T(8,128)(2,1)S(1)}, bf16[256,128]{1,0:T(8,128)(2,1)S(1)}, u32[]{:S(2)}, u32[]{:S(2)}) collective-permute-start(bf16[256,128]{1,0:T(8,128)(2,1)S(1)} %collective-permute-done.3.refs_3_), channel_id=1, source_target_pairs={{0,1},{1,0},{2,3},{3,2},{4,5},{5,4},{6,7},{7,6},{8,9},{9,8},{10,11... | collective-permute-start | bytes 196616 | tf_op jit(solution)/shard_map/ppermute | solution.py:34
  20.9 8.2 %collective-permute-start.11 = (bf16[16,128,128]{2,1,0:T(8,128)(2,1)}, bf16[16,128,128]{2,1,0:T(8,128)(2,1)S(1)}, u32[]{:S(2)}, u32[]{:S(2)}) collective-permute-start(bf16[16,128,128]{2,1,0:T(8,128)(2,1)} %get-tuple-element.68), channel_id=1, source_target_pairs={{0,1},{1,0},{2,3},{3,2},{4,5},{5,4},{6,7},{7,6},{8,9},{9,8},{10,11... | collective-permute-start | bytes 1572872 | tf_op jit(solution)/shard_map/ppermute | solution.py:34
  21.3 7.9 %collective-permute-start.12 = (bf16[16,128,128]{2,1,0:T(8,128)(2,1)}, bf16[16,128,128]{2,1,0:T(8,128)(2,1)S(1)}, u32[]{:S(2)}, u32[]{:S(2)}) collective-permute-start(bf16[16,128,128]{2,1,0:T(8,128)(2,1)} %get-tuple-element.69), channel_id=1, source_target_pairs={{0,1},{1,0},{2,3},{3,2},{4,5},{5,4},{6,7},{7,6},{8,9},{9,8},{10,11... | collective-permute-start | bytes 1572872 | tf_op jit(solution)/shard_map/ppermute | solution.py:34
  21.5 28.2 %collective-permute-start.20 = (bf16[2,16,128,128]{3,2,1,0:T(8,128)(2,1)S(1)}, bf16[2,16,128,128]{3,2,1,0:T(8,128)(2,1)S(1)}, u32[]{:S(2)}, u32[]{:S(2)}) collective-permute-start(bf16[2,16,128,128]{3,2,1,0:T(8,128)(2,1)S(1)} %get-tuple-element.82), channel_id=1, source_target_pairs={{0,3},{1,2},{2,1},{3,0},{4,7},{5,6},{6,5},{7,4},{8,11},{9,10},{10,... | collective-permute-start | bytes 3145736 | tf_op jit(solution)/shard_map/ppermute | solution.py:34
  22.8 1.3 %collective-permute-start.9 = (bf16[1,2,4,40,128]{4,3,1,0,2:T(8,128)(2,1)S(1)}, bf16[1,2,4,40,128]{4,3,1,0,2:T(8,128)(2,1)S(1)}, u32[]{:S(2)}, u32[]{:S(2)}) collective-permute-start(bf16[1,2,4,40,128]{4,3,1,0,2:T(8,128)(2,1)S(1)} %copy.13), channel_id=1, source_target_pairs={{0,1},{1,0},{2,3},{3,2},{4,5},{5,4},{6,7},{7,6},{8,9},{9,8},{10,11... | collective-permute-start | bytes 245768 | tf_op jit(solution)/shard_map/ppermute | solution.py:34
  24.2 4.9 %collective-permute-start.10 = (bf16[2,1,4,40,128]{4,3,1,0,2:T(8,128)(2,1)S(1)}, bf16[2,1,4,40,128]{4,3,1,0,2:T(8,128)(2,1)S(1)}, u32[]{:S(2)}, u32[]{:S(2)}) collective-permute-start(bf16[2,1,4,40,128]{4,3,1,0,2:T(8,128)(2,1)S(1)} %get-tuple-element.97), channel_id=1, source_target_pairs={{0,6},{1,7},{2,4},{3,5},{4,2},{5,3},{6,0},{7,1},{8,14},{9,15},{10,... | collective-permute-start | bytes 245768 | tf_op jit(solution)/shard_map/ppermute | solution.py:34
  29.2 5.9 %collective-permute-start.13 = (bf16[2,2,1,40,128]{4,3,1,0,2:T(8,128)(2,1)S(1)}, bf16[2,2,1,40,128]{4,3,1,0,2:T(8,128)(2,1)S(1)}, u32[]{:S(2)}, u32[]{:S(2)}) collective-permute-start(bf16[2,2,1,40,128]{4,3,1,0,2:T(8,128)(2,1)S(1)} %get-tuple-element.94), channel_id=1, source_target_pairs={{0,12},{1,13},{2,14},{3,15},{4,8},{5,9},{6,10},{7,11},{8,4},{9,5},... | collective-permute-start | bytes 122888 | tf_op jit(solution)/shard_map/ppermute | solution.py:34
  32.0 3.9 %collective-permute-start.14 = (bf16[2,2,1,40,128]{4,3,1,0,2:T(8,128)(2,1)S(1)}, bf16[2,2,1,40,128]{4,3,1,0,2:T(8,128)(2,1)S(1)}, u32[]{:S(2)}, u32[]{:S(2)}) collective-permute-start(bf16[2,2,1,40,128]{4,3,1,0,2:T(8,128)(2,1)S(1)} %get-tuple-element.93), channel_id=1, source_target_pairs={{0,8},{1,9},{2,10},{3,11},{4,12},{5,13},{6,14},{7,15},{8,0},{9,1},... | collective-permute-start | bytes 122888 | tf_op jit(solution)/shard_map/ppermute | solution.py:34
  32.0 3.9 %copy-start.4 = (f32[16,128]{1,0:T(8,128)S(1)}, f32[16,128]{1,0:T(8,128)}, u32[]{:S(2)}) copy-start(f32[16,128]{1,0:T(8,128)} %gate_ref.3) | copy-start | bytes 24580
  32.0 3.9 %copy-start.5 = (f32[2048]{0:T(1024)S(1)}, f32[2048]{0:T(1024)}, u32[]{:S(2)}) copy-start(f32[2048]{0:T(1024)} %param.16) | copy-start | bytes 24580
  32.0 3.9 %copy-start.6 = (f32[16]{0:T(128)S(1)}, f32[16]{0:T(128)}, u32[]{:S(2)}) copy-start(f32[16]{0:T(128)} %bias_ref.3) | copy-start | bytes 196
  32.0 3.8 %collective-permute-start.15 = (bf16[2,2,1,40,128]{4,3,1,0,2:T(8,128)(2,1)S(1)}, bf16[2,2,1,40,128]{4,3,1,0,2:T(8,128)(2,1)S(1)}, u32[]{:S(2)}, u32[]{:S(2)}) collective-permute-start(bf16[2,2,1,40,128]{4,3,1,0,2:T(8,128)(2,1)S(1)} %get-tuple-element.92), channel_id=1, source_target_pairs={{0,4},{1,5},{2,6},{3,7},{4,0},{5,1},{6,2},{7,3},{8,12},{9,13},{10,... | collective-permute-start | bytes 122888 | tf_op jit(solution)/shard_map/ppermute | solution.py:34
  35.0 4.1 %copy-start.7 = (bf16[12,128,128]{2,1,0:T(8,128)(2,1)S(1)}, bf16[12,128,128]{2,1,0:T(8,128)(2,1)}, u32[]{:S(2)}) copy-start(bf16[12,128,128]{2,1,0:T(8,128)(2,1)} %get-tuple-element.88) | copy-start | bytes 1179652
  35.0 4.3 %copy-start.3 = (s32[1,4,32]{2,1,0:T(4,128)S(1)}, s32[1,4,32]{2,1,0:T(4,128)}, u32[]{:S(2)}) copy-start(s32[1,4,32]{2,1,0:T(4,128)} %parent_ref.11) | copy-start | bytes 1540
  37.9 5.3 %collective-permute-start.16 = (bf16[8,2816]{1,0:T(8,128)(2,1)S(1)}, bf16[8,2816]{1,0:T(8,128)(2,1)S(1)}, u32[]{:S(2)}, u32[]{:S(2)}) collective-permute-start(bf16[8,2816]{1,0:T(8,128)(2,1)S(1)} %get-tuple-element.74), channel_id=1, source_target_pairs={{0,6},{1,7},{2,4},{3,5},{4,2},{5,3},{6,0},{7,1},{8,14},{9,15},{10,... | collective-permute-start | bytes 135176 | tf_op jit(solution)/shard_map/ppermute | solution.py:34
  39.1 19.0 %collective-permute-start.25 = (bf16[12,128,128]{2,1,0:T(8,128)(2,1)S(1)}, bf16[12,128,128]{2,1,0:T(8,128)(2,1)S(1)}, u32[]{:S(2)}, u32[]{:S(2)}) collective-permute-start(bf16[12,128,128]{2,1,0:T(8,128)(2,1)S(1)} %copy-done.7), channel_id=1, source_target_pairs={{0,2},{1,3},{2,0},{3,1},{4,6},{5,7},{6,4},{7,5},{8,10},{9,11},{10,... | collective-permute-start | bytes 1179656 | tf_op jit(solution)/shard_map/ppermute | solution.py:34
  43.3 8.5 %collective-permute-start.17 = (bf16[16,2816]{1,0:T(8,128)(2,1)S(1)}, bf16[16,2816]{1,0:T(8,128)(2,1)S(1)}, u32[]{:S(2)}, u32[]{:S(2)}) collective-permute-start(bf16[16,2816]{1,0:T(8,128)(2,1)S(1)} %pad_maximum_fusion.1.refs_0_), channel_id=1, source_target_pairs={{0,12},{1,13},{2,14},{3,15},{4,8},{5,9},{6,10},{7,11},{8,4},{9,5},... | collective-permute-start | bytes 270344 | tf_op jit(solution)/shard_map/ppermute | solution.py:34
  45.2 6.5 %collective-permute-start.18 = (bf16[16,2816]{1,0:T(8,128)(2,1)S(1)}, bf16[16,2816]{1,0:T(8,128)(2,1)S(1)}, u32[]{:S(2)}, u32[]{:S(2)}) collective-permute-start(bf16[16,2816]{1,0:T(8,128)(2,1)S(1)} %pad_maximum_fusion.1.refs_0_), channel_id=1, source_target_pairs={{0,8},{1,9},{2,10},{3,11},{4,12},{5,13},{6,14},{7,15},{8,0},{9,1},... | collective-permute-start | bytes 270344 | tf_op jit(solution)/shard_map/ppermute | solution.py:34
  45.2 6.5 %collective-permute-start.19 = (bf16[16,2816]{1,0:T(8,128)(2,1)S(1)}, bf16[16,2816]{1,0:T(8,128)(2,1)S(1)}, u32[]{:S(2)}, u32[]{:S(2)}) collective-permute-start(bf16[16,2816]{1,0:T(8,128)(2,1)S(1)} %pad_maximum_fusion.1.refs_0_), channel_id=1, source_target_pairs={{0,4},{1,5},{2,6},{3,7},{4,0},{5,1},{6,2},{7,3},{8,12},{9,13},{10,... | collective-permute-start | bytes 270344 | tf_op jit(solution)/shard_map/ppermute | solution.py:34
  49.6 7.2 %copy-start.1 = (bf16[2048,128]{1,0:T(8,128)(2,1)S(1)}, bf16[2048,128]{1,0:T(8,128)(2,1)}, u32[]{:S(2)}) copy-start(bf16[2048,128]{1,0:T(8,128)(2,1)} %weight_ref.1) | copy-start | bytes 1572868
  51.8 4.2 %collective-permute-start.21 = (bf16[16,2816]{1,0:T(8,128)(2,1)S(1)}, bf16[16,2816]{1,0:T(8,128)(2,1)S(1)}, u32[]{:S(2)}, u32[]{:S(2)}) collective-permute-start(bf16[16,2816]{1,0:T(8,128)(2,1)S(1)} %pad_maximum_fusion.1.refs_0_), channel_id=1, source_target_pairs={{0,1},{1,0},{2,3},{3,2},{4,5},{5,4},{6,7},{7,6},{8,9},{9,8},{10,11... | collective-permute-start | bytes 270344 | tf_op jit(solution)/shard_map/ppermute | solution.py:34
  55.1 1.3 %collective-permute-start.22 = (bf16[16,2816]{1,0:T(8,128)(2,1)S(1)}, bf16[16,2816]{1,0:T(8,128)(2,1)S(1)}, u32[]{:S(2)}, u32[]{:S(2)}) collective-permute-start(bf16[16,2816]{1,0:T(8,128)(2,1)S(1)} %collective-permute-done.17.refs_1_), channel_id=1, source_target_pairs={{0,1},{1,0},{2,3},{3,2},{4,5},{5,4},{6,7},{7,6},{8,9},{9,8},{10,11... | collective-permute-start | bytes 270344 | tf_op jit(solution)/shard_map/ppermute | solution.py:34
  55.1 1.4 %collective-permute-start.23 = (bf16[16,2816]{1,0:T(8,128)(2,1)S(1)}, bf16[16,2816]{1,0:T(8,128)(2,1)S(1)}, u32[]{:S(2)}, u32[]{:S(2)}) collective-permute-start(bf16[16,2816]{1,0:T(8,128)(2,1)S(1)} %collective-permute-done.18.refs_2_), channel_id=1, source_target_pairs={{0,1},{1,0},{2,3},{3,2},{4,5},{5,4},{6,7},{7,6},{8,9},{9,8},{10,11... | collective-permute-start | bytes 270344 | tf_op jit(solution)/shard_map/ppermute | solution.py:34
  55.6 1.3 %collective-permute-start.24 = (bf16[16,2816]{1,0:T(8,128)(2,1)S(1)}, bf16[16,2816]{1,0:T(8,128)(2,1)S(1)}, u32[]{:S(2)}, u32[]{:S(2)}) collective-permute-start(bf16[16,2816]{1,0:T(8,128)(2,1)S(1)} %collective-permute-done.19.refs_3_), channel_id=1, source_target_pairs={{0,1},{1,0},{2,3},{3,2},{4,5},{5,4},{6,7},{7,6},{8,9},{9,8},{10,11... | collective-permute-start | bytes 270344 | tf_op jit(solution)/shard_map/ppermute | solution.py:34

commit v8 on v7

--- a/solution.py
+++ b/solution.py
@@ -354,10 +354,14 @@
         rows.append(jnp.concatenate(lines, 1).astype(jnp.bfloat16))
     rest = jnp.dot(jnp.concatenate(rows, 0), weight_ref[...], preferred_element_type=jnp.float32)
     total = x_ref[...].astype(jnp.float32)
+    terms = []
     for _ in range(3):
-        term = rest.astype(jnp.bfloat16)
-        rest = rest - term.astype(jnp.float32)
-        total = total + jnp.dot(pick_ref[...], term, preferred_element_type=jnp.float32)
+        terms.append(rest.astype(jnp.bfloat16))
+        rest = rest - terms[-1].astype(jnp.float32)
+    sums = jnp.dot(pick_ref[...], jnp.concatenate(terms, 1), preferred_element_type=jnp.float32)
+    columns = x_ref.shape[1]
+    for part in range(3):
+        total = total + sums[:, part * columns : (part + 1) * columns]
     out_ref[...] = total.astype(jnp.bfloat16)
 
 
@@ -582,7 +586,7 @@
     held, near_gots = in_vmem(held), [tied["near"], tied["nearer"]]
     sources = [held, *near_gots, tied["first"]]
     normed, by_head = pl.pallas_call(
-        functools.partial(readout_kernel, recv_order, math.gcd(heads, 8), len(sources)),
+        functools.partial(readout_kernel, recv_order, heads, len(sources)),
         in_specs=[SCALARS] * 2 + [WHOLE] * (3 + len(sources) + len(received)),
         out_specs=[WHOLE] * 2,
         out_shape=[

time: 59.8 us -> 59.4 us (level)
  starting transfers between devices: 25.7 us -> 25.1 us
  transfers between devices with their start and end apart: 26 -> 26, of which waited for: 11 -> 11; matrix products, arithmetic and copies ran while one was open for 0% -> 0% of each run, Pallas kernels for 30% -> 29%
where the time goes in v8:
time: 59.4 us; the launch traced here: 58.6 us
  starting transfers between devices  25.1 us (42%)
  Pallas kernels  20.4 us (34%)
  waiting for transfers between devices  11.9 us (20%)
  between operations  0.88 us (1%)
    ppermute x26, starting transfers between devices, xor_permute(): lax.ppermute(block, 'rows', [(i, i ^ distance) for i in range(count)])  25.1 us
    ppermute x26, waiting for transfers between devices, xor_permute(): lax.ppermute(block, 'rows', [(i, i ^ distance) for i in range(count)])  11.9 us
    pallas_call x1, Pallas kernels, per_device(): pl.pallas_call(functools.partial(near_update_kernel, recv_order, head_blo...  3.62 us
    pallas_call x2, Pallas kernels, far_update(): pl.pallas_call(functools.partial(far_update_kernel, far_block, blocks, ow...  3 us
    pallas_call x1, Pallas kernels, per_device(): pl.pallas_call(functools.partial(stage_kernel, blocks, normed_order), in_...  2.93 us
    pallas_call x1, Pallas kernels, per_device(): pl.pallas_call(functools.partial(fetch_kernel, blocks), in_specs=[SCALARS...  2.81 us
    pallas_call x1, Pallas kernels, per_device(): pl.pallas_call(hold_kernel, in_specs=[PLACED], out_specs=WHOLE, out_shape...  2.21 us
    pallas_call x1, Pallas kernels, per_device(): pl.pallas_call(functools.partial(pick_kernel, blocks, piece, recv_order),...  2.08 us
  transfers between devices with their start and end apart: 26, of which 11 were waited for; matrix products, arithmetic and copies ran while one was open for 0% of the time, Pallas kernels for 29%

profile of v8, /device:TPU:1, one launch (start us, length us, event | category | flops | bytes accessed | tf_op | source)
XLA Modules:
  0.0 58.6 jit_solution(11203401897494292515)
XLA Ops:
  0.6 0.0 copy-start.2
  0.6 2.8 %fetch.1 = (bf16[128,128]{1,0:T(8,128)(2,1)S(1)}, bf16[20,128,128]{2,1,0:T(8,128)(2,1)S(1)}) custom-call(s32[1]{0:T(128)} %bitcast.me_ref, s32[1,4,32]{2,1,0:T(4,128)} %parent_ref.11, s32[1,128]{1,0:T(1,128)} %tokens_ref.1, s32[1,128]{1,0:T(1,128)} %tokens_ref.1, bf16[32768,128]{1,0:T(8,128)(2,1)} %table_ref.1, bf16[8,16,128,128]{3,2,1,0:T(8,128)(2,1)} %states_ref.7), custom_call_target="tpu_custom_call" | custom-call | tf_op jit(solution)/shard_map/fetch/pallas_call | solution.py:494
  3.5 2.1 %collective-permute-start.8 = (bf16[20,128,128]{2,1,0:T(8,128)(2,1)S(1)}, bf16[20,128,128]{2,1,0:T(8,128)(2,1)S(1)}, u32[]{:S(2)}, u32[]{:S(2)}) collective-permute-start(bf16[20,128,128]{2,1,0:T(8,128)(2,1)S(1)} %get-tuple-element.59), channel_id=1, source_target_pairs={{0,2},{1,3},{2,0},{3,1},{4,6},{5,7},{6,4},{7,5},{8,10},{9,11},{10,... | collective-permute-start | bytes 1966088 | tf_op jit(solution)/shard_map/ppermute | solution.py:34
  5.6 1.2 %collective-permute-start = (bf16[128,128]{1,0:T(8,128)(2,1)S(1)}, bf16[128,128]{1,0:T(8,128)(2,1)S(1)}, u32[]{:S(2)}, u32[]{:S(2)}) collective-permute-start(bf16[128,128]{1,0:T(8,128)(2,1)S(1)} %get-tuple-element.47.x_ref), channel_id=1, source_target_pairs={{0,6},{1,7},{2,4},{3,5},{4,2},{5,3},{6,0},{7,1},{8,14},{9,15},{10,... | collective-permute-start | bytes 98312 | tf_op jit(solution)/shard_map/ppermute | solution.py:34
  6.8 0.1 broadcast_in_dim.14
  6.9 2.1 %pick.1 = (bf16[640,384]{1,0:T(8,128)(2,1)S(1)}, bf16[2,16,128,128]{3,2,1,0:T(8,128)(2,1)S(1)}) custom-call(s32[1]{0:T(128)} %bitcast.me_ref, s32[1,4,32]{2,1,0:T(4,128)} %parent_ref.11, s32[8,128]{1,0:T(8,128)S(1)} %broadcast_in_dim.15.parents_ref, bf16[8,16,128,128]{3,2,1,0:T(8,128)(2,1)} %states_ref.7), custom_call_target="tpu_custom_call" | custom-call | tf_op jit(solution)/shard_map/pick/pallas_call | solution.py:509
  9.0 0.4 collective-permute-done
  9.4 3.3 %collective-permute-start.1 = (bf16[256,128]{1,0:T(8,128)(2,1)S(1)}, bf16[256,128]{1,0:T(8,128)(2,1)S(1)}, u32[]{:S(2)}, u32[]{:S(2)}) collective-permute-start(bf16[256,128]{1,0:T(8,128)(2,1)S(1)} %pad_maximum_fusion.2.refs_0_), channel_id=1, source_target_pairs={{0,12},{1,13},{2,14},{3,15},{4,8},{5,9},{6,10},{7,11},{8,4},{9,5},... | collective-permute-start | bytes 196616 | tf_op jit(solution)/shard_map/ppermute | solution.py:34
  12.7 0.0 collective-permute-start.2
  12.7 0.4 collective-permute-start.3
  13.0 2.9 %stage.1 = (bf16[16,128,128]{2,1,0:T(8,128)(2,1)}, bf16[16,128,128]{2,1,0:T(8,128)(2,1)}, bf16[12,128,128]{2,1,0:T(8,128)(2,1)}, f32[16,128]{1,0:T(8,128)S(1)}, bf16[128,176]{1,0:T(8,128)(2,1)S(1)}) custom-call(s32[1]{0:T(128)} %bitcast.me_ref, s32[1,4,32]{2,1,0:T(4,128)} %parent_ref.11, s32[8,128]{1,0:T(8,128)S(1)} %broadcast_in_dim.15.parents_ref, ...), custom_call_target="tpu_custom_call" | custom-call | tf_op jit(solution)/shard_map/stage/pallas_call | solution.py:520
  16.0 1.8 %collective-permute-done.2.refs_2_ = bf16[256,128]{1,0:T(8,128)(2,1)S(1)} collective-permute-done((bf16[256,128]{1,0:T(8,128)(2,1)S(1)}, bf16[256,128]{1,0:T(8,128)(2,1)S(1)}, u32[]{:S(2)}, u32[]{:S(2)}) %collective-permute-start.2) | collective-permute-done | bytes 65568 | tf_op jit(solution)/shard_map/ppermute | solution.py:34
  17.8 2.4 %collective-permute-start.4 = (bf16[256,128]{1,0:T(8,128)(2,1)S(1)}, bf16[256,128]{1,0:T(8,128)(2,1)S(1)}, u32[]{:S(2)}, u32[]{:S(2)}) collective-permute-start(bf16[256,128]{1,0:T(8,128)(2,1)S(1)} %pad_maximum_fusion.2.refs_0_), channel_id=1, source_target_pairs={{0,1},{1,0},{2,3},{3,2},{4,5},{5,4},{6,7},{7,6},{8,9},{9,8},{10,11... | collective-permute-start | bytes 196616 | tf_op jit(solution)/shard_map/ppermute | solution.py:34
  20.2 0.0 collective-permute-start.5
  20.3 0.5 collective-permute-start.6
  20.8 0.0 collective-permute-start.7
  20.8 0.4 collective-permute-done.4.refs_4_
  21.2 0.4 collective-permute-start.11
  21.5 0.2 collective-permute-start.12
  21.7 0.5 collective-permute-start.20
  22.2 0.8 %project.1 = bf16[640,128]{1,0:T(8,128)(2,1)S(1)} custom-call(s32[1]{0:T(128)} %bitcast.me_ref, bf16[3,2048,128]{2,1,0:T(8,128)(2,1)S(1)} %bitcast.11, bf16[640,384]{1,0:T(8,128)(2,1)S(1)} %get-tuple-element.54.pick_ref, bf16[256,128]{1,0:T(8,128)(2,1)S(1)} %pad_maximum_fusion.2.refs_0_, bf16[256,128]{1,0:T(8,128)(2,1)S(1)} %collective-permute-done.1.refs_1_, ...), custom_call_target="tpu_custom_call" | custom-call | tf_op jit(solution)/shard_map/project/pallas_call | solution.py:564
  23.0 0.2 collective-permute-start.9
  23.3 1.1 %collective-permute-done.9 = bf16[1,2,4,40,128]{4,3,1,0,2:T(8,128)(2,1)S(1)} collective-permute-done((bf16[1,2,4,40,128]{4,3,1,0,2:T(8,128)(2,1)S(1)}, bf16[1,2,4,40,128]{4,3,1,0,2:T(8,128)(2,1)S(1)}, u32[]{:S(2)}, u32[]{:S(2)}) %collective-permute-start.9) | collective-permute-done | bytes 81952 | tf_op jit(solution)/shard_map/ppermute | solution.py:34
  24.4 2.0 %collective-permute-start.10 = (bf16[2,1,4,40,128]{4,3,1,0,2:T(8,128)(2,1)S(1)}, bf16[2,1,4,40,128]{4,3,1,0,2:T(8,128)(2,1)S(1)}, u32[]{:S(2)}, u32[]{:S(2)}) collective-permute-start(bf16[2,1,4,40,128]{4,3,1,0,2:T(8,128)(2,1)S(1)} %get-tuple-element.97), channel_id=1, source_target_pairs={{0,6},{1,7},{2,4},{3,5},{4,2},{5,3},{6,0},{7,1},{8,14},{9,15},{10,... | collective-permute-start | bytes 245768 | tf_op jit(solution)/shard_map/ppermute | solution.py:34
  26.4 2.9 %collective-permute-done.10 = bf16[2,1,4,40,128]{4,3,1,0,2:T(8,128)(2,1)S(1)} collective-permute-done((bf16[2,1,4,40,128]{4,3,1,0,2:T(8,128)(2,1)S(1)}, bf16[2,1,4,40,128]{4,3,1,0,2:T(8,128)(2,1)S(1)}, u32[]{:S(2)}, u32[]{:S(2)}) %collective-permute-start.10) | collective-permute-done | bytes 81952 | tf_op jit(solution)/shard_map/ppermute | solution.py:34
  29.4 2.8 %collective-permute-start.13 = (bf16[2,2,1,40,128]{4,3,1,0,2:T(8,128)(2,1)S(1)}, bf16[2,2,1,40,128]{4,3,1,0,2:T(8,128)(2,1)S(1)}, u32[]{:S(2)}, u32[]{:S(2)}) collective-permute-start(bf16[2,2,1,40,128]{4,3,1,0,2:T(8,128)(2,1)S(1)} %get-tuple-element.94), channel_id=1, source_target_pairs={{0,12},{1,13},{2,14},{3,15},{4,8},{5,9},{6,10},{7,11},{8,4},{9,5},... | collective-permute-start | bytes 122888 | tf_op jit(solution)/shard_map/ppermute | solution.py:34
  32.2 0.8 %collective-permute-start.15 = (bf16[2,2,1,40,128]{4,3,1,0,2:T(8,128)(2,1)S(1)}, bf16[2,2,1,40,128]{4,3,1,0,2:T(8,128)(2,1)S(1)}, u32[]{:S(2)}, u32[]{:S(2)}) collective-permute-start(bf16[2,2,1,40,128]{4,3,1,0,2:T(8,128)(2,1)S(1)} %get-tuple-element.92), channel_id=1, source_target_pairs={{0,4},{1,5},{2,6},{3,7},{4,0},{5,1},{6,2},{7,3},{8,12},{9,13},{10,... | collective-permute-start | bytes 122888 | tf_op jit(solution)/shard_map/ppermute | solution.py:34
  33.0 2.2 %hold.1.refs_0_.states_ref = bf16[8,16,128,128]{3,2,1,0:T(8,128)(2,1)S(1)} custom-call(bf16[8,16,128,128]{3,2,1,0:T(8,128)(2,1)} %states_ref.7), custom_call_target="tpu_custom_call" | custom-call | tf_op jit(solution)/shard_map/hold/pallas_call | solution.py:541
  35.2 0.0 copy-start.3
  35.3 0.8 %collective-permute-done.14 = bf16[2,2,1,40,128]{4,3,1,0,2:T(8,128)(2,1)S(1)} collective-permute-done((bf16[2,2,1,40,128]{4,3,1,0,2:T(8,128)(2,1)S(1)}, bf16[2,2,1,40,128]{4,3,1,0,2:T(8,128)(2,1)S(1)}, u32[]{:S(2)}, u32[]{:S(2)}) %collective-permute-start.14) | collective-permute-done | bytes 40992 | tf_op jit(solution)/shard_map/ppermute | solution.py:34
  36.0 1.8 %readout.1 = (bf16[8,2816]{1,0:T(8,128)(2,1)S(1)}, bf16[16,40,128]{2,1,0:T(8,128)(2,1)S(1)}) custom-call(s32[1]{0:T(128)} %bitcast.me_ref, f32[16]{0:T(128)S(1)} %copy-done.6, f32[16,128]{1,0:T(8,128)S(1)} %get-tuple-element.52.place_ref, f32[16,128]{1,0:T(8,128)S(1)} %copy-done.4, f32[16,128]{1,0:T(8,128)S(1)} %bitcast.17, ...), custom_call_target="tpu_custom_call" | custom-call | tf_op jit(solution)/shard_map/readout/pallas_call | solution.py:588
  37.9 1.2 %collective-permute-start.16 = (bf16[8,2816]{1,0:T(8,128)(2,1)S(1)}, bf16[8,2816]{1,0:T(8,128)(2,1)S(1)}, u32[]{:S(2)}, u32[]{:S(2)}) collective-permute-start(bf16[8,2816]{1,0:T(8,128)(2,1)S(1)} %get-tuple-element.74), channel_id=1, source_target_pairs={{0,6},{1,7},{2,4},{3,5},{4,2},{5,3},{6,0},{7,1},{8,14},{9,15},{10,... | collective-permute-start | bytes 135176 | tf_op jit(solution)/shard_map/ppermute | solution.py:34
  39.1 0.2 collective-permute-start.25
  39.3 3.6 %near_update.1 = (bf16[8,16,128,128]{3,2,1,0:T(8,128)(2,1)}, bf16[16,128,16]{2,1,0:T(8,128)(2,1)S(1)}, f32[16,16,128]{2,1,0:T(8,128)S(1)}, f32[2,16,16,128]{3,2,1,0:T(8,128)S(1)}) custom-call(s32[1]{0:T(128)} %bitcast.me_ref, s32[1,4,32]{2,1,0:T(4,128)S(1)} %copy-done.3, f32[16]{0:T(128)S(1)} %copy-done.6, ...), custom_call_target="tpu_custom_call" | custom-call | tf_op jit(solution)/shard_map/near_update/pallas_call | solution.py:601
  42.9 3.0 %collective-permute-start.17 = (bf16[16,2816]{1,0:T(8,128)(2,1)S(1)}, bf16[16,2816]{1,0:T(8,128)(2,1)S(1)}, u32[]{:S(2)}, u32[]{:S(2)}) collective-permute-start(bf16[16,2816]{1,0:T(8,128)(2,1)S(1)} %pad_maximum_fusion.1.refs_0_), channel_id=1, source_target_pairs={{0,12},{1,13},{2,14},{3,15},{4,8},{5,9},{6,10},{7,11},{8,4},{9,5},... | collective-permute-start | bytes 270344 | tf_op jit(solution)/shard_map/ppermute | solution.py:34
  46.0 0.6 %collective-permute-start.19 = (bf16[16,2816]{1,0:T(8,128)(2,1)S(1)}, bf16[16,2816]{1,0:T(8,128)(2,1)S(1)}, u32[]{:S(2)}, u32[]{:S(2)}) collective-permute-start(bf16[16,2816]{1,0:T(8,128)(2,1)S(1)} %pad_maximum_fusion.1.refs_0_), channel_id=1, source_target_pairs={{0,4},{1,5},{2,6},{3,7},{4,0},{5,1},{6,2},{7,3},{8,12},{9,13},{10,... | collective-permute-start | bytes 270344 | tf_op jit(solution)/shard_map/ppermute | solution.py:34
  46.6 3.3 %collective-permute-done.20 = bf16[2,16,128,128]{3,2,1,0:T(8,128)(2,1)S(1)} collective-permute-done((bf16[2,16,128,128]{3,2,1,0:T(8,128)(2,1)S(1)}, bf16[2,16,128,128]{3,2,1,0:T(8,128)(2,1)S(1)}, u32[]{:S(2)}, u32[]{:S(2)}) %collective-permute-start.20) | collective-permute-done | bytes 1048608 | tf_op jit(solution)/shard_map/ppermute | solution.py:34
  49.9 2.4 %far_update.1.refs_1_ = bf16[8,16,128,128]{3,2,1,0:T(8,128)(2,1)} custom-call(s32[1]{0:T(128)} %bitcast.me_ref, s32[1,4,32]{2,1,0:T(4,128)S(1)} %copy-done.3, bf16[16,128,16]{2,1,0:T(8,128)(2,1)S(1)} %get-tuple-element.79.turned_ref, f32[16,16,128]{2,1,0:T(8,128)S(1)} %get-tuple-element.80.values_ref, ...), custom_call_target="tpu_custom_call", output_to_operand_aliasing={{}: (9, {})} | custom-call | tf_op jit(solution)/shard_map/far_update/pallas_call | solution.py:619
  52.3 2.8 %collective-permute-start.21 = (bf16[16,2816]{1,0:T(8,128)(2,1)S(1)}, bf16[16,2816]{1,0:T(8,128)(2,1)S(1)}, u32[]{:S(2)}, u32[]{:S(2)}) collective-permute-start(bf16[16,2816]{1,0:T(8,128)(2,1)S(1)} %pad_maximum_fusion.1.refs_0_), channel_id=1, source_target_pairs={{0,1},{1,0},{2,3},{3,2},{4,5},{5,4},{6,7},{7,6},{8,9},{9,8},{10,11... | collective-permute-start | bytes 270344 | tf_op jit(solution)/shard_map/ppermute | solution.py:34
  55.0 0.0 collective-permute-start.22
  55.0 0.5 collective-permute-start.23
  55.5 0.0 collective-permute-start.24
  55.5 0.4 collective-permute-done.21.refs_4_
  56.0 0.4 collective-permute-done.22.refs_5_
  56.3 0.2 collective-permute-done.23.refs_6_
  56.5 0.4 collective-permute-done.24.refs_7_
  56.8 1.1 %output.1 = bf16[128,128]{1,0:T(8,128)(2,1)} custom-call(bf16[128,128]{1,0:T(8,128)(2,1)S(1)} %get-tuple-element.47.x_ref, bf16[2048,128]{1,0:T(8,128)(2,1)S(1)} %copy-done.1, bf16[128,176]{1,0:T(8,128)(2,1)S(1)} %get-tuple-element.48.pick_ref, bf16[16,2816]{1,0:T(8,128)(2,1)S(1)} %pad_maximum_fusion.1.refs_0_, ...), custom_call_target="tpu_custom_call" | custom-call | tf_op jit(solution)/shard_map/output/pallas_call | solution.py:647
  58.0 0.6 %last_update.1 = bf16[8,16,128,128]{3,2,1,0:T(8,128)(2,1)} custom-call(s32[1]{0:T(128)} %bitcast.me_ref, s32[1,4,32]{2,1,0:T(4,128)S(1)} %copy-done.3, bf16[16,128,16]{2,1,0:T(8,128)(2,1)S(1)} %get-tuple-element.79.turned_ref, f32[16,16,128]{2,1,0:T(8,128)S(1)} %get-tuple-element.80.values_ref, ...), custom_call_target="tpu_custom_call", output_to_operand_aliasing={{}: (6, {})} | custom-call | tf_op jit(solution)/shard_map/last_update/pallas_call | solution.py:619
  (41 shorter events, 0.2 us)
Async XLA Ops:
  0.6 6.2 %copy-start.2 = (s32[1,4,32]{2,1,0:T(4,128)S(1)}, s32[1,4,32]{2,1,0:T(4,128)}, u32[]{:S(2)}) copy-start(s32[1,4,32]{2,1,0:T(4,128)} %parent_ref.11) | copy-start | bytes 1540
  3.5 18.7 %collective-permute-start.8 = (bf16[20,128,128]{2,1,0:T(8,128)(2,1)S(1)}, bf16[20,128,128]{2,1,0:T(8,128)(2,1)S(1)}, u32[]{:S(2)}, u32[]{:S(2)}) collective-permute-start(bf16[20,128,128]{2,1,0:T(8,128)(2,1)S(1)} %get-tuple-element.59), channel_id=1, source_target_pairs={{0,2},{1,3},{2,0},{3,1},{4,6},{5,7},{6,4},{7,5},{8,10},{9,11},{10,... | collective-permute-start | bytes 1966088 | tf_op jit(solution)/shard_map/ppermute | solution.py:34
  5.6 3.8 %collective-permute-start = (bf16[128,128]{1,0:T(8,128)(2,1)S(1)}, bf16[128,128]{1,0:T(8,128)(2,1)S(1)}, u32[]{:S(2)}, u32[]{:S(2)}) collective-permute-start(bf16[128,128]{1,0:T(8,128)(2,1)S(1)} %get-tuple-element.47.x_ref), channel_id=1, source_target_pairs={{0,6},{1,7},{2,4},{3,5},{4,2},{5,3},{6,0},{7,1},{8,14},{9,15},{10,... | collective-permute-start | bytes 98312 | tf_op jit(solution)/shard_map/ppermute | solution.py:34
  6.9 15.2 %copy-start = (bf16[2048,3,128]{2,0,1:T(8,128)(2,1)S(1)}, bf16[2048,3,128]{2,0,1:T(8,128)(2,1)}, u32[]{:S(2)}) copy-start(bf16[2048,3,128]{2,0,1:T(8,128)(2,1)} %param.13) | copy-start | bytes 4718596
  9.4 6.6 %collective-permute-start.1 = (bf16[256,128]{1,0:T(8,128)(2,1)S(1)}, bf16[256,128]{1,0:T(8,128)(2,1)S(1)}, u32[]{:S(2)}, u32[]{:S(2)}) collective-permute-start(bf16[256,128]{1,0:T(8,128)(2,1)S(1)} %pad_maximum_fusion.2.refs_0_), channel_id=1, source_target_pairs={{0,12},{1,13},{2,14},{3,15},{4,8},{5,9},{6,10},{7,11},{8,4},{9,5},... | collective-permute-start | bytes 196616 | tf_op jit(solution)/shard_map/ppermute | solution.py:34
  12.7 5.1 %collective-permute-start.2 = (bf16[256,128]{1,0:T(8,128)(2,1)S(1)}, bf16[256,128]{1,0:T(8,128)(2,1)S(1)}, u32[]{:S(2)}, u32[]{:S(2)}) collective-permute-start(bf16[256,128]{1,0:T(8,128)(2,1)S(1)} %pad_maximum_fusion.2.refs_0_), channel_id=1, source_target_pairs={{0,8},{1,9},{2,10},{3,11},{4,12},{5,13},{6,14},{7,15},{8,0},{9,1},... | collective-permute-start | bytes 196616 | tf_op jit(solution)/shard_map/ppermute | solution.py:34
  12.7 5.1 %collective-permute-start.3 = (bf16[256,128]{1,0:T(8,128)(2,1)S(1)}, bf16[256,128]{1,0:T(8,128)(2,1)S(1)}, u32[]{:S(2)}, u32[]{:S(2)}) collective-permute-start(bf16[256,128]{1,0:T(8,128)(2,1)S(1)} %pad_maximum_fusion.2.refs_0_), channel_id=1, source_target_pairs={{0,4},{1,5},{2,6},{3,7},{4,0},{5,1},{6,2},{7,3},{8,12},{9,13},{10,... | collective-permute-start | bytes 196616 | tf_op jit(solution)/shard_map/ppermute | solution.py:34
  17.8 3.3 %collective-permute-start.4 = (bf16[256,128]{1,0:T(8,128)(2,1)S(1)}, bf16[256,128]{1,0:T(8,128)(2,1)S(1)}, u32[]{:S(2)}, u32[]{:S(2)}) collective-permute-start(bf16[256,128]{1,0:T(8,128)(2,1)S(1)} %pad_maximum_fusion.2.refs_0_), channel_id=1, source_target_pairs={{0,1},{1,0},{2,3},{3,2},{4,5},{5,4},{6,7},{7,6},{8,9},{9,8},{10,11... | collective-permute-start | bytes 196616 | tf_op jit(solution)/shard_map/ppermute | solution.py:34
  20.2 1.3 %collective-permute-start.5 = (bf16[256,128]{1,0:T(8,128)(2,1)S(1)}, bf16[256,128]{1,0:T(8,128)(2,1)S(1)}, u32[]{:S(2)}, u32[]{:S(2)}) collective-permute-start(bf16[256,128]{1,0:T(8,128)(2,1)S(1)} %collective-permute-done.1.refs_1_), channel_id=1, source_target_pairs={{0,1},{1,0},{2,3},{3,2},{4,5},{5,4},{6,7},{7,6},{8,9},{9,8},{10,11... | collective-permute-start | bytes 196616 | tf_op jit(solution)/shard_map/ppermute | solution.py:34
  20.3 1.4 %collective-permute-start.6 = (bf16[256,128]{1,0:T(8,128)(2,1)S(1)}, bf16[256,128]{1,0:T(8,128)(2,1)S(1)}, u32[]{:S(2)}, u32[]{:S(2)}) collective-permute-start(bf16[256,128]{1,0:T(8,128)(2,1)S(1)} %collective-permute-done.2.refs_2_), channel_id=1, source_target_pairs={{0,1},{1,0},{2,3},{3,2},{4,5},{5,4},{6,7},{7,6},{8,9},{9,8},{10,11... | collective-permute-start | bytes 196616 | tf_op jit(solution)/shard_map/ppermute | solution.py:34
  20.8 1.4 %collective-permute-start.7 = (bf16[256,128]{1,0:T(8,128)(2,1)S(1)}, bf16[256,128]{1,0:T(8,128)(2,1)S(1)}, u32[]{:S(2)}, u32[]{:S(2)}) collective-permute-start(bf16[256,128]{1,0:T(8,128)(2,1)S(1)} %collective-permute-done.3.refs_3_), channel_id=1, source_target_pairs={{0,1},{1,0},{2,3},{3,2},{4,5},{5,4},{6,7},{7,6},{8,9},{9,8},{10,11... | collective-permute-start | bytes 196616 | tf_op jit(solution)/shard_map/ppermute | solution.py:34
  21.2 8.2 %collective-permute-start.11 = (bf16[16,128,128]{2,1,0:T(8,128)(2,1)}, bf16[16,128,128]{2,1,0:T(8,128)(2,1)S(1)}, u32[]{:S(2)}, u32[]{:S(2)}) collective-permute-start(bf16[16,128,128]{2,1,0:T(8,128)(2,1)} %get-tuple-element.68), channel_id=1, source_target_pairs={{0,1},{1,0},{2,3},{3,2},{4,5},{5,4},{6,7},{7,6},{8,9},{9,8},{10,11... | collective-permute-start | bytes 1572872 | tf_op jit(solution)/shard_map/ppermute | solution.py:34
  21.5 7.8 %collective-permute-start.12 = (bf16[16,128,128]{2,1,0:T(8,128)(2,1)}, bf16[16,128,128]{2,1,0:T(8,128)(2,1)S(1)}, u32[]{:S(2)}, u32[]{:S(2)}) collective-permute-start(bf16[16,128,128]{2,1,0:T(8,128)(2,1)} %get-tuple-element.69), channel_id=1, source_target_pairs={{0,1},{1,0},{2,3},{3,2},{4,5},{5,4},{6,7},{7,6},{8,9},{9,8},{10,11... | collective-permute-start | bytes 1572872 | tf_op jit(solution)/shard_map/ppermute | solution.py:34
  21.7 28.2 %collective-permute-start.20 = (bf16[2,16,128,128]{3,2,1,0:T(8,128)(2,1)S(1)}, bf16[2,16,128,128]{3,2,1,0:T(8,128)(2,1)S(1)}, u32[]{:S(2)}, u32[]{:S(2)}) collective-permute-start(bf16[2,16,128,128]{3,2,1,0:T(8,128)(2,1)S(1)} %get-tuple-element.82), channel_id=1, source_target_pairs={{0,3},{1,2},{2,1},{3,0},{4,7},{5,6},{6,5},{7,4},{8,11},{9,10},{10,... | collective-permute-start | bytes 3145736 | tf_op jit(solution)/shard_map/ppermute | solution.py:34
  23.0 1.3 %collective-permute-start.9 = (bf16[1,2,4,40,128]{4,3,1,0,2:T(8,128)(2,1)S(1)}, bf16[1,2,4,40,128]{4,3,1,0,2:T(8,128)(2,1)S(1)}, u32[]{:S(2)}, u32[]{:S(2)}) collective-permute-start(bf16[1,2,4,40,128]{4,3,1,0,2:T(8,128)(2,1)S(1)} %copy.13), channel_id=1, source_target_pairs={{0,1},{1,0},{2,3},{3,2},{4,5},{5,4},{6,7},{7,6},{8,9},{9,8},{10,11... | collective-permute-start | bytes 245768 | tf_op jit(solution)/shard_map/ppermute | solution.py:34
  24.4 4.9 %collective-permute-start.10 = (bf16[2,1,4,40,128]{4,3,1,0,2:T(8,128)(2,1)S(1)}, bf16[2,1,4,40,128]{4,3,1,0,2:T(8,128)(2,1)S(1)}, u32[]{:S(2)}, u32[]{:S(2)}) collective-permute-start(bf16[2,1,4,40,128]{4,3,1,0,2:T(8,128)(2,1)S(1)} %get-tuple-element.97), channel_id=1, source_target_pairs={{0,6},{1,7},{2,4},{3,5},{4,2},{5,3},{6,0},{7,1},{8,14},{9,15},{10,... | collective-permute-start | bytes 245768 | tf_op jit(solution)/shard_map/ppermute | solution.py:34
  29.4 5.9 %collective-permute-start.13 = (bf16[2,2,1,40,128]{4,3,1,0,2:T(8,128)(2,1)S(1)}, bf16[2,2,1,40,128]{4,3,1,0,2:T(8,128)(2,1)S(1)}, u32[]{:S(2)}, u32[]{:S(2)}) collective-permute-start(bf16[2,2,1,40,128]{4,3,1,0,2:T(8,128)(2,1)S(1)} %get-tuple-element.94), channel_id=1, source_target_pairs={{0,12},{1,13},{2,14},{3,15},{4,8},{5,9},{6,10},{7,11},{8,4},{9,5},... | collective-permute-start | bytes 122888 | tf_op jit(solution)/shard_map/ppermute | solution.py:34
  32.2 3.8 %collective-permute-start.14 = (bf16[2,2,1,40,128]{4,3,1,0,2:T(8,128)(2,1)S(1)}, bf16[2,2,1,40,128]{4,3,1,0,2:T(8,128)(2,1)S(1)}, u32[]{:S(2)}, u32[]{:S(2)}) collective-permute-start(bf16[2,2,1,40,128]{4,3,1,0,2:T(8,128)(2,1)S(1)} %get-tuple-element.93), channel_id=1, source_target_pairs={{0,8},{1,9},{2,10},{3,11},{4,12},{5,13},{6,14},{7,15},{8,0},{9,1},... | collective-permute-start | bytes 122888 | tf_op jit(solution)/shard_map/ppermute | solution.py:34
  32.2 3.8 %copy-start.4 = (f32[16,128]{1,0:T(8,128)S(1)}, f32[16,128]{1,0:T(8,128)}, u32[]{:S(2)}) copy-start(f32[16,128]{1,0:T(8,128)} %gate_ref.3) | copy-start | bytes 24580
  32.2 3.8 %copy-start.5 = (f32[2048]{0:T(1024)S(1)}, f32[2048]{0:T(1024)}, u32[]{:S(2)}) copy-start(f32[2048]{0:T(1024)} %param.16) | copy-start | bytes 24580
  32.2 3.8 %copy-start.6 = (f32[16]{0:T(128)S(1)}, f32[16]{0:T(128)}, u32[]{:S(2)}) copy-start(f32[16]{0:T(128)} %bias_ref.3) | copy-start | bytes 196
  32.2 3.8 %collective-permute-start.15 = (bf16[2,2,1,40,128]{4,3,1,0,2:T(8,128)(2,1)S(1)}, bf16[2,2,1,40,128]{4,3,1,0,2:T(8,128)(2,1)S(1)}, u32[]{:S(2)}, u32[]{:S(2)}) collective-permute-start(bf16[2,2,1,40,128]{4,3,1,0,2:T(8,128)(2,1)S(1)} %get-tuple-element.92), channel_id=1, source_target_pairs={{0,4},{1,5},{2,6},{3,7},{4,0},{5,1},{6,2},{7,3},{8,12},{9,13},{10,... | collective-permute-start | bytes 122888 | tf_op jit(solution)/shard_map/ppermute | solution.py:34
  35.2 3.8 %copy-start.7 = (bf16[12,128,128]{2,1,0:T(8,128)(2,1)S(1)}, bf16[12,128,128]{2,1,0:T(8,128)(2,1)}, u32[]{:S(2)}) copy-start(bf16[12,128,128]{2,1,0:T(8,128)(2,1)} %get-tuple-element.88) | copy-start | bytes 1179652
  35.2 4.1 %copy-start.3 = (s32[1,4,32]{2,1,0:T(4,128)S(1)}, s32[1,4,32]{2,1,0:T(4,128)}, u32[]{:S(2)}) copy-start(s32[1,4,32]{2,1,0:T(4,128)} %parent_ref.11) | copy-start | bytes 1540
  37.9 5.1 %collective-permute-start.16 = (bf16[8,2816]{1,0:T(8,128)(2,1)S(1)}, bf16[8,2816]{1,0:T(8,128)(2,1)S(1)}, u32[]{:S(2)}, u32[]{:S(2)}) collective-permute-start(bf16[8,2816]{1,0:T(8,128)(2,1)S(1)} %get-tuple-element.74), channel_id=1, source_target_pairs={{0,6},{1,7},{2,4},{3,5},{4,2},{5,3},{6,0},{7,1},{8,14},{9,15},{10,... | collective-permute-start | bytes 135176 | tf_op jit(solution)/shard_map/ppermute | solution.py:34
  39.1 18.9 %collective-permute-start.25 = (bf16[12,128,128]{2,1,0:T(8,128)(2,1)S(1)}, bf16[12,128,128]{2,1,0:T(8,128)(2,1)S(1)}, u32[]{:S(2)}, u32[]{:S(2)}) collective-permute-start(bf16[12,128,128]{2,1,0:T(8,128)(2,1)S(1)} %copy-done.7), channel_id=1, source_target_pairs={{0,2},{1,3},{2,0},{3,1},{4,6},{5,7},{6,4},{7,5},{8,10},{9,11},{10,... | collective-permute-start | bytes 1179656 | tf_op jit(solution)/shard_map/ppermute | solution.py:34
  42.9 9.3 %collective-permute-start.17 = (bf16[16,2816]{1,0:T(8,128)(2,1)S(1)}, bf16[16,2816]{1,0:T(8,128)(2,1)S(1)}, u32[]{:S(2)}, u32[]{:S(2)}) collective-permute-start(bf16[16,2816]{1,0:T(8,128)(2,1)S(1)} %pad_maximum_fusion.1.refs_0_), channel_id=1, source_target_pairs={{0,12},{1,13},{2,14},{3,15},{4,8},{5,9},{6,10},{7,11},{8,4},{9,5},... | collective-permute-start | bytes 270344 | tf_op jit(solution)/shard_map/ppermute | solution.py:34
  46.0 6.3 %collective-permute-start.18 = (bf16[16,2816]{1,0:T(8,128)(2,1)S(1)}, bf16[16,2816]{1,0:T(8,128)(2,1)S(1)}, u32[]{:S(2)}, u32[]{:S(2)}) collective-permute-start(bf16[16,2816]{1,0:T(8,128)(2,1)S(1)} %pad_maximum_fusion.1.refs_0_), channel_id=1, source_target_pairs={{0,8},{1,9},{2,10},{3,11},{4,12},{5,13},{6,14},{7,15},{8,0},{9,1},... | collective-permute-start | bytes 270344 | tf_op jit(solution)/shard_map/ppermute | solution.py:34
  46.0 6.3 %collective-permute-start.19 = (bf16[16,2816]{1,0:T(8,128)(2,1)S(1)}, bf16[16,2816]{1,0:T(8,128)(2,1)S(1)}, u32[]{:S(2)}, u32[]{:S(2)}) collective-permute-start(bf16[16,2816]{1,0:T(8,128)(2,1)S(1)} %pad_maximum_fusion.1.refs_0_), channel_id=1, source_target_pairs={{0,4},{1,5},{2,6},{3,7},{4,0},{5,1},{6,2},{7,3},{8,12},{9,13},{10,... | collective-permute-start | bytes 270344 | tf_op jit(solution)/shard_map/ppermute | solution.py:34
  49.8 7.0 %copy-start.1 = (bf16[2048,128]{1,0:T(8,128)(2,1)S(1)}, bf16[2048,128]{1,0:T(8,128)(2,1)}, u32[]{:S(2)}) copy-start(bf16[2048,128]{1,0:T(8,128)(2,1)} %weight_ref.1) | copy-start | bytes 1572868
  52.3 3.7 %collective-permute-start.21 = (bf16[16,2816]{1,0:T(8,128)(2,1)S(1)}, bf16[16,2816]{1,0:T(8,128)(2,1)S(1)}, u32[]{:S(2)}, u32[]{:S(2)}) collective-permute-start(bf16[16,2816]{1,0:T(8,128)(2,1)S(1)} %pad_maximum_fusion.1.refs_0_), channel_id=1, source_target_pairs={{0,1},{1,0},{2,3},{3,2},{4,5},{5,4},{6,7},{7,6},{8,9},{9,8},{10,11... | collective-permute-start | bytes 270344 | tf_op jit(solution)/shard_map/ppermute | solution.py:34
  55.0 1.3 %collective-permute-start.22 = (bf16[16,2816]{1,0:T(8,128)(2,1)S(1)}, bf16[16,2816]{1,0:T(8,128)(2,1)S(1)}, u32[]{:S(2)}, u32[]{:S(2)}) collective-permute-start(bf16[16,2816]{1,0:T(8,128)(2,1)S(1)} %collective-permute-done.17.refs_1_), channel_id=1, source_target_pairs={{0,1},{1,0},{2,3},{3,2},{4,5},{5,4},{6,7},{7,6},{8,9},{9,8},{10,11... | collective-permute-start | bytes 270344 | tf_op jit(solution)/shard_map/ppermute | solution.py:34
  55.0 1.4 %collective-permute-start.23 = (bf16[16,2816]{1,0:T(8,128)(2,1)S(1)}, bf16[16,2816]{1,0:T(8,128)(2,1)S(1)}, u32[]{:S(2)}, u32[]{:S(2)}) collective-permute-start(bf16[16,2816]{1,0:T(8,128)(2,1)S(1)} %collective-permute-done.18.refs_2_), channel_id=1, source_target_pairs={{0,1},{1,0},{2,3},{3,2},{4,5},{5,4},{6,7},{7,6},{8,9},{9,8},{10,11... | collective-permute-start | bytes 270344 | tf_op jit(solution)/shard_map/ppermute | solution.py:34
  55.5 1.3 %collective-permute-start.24 = (bf16[16,2816]{1,0:T(8,128)(2,1)S(1)}, bf16[16,2816]{1,0:T(8,128)(2,1)S(1)}, u32[]{:S(2)}, u32[]{:S(2)}) collective-permute-start(bf16[16,2816]{1,0:T(8,128)(2,1)S(1)} %collective-permute-done.19.refs_3_), channel_id=1, source_target_pairs={{0,1},{1,0},{2,3},{3,2},{4,5},{5,4},{6,7},{7,6},{8,9},{9,8},{10,11... | collective-permute-start | bytes 270344 | tf_op jit(solution)/shard_map/ppermute | solution.py:34

commit v9 on v8

--- a/solution.py
+++ b/solution.py
@@ -615,7 +615,7 @@
 
     far_block = math.gcd(extra, 4)
 
-    def far_update(before, gots, entries, name):
+    def far_update(before, gots, entries, name, far_block=far_block):
         return pl.pallas_call(
             functools.partial(far_update_kernel, far_block, blocks, own_rows, entries),
             in_specs=[SCALARS] * 2 + [WHOLE] * (3 + len(gots)) + [PLACED],
@@ -654,7 +654,7 @@
         name="output",
     )(local_columns, out_weight, out_pick, *every_normed)
     layer_out, last_got = lax.optimization_barrier((layer_out, last_got))
-    final = far_update(tied["done"], [last_got], [(2, 1, 0, 0, range(extra, heads))], "last_update")
+    final = far_update(tied["done"], [last_got], [(2, 1, 0, 0, range(extra, heads))], "last_update", math.gcd(extra, 2))
     return (layer_out[None], final)
 
 

time: 59.4 us -> 59.8 us (level)
  waiting for transfers between devices: 11.9 us -> 13.1 us
  starting transfers between devices: 25.1 us -> 24.1 us
    ppermute x26, waiting for transfers between devices: 11.9 us -> 13.1 us  [xor_permute(): lax.ppermute(block, 'rows', [(i, i ^ distance) for i in range(count)])]
    ppermute x26, starting transfers between devices: 25.1 us -> 24.1 us  [xor_permute(): lax.ppermute(block, 'rows', [(i, i ^ distance) for i in range(count)])]
  transfers between devices with their start and end apart: 26 -> 26, of which waited for: 11 -> 12; matrix products, arithmetic and copies ran while one was open for 0% -> 0% of each run, Pallas kernels for 29% -> 29%
where the time goes in v9:
time: 59.8 us; the launch traced here: 58.6 us
  starting transfers between devices  24.1 us (40%)
  Pallas kernels  20.3 us (34%)
  waiting for transfers between devices  13.1 us (22%)
  between operations  0.87 us (1%)
    ppermute x26, starting transfers between devices, xor_permute(): lax.ppermute(block, 'rows', [(i, i ^ distance) for i in range(count)])  24.1 us
    ppermute x26, waiting for transfers between devices, xor_permute(): lax.ppermute(block, 'rows', [(i, i ^ distance) for i in range(count)])  13.1 us
    pallas_call x1, Pallas kernels, per_device(): pl.pallas_call(functools.partial(near_update_kernel, recv_order, head_blo...  3.89 us
    pallas_call x1, Pallas kernels, per_device(): pl.pallas_call(functools.partial(stage_kernel, blocks, normed_order), in_...  2.93 us
    pallas_call x2, Pallas kernels, far_update(): pl.pallas_call(functools.partial(far_update_kernel, far_block, blocks, ow...  2.77 us
    pallas_call x1, Pallas kernels, per_device(): pl.pallas_call(functools.partial(fetch_kernel, blocks), in_specs=[SCALARS...  2.59 us
    pallas_call x1, Pallas kernels, per_device(): pl.pallas_call(hold_kernel, in_specs=[PLACED], out_specs=WHOLE, out_shape...  2.21 us
    pallas_call x1, Pallas kernels, per_device(): pl.pallas_call(functools.partial(pick_kernel, blocks, piece, recv_order),...  2.08 us
  transfers between devices with their start and end apart: 26, of which 12 were waited for; matrix products, arithmetic and copies ran while one was open for 0% of the time, Pallas kernels for 29%

profile of v9, /device:TPU:1, one launch (start us, length us, event | category | flops | bytes accessed | tf_op | source)
XLA Modules:
  0.0 58.6 jit_solution(5080175549261251586)
XLA Ops:
  0.6 0.0 copy-start.2
  0.6 2.6 %fetch.1 = (bf16[128,128]{1,0:T(8,128)(2,1)S(1)}, bf16[20,128,128]{2,1,0:T(8,128)(2,1)S(1)}) custom-call(s32[1]{0:T(128)} %bitcast.me_ref, s32[1,4,32]{2,1,0:T(4,128)} %parent_ref.11, s32[1,128]{1,0:T(1,128)} %tokens_ref.1, s32[1,128]{1,0:T(1,128)} %tokens_ref.1, bf16[32768,128]{1,0:T(8,128)(2,1)} %table_ref.1, bf16[8,16,128,128]{3,2,1,0:T(8,128)(2,1)} %states_ref.7), custom_call_target="tpu_custom_call" | custom-call | tf_op jit(solution)/shard_map/fetch/pallas_call | solution.py:494
  3.2 2.1 %collective-permute-start.8 = (bf16[20,128,128]{2,1,0:T(8,128)(2,1)S(1)}, bf16[20,128,128]{2,1,0:T(8,128)(2,1)S(1)}, u32[]{:S(2)}, u32[]{:S(2)}) collective-permute-start(bf16[20,128,128]{2,1,0:T(8,128)(2,1)S(1)} %get-tuple-element.59), channel_id=1, source_target_pairs={{0,2},{1,3},{2,0},{3,1},{4,6},{5,7},{6,4},{7,5},{8,10},{9,11},{10,... | collective-permute-start | bytes 1966088 | tf_op jit(solution)/shard_map/ppermute | solution.py:34
  5.4 1.2 %collective-permute-start = (bf16[128,128]{1,0:T(8,128)(2,1)S(1)}, bf16[128,128]{1,0:T(8,128)(2,1)S(1)}, u32[]{:S(2)}, u32[]{:S(2)}) collective-permute-start(bf16[128,128]{1,0:T(8,128)(2,1)S(1)} %get-tuple-element.47.x_ref), channel_id=1, source_target_pairs={{0,6},{1,7},{2,4},{3,5},{4,2},{5,3},{6,0},{7,1},{8,14},{9,15},{10,... | collective-permute-start | bytes 98312 | tf_op jit(solution)/shard_map/ppermute | solution.py:34
  6.6 0.1 broadcast_in_dim.14
  6.7 2.1 %pick.1 = (bf16[640,384]{1,0:T(8,128)(2,1)S(1)}, bf16[2,16,128,128]{3,2,1,0:T(8,128)(2,1)S(1)}) custom-call(s32[1]{0:T(128)} %bitcast.me_ref, s32[1,4,32]{2,1,0:T(4,128)} %parent_ref.11, s32[8,128]{1,0:T(8,128)S(1)} %broadcast_in_dim.15.parents_ref, bf16[8,16,128,128]{3,2,1,0:T(8,128)(2,1)} %states_ref.7), custom_call_target="tpu_custom_call" | custom-call | tf_op jit(solution)/shard_map/pick/pallas_call | solution.py:509
  8.8 0.4 collective-permute-done
  9.2 3.3 %collective-permute-start.1 = (bf16[256,128]{1,0:T(8,128)(2,1)S(1)}, bf16[256,128]{1,0:T(8,128)(2,1)S(1)}, u32[]{:S(2)}, u32[]{:S(2)}) collective-permute-start(bf16[256,128]{1,0:T(8,128)(2,1)S(1)} %pad_maximum_fusion.2.refs_0_), channel_id=1, source_target_pairs={{0,12},{1,13},{2,14},{3,15},{4,8},{5,9},{6,10},{7,11},{8,4},{9,5},... | collective-permute-start | bytes 196616 | tf_op jit(solution)/shard_map/ppermute | solution.py:34
  12.5 0.4 collective-permute-start.3
  12.8 2.9 %stage.1 = (bf16[16,128,128]{2,1,0:T(8,128)(2,1)}, bf16[16,128,128]{2,1,0:T(8,128)(2,1)}, bf16[12,128,128]{2,1,0:T(8,128)(2,1)}, f32[16,128]{1,0:T(8,128)S(1)}, bf16[128,176]{1,0:T(8,128)(2,1)S(1)}) custom-call(s32[1]{0:T(128)} %bitcast.me_ref, s32[1,4,32]{2,1,0:T(4,128)} %parent_ref.11, s32[8,128]{1,0:T(8,128)S(1)} %broadcast_in_dim.15.parents_ref, ...), custom_call_target="tpu_custom_call" | custom-call | tf_op jit(solution)/shard_map/stage/pallas_call | solution.py:520
  15.8 1.8 %collective-permute-done.2.refs_2_ = bf16[256,128]{1,0:T(8,128)(2,1)S(1)} collective-permute-done((bf16[256,128]{1,0:T(8,128)(2,1)S(1)}, bf16[256,128]{1,0:T(8,128)(2,1)S(1)}, u32[]{:S(2)}, u32[]{:S(2)}) %collective-permute-start.2) | collective-permute-done | bytes 65568 | tf_op jit(solution)/shard_map/ppermute | solution.py:34
  17.6 2.4 %collective-permute-start.4 = (bf16[256,128]{1,0:T(8,128)(2,1)S(1)}, bf16[256,128]{1,0:T(8,128)(2,1)S(1)}, u32[]{:S(2)}, u32[]{:S(2)}) collective-permute-start(bf16[256,128]{1,0:T(8,128)(2,1)S(1)} %pad_maximum_fusion.2.refs_0_), channel_id=1, source_target_pairs={{0,1},{1,0},{2,3},{3,2},{4,5},{5,4},{6,7},{7,6},{8,9},{9,8},{10,11... | collective-permute-start | bytes 196616 | tf_op jit(solution)/shard_map/ppermute | solution.py:34
  20.0 0.0 collective-permute-start.5
  20.0 0.5 collective-permute-start.6
  20.5 0.0 collective-permute-start.7
  20.5 0.4 collective-permute-done.4.refs_4_
  20.9 0.4 collective-permute-start.11
  21.3 0.2 collective-permute-start.12
  21.5 0.5 collective-permute-start.20
  22.0 0.8 %project.1 = bf16[640,128]{1,0:T(8,128)(2,1)S(1)} custom-call(s32[1]{0:T(128)} %bitcast.me_ref, bf16[3,2048,128]{2,1,0:T(8,128)(2,1)S(1)} %bitcast.11, bf16[640,384]{1,0:T(8,128)(2,1)S(1)} %get-tuple-element.54.pick_ref, bf16[256,128]{1,0:T(8,128)(2,1)S(1)} %pad_maximum_fusion.2.refs_0_, bf16[256,128]{1,0:T(8,128)(2,1)S(1)} %collective-permute-done.1.refs_1_, ...), custom_call_target="tpu_custom_call" | custom-call | tf_op jit(solution)/shard_map/project/pallas_call | solution.py:564
  22.8 0.2 collective-permute-start.9
  23.1 1.1 %collective-permute-done.9 = bf16[1,2,4,40,128]{4,3,1,0,2:T(8,128)(2,1)S(1)} collective-permute-done((bf16[1,2,4,40,128]{4,3,1,0,2:T(8,128)(2,1)S(1)}, bf16[1,2,4,40,128]{4,3,1,0,2:T(8,128)(2,1)S(1)}, u32[]{:S(2)}, u32[]{:S(2)}) %collective-permute-start.9) | collective-permute-done | bytes 81952 | tf_op jit(solution)/shard_map/ppermute | solution.py:34
  24.2 2.0 %collective-permute-start.10 = (bf16[2,1,4,40,128]{4,3,1,0,2:T(8,128)(2,1)S(1)}, bf16[2,1,4,40,128]{4,3,1,0,2:T(8,128)(2,1)S(1)}, u32[]{:S(2)}, u32[]{:S(2)}) collective-permute-start(bf16[2,1,4,40,128]{4,3,1,0,2:T(8,128)(2,1)S(1)} %get-tuple-element.97), channel_id=1, source_target_pairs={{0,6},{1,7},{2,4},{3,5},{4,2},{5,3},{6,0},{7,1},{8,14},{9,15},{10,... | collective-permute-start | bytes 245768 | tf_op jit(solution)/shard_map/ppermute | solution.py:34
  26.2 2.9 %collective-permute-done.10 = bf16[2,1,4,40,128]{4,3,1,0,2:T(8,128)(2,1)S(1)} collective-permute-done((bf16[2,1,4,40,128]{4,3,1,0,2:T(8,128)(2,1)S(1)}, bf16[2,1,4,40,128]{4,3,1,0,2:T(8,128)(2,1)S(1)}, u32[]{:S(2)}, u32[]{:S(2)}) %collective-permute-start.10) | collective-permute-done | bytes 81952 | tf_op jit(solution)/shard_map/ppermute | solution.py:34
  29.2 2.8 %collective-permute-start.13 = (bf16[2,2,1,40,128]{4,3,1,0,2:T(8,128)(2,1)S(1)}, bf16[2,2,1,40,128]{4,3,1,0,2:T(8,128)(2,1)S(1)}, u32[]{:S(2)}, u32[]{:S(2)}) collective-permute-start(bf16[2,2,1,40,128]{4,3,1,0,2:T(8,128)(2,1)S(1)} %get-tuple-element.94), channel_id=1, source_target_pairs={{0,12},{1,13},{2,14},{3,15},{4,8},{5,9},{6,10},{7,11},{8,4},{9,5},... | collective-permute-start | bytes 122888 | tf_op jit(solution)/shard_map/ppermute | solution.py:34
  32.0 0.8 %collective-permute-start.15 = (bf16[2,2,1,40,128]{4,3,1,0,2:T(8,128)(2,1)S(1)}, bf16[2,2,1,40,128]{4,3,1,0,2:T(8,128)(2,1)S(1)}, u32[]{:S(2)}, u32[]{:S(2)}) collective-permute-start(bf16[2,2,1,40,128]{4,3,1,0,2:T(8,128)(2,1)S(1)} %get-tuple-element.92), channel_id=1, source_target_pairs={{0,4},{1,5},{2,6},{3,7},{4,0},{5,1},{6,2},{7,3},{8,12},{9,13},{10,... | collective-permute-start | bytes 122888 | tf_op jit(solution)/shard_map/ppermute | solution.py:34
  32.8 2.2 %hold.1.refs_0_.states_ref = bf16[8,16,128,128]{3,2,1,0:T(8,128)(2,1)S(1)} custom-call(bf16[8,16,128,128]{3,2,1,0:T(8,128)(2,1)} %states_ref.7), custom_call_target="tpu_custom_call" | custom-call | tf_op jit(solution)/shard_map/hold/pallas_call | solution.py:541
  35.0 0.0 copy-start.3
  35.1 0.8 %collective-permute-done.14 = bf16[2,2,1,40,128]{4,3,1,0,2:T(8,128)(2,1)S(1)} collective-permute-done((bf16[2,2,1,40,128]{4,3,1,0,2:T(8,128)(2,1)S(1)}, bf16[2,2,1,40,128]{4,3,1,0,2:T(8,128)(2,1)S(1)}, u32[]{:S(2)}, u32[]{:S(2)}) %collective-permute-start.14) | collective-permute-done | bytes 40992 | tf_op jit(solution)/shard_map/ppermute | solution.py:34
  35.9 1.8 %readout.1 = (bf16[8,2816]{1,0:T(8,128)(2,1)S(1)}, bf16[16,40,128]{2,1,0:T(8,128)(2,1)S(1)}) custom-call(s32[1]{0:T(128)} %bitcast.me_ref, f32[16]{0:T(128)S(1)} %copy-done.6, f32[16,128]{1,0:T(8,128)S(1)} %get-tuple-element.52.place_ref, f32[16,128]{1,0:T(8,128)S(1)} %copy-done.4, f32[16,128]{1,0:T(8,128)S(1)} %bitcast.17, ...), custom_call_target="tpu_custom_call" | custom-call | tf_op jit(solution)/shard_map/readout/pallas_call | solution.py:588
  37.7 1.2 %collective-permute-start.16 = (bf16[8,2816]{1,0:T(8,128)(2,1)S(1)}, bf16[8,2816]{1,0:T(8,128)(2,1)S(1)}, u32[]{:S(2)}, u32[]{:S(2)}) collective-permute-start(bf16[8,2816]{1,0:T(8,128)(2,1)S(1)} %get-tuple-element.74), channel_id=1, source_target_pairs={{0,6},{1,7},{2,4},{3,5},{4,2},{5,3},{6,0},{7,1},{8,14},{9,15},{10,... | collective-permute-start | bytes 135176 | tf_op jit(solution)/shard_map/ppermute | solution.py:34
  38.9 0.2 collective-permute-start.25
  39.1 3.9 %near_update.1 = (bf16[8,16,128,128]{3,2,1,0:T(8,128)(2,1)}, bf16[16,128,16]{2,1,0:T(8,128)(2,1)S(1)}, f32[16,16,128]{2,1,0:T(8,128)S(1)}, f32[2,16,16,128]{3,2,1,0:T(8,128)S(1)}) custom-call(s32[1]{0:T(128)} %bitcast.me_ref, s32[1,4,32]{2,1,0:T(4,128)S(1)} %copy-done.3, f32[16]{0:T(128)S(1)} %copy-done.6, ...), custom_call_target="tpu_custom_call" | custom-call | tf_op jit(solution)/shard_map/near_update/pallas_call | solution.py:601
  43.0 2.5 %collective-permute-start.17 = (bf16[16,2816]{1,0:T(8,128)(2,1)S(1)}, bf16[16,2816]{1,0:T(8,128)(2,1)S(1)}, u32[]{:S(2)}, u32[]{:S(2)}) collective-permute-start(bf16[16,2816]{1,0:T(8,128)(2,1)S(1)} %pad_maximum_fusion.1.refs_0_), channel_id=1, source_target_pairs={{0,12},{1,13},{2,14},{3,15},{4,8},{5,9},{6,10},{7,11},{8,4},{9,5},... | collective-permute-start | bytes 270344 | tf_op jit(solution)/shard_map/ppermute | solution.py:34
  45.5 0.1 collective-permute-start.18
  45.6 1.1 %collective-permute-start.19 = (bf16[16,2816]{1,0:T(8,128)(2,1)S(1)}, bf16[16,2816]{1,0:T(8,128)(2,1)S(1)}, u32[]{:S(2)}, u32[]{:S(2)}) collective-permute-start(bf16[16,2816]{1,0:T(8,128)(2,1)S(1)} %pad_maximum_fusion.1.refs_0_), channel_id=1, source_target_pairs={{0,4},{1,5},{2,6},{3,7},{4,0},{5,1},{6,2},{7,3},{8,12},{9,13},{10,... | collective-permute-start | bytes 270344 | tf_op jit(solution)/shard_map/ppermute | solution.py:34
  46.6 3.0 %collective-permute-done.20 = bf16[2,16,128,128]{3,2,1,0:T(8,128)(2,1)S(1)} collective-permute-done((bf16[2,16,128,128]{3,2,1,0:T(8,128)(2,1)S(1)}, bf16[2,16,128,128]{3,2,1,0:T(8,128)(2,1)S(1)}, u32[]{:S(2)}, u32[]{:S(2)}) %collective-permute-start.20) | collective-permute-done | bytes 1048608 | tf_op jit(solution)/shard_map/ppermute | solution.py:34
  49.6 2.1 %far_update.1.refs_1_ = bf16[8,16,128,128]{3,2,1,0:T(8,128)(2,1)} custom-call(s32[1]{0:T(128)} %bitcast.me_ref, s32[1,4,32]{2,1,0:T(4,128)S(1)} %copy-done.3, bf16[16,128,16]{2,1,0:T(8,128)(2,1)S(1)} %get-tuple-element.79.turned_ref, f32[16,16,128]{2,1,0:T(8,128)S(1)} %get-tuple-element.80.values_ref, ...), custom_call_target="tpu_custom_call", output_to_operand_aliasing={{}: (9, {})} | custom-call | tf_op jit(solution)/shard_map/far_update/pallas_call | solution.py:619
  51.8 1.5 %collective-permute-done.18.refs_2_ = bf16[16,2816]{1,0:T(8,128)(2,1)S(1)} collective-permute-done((bf16[16,2816]{1,0:T(8,128)(2,1)S(1)}, bf16[16,2816]{1,0:T(8,128)(2,1)S(1)}, u32[]{:S(2)}, u32[]{:S(2)}) %collective-permute-start.18) | collective-permute-done | bytes 90144 | tf_op jit(solution)/shard_map/ppermute | solution.py:34
  53.2 1.8 %collective-permute-start.21 = (bf16[16,2816]{1,0:T(8,128)(2,1)S(1)}, bf16[16,2816]{1,0:T(8,128)(2,1)S(1)}, u32[]{:S(2)}, u32[]{:S(2)}) collective-permute-start(bf16[16,2816]{1,0:T(8,128)(2,1)S(1)} %pad_maximum_fusion.1.refs_0_), channel_id=1, source_target_pairs={{0,1},{1,0},{2,3},{3,2},{4,5},{5,4},{6,7},{7,6},{8,9},{9,8},{10,11... | collective-permute-start | bytes 270344 | tf_op jit(solution)/shard_map/ppermute | solution.py:34
  55.0 0.0 collective-permute-start.22
  55.0 0.5 collective-permute-start.23
  55.5 0.4 collective-permute-done.21.refs_4_
  55.9 0.4 collective-permute-done.22.refs_5_
  56.3 0.2 collective-permute-done.23.refs_6_
  56.4 0.4 collective-permute-done.24.refs_7_
  56.8 1.2 %output.1 = bf16[128,128]{1,0:T(8,128)(2,1)} custom-call(bf16[128,128]{1,0:T(8,128)(2,1)S(1)} %get-tuple-element.47.x_ref, bf16[2048,128]{1,0:T(8,128)(2,1)S(1)} %copy-done.1, bf16[128,176]{1,0:T(8,128)(2,1)S(1)} %get-tuple-element.48.pick_ref, bf16[16,2816]{1,0:T(8,128)(2,1)S(1)} %pad_maximum_fusion.1.refs_0_, ...), custom_call_target="tpu_custom_call" | custom-call | tf_op jit(solution)/shard_map/output/pallas_call | solution.py:647
  57.9 0.7 %last_update.1 = bf16[8,16,128,128]{3,2,1,0:T(8,128)(2,1)} custom-call(s32[1]{0:T(128)} %bitcast.me_ref, s32[1,4,32]{2,1,0:T(4,128)S(1)} %copy-done.3, bf16[16,128,16]{2,1,0:T(8,128)(2,1)S(1)} %get-tuple-element.79.turned_ref, f32[16,16,128]{2,1,0:T(8,128)S(1)} %get-tuple-element.80.values_ref, ...), custom_call_target="tpu_custom_call", output_to_operand_aliasing={{}: (6, {})} | custom-call | tf_op jit(solution)/shard_map/last_update/pallas_call | solution.py:619
  (41 shorter events, 0.2 us)
Async XLA Ops:
  0.6 6.0 %copy-start.2 = (s32[1,4,32]{2,1,0:T(4,128)S(1)}, s32[1,4,32]{2,1,0:T(4,128)}, u32[]{:S(2)}) copy-start(s32[1,4,32]{2,1,0:T(4,128)} %parent_ref.11) | copy-start | bytes 1540
  3.2 18.7 %collective-permute-start.8 = (bf16[20,128,128]{2,1,0:T(8,128)(2,1)S(1)}, bf16[20,128,128]{2,1,0:T(8,128)(2,1)S(1)}, u32[]{:S(2)}, u32[]{:S(2)}) collective-permute-start(bf16[20,128,128]{2,1,0:T(8,128)(2,1)S(1)} %get-tuple-element.59), channel_id=1, source_target_pairs={{0,2},{1,3},{2,0},{3,1},{4,6},{5,7},{6,4},{7,5},{8,10},{9,11},{10,... | collective-permute-start | bytes 1966088 | tf_op jit(solution)/shard_map/ppermute | solution.py:34
  5.4 3.8 %collective-permute-start = (bf16[128,128]{1,0:T(8,128)(2,1)S(1)}, bf16[128,128]{1,0:T(8,128)(2,1)S(1)}, u32[]{:S(2)}, u32[]{:S(2)}) collective-permute-start(bf16[128,128]{1,0:T(8,128)(2,1)S(1)} %get-tuple-element.47.x_ref), channel_id=1, source_target_pairs={{0,6},{1,7},{2,4},{3,5},{4,2},{5,3},{6,0},{7,1},{8,14},{9,15},{10,... | collective-permute-start | bytes 98312 | tf_op jit(solution)/shard_map/ppermute | solution.py:34
  6.7 15.3 %copy-start = (bf16[2048,3,128]{2,0,1:T(8,128)(2,1)S(1)}, bf16[2048,3,128]{2,0,1:T(8,128)(2,1)}, u32[]{:S(2)}) copy-start(bf16[2048,3,128]{2,0,1:T(8,128)(2,1)} %param.13) | copy-start | bytes 4718596
  9.2 6.6 %collective-permute-start.1 = (bf16[256,128]{1,0:T(8,128)(2,1)S(1)}, bf16[256,128]{1,0:T(8,128)(2,1)S(1)}, u32[]{:S(2)}, u32[]{:S(2)}) collective-permute-start(bf16[256,128]{1,0:T(8,128)(2,1)S(1)} %pad_maximum_fusion.2.refs_0_), channel_id=1, source_target_pairs={{0,12},{1,13},{2,14},{3,15},{4,8},{5,9},{6,10},{7,11},{8,4},{9,5},... | collective-permute-start | bytes 196616 | tf_op jit(solution)/shard_map/ppermute | solution.py:34
  12.5 5.1 %collective-permute-start.2 = (bf16[256,128]{1,0:T(8,128)(2,1)S(1)}, bf16[256,128]{1,0:T(8,128)(2,1)S(1)}, u32[]{:S(2)}, u32[]{:S(2)}) collective-permute-start(bf16[256,128]{1,0:T(8,128)(2,1)S(1)} %pad_maximum_fusion.2.refs_0_), channel_id=1, source_target_pairs={{0,8},{1,9},{2,10},{3,11},{4,12},{5,13},{6,14},{7,15},{8,0},{9,1},... | collective-permute-start | bytes 196616 | tf_op jit(solution)/shard_map/ppermute | solution.py:34
  12.5 5.1 %collective-permute-start.3 = (bf16[256,128]{1,0:T(8,128)(2,1)S(1)}, bf16[256,128]{1,0:T(8,128)(2,1)S(1)}, u32[]{:S(2)}, u32[]{:S(2)}) collective-permute-start(bf16[256,128]{1,0:T(8,128)(2,1)S(1)} %pad_maximum_fusion.2.refs_0_), channel_id=1, source_target_pairs={{0,4},{1,5},{2,6},{3,7},{4,0},{5,1},{6,2},{7,3},{8,12},{9,13},{10,... | collective-permute-start | bytes 196616 | tf_op jit(solution)/shard_map/ppermute | solution.py:34
  17.6 3.3 %collective-permute-start.4 = (bf16[256,128]{1,0:T(8,128)(2,1)S(1)}, bf16[256,128]{1,0:T(8,128)(2,1)S(1)}, u32[]{:S(2)}, u32[]{:S(2)}) collective-permute-start(bf16[256,128]{1,0:T(8,128)(2,1)S(1)} %pad_maximum_fusion.2.refs_0_), channel_id=1, source_target_pairs={{0,1},{1,0},{2,3},{3,2},{4,5},{5,4},{6,7},{7,6},{8,9},{9,8},{10,11... | collective-permute-start | bytes 196616 | tf_op jit(solution)/shard_map/ppermute | solution.py:34
  20.0 1.3 %collective-permute-start.5 = (bf16[256,128]{1,0:T(8,128)(2,1)S(1)}, bf16[256,128]{1,0:T(8,128)(2,1)S(1)}, u32[]{:S(2)}, u32[]{:S(2)}) collective-permute-start(bf16[256,128]{1,0:T(8,128)(2,1)S(1)} %collective-permute-done.1.refs_1_), channel_id=1, source_target_pairs={{0,1},{1,0},{2,3},{3,2},{4,5},{5,4},{6,7},{7,6},{8,9},{9,8},{10,11... | collective-permute-start | bytes 196616 | tf_op jit(solution)/shard_map/ppermute | solution.py:34
  20.0 1.4 %collective-permute-start.6 = (bf16[256,128]{1,0:T(8,128)(2,1)S(1)}, bf16[256,128]{1,0:T(8,128)(2,1)S(1)}, u32[]{:S(2)}, u32[]{:S(2)}) collective-permute-start(bf16[256,128]{1,0:T(8,128)(2,1)S(1)} %collective-permute-done.2.refs_2_), channel_id=1, source_target_pairs={{0,1},{1,0},{2,3},{3,2},{4,5},{5,4},{6,7},{7,6},{8,9},{9,8},{10,11... | collective-permute-start | bytes 196616 | tf_op jit(solution)/shard_map/ppermute | solution.py:34
  20.5 1.4 %collective-permute-start.7 = (bf16[256,128]{1,0:T(8,128)(2,1)S(1)}, bf16[256,128]{1,0:T(8,128)(2,1)S(1)}, u32[]{:S(2)}, u32[]{:S(2)}) collective-permute-start(bf16[256,128]{1,0:T(8,128)(2,1)S(1)} %collective-permute-done.3.refs_3_), channel_id=1, source_target_pairs={{0,1},{1,0},{2,3},{3,2},{4,5},{5,4},{6,7},{7,6},{8,9},{9,8},{10,11... | collective-permute-start | bytes 196616 | tf_op jit(solution)/shard_map/ppermute | solution.py:34
  20.9 8.2 %collective-permute-start.11 = (bf16[16,128,128]{2,1,0:T(8,128)(2,1)}, bf16[16,128,128]{2,1,0:T(8,128)(2,1)S(1)}, u32[]{:S(2)}, u32[]{:S(2)}) collective-permute-start(bf16[16,128,128]{2,1,0:T(8,128)(2,1)} %get-tuple-element.68), channel_id=1, source_target_pairs={{0,1},{1,0},{2,3},{3,2},{4,5},{5,4},{6,7},{7,6},{8,9},{9,8},{10,11... | collective-permute-start | bytes 1572872 | tf_op jit(solution)/shard_map/ppermute | solution.py:34
  21.3 7.9 %collective-permute-start.12 = (bf16[16,128,128]{2,1,0:T(8,128)(2,1)}, bf16[16,128,128]{2,1,0:T(8,128)(2,1)S(1)}, u32[]{:S(2)}, u32[]{:S(2)}) collective-permute-start(bf16[16,128,128]{2,1,0:T(8,128)(2,1)} %get-tuple-element.69), channel_id=1, source_target_pairs={{0,1},{1,0},{2,3},{3,2},{4,5},{5,4},{6,7},{7,6},{8,9},{9,8},{10,11... | collective-permute-start | bytes 1572872 | tf_op jit(solution)/shard_map/ppermute | solution.py:34
  21.5 28.2 %collective-permute-start.20 = (bf16[2,16,128,128]{3,2,1,0:T(8,128)(2,1)S(1)}, bf16[2,16,128,128]{3,2,1,0:T(8,128)(2,1)S(1)}, u32[]{:S(2)}, u32[]{:S(2)}) collective-permute-start(bf16[2,16,128,128]{3,2,1,0:T(8,128)(2,1)S(1)} %get-tuple-element.82), channel_id=1, source_target_pairs={{0,3},{1,2},{2,1},{3,0},{4,7},{5,6},{6,5},{7,4},{8,11},{9,10},{10,... | collective-permute-start | bytes 3145736 | tf_op jit(solution)/shard_map/ppermute | solution.py:34
  22.8 1.3 %collective-permute-start.9 = (bf16[1,2,4,40,128]{4,3,1,0,2:T(8,128)(2,1)S(1)}, bf16[1,2,4,40,128]{4,3,1,0,2:T(8,128)(2,1)S(1)}, u32[]{:S(2)}, u32[]{:S(2)}) collective-permute-start(bf16[1,2,4,40,128]{4,3,1,0,2:T(8,128)(2,1)S(1)} %copy.13), channel_id=1, source_target_pairs={{0,1},{1,0},{2,3},{3,2},{4,5},{5,4},{6,7},{7,6},{8,9},{9,8},{10,11... | collective-permute-start | bytes 245768 | tf_op jit(solution)/shard_map/ppermute | solution.py:34
  24.2 4.9 %collective-permute-start.10 = (bf16[2,1,4,40,128]{4,3,1,0,2:T(8,128)(2,1)S(1)}, bf16[2,1,4,40,128]{4,3,1,0,2:T(8,128)(2,1)S(1)}, u32[]{:S(2)}, u32[]{:S(2)}) collective-permute-start(bf16[2,1,4,40,128]{4,3,1,0,2:T(8,128)(2,1)S(1)} %get-tuple-element.97), channel_id=1, source_target_pairs={{0,6},{1,7},{2,4},{3,5},{4,2},{5,3},{6,0},{7,1},{8,14},{9,15},{10,... | collective-permute-start | bytes 245768 | tf_op jit(solution)/shard_map/ppermute | solution.py:34
  29.2 5.9 %collective-permute-start.13 = (bf16[2,2,1,40,128]{4,3,1,0,2:T(8,128)(2,1)S(1)}, bf16[2,2,1,40,128]{4,3,1,0,2:T(8,128)(2,1)S(1)}, u32[]{:S(2)}, u32[]{:S(2)}) collective-permute-start(bf16[2,2,1,40,128]{4,3,1,0,2:T(8,128)(2,1)S(1)} %get-tuple-element.94), channel_id=1, source_target_pairs={{0,12},{1,13},{2,14},{3,15},{4,8},{5,9},{6,10},{7,11},{8,4},{9,5},... | collective-permute-start | bytes 122888 | tf_op jit(solution)/shard_map/ppermute | solution.py:34
  32.0 3.9 %collective-permute-start.14 = (bf16[2,2,1,40,128]{4,3,1,0,2:T(8,128)(2,1)S(1)}, bf16[2,2,1,40,128]{4,3,1,0,2:T(8,128)(2,1)S(1)}, u32[]{:S(2)}, u32[]{:S(2)}) collective-permute-start(bf16[2,2,1,40,128]{4,3,1,0,2:T(8,128)(2,1)S(1)} %get-tuple-element.93), channel_id=1, source_target_pairs={{0,8},{1,9},{2,10},{3,11},{4,12},{5,13},{6,14},{7,15},{8,0},{9,1},... | collective-permute-start | bytes 122888 | tf_op jit(solution)/shard_map/ppermute | solution.py:34
  32.0 3.9 %copy-start.4 = (f32[16,128]{1,0:T(8,128)S(1)}, f32[16,128]{1,0:T(8,128)}, u32[]{:S(2)}) copy-start(f32[16,128]{1,0:T(8,128)} %gate_ref.3) | copy-start | bytes 24580
  32.0 3.9 %copy-start.5 = (f32[2048]{0:T(1024)S(1)}, f32[2048]{0:T(1024)}, u32[]{:S(2)}) copy-start(f32[2048]{0:T(1024)} %param.16) | copy-start | bytes 24580
  32.0 3.9 %copy-start.6 = (f32[16]{0:T(128)S(1)}, f32[16]{0:T(128)}, u32[]{:S(2)}) copy-start(f32[16]{0:T(128)} %bias_ref.3) | copy-start | bytes 196
  32.0 3.8 %collective-permute-start.15 = (bf16[2,2,1,40,128]{4,3,1,0,2:T(8,128)(2,1)S(1)}, bf16[2,2,1,40,128]{4,3,1,0,2:T(8,128)(2,1)S(1)}, u32[]{:S(2)}, u32[]{:S(2)}) collective-permute-start(bf16[2,2,1,40,128]{4,3,1,0,2:T(8,128)(2,1)S(1)} %get-tuple-element.92), channel_id=1, source_target_pairs={{0,4},{1,5},{2,6},{3,7},{4,0},{5,1},{6,2},{7,3},{8,12},{9,13},{10,... | collective-permute-start | bytes 122888 | tf_op jit(solution)/shard_map/ppermute | solution.py:34
  35.0 3.8 %copy-start.7 = (bf16[12,128,128]{2,1,0:T(8,128)(2,1)S(1)}, bf16[12,128,128]{2,1,0:T(8,128)(2,1)}, u32[]{:S(2)}) copy-start(bf16[12,128,128]{2,1,0:T(8,128)(2,1)} %get-tuple-element.88) | copy-start | bytes 1179652
  35.0 4.0 %copy-start.3 = (s32[1,4,32]{2,1,0:T(4,128)S(1)}, s32[1,4,32]{2,1,0:T(4,128)}, u32[]{:S(2)}) copy-start(s32[1,4,32]{2,1,0:T(4,128)} %parent_ref.11) | copy-start | bytes 1540
  37.7 5.3 %collective-permute-start.16 = (bf16[8,2816]{1,0:T(8,128)(2,1)S(1)}, bf16[8,2816]{1,0:T(8,128)(2,1)S(1)}, u32[]{:S(2)}, u32[]{:S(2)}) collective-permute-start(bf16[8,2816]{1,0:T(8,128)(2,1)S(1)} %get-tuple-element.74), channel_id=1, source_target_pairs={{0,6},{1,7},{2,4},{3,5},{4,2},{5,3},{6,0},{7,1},{8,14},{9,15},{10,... | collective-permute-start | bytes 135176 | tf_op jit(solution)/shard_map/ppermute | solution.py:34
  38.9 19.1 %collective-permute-start.25 = (bf16[12,128,128]{2,1,0:T(8,128)(2,1)S(1)}, bf16[12,128,128]{2,1,0:T(8,128)(2,1)S(1)}, u32[]{:S(2)}, u32[]{:S(2)}) collective-permute-start(bf16[12,128,128]{2,1,0:T(8,128)(2,1)S(1)} %copy-done.7), channel_id=1, source_target_pairs={{0,2},{1,3},{2,0},{3,1},{4,6},{5,7},{6,4},{7,5},{8,10},{9,11},{10,... | collective-permute-start | bytes 1179656 | tf_op jit(solution)/shard_map/ppermute | solution.py:34
  43.0 8.7 %collective-permute-start.17 = (bf16[16,2816]{1,0:T(8,128)(2,1)S(1)}, bf16[16,2816]{1,0:T(8,128)(2,1)S(1)}, u32[]{:S(2)}, u32[]{:S(2)}) collective-permute-start(bf16[16,2816]{1,0:T(8,128)(2,1)S(1)} %pad_maximum_fusion.1.refs_0_), channel_id=1, source_target_pairs={{0,12},{1,13},{2,14},{3,15},{4,8},{5,9},{6,10},{7,11},{8,4},{9,5},... | collective-permute-start | bytes 270344 | tf_op jit(solution)/shard_map/ppermute | solution.py:34
  45.5 7.8 %collective-permute-start.18 = (bf16[16,2816]{1,0:T(8,128)(2,1)S(1)}, bf16[16,2816]{1,0:T(8,128)(2,1)S(1)}, u32[]{:S(2)}, u32[]{:S(2)}) collective-permute-start(bf16[16,2816]{1,0:T(8,128)(2,1)S(1)} %pad_maximum_fusion.1.refs_0_), channel_id=1, source_target_pairs={{0,8},{1,9},{2,10},{3,11},{4,12},{5,13},{6,14},{7,15},{8,0},{9,1},... | collective-permute-start | bytes 270344 | tf_op jit(solution)/shard_map/ppermute | solution.py:34
  45.6 7.7 %collective-permute-start.19 = (bf16[16,2816]{1,0:T(8,128)(2,1)S(1)}, bf16[16,2816]{1,0:T(8,128)(2,1)S(1)}, u32[]{:S(2)}, u32[]{:S(2)}) collective-permute-start(bf16[16,2816]{1,0:T(8,128)(2,1)S(1)} %pad_maximum_fusion.1.refs_0_), channel_id=1, source_target_pairs={{0,4},{1,5},{2,6},{3,7},{4,0},{5,1},{6,2},{7,3},{8,12},{9,13},{10,... | collective-permute-start | bytes 270344 | tf_op jit(solution)/shard_map/ppermute | solution.py:34
  49.6 7.2 %copy-start.1 = (bf16[2048,128]{1,0:T(8,128)(2,1)S(1)}, bf16[2048,128]{1,0:T(8,128)(2,1)}, u32[]{:S(2)}) copy-start(bf16[2048,128]{1,0:T(8,128)(2,1)} %weight_ref.1) | copy-start | bytes 1572868
  53.2 2.7 %collective-permute-start.21 = (bf16[16,2816]{1,0:T(8,128)(2,1)S(1)}, bf16[16,2816]{1,0:T(8,128)(2,1)S(1)}, u32[]{:S(2)}, u32[]{:S(2)}) collective-permute-start(bf16[16,2816]{1,0:T(8,128)(2,1)S(1)} %pad_maximum_fusion.1.refs_0_), channel_id=1, source_target_pairs={{0,1},{1,0},{2,3},{3,2},{4,5},{5,4},{6,7},{7,6},{8,9},{9,8},{10,11... | collective-permute-start | bytes 270344 | tf_op jit(solution)/shard_map/ppermute | solution.py:34
  55.0 1.3 %collective-permute-start.22 = (bf16[16,2816]{1,0:T(8,128)(2,1)S(1)}, bf16[16,2816]{1,0:T(8,128)(2,1)S(1)}, u32[]{:S(2)}, u32[]{:S(2)}) collective-permute-start(bf16[16,2816]{1,0:T(8,128)(2,1)S(1)} %collective-permute-done.17.refs_1_), channel_id=1, source_target_pairs={{0,1},{1,0},{2,3},{3,2},{4,5},{5,4},{6,7},{7,6},{8,9},{9,8},{10,11... | collective-permute-start | bytes 270344 | tf_op jit(solution)/shard_map/ppermute | solution.py:34
  55.0 1.4 %collective-permute-start.23 = (bf16[16,2816]{1,0:T(8,128)(2,1)S(1)}, bf16[16,2816]{1,0:T(8,128)(2,1)S(1)}, u32[]{:S(2)}, u32[]{:S(2)}) collective-permute-start(bf16[16,2816]{1,0:T(8,128)(2,1)S(1)} %collective-permute-done.18.refs_2_), channel_id=1, source_target_pairs={{0,1},{1,0},{2,3},{3,2},{4,5},{5,4},{6,7},{7,6},{8,9},{9,8},{10,11... | collective-permute-start | bytes 270344 | tf_op jit(solution)/shard_map/ppermute | solution.py:34
  55.5 1.3 %collective-permute-start.24 = (bf16[16,2816]{1,0:T(8,128)(2,1)S(1)}, bf16[16,2816]{1,0:T(8,128)(2,1)S(1)}, u32[]{:S(2)}, u32[]{:S(2)}) collective-permute-start(bf16[16,2816]{1,0:T(8,128)(2,1)S(1)} %collective-permute-done.19.refs_3_), channel_id=1, source_target_pairs={{0,1},{1,0},{2,3},{3,2},{4,5},{5,4},{6,7},{7,6},{8,9},{9,8},{10,11... | collective-permute-start | bytes 270344 | tf_op jit(solution)/shard_map/ppermute | solution.py:34
